TPU v7x, 32 devices: a whole 2x2x4 slice. The times are simulated.
32 devices in a mesh: crops: 2 (over x), tile: 16 (over z, y, core).
Axes of the slice: x: 2, y: 2, z: 4, core: 2. Of those that a mesh axis runs over, the one named last changes fastest.
Arguments:
- pair_input: bfloat16 [1024, 512, 128], P(('crops', 'tile')), parts along dimension 0, may hold values from -40 to 40
- d_update: bfloat16 [1024, 512, 128], P(('crops', 'tile')), parts along dimension 0, may hold values from -6 to 6
- token_mask: int32 [1024], P('crops'), parts along dimension 0, may hold values 0 or 1
- ln_in_gain: float32 [128], replicated, may hold values from 0.25 to 1.75
- ln_in_bias: float32 [128], replicated, may hold values from -2 to 2
- w_ab: bfloat16 [128, 512], replicated, may hold values from -0.5 to 0.5
- w_gate: bfloat16 [128, 128], replicated, may hold values from -0.5 to 0.5
- ln_out_gain: float32 [128], replicated, may hold values from 0.25 to 1.75
- ln_out_bias: float32 [128], replicated, may hold values from -2 to 2
- w_out: bfloat16 [128, 128], replicated, may hold values from -0.5 to 0.5
Outputs:
- pair_grad: bfloat16 [1024, 512, 128], P(('crops', 'tile')), parts along dimension 0
- grad_w_ab: float32 [256, 512], P('crops'), parts along dimension 0
- grad_w_gate: float32 [256, 128], P('crops'), parts along dimension 0
- grad_w_out: float32 [256, 128], P('crops'), parts along dimension 0
There are 2 independent parts, one for each index of `crops`. A program takes and returns all parts, laid end to end along the dimension named above; an argument that names none is the same for every part. Nothing has to cross between parts.
All inputs are finite; a program needn't handle non-finite values.
Results may differ from a plain program's by a relative error of at most 0.015.
Values may be sent and summed in bfloat16 or wider, within the bound.
No kernel may reach another device: no remote copies, remote signals or barrier semaphores. Data moves between devices by JAX's collectives and lax.ppermute only.
A program may use at most 192 MiB of HBM per device.

v0:
```python
import jax
import jax.numpy as jnp
from jax import lax
from jax.sharding import PartitionSpec as P

EPS = 1e-05


def norm_stats(value, axis_id):
    center = jnp.mean(value, axis=axis_id, keepdims=True)
    centered = value - center
    variance = jnp.mean(centered * centered, axis=axis_id, keepdims=True)
    inv_std = lax.rsqrt(variance + EPS)
    return (centered * inv_std, inv_std)


def norm_back(upstream, scaled, inv_std, axis_id):
    mean_up = jnp.mean(upstream, axis=axis_id, keepdims=True)
    mean_cross = jnp.mean(upstream * scaled, axis=axis_id, keepdims=True)
    return inv_std * (upstream - mean_up - scaled * mean_cross)


def send_factors(factor_a, factor_b):
    moved = (
        lax.all_to_all(factor_a, "tile", split_axis=2, concat_axis=0, tiled=True),
        lax.all_to_all(factor_b, "tile", split_axis=2, concat_axis=0, tiled=True),
    )
    owners = (jnp.transpose(moved[0], (2, 0, 1)), jnp.transpose(moved[1], (2, 0, 1)))
    return owners


def return_products(owner_prod):
    tiles = lax.all_to_all(
        jnp.transpose(owner_prod, (1, 2, 0)), "tile", split_axis=0, concat_axis=2, tiled=True
    )
    return tiles


def send_grads(grad_prod):
    owners = jnp.transpose(
        lax.all_to_all(grad_prod, "tile", split_axis=2, concat_axis=0, tiled=True), (2, 0, 1)
    )
    return owners


def return_grads(owner_fac_a, owner_fac_b):
    tiles = (
        lax.all_to_all(
            jnp.transpose(owner_fac_a, (1, 2, 0)), "tile", split_axis=0, concat_axis=2, tiled=True
        ),
        lax.all_to_all(
            jnp.transpose(owner_fac_b, (1, 2, 0)), "tile", split_axis=0, concat_axis=2, tiled=True
        ),
    )
    return tiles


def body(
    pair_input,
    d_update,
    token_mask,
    ln_in_gain,
    ln_in_bias,
    w_ab,
    w_gate,
    ln_out_gain,
    ln_out_bias,
    w_out,
):
    row_count = pair_input.shape[0]
    hidden = w_out.shape[0]
    crop_len = pair_input.shape[1]
    first_row = lax.axis_index("tile") * row_count
    col_valid = token_mask.astype(jnp.float32)
    row_valid = lax.dynamic_slice_in_dim(col_valid, first_row, row_count)
    pair_mask = row_valid[:, None] * col_valid[None, :]
    layout_form = "rne"
    chan_axis = 2
    gain_shape = (hidden,)
    mask_view = pair_mask[:, :, None]
    z_hat, inv_in = norm_stats(pair_input.astype(jnp.float32), 2)
    normed = (z_hat * ln_in_gain + ln_in_bias).astype(jnp.bfloat16)
    projected = jnp.einsum(
        "rnc,ce->" + layout_form, normed, w_ab, preferred_element_type=jnp.float32
    )
    value_a = lax.slice_in_dim(projected, 0, hidden, axis=chan_axis)
    gate_a = lax.slice_in_dim(projected, hidden, 2 * hidden, axis=chan_axis)
    value_b = lax.slice_in_dim(projected, 2 * hidden, 3 * hidden, axis=chan_axis)
    gate_b = lax.slice_in_dim(projected, 3 * hidden, 4 * hidden, axis=chan_axis)
    sig_a = jax.nn.sigmoid(gate_a)
    sig_b = jax.nn.sigmoid(gate_b)
    factor_a = (mask_view * sig_a * value_a).astype(jnp.bfloat16)
    factor_b = (mask_view * sig_b * value_b).astype(jnp.bfloat16)
    gate = jax.nn.sigmoid(
        jnp.einsum("rnc,cd->rnd", normed, w_gate, preferred_element_type=jnp.float32)
    )
    owner_a, owner_b = send_factors(factor_a, factor_b)
    owner_prod = jnp.einsum(
        "hik,hjk->hij", owner_a, owner_b, preferred_element_type=jnp.float32
    ).astype(jnp.bfloat16)
    product = return_products(owner_prod)
    x_hat, inv_std = norm_stats(product.astype(jnp.float32), chan_axis)
    x_norm = (x_hat * ln_out_gain + ln_out_bias).astype(jnp.bfloat16)
    out_lin = jnp.einsum(
        layout_form + ",ec->rnc", x_norm, w_out, preferred_element_type=jnp.float32
    )
    upstream = d_update.astype(jnp.float32)
    grad_lin = (upstream * gate).astype(jnp.bfloat16)
    gate_back = (upstream * out_lin * gate * (1.0 - gate)).astype(jnp.bfloat16)
    grad_xnorm = jnp.einsum(
        "rnc,ec->" + layout_form, grad_lin, w_out, preferred_element_type=jnp.float32
    )
    grad_prod = norm_back(grad_xnorm * ln_out_gain, x_hat, inv_std, chan_axis).astype(jnp.bfloat16)
    owner_grad = send_grads(grad_prod)
    owner_fac_a = jnp.einsum(
        "hij,hjk->hik", owner_grad, owner_b, preferred_element_type=jnp.float32
    ).astype(jnp.bfloat16)
    owner_fac_b = jnp.einsum(
        "hij,hik->hjk", owner_grad, owner_a, preferred_element_type=jnp.float32
    ).astype(jnp.bfloat16)
    grad_fac_a, grad_fac_b = return_grads(owner_fac_a, owner_fac_b)
    masked_a = grad_fac_a.astype(jnp.float32) * mask_view
    masked_b = grad_fac_b.astype(jnp.float32) * mask_view
    grad_proj = jnp.concatenate(
        [
            masked_a * sig_a,
            masked_a * value_a * sig_a * (1.0 - sig_a),
            masked_b * sig_b,
            masked_b * value_b * sig_b * (1.0 - sig_b),
        ],
        axis=chan_axis,
    ).astype(jnp.bfloat16)
    grad_normed = jnp.einsum(
        layout_form + ",ce->rnc", grad_proj, w_ab, preferred_element_type=jnp.float32
    )
    grad_normed = grad_normed + jnp.einsum(
        "rnd,cd->rnc", gate_back, w_gate, preferred_element_type=jnp.float32
    )
    pair_grad = norm_back(grad_normed * ln_in_gain, z_hat, inv_in, 2).astype(jnp.bfloat16)
    local_ab = jnp.einsum(
        "rnc," + layout_form + "->ce", normed, grad_proj, preferred_element_type=jnp.float32
    )
    local_gate = jnp.einsum("rnc,rnd->cd", normed, gate_back, preferred_element_type=jnp.float32)
    local_out = jnp.einsum(
        layout_form + ",rnc->ec", x_norm, grad_lin, preferred_element_type=jnp.float32
    )
    sum_ab, sum_gate, sum_out = (
        lax.psum(local_ab.astype(jnp.bfloat16), "tile").astype(jnp.float32),
        lax.psum(local_gate.astype(jnp.bfloat16), "tile").astype(jnp.float32),
        lax.psum(local_out.astype(jnp.bfloat16), "tile").astype(jnp.float32),
    )
    return (pair_grad, sum_ab / crop_len, sum_gate / crop_len, sum_out / crop_len)


def solution(mesh):
    placed = (
        P(("crops", "tile"), None, None),
        P(("crops", "tile"), None, None),
        P("crops"),
        P(),
        P(),
        P(),
        P(),
        P(),
        P(),
        P(),
    )
    return jax.shard_map(
        body,
        mesh=mesh,
        in_specs=placed,
        out_specs=(
            P(("crops", "tile"), None, None),
            P("crops", None),
            P("crops", None),
            P("crops", None),
        ),
        check_vma=False,
    )
```

profile of v0, /device:TPU:0, one launch (start us, length us, event | category | flops | bytes accessed | tf_op | source)
XLA Modules:
  0.0 886.8 jit_solution(13782229884059671087)
XLA Ops:
  8.1 6.4 copy.36
  14.5 3.1 convert_reduce_fusion
  17.6 3.6 fusion.11
  21.9 2.1 fusion.6
  24.0 1.9 copy-done.4
  26.0 13.3 %fusion.32 = f32[32,512,512]{1,2,0:T(8,128)} fusion(bf16[32,512,128]{1,2,0:T(8,128)(2,1)S(1)} %fusion.6, bf16[128,512]{1,0:T(8,128)(2,1)S(1)} %copy-done), kind=kOutput, calls=%fused_computation.62 | convolution fusion | flops 2147483648 | bytes 37879808 | tf_op jit(solution)/shard_map/rnc,ce->rne/dot_general | solution.py:83
  39.3 15.4 %multiply_convert_fusion.5 = (bf16[32,512,128]{1,2,0:T(8,128)(2,1)S(1)}, bf16[32,512,128]{1,2,0:T(8,128)(2,1)}) fusion(f32[32,512,512]{1,2,0:T(8,128)} %fusion.32, f32[32,512]{1,0:T(8,128)S(1)} %broadcast_multiply_fusion), kind=kLoop, calls=%fused_computation.46 | loop fusion | flops 25165824 | bytes 42008576 | tf_op jit(solution)/shard_map/convert_element_type | solution.py:93
  54.7 4.4 copy.41
  59.1 7.4 all-to-all-start.1
  66.6 6.5 copy.39
  73.1 71.2 %all-to-all-done.1 = bf16[32,512,128]{1,0,2:T(8,128)(2,1)} async-done(((bf16[32,512,128]{1,0,2:T(8,128)(2,1)}), bf16[32,512,128]{1,0,2:T(8,128)(2,1)}, u32[]{:S(2)}, u32[]{:S(2)}) %all-to-all-start.1) | async-done | bytes 4194336 | tf_op jit(solution)/shard_map/all_to_all | solution.py:26
  144.2 19.7 %all-to-all-start = ((bf16[32,512,128]{1,0,2:T(8,128)(2,1)}), bf16[32,512,128]{1,0,2:T(8,128)(2,1)}, u32[]{:S(2)}, u32[]{:S(2)}) async-start(bf16[32,512,128]{1,0,2:T(8,128)(2,1)} %copy.39), calls=%async_computation | async-start | bytes 8388608 | tf_op jit(solution)/shard_map/all_to_all | solution.py:25
  163.9 4.7 copy.42
  168.7 72.9 %all-to-all-done = bf16[32,512,128]{1,0,2:T(8,128)(2,1)} async-done(((bf16[32,512,128]{1,0,2:T(8,128)(2,1)}), bf16[32,512,128]{1,0,2:T(8,128)(2,1)}, u32[]{:S(2)}, u32[]{:S(2)}) %all-to-all-start) | async-done | bytes 4194336 | tf_op jit(solution)/shard_map/all_to_all | solution.py:25
  241.6 2.7 copy.40
  245.1 2.4 convert_bitcast_fusion.2
  247.4 4.3 copy.43
  251.8 20.0 %all-to-all-start.2 = ((bf16[512,512,8]{1,2,0:T(8,128)(2,1)}), bf16[512,512,8]{1,2,0:T(8,128)(2,1)}, u32[]{:S(2)}, u32[]{:S(2)}) async-start(bf16[512,512,8]{1,2,0:T(8,128)(2,1)} %copy.43), calls=%async_computation.2 | async-start | bytes 8388608 | tf_op jit(solution)/shard_map/all_to_all | solution.py:33
  271.8 6.5 copy.45
  278.3 8.3 add_divide_fusion
  286.6 62.8 %all-to-all-done.2 = bf16[512,512,8]{1,2,0:T(8,128)(2,1)} async-done(((bf16[512,512,8]{1,2,0:T(8,128)(2,1)}), bf16[512,512,8]{1,2,0:T(8,128)(2,1)}, u32[]{:S(2)}, u32[]{:S(2)}) %all-to-all-start.2) | async-done | bytes 4194336 | tf_op jit(solution)/shard_map/all_to_all | solution.py:33
  349.5 3.4 bitcast_convert_fusion
  354.1 1.4 fusion.24
  357.8 5.2 multiply_reduce_fusion.1
  363.0 6.9 add_convert_fusion
  369.9 2.4 copy.49
  372.3 112.2 %all_to_all.81 = bf16[32,512,128]{1,0,2:T(8,128)(2,1)S(1)} all-to-all(bf16[32,512,128]{1,0,2:T(8,128)(2,1)S(1)} %copy.49), channel_id=1, replica_groups=mesh['crops'=2,'tile'=16] {'tile'}, dimensions={2} | all-to-all | bytes 8388608 | tf_op jit(solution)/shard_map/all_to_all | solution.py:41
  484.8 2.4 convert_bitcast_fusion
  487.2 4.3 copy.54
  491.5 5.4 all-to-all-start.5
  496.9 5.8 convert_bitcast_fusion.1
  502.7 4.3 copy.51
  507.1 67.5 %all-to-all-done.5 = bf16[512,512,8]{1,2,0:T(8,128)(2,1)} async-done(((bf16[512,512,8]{1,2,0:T(8,128)(2,1)}), bf16[512,512,8]{1,2,0:T(8,128)(2,1)}, u32[]{:S(2)}, u32[]{:S(2)}) %all-to-all-start.5) | async-done | bytes 4194336 | tf_op jit(solution)/shard_map/all_to_all | solution.py:51
  574.6 19.7 %all-to-all-start.4 = ((bf16[512,512,8]{1,2,0:T(8,128)(2,1)}), bf16[512,512,8]{1,2,0:T(8,128)(2,1)}, u32[]{:S(2)}, u32[]{:S(2)}) async-start(bf16[512,512,8]{1,2,0:T(8,128)(2,1)} %copy.51), calls=%async_computation.4 | async-start | bytes 8388608 | tf_op jit(solution)/shard_map/all_to_all | solution.py:48
  594.6 8.4 fusion.15
  603.1 1.9 fusion.29
  605.2 1.6 copy-done.3
  608.0 5.6 fusion.30
  613.7 121.8 %all-reduce.6.cloned.1.call-done = (bf16[128,128]{1,0:T(8,128)(2,1)}, bf16[128,128]{1,0:T(8,128)(2,1)}) async-done(((bf16[128,128]{1,0:T(8,128)(2,1)}, bf16[128,128]{1,0:T(8,128)(2,1)}), (bf16[128,128]{1,0:T(8,128)(2,1)}, bf16[128,128]{1,0:T(8,128)(2,1)})) %all-reduce.6.cloned.1.call-update) | async-done | bytes 65552 | tf_op jit(solution)/shard_map/psum | solution.py:149
  738.3 18.1 %multiply_convert_fusion.3 = (bf16[32,512,128]{1,2,0:T(8,128)(2,1)S(1)}, bf16[32,512,128]{1,2,0:T(8,128)(2,1)S(1)}, bf16[32,512,128]{1,2,0:T(8,128)(2,1)}, bf16[32,512,128]{1,2,0:T(8,128)(2,1)}) fusion(f32[32,512]{1,0:T(8,128)S(1)} %broadcast_multiply_fusion, f32[32,512,512]{1,2,0:T(8,128)} %fusion.32, bf16[16,32,512,8]{2,3,1,0:T(8,128)(2,1)} %bitcast.41, ...), kind=kLoop, calls=%fused_computation.42 | loop fusion | flops 50331648 | bytes 58785792 | tf_op jit(solution)/shard_map/convert.11
  756.4 2.0 copy-done.9
  759.7 10.0 %fusion.28 = bf16[128,512]{1,0:T(8,128)(2,1)} fusion(bf16[32,512,128]{1,2,0:T(8,128)(2,1)S(1)} %copy-done.6, bf16[32,512,128]{1,2,0:T(8,128)(2,1)} %get-tuple-element.22, bf16[32,512,128]{1,2,0:T(8,128)(2,1)} %get-tuple-element.23, bf16[32,512,128]{1,2,0:T(8,128)(2,1)S(1)} %get-tuple-element.19, bf16[32,512,128]{1,2,0:T(8,128)(2,1)S(1)} %get-tuple-element.18), kind=kOutput, calls=%fused_computation.55 | convolution fusion | flops 2214658048 | bytes 21102592 | tf_op jit(solution)/shard_map/rnc,rne->ce/dot_general | solution.py:140
  769.7 9.8 %fusion.26 = f32[32,512,128]{1,2,0:T(8,128)} fusion(bf16[32,512,128]{1,2,0:T(8,128)(2,1)} %get-tuple-element.22, bf16[32,512,128]{1,2,0:T(8,128)(2,1)} %get-tuple-element.23, bf16[32,512,128]{1,2,0:T(8,128)(2,1)} %copy-done.10, bf16[32,512,128]{1,2,0:T(8,128)(2,1)} %copy-done.9, bf16[128,512]{1,0:T(8,128)(2,1)S(1)} %copy-done), kind=kOutput, calls=%fused_computation.53 | convolution fusion | flops 2214592512 | bytes 25296896 | tf_op jit(solution)/shard_map/rne,ce->rnc/dot_general | solution.py:133
  779.5 9.6 %fusion.43 = (f32[32,512]{1,0:T(8,128)S(1)}, f32[32,512]{1,0:T(8,128)S(1)}, f32[32,512,128]{1,2,0:T(8,128)}) fusion(f32[32,512]{1,0:T(8,128)S(1)} %copy-done.18, f32[32,512]{1,0:T(8,128)S(1)} %copy-done.16, bf16[32,512,128]{1,2,0:T(8,128)(2,1)} %copy.36, f32[128]{0:T(128)S(1)} %copy-done.23, f32[32,512,128]{1,2,0:T(8,128)} %fusion.26, ...), kind=kOutput, calls=%fused_computation.83 | convolution fusion | flops 553615360 | bytes 25461248 | tf_op jit(solution)/shard_map/rnd,cd->rnc/dot_general | solution.py:136
  789.1 7.3 fusion.10
  796.4 6.4 copy.63
  802.8 75.1 %all-reduce.4.cloned.1.call-done = bf16[128,512]{1,0:T(8,128)(2,1)} async-done(((bf16[128,512]{1,0:T(8,128)(2,1)}), bf16[128,512]{1,0:T(8,128)(2,1)}) %all-reduce.4.cloned.1.call-update) | async-done | bytes 131088 | tf_op jit(solution)/shard_map/psum | solution.py:148
  877.9 1.6 convert_multiply_fusion.2
  (73 shorter events, 12.0 us)
Async XLA Ops:
  7.2 18.8 %copy-start = (bf16[128,512]{1,0:T(8,128)(2,1)S(1)}, bf16[128,512]{1,0:T(8,128)(2,1)}, u32[]{:S(2)}) copy-start(bf16[128,512]{1,0:T(8,128)(2,1)} %param.15) | copy-start | bytes 393220
  8.1 13.8 %copy-start.22 = (f32[128]{0:T(128)S(1)}, f32[128]{0:T(128)}, u32[]{:S(2)}) copy-start(f32[128]{0:T(128)} %param.13) | copy-start | bytes 1540
  8.1 13.8 %copy-start.24 = (f32[128]{0:T(128)S(1)}, f32[128]{0:T(128)}, u32[]{:S(2)}) copy-start(f32[128]{0:T(128)} %param.14) | copy-start | bytes 1540
  14.5 7.4 copy-start.1
  17.6 3.6 copy-start.15
  21.3 0.6 copy-start.17
  24.0 1.9 copy-start.4
  59.1 85.1 %all-to-all-start.1 = ((bf16[32,512,128]{1,0,2:T(8,128)(2,1)}), bf16[32,512,128]{1,0,2:T(8,128)(2,1)}, u32[]{:S(2)}, u32[]{:S(2)}) async-start(bf16[32,512,128]{1,0,2:T(8,128)(2,1)} %copy.41), calls=%async_computation.1 | async-start | bytes 8388608 | tf_op jit(solution)/shard_map/all_to_all | solution.py:26
  144.2 97.4 %all-to-all-start = ((bf16[32,512,128]{1,0,2:T(8,128)(2,1)}), bf16[32,512,128]{1,0,2:T(8,128)(2,1)}, u32[]{:S(2)}, u32[]{:S(2)}) async-start(bf16[32,512,128]{1,0,2:T(8,128)(2,1)} %copy.39), calls=%async_computation | async-start | bytes 8388608 | tf_op jit(solution)/shard_map/all_to_all | solution.py:25
  241.6 3.4 copy-start.11
  244.3 3.1 copy-start.12
  251.8 26.5 %copy-start.20 = (bf16[128,128]{1,0:T(8,128)(2,1)S(1)}, bf16[128,128]{1,0:T(8,128)(2,1)}, u32[]{:S(2)}) copy-start(bf16[128,128]{1,0:T(8,128)(2,1)} %param.16) | copy-start | bytes 98308
  251.8 97.7 %all-to-all-start.2 = ((bf16[512,512,8]{1,2,0:T(8,128)(2,1)}), bf16[512,512,8]{1,2,0:T(8,128)(2,1)}, u32[]{:S(2)}, u32[]{:S(2)}) async-start(bf16[512,512,8]{1,2,0:T(8,128)(2,1)} %copy.43), calls=%async_computation.2 | async-start | bytes 8388608 | tf_op jit(solution)/shard_map/all_to_all | solution.py:33
  352.8 2.7 slice-start
  352.8 3.5 copy-start.2
  352.9 3.5 copy-start.19
  352.9 3.4 copy-start.21
  354.1 3.7 slice-start.1
  357.8 5.2 copy-start.25
  372.3 112.5 %copy-start.13 = (bf16[32,512,16,8]{1,0,2,3:T(8,128)(2,1)S(1)}, bf16[32,512,16,8]{1,0,2,3:T(8,128)(2,1)}, u32[]{:S(2)}) copy-start(bf16[32,512,16,8]{1,0,2,3:T(8,128)(2,1)} %copy-done.12) | copy-start | bytes 12582916
  484.8 2.4 copy-start.14
  491.5 83.0 %all-to-all-start.5 = ((bf16[512,512,8]{1,2,0:T(8,128)(2,1)}), bf16[512,512,8]{1,2,0:T(8,128)(2,1)}, u32[]{:S(2)}, u32[]{:S(2)}) async-start(bf16[512,512,8]{1,2,0:T(8,128)(2,1)} %copy.54), calls=%async_computation.5 | async-start | bytes 8388608 | tf_op jit(solution)/shard_map/all_to_all | solution.py:51
  574.6 163.7 %all-to-all-start.4 = ((bf16[512,512,8]{1,2,0:T(8,128)(2,1)}), bf16[512,512,8]{1,2,0:T(8,128)(2,1)}, u32[]{:S(2)}, u32[]{:S(2)}) async-start(bf16[512,512,8]{1,2,0:T(8,128)(2,1)} %copy.51), calls=%async_computation.4 | async-start | bytes 8388608 | tf_op jit(solution)/shard_map/all_to_all | solution.py:48
  594.3 141.2 %all-reduce.6.cloned.1.call-start = ((), (), s32[]{:S(2)}) async-start(), calls=%async_computation.7 | async-start | bytes 131072 | tf_op jit(solution)/shard_map/psum | solution.py:149
  594.6 8.5 copy-start.5
  603.0 2.2 copy-start.7
  603.0 3.7 copy-start.3
  603.1 5.0 copy-start.8
  613.6 264.2 %all-reduce.4.cloned.1.call-start = ((), (), s32[]{:S(2)}) async-start(), calls=%async_computation.6 | async-start | bytes 262144 | tf_op jit(solution)/shard_map/psum | solution.py:148
  738.3 21.4 %copy-start.6 = (bf16[32,512,128]{1,2,0:T(8,128)(2,1)S(1)}, bf16[32,512,128]{1,2,0:T(8,128)(2,1)}, u32[]{:S(2)}) copy-start(bf16[32,512,128]{1,2,0:T(8,128)(2,1)} %copy-done.4) | copy-start | bytes 12582916
  756.4 2.1 copy-start.9
  756.4 3.2 copy-start.10
  769.7 9.8 %copy-start.16 = (f32[32,512]{1,0:T(8,128)S(1)}, f32[32,512]{1,0:T(8,128)}, u32[]{:S(2)}) copy-start(f32[32,512]{1,0:T(8,128)} %copy-done.15) | copy-start | bytes 196612
  769.7 9.8 %copy-start.18 = (f32[32,512]{1,0:T(8,128)S(1)}, f32[32,512]{1,0:T(8,128)}, u32[]{:S(2)}) copy-start(f32[32,512]{1,0:T(8,128)} %copy-done.17) | copy-start | bytes 196612
  769.7 9.8 %copy-start.23 = (f32[128]{0:T(128)S(1)}, f32[128]{0:T(128)}, u32[]{:S(2)}) copy-start(f32[128]{0:T(128)} %param.13) | copy-start | bytes 1540
Sparse Core Ops, SparseCore 0:
  613.8 121.6 all-reduce.5
  789.2 88.5 all-reduce.3
where the time goes:
time: 898 us; the launch traced here: 887 us
  waiting for transfers between devices  471 us (52%)
  blocking collectives  112 us (12%)
  matrix products  82.7 us (9%)
  starting transfers between devices  72.5 us (8%)
  other arithmetic  67.7 us (8%)
  local copies, waits for them, and re-layouts  65.4 us (7%)
  between operations  14.9 us (2%)
    psum x1, waiting for transfers between devices, body(): lax.psum(local_gate.astype(jnp.bfloat16), 'tile').astype(jnp.float32)  122 us
    all_to_all x1, blocking collectives, send_grads(): lax.all_to_all(grad_prod, 'tile', split_axis=2, concat_axis=0, tiled=True)  112 us
    psum x1, waiting for transfers between devices, body(): lax.psum(local_ab.astype(jnp.bfloat16), 'tile').astype(jnp.float32)  75.1 us
    all_to_all x1, waiting for transfers between devices, send_factors(): lax.all_to_all(factor_a, 'tile', split_axis=2, concat_axis=0, tiled=True)  72.9 us
    all_to_all x1, waiting for transfers between devices, send_factors(): lax.all_to_all(factor_b, 'tile', split_axis=2, concat_axis=0, tiled=True)  71.2 us
    all_to_all x1, waiting for transfers between devices, return_grads(): lax.all_to_all(jnp.transpose(owner_fac_b, (1, 2, 0)), 'tile', split_axis=...  67.5 us
    all_to_all x1, waiting for transfers between devices, return_products(): lax.all_to_all(jnp.transpose(owner_prod, (1, 2, 0)), 'tile', split_axis=0...  62.8 us
    unnamed x59, local copies, waits for them, and re-layouts  31.2 us
  transfers between devices with their start and end apart: 7, of which 6 were waited for; matrix products, arithmetic and copies ran while one was open for 8% of the time, Pallas kernels for 0%

commit v1 on v0

v1 whole, which is shorter than its diff:
```python
import functools

import jax
import jax.numpy as jnp
from jax import lax
from jax.experimental import pallas as pl
from jax.experimental.pallas import tpu as pltpu
from jax.sharding import PartitionSpec as P

EPS = 1e-05
F32 = jnp.float32
BF16 = jnp.bfloat16
NN = (((1,), (0,)), ((), ()))
NT = (((1,), (1,)), ((), ()))
TN = (((0,), (0,)), ((), ()))


def params(steps):
    return pltpu.CompilerParams(
        dimension_semantics=("arbitrary",) * steps, vmem_limit_bytes=50 * 1024 * 1024
    )


def dot(left, right, form=NN):
    return lax.dot_general(left, right, form, preferred_element_type=F32)


def sigmoid(value):
    return 0.5 * jnp.tanh(0.5 * value) + 0.5


def col_mean(value):
    return jnp.mean(value, axis=0, keepdims=True)


def stats(value):
    centered = value - col_mean(value)
    inv_std = lax.rsqrt(col_mean(centered * centered) + EPS)
    return centered * inv_std, inv_std


def norm_back(upstream, scaled, inv_std):
    return inv_std * (upstream - col_mean(upstream) - scaled * col_mean(upstream * scaled))


def turned(ref, row):
    return ref[row].astype(F32).T


def factors_kernel(x_ref, mask_ref, gain_ref, bias_ref, w_ref, fa_ref, fb_ref, sa_ref, sb_ref):
    rows, cols, chans = x_ref.shape
    hidden = fa_ref.shape[0]

    @pl.loop(0, rows)
    def _(row):
        z_hat, _ = stats(turned(x_ref, row))
        normed = (z_hat * gain_ref[...] + bias_ref[...]).astype(BF16)
        mask = mask_ref[pl.ds(row, 1), :]
        proj = dot(w_ref[...], normed)
        value_a, gate_a = proj[:hidden], proj[hidden : 2 * hidden]
        value_b, gate_b = proj[2 * hidden : 3 * hidden], proj[3 * hidden :]
        store_rows(sa_ref, row, rows, mask * sigmoid(gate_a) * value_a)
        store_rows(sb_ref, row, rows, mask * sigmoid(gate_b) * value_b)

    gather_out(sa_ref, fa_ref)
    gather_out(sb_ref, fb_ref)


def store_rows(ref, row, rows, value):
    hidden = value.shape[0]
    for lane in range(ref.shape[0]):
        ref[lane, pl.ds(row, hidden, stride=rows), :] = value[:, lane * 128 : (lane + 1) * 128]


def load_rows(ref, row, rows):
    hidden = ref.shape[1] // rows
    return jnp.concatenate(
        [ref[lane, pl.ds(row, hidden, stride=rows), :] for lane in range(ref.shape[0])], axis=1
    )


def gather_out(scratch, out_ref):
    hidden, rows, cols = out_ref.shape
    for lane in range(scratch.shape[0]):
        out_ref[:, :, lane * 128 : (lane + 1) * 128] = (
            scratch[lane].reshape(hidden, rows, 128).astype(BF16)
        )


def spread_in(in_ref, scratch):
    hidden, rows, cols = in_ref.shape
    for lane in range(scratch.shape[0]):
        scratch[lane] = (
            in_ref[:, :, lane * 128 : (lane + 1) * 128].astype(F32).reshape(hidden * rows, 128)
        )


def whole(array):
    return pl.BlockSpec(array.shape, lambda *_: (0,) * array.ndim)


def row_block(rows, cols, chans):
    return pl.BlockSpec((rows, cols, chans), lambda i, j: (i, j, 0))


def chan_block(hidden, rows, cols):
    return pl.BlockSpec((hidden, rows, cols), lambda i, j: (0, i, j))


def plane(rows, cols):
    return pltpu.VMEM((cols // 128, rows * 128, 128), F32)


def make_factors(x, mask, gain, bias, w_t, rows, cols):
    count, crop, chans = x.shape
    hidden = w_t.shape[0] // 4
    out = jax.ShapeDtypeStruct((hidden, count, crop), BF16)
    return pl.pallas_call(
        factors_kernel,
        grid=(count // rows, crop // cols),
        in_specs=[
            row_block(rows, cols, chans),
            pl.BlockSpec((rows, cols), lambda i, j: (i, j)),
            whole(gain),
            whole(bias),
            whole(w_t),
        ],
        out_specs=[chan_block(hidden, rows, cols)] * 2,
        out_shape=[out, out],
        scratch_shapes=[pltpu.VMEM((cols // 128, rows * hidden, 128), F32)] * 2,
        compiler_params=params(2),
        name="factors",
    )(x, mask, gain, bias, w_t)


def product_kernel(a_ref, b_ref, p_ref):
    src, _, rows, crop = a_ref.shape
    a = a_ref[...].reshape(src * rows, crop)
    b = b_ref[...].reshape(crop, crop)
    p_ref[...] = dot(a, b, NT).astype(BF16).reshape(p_ref.shape)


def own_block(array):
    src, _, rows, crop = array.shape
    return pl.BlockSpec((src, 1, rows, crop), lambda h: (0, h, 0, 0))


def make_product(a, b):
    return pl.pallas_call(
        product_kernel,
        grid=(a.shape[1],),
        in_specs=[own_block(a), own_block(b)],
        out_specs=own_block(a),
        out_shape=jax.ShapeDtypeStruct(a.shape, BF16),
        compiler_params=params(1),
        name="product",
    )(a, b)


def back_kernel(g_ref, a_ref, b_ref, da_ref, db_ref):
    src, _, rows, crop = a_ref.shape
    g = g_ref[...].reshape(src * rows, crop)
    a = a_ref[...].reshape(src * rows, crop)
    b = b_ref[...].reshape(crop, crop)
    da_ref[...] = dot(g, b).astype(BF16).reshape(da_ref.shape)
    db_ref[...] = dot(g, a, TN).astype(BF16).reshape(db_ref.shape)


def make_back(g, a, b):
    return pl.pallas_call(
        back_kernel,
        grid=(a.shape[1],),
        in_specs=[own_block(g), own_block(a), own_block(b)],
        out_specs=[own_block(a), own_block(b)],
        out_shape=[jax.ShapeDtypeStruct(a.shape, BF16), jax.ShapeDtypeStruct(b.shape, BF16)],
        compiler_params=params(1),
        name="back",
    )(g, a, b)


def middle_kernel(
    x_ref, d_ref, p_ref, gain_ref, bias_ref, wg_ref, og_ref, ob_ref, wo_ref, wot_ref,
    g_ref, gb_ref, gwo_ref, gwg_ref, s_ref,
):
    rows, cols, chans = x_ref.shape

    @pl.when((pl.program_id(0) == 0) & (pl.program_id(1) == 0))
    def _():
        gwo_ref[...] = jnp.zeros_like(gwo_ref)
        gwg_ref[...] = jnp.zeros_like(gwg_ref)

    spread_in(p_ref, s_ref)

    @pl.loop(0, rows)
    def _(row):
        z_hat, _ = stats(turned(x_ref, row))
        normed = (z_hat * gain_ref[...] + bias_ref[...]).astype(BF16)
        gate = sigmoid(dot(wg_ref[...], normed))
        x_hat, inv_std = stats(load_rows(s_ref, row, rows))
        x_norm = (x_hat * og_ref[...] + ob_ref[...]).astype(BF16)
        out_lin = dot(wot_ref[...], x_norm)
        lin = turned(d_ref, row) * gate
        grad_lin = lin.astype(BF16)
        gate_back = (lin * out_lin * (1.0 - gate)).astype(BF16)
        upstream = dot(wo_ref[...], grad_lin) * og_ref[...]
        store_rows(s_ref, row, rows, norm_back(upstream, x_hat, inv_std))
        gb_ref[row] = gate_back
        gwo_ref[...] += dot(x_norm, grad_lin, NT)
        gwg_ref[...] += dot(normed, gate_back, NT)

    gather_out(s_ref, g_ref)


def make_middle(x, d, p, gain, bias, w_gate_t, out_gain, out_bias, w_out, w_out_t, rows, cols):
    count, crop, chans = x.shape
    hidden = w_out.shape[0]
    grads = [jax.ShapeDtypeStruct((hidden, chans), F32), jax.ShapeDtypeStruct((chans, chans), F32)]
    small = [gain, bias, w_gate_t, out_gain, out_bias, w_out, w_out_t]
    return pl.pallas_call(
        middle_kernel,
        grid=(count // rows, crop // cols),
        in_specs=[row_block(rows, cols, chans)] * 2
        + [chan_block(hidden, rows, cols)]
        + [whole(value) for value in small],
        out_specs=[
            chan_block(hidden, rows, cols),
            pl.BlockSpec((rows, chans, cols), lambda i, j: (i, 0, j)),
        ]
        + [whole(value) for value in grads],
        out_shape=[
            jax.ShapeDtypeStruct((hidden, count, crop), BF16),
            jax.ShapeDtypeStruct((count, chans, crop), BF16),
        ]
        + grads,
        scratch_shapes=[pltpu.VMEM((cols // 128, rows * hidden, 128), F32)],
        compiler_params=params(2),
        name="middle",
    )(x, d, p, *small)


def last_kernel(
    x_ref, mask_ref, ga_ref, gb_ref, gate_ref, gain_ref, bias_ref, wt_ref, wcat_ref,
    out_ref, gw_ref, sa_ref, sb_ref,
):
    rows, cols, chans = x_ref.shape
    hidden = ga_ref.shape[0]

    @pl.when((pl.program_id(0) == 0) & (pl.program_id(1) == 0))
    def _():
        gw_ref[...] = jnp.zeros_like(gw_ref)

    spread_in(ga_ref, sa_ref)
    spread_in(gb_ref, sb_ref)

    @pl.loop(0, rows)
    def _(row):
        z_hat, inv_in = stats(turned(x_ref, row))
        normed = (z_hat * gain_ref[...] + bias_ref[...]).astype(BF16)
        mask = mask_ref[pl.ds(row, 1), :]
        proj = dot(wt_ref[...], normed)
        sides = []
        for side, ref in enumerate((sa_ref, sb_ref)):
            value = proj[2 * side * hidden : (2 * side + 1) * hidden]
            sig = sigmoid(proj[(2 * side + 1) * hidden : (2 * side + 2) * hidden])
            to_value = load_rows(ref, row, rows) * mask * sig
            sides += [to_value.astype(BF16), (to_value * value * (1.0 - sig)).astype(BF16)]
        grad_proj = jnp.concatenate(sides, axis=0)
        every = jnp.concatenate([grad_proj, gate_ref[row]], axis=0)
        upstream = dot(wcat_ref[...], every) * gain_ref[...]
        out_ref[row] = norm_back(upstream, z_hat, inv_in).T.astype(BF16)
        gw_ref[...] += dot(normed, grad_proj, NT)


def make_last(x, mask, grad_a, grad_b, gate_back, gain, bias, w_t, w_cat, rows, cols):
    count, crop, chans = x.shape
    hidden = w_t.shape[0] // 4
    grad = jax.ShapeDtypeStruct((chans, 4 * hidden), F32)
    small = [gain, bias, w_t, w_cat]
    return pl.pallas_call(
        last_kernel,
        grid=(count // rows, crop // cols),
        in_specs=[
            row_block(rows, cols, chans),
            pl.BlockSpec((rows, cols), lambda i, j: (i, j)),
            chan_block(hidden, rows, cols),
            chan_block(hidden, rows, cols),
            pl.BlockSpec((rows, chans, cols), lambda i, j: (i, 0, j)),
        ]
        + [whole(value) for value in small],
        out_specs=[row_block(rows, cols, chans), whole(grad)],
        out_shape=[jax.ShapeDtypeStruct(x.shape, BF16), grad],
        scratch_shapes=[pltpu.VMEM((cols // 128, rows * hidden, 128), F32)] * 2,
        compiler_params=params(2),
        name="last",
    )(x, mask, grad_a, grad_b, gate_back, *small)


def swap(array):
    return lax.all_to_all(array, "tile", split_axis=0, concat_axis=0, tiled=True)


def tile_sum(array, tiles):
    chans, width = array.shape
    parts = swap(array.astype(BF16)).reshape(tiles, chans // tiles, width)
    part = jnp.sum(parts.astype(F32), axis=0).astype(BF16)
    return swap(jnp.broadcast_to(part[None], (tiles,) + part.shape).reshape(chans, width)).astype(F32)


def body(
    tiles, x, d, token_mask, ln_in_gain, ln_in_bias, w_ab, w_gate, ln_out_gain, ln_out_bias, w_out
):
    count, crop, chans = x.shape
    hidden = w_out.shape[0]
    rows, cols = 16, 256
    valid = token_mask.astype(F32)
    own_valid = lax.dynamic_slice_in_dim(valid, lax.axis_index("tile") * count, count)
    mask = own_valid[:, None] * valid[None, :]
    gain, bias = ln_in_gain[:, None], ln_in_bias[:, None]
    out_gain, out_bias = ln_out_gain[:, None], ln_out_bias[:, None]
    w_t = w_ab.T
    w_cat = jnp.concatenate([w_ab, w_gate], axis=1)
    owned = (tiles, hidden // tiles, count, crop)

    factor_a, factor_b = make_factors(x, mask, gain, bias, w_t, rows, cols)
    owner_a = swap(factor_a).reshape(owned)
    owner_b = swap(factor_b).reshape(owned)
    owner_p = make_product(owner_a, owner_b)
    product = swap(owner_p.reshape(hidden, count, crop))
    grad_prod, gate_back, local_out, local_gate = make_middle(
        x, d, product, gain, bias, w_gate.T, out_gain, out_bias, w_out, w_out.T, rows, cols
    )
    owner_g = swap(grad_prod).reshape(owned)
    owner_da, owner_db = make_back(owner_g, owner_a, owner_b)
    grad_a = swap(owner_da.reshape(hidden, count, crop))
    grad_b = swap(owner_db.reshape(hidden, count, crop))
    pair_grad, local_ab = make_last(
        x, mask, grad_a, grad_b, gate_back, gain, bias, w_t, w_cat, rows, cols
    )
    local = jnp.concatenate([local_ab, local_gate, local_out], axis=1)
    total = tile_sum(local, tiles) / crop
    width = 4 * hidden
    return (pair_grad, total[:, :width], total[:, width : width + chans], total[:, width + chans :])


def solution(mesh):
    pairs = P(("crops", "tile"), None, None)
    return jax.shard_map(
        functools.partial(body, mesh.shape["tile"]),
        mesh=mesh,
        in_specs=(pairs, pairs, P("crops")) + (P(),) * 7,
        out_specs=(pairs,) + (P("crops", None),) * 3,
        check_vma=False,
    )
```

time: 898 us -> 776 us (0.86); the launches traced: 887 us -> 775 us
  blocking collectives: 112 us -> 447 us
  waiting for transfers between devices: 471 us -> 155 us
  Pallas kernels: 0 us -> 156 us
  matrix products: 82.7 us -> 0 us
  other arithmetic: 67.7 us -> 0.89 us
  starting transfers between devices: 72.5 us -> 11 us
  local copies, waits for them, and re-layouts: 65.4 us -> 4.5 us
  between operations: 14.9 us -> 0.76 us
    all_to_all x1 -> x6, blocking collectives: 112 us -> 447 us  [swap(): lax.all_to_all(array, 'tile', split_axis=0, concat_axis=0, tiled=True)]
    psum x2 -> x0, waiting for transfers between devices: 197 us -> none  [the longest x1 122 us: body(): lax.psum(local_gate.astype(jnp.bfloat16), 'tile').astype(jnp.float32)]
    pallas_call x0 -> x5, Pallas kernels: none -> 156 us  [the longest x1 55.8 us: make_last(): pl.pallas_call(last_kernel, grid=(count // rows, crop // cols), in_specs=...]
    all_to_all x5 -> x2, waiting for transfers between devices: 274 us -> 155 us  [swap(): lax.all_to_all(array, 'tile', split_axis=0, concat_axis=0, tiled=True)]
    dot_general x12 -> x0, matrix products: 82.7 us -> none  [the longest x1 13.3 us: body(): jnp.einsum('rnc,ce->' + layout_form, normed, w_ab, preferred_element_type...]
    all_to_all x5 -> x2, starting transfers between devices: 72.2 us -> 11 us  [swap(): lax.all_to_all(array, 'tile', split_axis=0, concat_axis=0, tiled=True)]
    convert_element_type x6 -> x1, other arithmetic: 35.7 us -> 0.68 us  [body(): valid = token_mask.astype(F32)]
    unnamed x59 -> x15, local copies, waits for them, and re-layouts: 31.2 us -> 1.27 us
  transfers between devices with their start and end apart: 7 -> 2, of which waited for: 6 -> 2; matrix products, arithmetic and copies ran while one was open for 8% -> 0% of each run, Pallas kernels for 0% -> 0%
where the time goes in v1:
time: 776 us; the launch traced here: 775 us
  blocking collectives  447 us (58%)
  Pallas kernels  156 us (20%)
  waiting for transfers between devices  155 us (20%)
  starting transfers between devices  11 us (1%)
    all_to_all x6, blocking collectives, swap(): lax.all_to_all(array, 'tile', split_axis=0, concat_axis=0, tiled=True)  447 us
    all_to_all x2, waiting for transfers between devices, swap(): lax.all_to_all(array, 'tile', split_axis=0, concat_axis=0, tiled=True)  155 us
    pallas_call x1, Pallas kernels, make_last(): pl.pallas_call(last_kernel, grid=(count // rows, crop // cols), in_specs=...  55.8 us
    pallas_call x1, Pallas kernels, make_middle(): pl.pallas_call(middle_kernel, grid=(count // rows, crop // cols), in_spec...  43.2 us
    pallas_call x1, Pallas kernels, make_factors(): pl.pallas_call(factors_kernel, grid=(count // rows, crop // cols), in_spe...  35.7 us
  transfers between devices with their start and end apart: 2, of which 2 were waited for; matrix products, arithmetic and copies ran while one was open for 0% of the time, Pallas kernels for 0%

profile of v1, /device:TPU:0, one launch (start us, length us, event | category | flops | bytes accessed | tf_op | source)
XLA Modules:
  0.0 774.7 jit_solution(2053645200269918483)
XLA Ops:
  0.6 0.7 convert_element_type.11
  1.3 0.1 dynamic_slice.3
  1.4 0.1 broadcast_multiply_fusion.mask_ref
  1.5 0.8 copy.15.gain_ref
  2.2 0.8 copy.16.bias_ref
  3.0 1.0 copy.14
  4.0 35.7 %factors.1 = (bf16[128,32,512]{2,1,0:T(8,128)(2,1)}, bf16[128,32,512]{2,1,0:T(8,128)(2,1)}) custom-call(bf16[32,512,128]{2,1,0:T(8,128)(2,1)} %x_ref.5, f32[32,512]{1,0:T(8,128)S(1)} %broadcast_multiply_fusion.mask_ref, f32[128,1]{1,0:T(8,128)S(1)} %copy.15.gain_ref, f32[128,1]{1,0:T(8,128)S(1)} %copy.16.bias_ref, bf16[512,128]{1,0:T(8,128)(2,1)S(1)} %bitcast.21), custom_call_target="tpu_custom_call" | custom-call | tf_op jit(solution)/shard_map/factors/pallas_call | solution.py:118
  39.7 0.0 copy-start.1
  39.7 100.0 %all_to_all.42 = bf16[128,32,512]{2,1,0:T(8,128)(2,1)} all-to-all(bf16[128,32,512]{2,1,0:T(8,128)(2,1)} %get-tuple-element.14), channel_id=1, replica_groups=mesh['crops'=2,'tile'=16] {'tile'}, dimensions={0} | all-to-all | bytes 8388608 | tf_op jit(solution)/shard_map/all_to_all | solution.py:299
  139.7 0.0 copy-done.1
  139.7 97.5 %all_to_all.43 = bf16[128,32,512]{2,1,0:T(8,128)(2,1)} all-to-all(bf16[128,32,512]{2,1,0:T(8,128)(2,1)S(1)} %copy-done.1), channel_id=1, replica_groups=mesh['crops'=2,'tile'=16] {'tile'}, dimensions={0} | all-to-all | bytes 8388608 | tf_op jit(solution)/shard_map/all_to_all | solution.py:299
  237.2 8.9 %product.1 = bf16[16,8,32,512]{3,2,1,0:T(8,128)(2,1)} custom-call(bf16[16,8,32,512]{3,2,1,0:T(8,128)(2,1)} %bitcast.25, bf16[16,8,32,512]{3,2,1,0:T(8,128)(2,1)} %bitcast.27), custom_call_target="tpu_custom_call" | custom-call | tf_op jit(solution)/shard_map/product/pallas_call | solution.py:149
  246.1 0.0 copy-start.4
  246.1 0.0 copy-start.5
  246.1 0.0 copy-start.3
  246.1 0.0 copy-start
  246.1 5.5 all-to-all-start.2
  251.6 0.0 copy-done.4
  251.6 0.1 copy.21.og_ref
  251.7 0.0 copy-done.5
  251.7 0.1 copy.22.ob_ref
  251.8 0.0 copy-done.3
  251.8 0.1 copy.17
  251.9 0.0 copy-done
  252.0 0.1 copy.18
  252.1 77.2 %all-to-all-done.2.p_ref = bf16[128,32,512]{2,1,0:T(8,128)(2,1)} async-done(((bf16[128,32,512]{2,1,0:T(8,128)(2,1)}), bf16[128,32,512]{2,1,0:T(8,128)(2,1)}, u32[]{:S(2)}, u32[]{:S(2)}) %all-to-all-start.2) | async-done | bytes 4194336 | tf_op jit(solution)/shard_map/all_to_all | solution.py:299
  329.3 43.2 %middle.1 = (bf16[128,32,512]{2,1,0:T(8,128)(2,1)}, bf16[32,128,512]{2,1,0:T(8,128)(2,1)}, f32[128,128]{1,0:T(8,128)S(1)}, f32[128,128]{1,0:T(8,128)S(1)}) custom-call(bf16[32,512,128]{2,1,0:T(8,128)(2,1)} %x_ref.5, bf16[32,512,128]{2,1,0:T(8,128)(2,1)} %d_ref.1, bf16[128,32,512]{2,1,0:T(8,128)(2,1)} %all-to-all-done.2.p_ref, f32[128,1]{1,0:T(8,128)S(1)} %copy.15.gain_ref, ...), custom_call_target="tpu_custom_call" | custom-call | tf_op jit(solution)/shard_map/middle/pallas_call | solution.py:219
  372.5 112.0 %all_to_all.44 = bf16[128,32,512]{2,1,0:T(8,128)(2,1)} all-to-all(bf16[128,32,512]{2,1,0:T(8,128)(2,1)} %get-tuple-element.16), channel_id=1, replica_groups=mesh['crops'=2,'tile'=16] {'tile'}, dimensions={0} | all-to-all | bytes 8388608 | tf_op jit(solution)/shard_map/all_to_all | solution.py:299
  484.5 11.9 %back.1 = (bf16[16,8,32,512]{3,2,1,0:T(8,128)(2,1)}, bf16[16,8,32,512]{3,2,1,0:T(8,128)(2,1)}) custom-call(bf16[16,8,32,512]{3,2,1,0:T(8,128)(2,1)} %bitcast.30, bf16[16,8,32,512]{3,2,1,0:T(8,128)(2,1)} %bitcast.26, bf16[16,8,32,512]{3,2,1,0:T(8,128)(2,1)} %bitcast.28), custom_call_target="tpu_custom_call" | custom-call | tf_op jit(solution)/shard_map/back/pallas_call | solution.py:170
  496.4 97.7 %all_to_all.45.ga_ref = bf16[128,32,512]{2,1,0:T(8,128)(2,1)} all-to-all(bf16[128,32,512]{2,1,0:T(8,128)(2,1)} %bitcast.32), channel_id=1, replica_groups=mesh['crops'=2,'tile'=16] {'tile'}, dimensions={0} | all-to-all | bytes 8388608 | tf_op jit(solution)/shard_map/all_to_all | solution.py:299
  594.1 0.0 copy-start.2
  594.1 5.5 all-to-all-start.5
  599.6 0.0 copy-done.2
  599.6 77.6 %all-to-all-done.5.gb_ref = bf16[128,32,512]{2,1,0:T(8,128)(2,1)} async-done(((bf16[128,32,512]{2,1,0:T(8,128)(2,1)}), bf16[128,32,512]{2,1,0:T(8,128)(2,1)}, u32[]{:S(2)}, u32[]{:S(2)}) %all-to-all-start.5) | async-done | bytes 4194336 | tf_op jit(solution)/shard_map/all_to_all | solution.py:299
  677.3 55.8 %last.1 = (bf16[32,512,128]{2,1,0:T(8,128)(2,1)}, f32[128,512]{1,0:T(8,128)S(1)}) custom-call(bf16[32,512,128]{2,1,0:T(8,128)(2,1)} %x_ref.5, f32[32,512]{1,0:T(8,128)S(1)} %broadcast_multiply_fusion.mask_ref, bf16[128,32,512]{2,1,0:T(8,128)(2,1)} %all_to_all.45.ga_ref, bf16[128,32,512]{2,1,0:T(8,128)(2,1)} %all-to-all-done.5.gb_ref, ...), custom_call_target="tpu_custom_call" | custom-call | tf_op jit(solution)/shard_map/last/pallas_call | solution.py:279
  733.2 28.4 %all_to_all.46 = bf16[16,8,768]{2,1,0:T(8,128)(2,1)S(1)} all-to-all(bf16[16,8,768]{2,1,0:T(8,128)(2,1)S(1)} %pad_maximum_fusion), channel_id=1, replica_groups=mesh['crops'=2,'tile'=16] {'tile'}, dimensions={0} | all-to-all | bytes 393216 | tf_op jit(solution)/shard_map/all_to_all | solution.py:299
  761.6 11.6 %all_to_all.47 = bf16[16,8,768]{2,1,0:T(8,128)(2,1)S(1)} all-to-all(bf16[16,8,768]{2,1,0:T(8,128)(2,1)S(1)} %broadcast_in_dim.24), channel_id=1, replica_groups=mesh['crops'=2,'tile'=16] {'tile'}, dimensions={0} | all-to-all | bytes 393216 | tf_op jit(solution)/shard_map/all_to_all | solution.py:299
  773.3 0.7 slice.12
  774.0 0.7 fusion
  (7 shorter events, 0.1 us)
Async XLA Ops:
  39.7 100.0 %copy-start.1 = (bf16[128,32,512]{2,1,0:T(8,128)(2,1)S(1)}, bf16[128,32,512]{2,1,0:T(8,128)(2,1)}, u32[]{:S(2)}) copy-start(bf16[128,32,512]{2,1,0:T(8,128)(2,1)} %get-tuple-element.15) | copy-start | bytes 12582916
  246.1 5.5 copy-start.4
  246.1 5.6 copy-start.5
  246.1 5.8 copy-start.3
  246.1 5.9 copy-start
  246.1 83.2 %all-to-all-start.2 = ((bf16[128,32,512]{2,1,0:T(8,128)(2,1)}), bf16[128,32,512]{2,1,0:T(8,128)(2,1)}, u32[]{:S(2)}, u32[]{:S(2)}) async-start(bf16[128,32,512]{2,1,0:T(8,128)(2,1)} %bitcast.29), calls=%async_computation.2 | async-start | bytes 8388608 | tf_op jit(solution)/shard_map/all_to_all | solution.py:299
  594.1 5.5 copy-start.2
  594.1 83.2 %all-to-all-start.5 = ((bf16[128,32,512]{2,1,0:T(8,128)(2,1)}), bf16[128,32,512]{2,1,0:T(8,128)(2,1)}, u32[]{:S(2)}, u32[]{:S(2)}) async-start(bf16[128,32,512]{2,1,0:T(8,128)(2,1)} %bitcast.31), calls=%async_computation.5 | async-start | bytes 8388608 | tf_op jit(solution)/shard_map/all_to_all | solution.py:299

commit v2 on v1

v2 whole, which is shorter than its diff:
```python
import functools

import jax
import jax.numpy as jnp
from jax import lax
from jax.experimental import pallas as pl
from jax.experimental.pallas import tpu as pltpu
from jax.sharding import PartitionSpec as P

EPS = 1e-05
F32 = jnp.float32
BF16 = jnp.bfloat16
NN = (((1,), (0,)), ((), ()))
NT = (((1,), (1,)), ((), ()))
TN = (((0,), (0,)), ((), ()))


def params(steps):
    return pltpu.CompilerParams(
        dimension_semantics=("arbitrary",) * steps, vmem_limit_bytes=50 * 1024 * 1024
    )


def dot(left, right, form=NN):
    return lax.dot_general(left, right, form, preferred_element_type=F32)


def sigmoid(value):
    return 0.5 * jnp.tanh(0.5 * value) + 0.5


def col_mean(value):
    return jnp.mean(value, axis=0, keepdims=True)


def stats(value):
    centered = value - col_mean(value)
    inv_std = lax.rsqrt(col_mean(centered * centered) + EPS)
    return centered * inv_std, inv_std


def norm_back(upstream, scaled, inv_std):
    return inv_std * (upstream - col_mean(upstream) - scaled * col_mean(upstream * scaled))


def turned(ref, row, count):
    block = ref[pl.ds(row, count)]
    return block.reshape(-1, block.shape[-1]).astype(F32).T


def lane_parts(scratch, count):
    return [(at, lane) for at in range(count) for lane in range(scratch.shape[0])]


def store_rows(scratch, row, count, rows, value):
    hidden = value.shape[0]
    for part, (at, lane) in enumerate(lane_parts(scratch, count)):
        scratch[lane, pl.ds(row + at, hidden, stride=rows), :] = value[:, part * 128 : (part + 1) * 128]


def load_rows(scratch, row, count, rows):
    hidden = scratch.shape[1] // rows
    return jnp.concatenate(
        [
            scratch[lane, pl.ds(row + at, hidden, stride=rows), :]
            for at, lane in lane_parts(scratch, count)
        ],
        axis=1,
    )


def gather_out(scratch, out_ref):
    hidden, rows, cols = out_ref.shape
    for lane in range(scratch.shape[0]):
        out_ref[:, :, lane * 128 : (lane + 1) * 128] = (
            scratch[lane].reshape(hidden, rows, 128).astype(BF16)
        )


def spread_in(in_ref, scratch):
    hidden, rows, cols = in_ref.shape
    for lane in range(scratch.shape[0]):
        scratch[lane] = (
            in_ref[:, :, lane * 128 : (lane + 1) * 128].astype(F32).reshape(hidden * rows, 128)
        )


def flat_rows(ref, row, count):
    return jnp.concatenate([ref[pl.ds(row + at, 1), :] for at in range(count)], axis=1)


def whole(array):
    return pl.BlockSpec(array.shape, lambda *_: (0,) * array.ndim)


class Plan:
    def __init__(self, tiles, count, crop):
        self.tiles, self.count, self.crop = tiles, count, crop
        self.half = tiles // 2
        self.subs = 2 if count % 32 == 0 else 1
        self.rows = count // self.subs
        self.width = self.half * self.rows
        self.blocks = crop // self.width
        self.step = max(1, 512 // self.width)
        self.groups = [
            [side * self.half + at for at in range(self.half)] for side in range(2)
        ]
        self.partner = [(at, (at + self.half) % tiles) for at in range(tiles)]

    def view(self, array):
        return array.reshape(self.count, self.tiles, self.subs, self.rows, array.shape[-1])

    def pair_spec(self, chans, index):
        return pl.BlockSpec((self.rows, self.half, 1, self.rows, chans), index)

    def scratch(self, hidden):
        return pltpu.VMEM((self.width // 128, self.rows * hidden, 128), F32)

    def swap(self, array):
        return lax.all_to_all(
            array, "tile", split_axis=0, concat_axis=0, axis_index_groups=self.groups, tiled=True
        )

    def exchange(self, array):
        return lax.ppermute(array, "tile", self.partner)


def factors_kernel(step, x_ref, mask_ref, gain_ref, bias_ref, w_ref, fa_ref, fb_ref, sa_ref, sb_ref):
    rows = x_ref.shape[0]
    hidden = fa_ref.shape[0]

    @pl.loop(0, rows // step)
    def _(turn):
        row = pl.multiple_of(turn * step, step)
        z_hat, _ = stats(turned(x_ref, row, step))
        normed = (z_hat * gain_ref[...] + bias_ref[...]).astype(BF16)
        mask = flat_rows(mask_ref, row, step)
        proj = dot(w_ref[...], normed)
        value_a, gate_a = proj[:hidden], proj[hidden : 2 * hidden]
        value_b, gate_b = proj[2 * hidden : 3 * hidden], proj[3 * hidden :]
        store_rows(sb_ref, row, step, rows, mask * sigmoid(gate_b) * value_b)
        store_rows(sa_ref, row, step, rows, mask * sigmoid(gate_a) * value_a)

    gather_out(sa_ref, fa_ref)
    gather_out(sb_ref, fb_ref)


def make_factors(plan, sub, x, mask, gain, bias, w_t):
    chans = x.shape[-1]
    hidden = w_t.shape[0] // 4
    out = jax.ShapeDtypeStruct((hidden, plan.rows, plan.crop), BF16)
    out_spec = pl.BlockSpec((hidden, plan.rows, plan.width), lambda j: (0, 0, j))
    return pl.pallas_call(
        functools.partial(factors_kernel, plan.step),
        grid=(plan.blocks,),
        in_specs=[
            plan.pair_spec(chans, lambda j: (sub, j % 2, j // 2, 0, 0)),
            pl.BlockSpec((plan.rows, plan.width), lambda j: (sub, j)),
            whole(gain),
            whole(bias),
            whole(w_t),
        ],
        out_specs=[out_spec] * 2,
        out_shape=[out, out],
        scratch_shapes=[plan.scratch(hidden)] * 2,
        compiler_params=params(1),
        name="factors",
    )(x, mask, gain, bias, w_t)


def matrix(refs):
    parts = [ref[...].reshape(-1, ref.shape[-1]) for ref in refs]
    return jnp.concatenate(parts, axis=0) if len(parts) > 1 else parts[0]


def by_sub(ref, subs):
    rows = ref.shape[2] // subs
    parts = [
        ref[:, 0, sub * rows : (sub + 1) * rows, :].reshape(-1, ref.shape[3]) for sub in range(subs)
    ]
    return jnp.concatenate(parts, axis=0) if subs > 1 else parts[0]


def to_subs(ref, value, subs):
    tiles, _, rows, cols = ref.shape
    part = value.shape[0] // subs
    for sub in range(subs):
        ref[:, 0, sub * (rows // subs) : (sub + 1) * (rows // subs), :] = value[
            sub * part : (sub + 1) * part
        ].astype(BF16).reshape(tiles, rows // subs, cols)


def own_spec(array):
    src, _, rows, cols = array.shape
    return pl.BlockSpec((src, 1, rows, cols), lambda h: (0, h, 0, 0))


def product_kernel(subs, count, *refs):
    a, b, p_ref = refs[:subs], refs[subs : subs + count], refs[subs + count]
    to_subs(p_ref, dot(matrix(a), matrix(b), NT), subs)


def make_product(plan, a, b):
    tiles, chans, rows, _ = a[0].shape
    out = jax.ShapeDtypeStruct((tiles, chans, plan.count, len(b) * plan.width), BF16)
    return pl.pallas_call(
        functools.partial(product_kernel, plan.subs, len(b)),
        grid=(chans,),
        in_specs=[own_spec(value) for value in (*a, *b)],
        out_specs=own_spec(out),
        out_shape=out,
        compiler_params=params(1),
        name="product",
    )(*a, *b)


def grad_b_kernel(subs, g_ref, *refs):
    a, outs = refs[:subs], refs[subs:]
    grad = dot(by_sub(g_ref, subs), matrix(a), TN).astype(BF16)
    size = grad.shape[0] // len(outs)
    for at, out in enumerate(outs):
        out[...] = grad[at * size : (at + 1) * size].reshape(out.shape)


def make_grad_b(plan, g, a):
    outs = g.shape[-1] // plan.width
    return pl.pallas_call(
        functools.partial(grad_b_kernel, plan.subs),
        grid=(g.shape[1],),
        in_specs=[own_spec(value) for value in (g, *a)],
        out_specs=[own_spec(a[0])] * outs,
        out_shape=[jax.ShapeDtypeStruct(a[0].shape, BF16)] * outs,
        compiler_params=params(1),
        name="grad_b",
    )(g, *a)


def grad_a_kernel(subs, count, *refs):
    g, b, out = refs[:count], refs[count:-1], refs[-1]
    rows = jnp.concatenate([by_sub(ref, subs) for ref in g], axis=1)
    to_subs(out, dot(rows, matrix(b)), subs)


def make_grad_a(plan, g, b):
    tiles, chans, _, _ = b[0].shape
    out = jax.ShapeDtypeStruct((tiles, chans, plan.count, plan.crop), BF16)
    return pl.pallas_call(
        functools.partial(grad_a_kernel, plan.subs, len(g)),
        grid=(chans,),
        in_specs=[own_spec(value) for value in (*g, *b)],
        out_specs=own_spec(out),
        out_shape=out,
        compiler_params=params(1),
        name="grad_a",
    )(*g, *b)


def middle_kernel(
    step, _, x_ref, d_ref, p_ref, gain_ref, bias_ref, wg_ref, og_ref, ob_ref, wo_ref, wot_ref, *refs
):
    g_ref, gb_ref, gwo_ref, gwg_ref, s_ref = refs[-5:]
    rows = x_ref.shape[0]
    width = gb_ref.shape[-1]

    @pl.when((pl.program_id(0) == 0) & (pl.program_id(1) == 0))
    def _():
        gwo_ref[...] = jnp.zeros_like(gwo_ref)
        gwg_ref[...] = jnp.zeros_like(gwg_ref)

    spread_in(p_ref, s_ref)

    @pl.loop(0, rows // step)
    def _(turn):
        row = pl.multiple_of(turn * step, step)
        z_hat, _ = stats(turned(x_ref, row, step))
        normed = (z_hat * gain_ref[...] + bias_ref[...]).astype(BF16)
        gate = sigmoid(dot(wg_ref[...], normed))
        x_hat, inv_std = stats(load_rows(s_ref, row, step, rows))
        x_norm = (x_hat * og_ref[...] + ob_ref[...]).astype(BF16)
        out_lin = dot(wot_ref[...], x_norm)
        lin = turned(d_ref, row, step) * gate
        grad_lin = lin.astype(BF16)
        gate_back = (lin * out_lin * (1.0 - gate)).astype(BF16)
        upstream = dot(wo_ref[...], grad_lin) * og_ref[...]
        store_rows(s_ref, row, step, rows, norm_back(upstream, x_hat, inv_std))
        for at in range(step):
            gb_ref[row + at] = gate_back[:, at * width : (at + 1) * width]
        gwo_ref[...] += dot(x_norm, grad_lin, NT)
        gwg_ref[...] += dot(normed, gate_back, NT)

    gather_out(s_ref, g_ref)


def make_middle(plan, table, before, x, d, p, small):
    chans = x.shape[-1]
    hidden = p.shape[0]
    cut = table.shape[0]
    grads = [jax.ShapeDtypeStruct((hidden, chans), F32), jax.ShapeDtypeStruct((chans, chans), F32)]
    pairs = plan.pair_spec(chans, lambda i, j, at: (i, at[j, 0], at[j, 1], 0, 0))
    channel = pl.BlockSpec((hidden, plan.rows, plan.width), lambda i, j, at: (0, i, j))
    kept = [] if before is None else [before]
    return pl.pallas_call(
        functools.partial(middle_kernel, plan.step),
        grid_spec=pltpu.PrefetchScalarGridSpec(
            num_scalar_prefetch=1,
            grid=(plan.subs, cut),
            in_specs=[pairs, pairs, channel]
            + [whole(value) for value in small]
            + [pl.BlockSpec(memory_space=pl.ANY) for _ in kept],
            out_specs=[
                channel,
                pl.BlockSpec(
                    (plan.rows, chans, plan.width),
                    lambda i, j, at: (i, 0, at[j, 1] * 2 + at[j, 0]),
                ),
            ]
            + [whole(value) for value in grads],
            scratch_shapes=[plan.scratch(hidden)],
        ),
        out_shape=[
            jax.ShapeDtypeStruct(p.shape, BF16),
            jax.ShapeDtypeStruct((plan.count, chans, plan.crop), BF16),
        ]
        + grads,
        input_output_aliases={4 + len(small): 1} if kept else {},
        compiler_params=params(2),
        name="middle",
    )(table, x, d, p, *small, *kept)


def last_kernel(
    step, x_ref, mask_ref, ga_ref, gb_ref, gate_ref, gain_ref, bias_ref, wt_ref, wcat_ref, *refs
):
    out_ref, gw_ref, sa_ref, sb_ref = refs[-4:]
    rows = x_ref.shape[0]
    hidden = ga_ref.shape[0]

    @pl.when(pl.program_id(0) == 0)
    def _():
        gw_ref[...] = jnp.zeros_like(gw_ref)

    spread_in(ga_ref, sa_ref)
    spread_in(gb_ref, sb_ref)

    @pl.loop(0, rows // step)
    def _(turn):
        row = pl.multiple_of(turn * step, step)
        z_hat, inv_in = stats(turned(x_ref, row, step))
        normed = (z_hat * gain_ref[...] + bias_ref[...]).astype(BF16)
        mask = flat_rows(mask_ref, row, step)
        proj = dot(wt_ref[...], normed)
        sides = []
        for side, ref in enumerate((sa_ref, sb_ref)):
            value = proj[2 * side * hidden : (2 * side + 1) * hidden]
            sig = sigmoid(proj[(2 * side + 1) * hidden : (2 * side + 2) * hidden])
            to_value = load_rows(ref, row, step, rows) * mask * sig
            sides += [to_value.astype(BF16), (to_value * value * (1.0 - sig)).astype(BF16)]
        grad_proj = jnp.concatenate(sides, axis=0)
        gate_back = jnp.concatenate([gate_ref[row + at] for at in range(step)], axis=1)
        every = jnp.concatenate([grad_proj, gate_back], axis=0)
        upstream = dot(wcat_ref[...], every) * gain_ref[...]
        grad = norm_back(upstream, z_hat, inv_in).T.astype(BF16)
        out_ref[pl.ds(row, step)] = grad.reshape((step,) + out_ref.shape[1:])
        gw_ref[...] += dot(normed, grad_proj, NT)


def make_last(plan, sub, before, x, mask, grad_a, grad_b, gate_back, small):
    chans = x.shape[-1]
    hidden = grad_a.shape[0]
    grad = jax.ShapeDtypeStruct((chans, 4 * hidden), F32)
    pairs = plan.pair_spec(chans, lambda j: (sub, j % 2, j // 2, 0, 0))
    channel = (hidden, plan.rows, plan.width)
    kept = [] if before is None else [before]
    return pl.pallas_call(
        functools.partial(last_kernel, plan.step),
        grid=(plan.blocks,),
        in_specs=[
            pairs,
            pl.BlockSpec((plan.rows, plan.width), lambda j: (sub, j)),
            pl.BlockSpec(channel, lambda j: (0, sub, j)),
            pl.BlockSpec(channel, lambda j: (0, 0, j)),
            pl.BlockSpec((plan.rows, chans, plan.width), lambda j: (sub, 0, j)),
        ]
        + [whole(value) for value in small]
        + [pl.BlockSpec(memory_space=pl.ANY) for _ in kept],
        out_specs=[pairs, whole(grad)],
        out_shape=[jax.ShapeDtypeStruct(x.shape, BF16), grad],
        scratch_shapes=[plan.scratch(hidden)] * 2,
        input_output_aliases={5 + len(small): 0} if kept else {},
        compiler_params=params(1),
        name="last",
    )(x, mask, grad_a, grad_b, gate_back, *small, *kept)


def swap_all(array):
    return lax.all_to_all(array, "tile", split_axis=0, concat_axis=0, tiled=True)


def tile_sum(array, tiles):
    chans, width = array.shape
    parts = swap_all(array.astype(BF16)).reshape(tiles, chans // tiles, width)
    part = jnp.sum(parts.astype(F32), axis=0).astype(BF16)
    spread = jnp.broadcast_to(part[None], (tiles,) + part.shape).reshape(chans, width)
    return swap_all(spread).astype(F32)


def body(
    tiles, x, d, token_mask, ln_in_gain, ln_in_bias, w_ab, w_gate, ln_out_gain, ln_out_bias, w_out
):
    count, crop, chans = x.shape
    hidden = w_out.shape[0]
    plan = Plan(tiles, count, crop)
    me = lax.axis_index("tile")
    side = (me // plan.half).astype(jnp.int32)
    valid = token_mask.astype(F32)
    own_valid = lax.dynamic_slice_in_dim(valid, me * count, count)
    turned_valid = valid.reshape(tiles, plan.subs, plan.rows).transpose(1, 0, 2).reshape(crop)
    mask = own_valid[:, None] * turned_valid[None, :]
    gain, bias = ln_in_gain[:, None], ln_in_bias[:, None]
    w_t = w_ab.T
    w_cat = jnp.concatenate([w_ab, w_gate], axis=1)
    mid = [gain, bias, w_gate.T, ln_out_gain[:, None], ln_out_bias[:, None], w_out, w_out.T]
    x, d = plan.view(x), plan.view(d)
    owned = lambda array: array.reshape(plan.half, hidden // plan.half, *array.shape[1:])
    joined = lambda array: array.reshape(hidden, *array.shape[2:])
    every = range(plan.subs)

    own_a, own_b, other_b = [], [], []
    for sub in every:
        factor_a, factor_b = make_factors(plan, sub, x, mask, gain, bias, w_t)
        own_b.append(owned(plan.swap(factor_b)))
        other_b.append(plan.exchange(own_b[sub]))
        own_a.append(owned(plan.swap(factor_a)))

    gate_back, local_mid, owner_g, grad_own, grad_other = None, [], [], [], []
    turns = [([sub], [(1 - side, sub)], [other_b[sub]]) for sub in every]
    turns += [(list(every), [(side, sub) for sub in every], own_b)]
    for which, (subs, at, b) in enumerate(turns):
        table = jnp.stack([jnp.stack([half, jnp.int32(sub)]) for half, sub in at])
        product = plan.swap(joined(make_product(plan, own_a, b)))
        grad_prod, gate_back, *local = make_middle(plan, table, gate_back, x, d, product, mid)
        local_mid.append(jnp.concatenate(local[::-1], axis=1))
        owner_g.append(owned(plan.swap(grad_prod)))
        grads = make_grad_b(plan, owner_g[which], own_a)
        if which < plan.subs:
            grad_other.append(plan.exchange(grads[0]))
        else:
            grad_own = grads
    sum_mid = tile_sum(sum(local_mid), tiles) / crop
    grad_a = plan.swap(joined(make_grad_a(plan, owner_g, other_b + own_b)))
    pair_grad, local_ab = None, []
    for sub in every:
        whole_b = (grad_own[sub].astype(F32) + grad_other[sub].astype(F32)).astype(BF16)
        grad_b = plan.swap(joined(whole_b))
        pair_grad, local = make_last(
            plan, sub, pair_grad, x, mask, grad_a, grad_b, gate_back, [gain, bias, w_t, w_cat]
        )
        local_ab.append(local)
    sum_ab = tile_sum(sum(local_ab), tiles) / crop
    return (pair_grad.reshape(count, crop, chans), sum_ab, sum_mid[:, :chans], sum_mid[:, chans:])


def solution(mesh):
    pairs = P(("crops", "tile"), None, None)
    return jax.shard_map(
        functools.partial(body, mesh.shape["tile"]),
        mesh=mesh,
        in_specs=(pairs, pairs, P("crops")) + (P(),) * 7,
        out_specs=(pairs,) + (P("crops", None),) * 3,
        check_vma=False,
    )
```

time: 776 us -> 750 us (0.966)
  blocking collectives: 447 us -> 89.1 us
  waiting for transfers between devices: 155 us -> 387 us
  starting transfers between devices: 11 us -> 67.3 us
  Pallas kernels: 156 us -> 179 us
  local copies, waits for them, and re-layouts: 4.5 us -> 13.5 us
  other arithmetic: 0.89 us -> 9.46 us
    all_to_all x6 -> x3, blocking collectives: 447 us -> 89.1 us  [swap(): lax.all_to_all(array, 'tile', split_axis=0, concat_axis=0, axis_index_gro...]
    ppermute x0 -> x4, waiting for transfers between devices: none -> 309 us  [exchange(): return lax.ppermute(array, 'tile', self.partner)]
    all_to_all x2 -> x14, waiting for transfers between devices: 155 us -> 78.5 us  [the longest x10 56.5 us: swap(): lax.all_to_all(array, 'tile', split_axis=0, concat_axis=0, axis_index_gro...]
    all_to_all x2 -> x14, starting transfers between devices: 11 us -> 59 us  [the longest x10 41.1 us: swap(): lax.all_to_all(array, 'tile', split_axis=0, concat_axis=0, axis_index_gro...]
    pallas_call x5 -> x14, Pallas kernels: 156 us -> 179 us  [the longest x2 39 us: make_last(): pl.pallas_call(functools.partial(last_kernel, plan.step), grid=(plan.bloc...]
    ppermute x0 -> x4, starting transfers between devices: none -> 8.34 us  [exchange(): return lax.ppermute(array, 'tile', self.partner)]
    unnamed x15 -> x38, local copies, waits for them, and re-layouts: 1.27 us -> 9.51 us
  transfers between devices with their start and end apart: 2 -> 18, of which waited for: 2 -> 12; matrix products, arithmetic and copies ran while one was open for 0% -> 1% of each run, Pallas kernels for 0% -> 21%
where the time goes in v2:
time: 750 us; the launch traced here: 746 us
  waiting for transfers between devices  387 us (52%)
  Pallas kernels  179 us (24%)
  blocking collectives  89.1 us (12%)
  starting transfers between devices  67.3 us (9%)
  local copies, waits for them, and re-layouts  13.5 us (2%)
  other arithmetic  9.46 us (1%)
    ppermute x4, waiting for transfers between devices, exchange(): return lax.ppermute(array, 'tile', self.partner)  309 us
    all_to_all x3, blocking collectives, swap(): lax.all_to_all(array, 'tile', split_axis=0, concat_axis=0, axis_index_gro...  89.1 us
    all_to_all x10, waiting for transfers between devices, swap(): lax.all_to_all(array, 'tile', split_axis=0, concat_axis=0, axis_index_gro...  56.5 us
    all_to_all x10, starting transfers between devices, swap(): lax.all_to_all(array, 'tile', split_axis=0, concat_axis=0, axis_index_gro...  41.1 us
    pallas_call x2, Pallas kernels, make_last(): pl.pallas_call(functools.partial(last_kernel, plan.step), grid=(plan.bloc...  39 us
    pallas_call x3, Pallas kernels, make_middle(): pl.pallas_call(functools.partial(middle_kernel, plan.step), grid_spec=plt...  36.6 us
    pallas_call x3, Pallas kernels, make_grad_b(): pl.pallas_call(functools.partial(grad_b_kernel, plan.subs), grid=(g.shape...  33.7 us
    pallas_call x3, Pallas kernels, make_product(): pl.pallas_call(functools.partial(product_kernel, plan.subs, len(b)), grid...  31.9 us
  transfers between devices with their start and end apart: 18, of which 12 were waited for; matrix products, arithmetic and copies ran while one was open for 1% of the time, Pallas kernels for 21%

profile of v2, /device:TPU:0, one launch (start us, length us, event | category | flops | bytes accessed | tf_op | source)
XLA Modules:
  0.0 746.4 jit_solution(8366324769283163145)
XLA Ops:
  4.2 12.0 %factors.2 = (bf16[128,16,512]{2,1,0:T(8,128)(2,1)S(1)}, bf16[128,16,512]{2,1,0:T(8,128)(2,1)}) custom-call(bf16[32,16,2,16,128]{4,3,2,1,0:T(8,128)(2,1)} %bitcast.75, f32[32,512]{1,0:T(8,128)S(1)} %broadcast_multiply_fusion.mask_ref, f32[128,1]{1,0:T(8,128)S(1)} %copy.65.gain_ref, f32[128,1]{1,0:T(8,128)S(1)} %copy.66.bias_ref, bf16[512,128]{1,0:T(8,128)(2,1)S(1)} %bitcast.59), custom_call_target="tpu_custom_call" | custom-call | tf_op jit(solution)/shard_map/factors/pallas_call | solution.py:153
  17.6 5.2 all-to-all-start
  22.8 12.1 %factors.3 = (bf16[128,16,512]{2,1,0:T(8,128)(2,1)S(1)}, bf16[128,16,512]{2,1,0:T(8,128)(2,1)}) custom-call(bf16[32,16,2,16,128]{4,3,2,1,0:T(8,128)(2,1)} %bitcast.76, f32[32,512]{1,0:T(8,128)S(1)} %broadcast_multiply_fusion.mask_ref, f32[128,1]{1,0:T(8,128)S(1)} %copy.65.gain_ref, f32[128,1]{1,0:T(8,128)S(1)} %copy.66.bias_ref, bf16[512,128]{1,0:T(8,128)(2,1)S(1)} %bitcast.60), custom_call_target="tpu_custom_call" | custom-call | tf_op jit(solution)/shard_map/factors/pallas_call | solution.py:153
  36.2 12.3 %all-to-all-done = bf16[128,16,512]{2,1,0:T(8,128)(2,1)S(1)} async-done(((bf16[128,16,512]{2,1,0:T(8,128)(2,1)}), bf16[128,16,512]{2,1,0:T(8,128)(2,1)S(1)}, u32[]{:S(2)}, u32[]{:S(2)}) %all-to-all-start) | async-done | bytes 2097184 | tf_op jit(solution)/shard_map/all_to_all | solution.py:120
  48.5 30.6 %all_to_all.92 = bf16[128,16,512]{2,1,0:T(8,128)(2,1)} all-to-all(bf16[128,16,512]{2,1,0:T(8,128)(2,1)} %copy-done.6), channel_id=1, replica_groups={{0,1,2,3,4,5,6,7},{8,9,10,11,12,13,14,15},{16,17,18,19,20,21,22,23},{24..., dimensions={0} | all-to-all | bytes 4194304 | tf_op jit(solution)/shard_map/all_to_all | solution.py:120
  79.1 29.3 %all_to_all.93 = bf16[128,16,512]{2,1,0:T(8,128)(2,1)} all-to-all(bf16[128,16,512]{2,1,0:T(8,128)(2,1)S(1)} %copy-done.11), channel_id=1, replica_groups={{0,1,2,3,4,5,6,7},{8,9,10,11,12,13,14,15},{16,17,18,19,20,21,22,23},{24..., dimensions={0} | all-to-all | bytes 4194304 | tf_op jit(solution)/shard_map/all_to_all | solution.py:120
  108.4 29.2 %all_to_all.94 = bf16[128,16,512]{2,1,0:T(8,128)(2,1)} all-to-all(bf16[128,16,512]{2,1,0:T(8,128)(2,1)S(1)} %copy-done.12), channel_id=1, replica_groups={{0,1,2,3,4,5,6,7},{8,9,10,11,12,13,14,15},{16,17,18,19,20,21,22,23},{24..., dimensions={0} | all-to-all | bytes 4194304 | tf_op jit(solution)/shard_map/all_to_all | solution.py:120
  137.6 11.3 %product.5 = bf16[8,16,32,256]{3,2,1,0:T(8,128)(2,1)S(1)} custom-call(bf16[8,16,16,512]{3,2,1,0:T(8,128)(2,1)} %bitcast.46, bf16[8,16,16,512]{3,2,1,0:T(8,128)(2,1)} %bitcast.82, bf16[8,16,16,512]{3,2,1,0:T(8,128)(2,1)} %bitcast.91, bf16[8,16,16,512]{3,2,1,0:T(8,128)(2,1)} %bitcast.94), custom_call_target="tpu_custom_call" | custom-call | tf_op jit(solution)/shard_map/product/pallas_call | solution.py:206
  150.2 4.5 all-to-all-start.8
  154.7 2.7 collective-permute-start
  157.7 136.6 %collective-permute-done.refs_2_.refs_3_ = bf16[8,16,16,512]{3,2,1,0:T(8,128)(2,1)S(1)} collective-permute-done((bf16[8,16,16,512]{3,2,1,0:T(8,128)(2,1)}, bf16[8,16,16,512]{3,2,1,0:T(8,128)(2,1)S(1)}, u32[]{:S(2)}, u32[]{:S(2)}) %collective-permute-start) | collective-permute-done | bytes 2097184 | tf_op jit(solution)/shard_map/ppermute | solution.py:125
  295.6 10.3 %product.3 = bf16[8,16,32,128]{3,2,1,0:T(8,128)(2,1)S(1)} custom-call(bf16[8,16,16,512]{3,2,1,0:T(8,128)(2,1)S(1)} %bitcast.50, bf16[8,16,16,512]{3,2,1,0:T(8,128)(2,1)} %bitcast.83, bf16[8,16,16,512]{3,2,1,0:T(8,128)(2,1)} %copy-done.9), custom_call_target="tpu_custom_call" | custom-call | tf_op jit(solution)/shard_map/product/pallas_call | solution.py:206
  306.9 3.6 all-to-all-start.3
  310.4 28.4 %collective-permute-done.1.refs_2_.refs_4_ = bf16[8,16,16,512]{3,2,1,0:T(8,128)(2,1)} collective-permute-done((bf16[8,16,16,512]{3,2,1,0:T(8,128)(2,1)}, bf16[8,16,16,512]{3,2,1,0:T(8,128)(2,1)}, u32[]{:S(2)}, u32[]{:S(2)}) %collective-permute-start.1) | collective-permute-done | bytes 2097184 | tf_op jit(solution)/shard_map/ppermute | solution.py:125
  338.8 10.3 %product.4 = bf16[8,16,32,128]{3,2,1,0:T(8,128)(2,1)S(1)} custom-call(bf16[8,16,16,512]{3,2,1,0:T(8,128)(2,1)S(1)} %bitcast.51, bf16[8,16,16,512]{3,2,1,0:T(8,128)(2,1)} %bitcast.84, bf16[8,16,16,512]{3,2,1,0:T(8,128)(2,1)} %collective-permute-done.1.refs_2_.refs_4_), custom_call_target="tpu_custom_call" | custom-call | tf_op jit(solution)/shard_map/product/pallas_call | solution.py:206
  350.1 3.7 all-to-all-start.6
  354.4 9.7 %middle.3 = (bf16[128,32,128]{2,1,0:T(8,128)(2,1)S(1)}, bf16[32,128,512]{2,1,0:T(8,128)(2,1)}, f32[128,128]{1,0:T(8,128)S(1)}, f32[128,128]{1,0:T(8,128)S(1)}) custom-call(s32[1,2]{1,0:T(1,128)S(1)} %fusion.5._, bf16[32,16,2,16,128]{4,3,2,1,0:T(8,128)(2,1)} %bitcast.77, bf16[32,16,2,16,128]{4,3,2,1,0:T(8,128)(2,1)} %bitcast.88, ...), custom_call_target="tpu_custom_call" | custom-call | tf_op jit(solution)/shard_map/middle/pallas_call | solution.py:302
  365.0 3.1 all-to-all-done.6.p_ref
  368.2 3.6 all-to-all-start.4
  371.9 9.8 %middle.4 = (bf16[128,32,128]{2,1,0:T(8,128)(2,1)}, bf16[32,128,512]{2,1,0:T(8,128)(2,1)}, f32[128,128]{1,0:T(8,128)S(1)}, f32[128,128]{1,0:T(8,128)S(1)}) custom-call(s32[1,2]{1,0:T(1,128)S(1)} %fusion.3._, bf16[32,16,2,16,128]{4,3,2,1,0:T(8,128)(2,1)} %bitcast.78, bf16[32,16,2,16,128]{4,3,2,1,0:T(8,128)(2,1)} %bitcast.89, ...), custom_call_target="tpu_custom_call", output_to_operand_aliasing={{1}: (11, {})} | custom-call | tf_op jit(solution)/shard_map/middle/pallas_call | solution.py:302
  381.7 17.1 %middle.5 = (bf16[128,32,256]{2,1,0:T(8,128)(2,1)}, bf16[32,128,512]{2,1,0:T(8,128)(2,1)}, f32[128,128]{1,0:T(8,128)S(1)}, f32[128,128]{1,0:T(8,128)S(1)}) custom-call(s32[2,2]{1,0:T(2,128)S(1)} %pad_add_fusion._, bf16[32,16,2,16,128]{4,3,2,1,0:T(8,128)(2,1)} %bitcast.79, bf16[32,16,2,16,128]{4,3,2,1,0:T(8,128)(2,1)} %bitcast.90, ...), custom_call_target="tpu_custom_call", output_to_operand_aliasing={{1}: (11, {})} | custom-call | tf_op jit(solution)/shard_map/middle/pallas_call | solution.py:302
  398.8 4.4 all-to-all-start.9
  403.2 11.4 %grad_b.5 = bf16[8,16,16,512]{3,2,1,0:T(8,128)(2,1)} custom-call(bf16[8,16,32,128]{3,2,1,0:T(8,128)(2,1)S(1)} %bitcast.52, bf16[8,16,16,512]{3,2,1,0:T(8,128)(2,1)} %bitcast.47, bf16[8,16,16,512]{3,2,1,0:T(8,128)(2,1)} %bitcast.85), custom_call_target="tpu_custom_call" | custom-call | tf_op jit(solution)/shard_map/grad_b/pallas_call | solution.py:227
  414.6 3.0 collective-permute-start.3
  417.6 23.6 %all-to-all-done.9 = bf16[128,32,256]{2,1,0:T(8,128)(2,1)} async-done(((bf16[128,32,256]{2,1,0:T(8,128)(2,1)}), bf16[128,32,256]{2,1,0:T(8,128)(2,1)}, u32[]{:S(2)}, u32[]{:S(2)}) %all-to-all-start.9) | async-done | bytes 2097184 | tf_op jit(solution)/shard_map/all_to_all | solution.py:120
  441.2 3.6 all-to-all-start.7
  444.7 12.1 %grad_b.3 = (bf16[8,16,16,512]{3,2,1,0:T(8,128)(2,1)S(1)}, bf16[8,16,16,512]{3,2,1,0:T(8,128)(2,1)}) custom-call(bf16[8,16,32,256]{3,2,1,0:T(8,128)(2,1)} %bitcast.25.refs_2_.g_ref, bf16[8,16,16,512]{3,2,1,0:T(8,128)(2,1)} %bitcast.48, bf16[8,16,16,512]{3,2,1,0:T(8,128)(2,1)} %bitcast.86), custom_call_target="tpu_custom_call" | custom-call | tf_op jit(solution)/shard_map/grad_b/pallas_call | solution.py:227
  456.8 52.2 %collective-permute-done.3 = bf16[8,16,16,512]{3,2,1,0:T(8,128)(2,1)} collective-permute-done((bf16[8,16,16,512]{3,2,1,0:T(8,128)(2,1)}, bf16[8,16,16,512]{3,2,1,0:T(8,128)(2,1)}, u32[]{:S(2)}, u32[]{:S(2)}) %collective-permute-start.3) | collective-permute-done | bytes 2097184 | tf_op jit(solution)/shard_map/ppermute | solution.py:125
  509.0 4.0 add_convert_fusion
  513.0 4.4 all-to-all-start.12
  517.4 13.6 %grad_a.1 = bf16[8,16,32,512]{3,2,1,0:T(8,128)(2,1)} custom-call(bf16[8,16,32,128]{3,2,1,0:T(8,128)(2,1)S(1)} %bitcast.53, bf16[8,16,32,128]{3,2,1,0:T(8,128)(2,1)S(1)} %bitcast.54, bf16[8,16,32,256]{3,2,1,0:T(8,128)(2,1)} %bitcast.25.refs_2_.g_ref, bf16[8,16,16,512]{3,2,1,0:T(8,128)(2,1)} %copy-done.9, ...), custom_call_target="tpu_custom_call" | custom-call | tf_op jit(solution)/shard_map/grad_a/pallas_call | solution.py:247
  531.0 12.1 %all-to-all-done.12.gb_ref = bf16[128,16,512]{2,1,0:T(8,128)(2,1)} async-done(((bf16[128,16,512]{2,1,0:T(8,128)(2,1)}), bf16[128,16,512]{2,1,0:T(8,128)(2,1)}, u32[]{:S(2)}, u32[]{:S(2)}) %all-to-all-start.12) | async-done | bytes 2097184 | tf_op jit(solution)/shard_map/all_to_all | solution.py:120
  543.1 4.5 all-to-all-start.10
  547.7 10.3 %grad_b.4 = bf16[8,16,16,512]{3,2,1,0:T(8,128)(2,1)S(1)} custom-call(bf16[8,16,32,128]{3,2,1,0:T(8,128)(2,1)S(1)} %bitcast.55, bf16[8,16,16,512]{3,2,1,0:T(8,128)(2,1)} %bitcast.49, bf16[8,16,16,512]{3,2,1,0:T(8,128)(2,1)} %bitcast.87), custom_call_target="tpu_custom_call" | custom-call | tf_op jit(solution)/shard_map/grad_b/pallas_call | solution.py:227
  557.9 2.3 collective-permute-start.2
  560.3 91.5 %collective-permute-done.2 = bf16[8,16,16,512]{3,2,1,0:T(8,128)(2,1)S(1)} collective-permute-done((bf16[8,16,16,512]{3,2,1,0:T(8,128)(2,1)S(1)}, bf16[8,16,16,512]{3,2,1,0:T(8,128)(2,1)S(1)}, u32[]{:S(2)}, u32[]{:S(2)}) %collective-permute-start.2) | collective-permute-done | bytes 2097184 | tf_op jit(solution)/shard_map/ppermute | solution.py:125
  651.8 2.3 add_convert_fusion.1
  654.1 3.7 all-to-all-start.11
  658.5 19.5 %last.2 = (bf16[32,16,2,16,128]{4,3,2,1,0:T(8,128)(2,1)}, f32[128,512]{1,0:T(8,128)S(1)}) custom-call(bf16[32,16,2,16,128]{4,3,2,1,0:T(8,128)(2,1)} %bitcast.80, f32[32,512]{1,0:T(8,128)S(1)} %broadcast_multiply_fusion.mask_ref, bf16[128,32,512]{2,1,0:T(8,128)(2,1)} %all-to-all-done.10.ga_ref, bf16[128,16,512]{2,1,0:T(8,128)(2,1)} %all-to-all-done.12.gb_ref, ...), custom_call_target="tpu_custom_call" | custom-call | tf_op jit(solution)/shard_map/last/pallas_call | solution.py:374
  678.0 5.4 all-to-all-done.11.gb_ref
  683.4 4.9 all-to-all-start.15
  688.4 19.6 %last.3 = (bf16[32,16,2,16,128]{4,3,2,1,0:T(8,128)(2,1)}, f32[128,512]{1,0:T(8,128)S(1)}) custom-call(bf16[32,16,2,16,128]{4,3,2,1,0:T(8,128)(2,1)} %bitcast.81, f32[32,512]{1,0:T(8,128)S(1)} %broadcast_multiply_fusion.mask_ref, bf16[128,32,512]{2,1,0:T(8,128)(2,1)} %all-to-all-done.10.ga_ref, ...), custom_call_target="tpu_custom_call", output_to_operand_aliasing={{0}: (9, {})} | custom-call | tf_op jit(solution)/shard_map/last/pallas_call | solution.py:374
  708.6 6.0 all-to-all-start.13
  714.6 7.9 %all-to-all-done.13 = bf16[16,8,512]{2,1,0:T(8,128)(2,1)S(1)} async-done(((bf16[16,8,512]{2,1,0:T(8,128)(2,1)}), bf16[16,8,512]{2,1,0:T(8,128)(2,1)S(1)}, u32[]{:S(2)}, u32[]{:S(2)}) %all-to-all-start.13) | async-done | bytes 131104 | tf_op jit(solution)/shard_map/all_to_all | solution.py:396
  723.2 3.5 all-to-all-start.16
  726.7 6.8 all-to-all-done.16
  734.2 3.5 all-to-all-start.14
  738.4 7.2 all-to-all-done.14
  (69 shorter events, 17.0 us)
Async XLA Ops:
  16.2 1.4 copy-start.5
  17.6 30.9 %all-to-all-start = ((bf16[128,16,512]{2,1,0:T(8,128)(2,1)}), bf16[128,16,512]{2,1,0:T(8,128)(2,1)S(1)}, u32[]{:S(2)}, u32[]{:S(2)}) async-start(bf16[128,16,512]{2,1,0:T(8,128)(2,1)} %copy-done.5), calls=%async_computation | async-start | bytes 4194304 | tf_op jit(solution)/shard_map/all_to_all | solution.py:120
  34.9 1.3 copy-start.6
  48.5 30.6 %copy-start = (bf16[128,16,512]{2,1,0:T(8,128)(2,1)}, bf16[128,16,512]{2,1,0:T(8,128)(2,1)S(1)}, u32[]{:S(2)}) copy-start(bf16[128,16,512]{2,1,0:T(8,128)(2,1)S(1)} %all-to-all-done) | copy-start | bytes 6291460
  48.5 30.6 %copy-start.11 = (bf16[128,16,512]{2,1,0:T(8,128)(2,1)S(1)}, bf16[128,16,512]{2,1,0:T(8,128)(2,1)}, u32[]{:S(2)}) copy-start(bf16[128,16,512]{2,1,0:T(8,128)(2,1)} %get-tuple-element.28) | copy-start | bytes 6291460
  79.1 29.3 %copy-start.12 = (bf16[128,16,512]{2,1,0:T(8,128)(2,1)S(1)}, bf16[128,16,512]{2,1,0:T(8,128)(2,1)}, u32[]{:S(2)}) copy-start(bf16[128,16,512]{2,1,0:T(8,128)(2,1)} %get-tuple-element.30) | copy-start | bytes 6291460
  148.9 1.3 copy-start.2
  150.2 145.4 %copy-start.1 = (bf16[128,16,512]{2,1,0:T(8,128)(2,1)S(1)}, bf16[128,16,512]{2,1,0:T(8,128)(2,1)}, u32[]{:S(2)}) copy-start(bf16[128,16,512]{2,1,0:T(8,128)(2,1)} %copy-done) | copy-start | bytes 6291460
  150.2 156.7 %all-to-all-start.8 = ((bf16[128,32,256]{2,1,0:T(8,128)(2,1)}), bf16[128,32,256]{2,1,0:T(8,128)(2,1)}, u32[]{:S(2)}, u32[]{:S(2)}) async-start(bf16[128,32,256]{2,1,0:T(8,128)(2,1)} %bitcast.56), calls=%async_computation.8 | async-start | bytes 4194304 | tf_op jit(solution)/shard_map/all_to_all | solution.py:120
  154.7 139.6 %collective-permute-start = (bf16[8,16,16,512]{3,2,1,0:T(8,128)(2,1)}, bf16[8,16,16,512]{3,2,1,0:T(8,128)(2,1)S(1)}, u32[]{:S(2)}, u32[]{:S(2)}) collective-permute-start(bf16[8,16,16,512]{3,2,1,0:T(8,128)(2,1)} %bitcast.92), channel_id=1, source_target_pairs={{0,8},{1,9},{2,10},{3,11},{4,12},{5,13},{6,14},{7,15},{8,0},{9,1},... | collective-permute-start | bytes 6291464 | tf_op jit(solution)/shard_map/ppermute | solution.py:125
  157.4 181.4 %collective-permute-start.1 = (bf16[8,16,16,512]{3,2,1,0:T(8,128)(2,1)}, bf16[8,16,16,512]{3,2,1,0:T(8,128)(2,1)}, u32[]{:S(2)}, u32[]{:S(2)}) collective-permute-start(bf16[8,16,16,512]{3,2,1,0:T(8,128)(2,1)} %bitcast.95), channel_id=1, source_target_pairs={{0,8},{1,9},{2,10},{3,11},{4,12},{5,13},{6,14},{7,15},{8,0},{9,1},... | collective-permute-start | bytes 6291464 | tf_op jit(solution)/shard_map/ppermute | solution.py:125
  294.2 1.3 copy-start.9
  305.9 1.0 copy-start.4
  306.9 43.2 %all-to-all-start.3 = ((bf16[128,32,128]{2,1,0:T(8,128)(2,1)}), bf16[128,32,128]{2,1,0:T(8,128)(2,1)S(1)}, u32[]{:S(2)}, u32[]{:S(2)}) async-start(bf16[128,32,128]{2,1,0:T(8,128)(2,1)} %bitcast.58), calls=%async_computation.3 | async-start | bytes 2097152 | tf_op jit(solution)/shard_map/all_to_all | solution.py:120
  349.1 1.0 copy-start.3
  350.1 3.7 copy-start.14
  350.1 3.9 copy-start.15
  350.1 4.0 copy-start.16
  350.1 4.1 copy-start.8
  350.1 18.1 %all-to-all-start.6 = ((bf16[128,32,128]{2,1,0:T(8,128)(2,1)}), bf16[128,32,128]{2,1,0:T(8,128)(2,1)S(1)}, u32[]{:S(2)}, u32[]{:S(2)}) async-start(bf16[128,32,128]{2,1,0:T(8,128)(2,1)} %bitcast.57), calls=%async_computation.6 | async-start | bytes 2097152 | tf_op jit(solution)/shard_map/all_to_all | solution.py:120
  364.1 1.0 copy-start.7
  368.2 30.7 %all-to-all-start.4 = ((bf16[128,32,128]{2,1,0:T(8,128)(2,1)}), bf16[128,32,128]{2,1,0:T(8,128)(2,1)S(1)}, u32[]{:S(2)}, u32[]{:S(2)}) async-start(bf16[128,32,128]{2,1,0:T(8,128)(2,1)} %copy-done.7), calls=%async_computation.4 | async-start | bytes 2097152 | tf_op jit(solution)/shard_map/all_to_all | solution.py:120
  398.8 42.3 %all-to-all-start.9 = ((bf16[128,32,256]{2,1,0:T(8,128)(2,1)}), bf16[128,32,256]{2,1,0:T(8,128)(2,1)}, u32[]{:S(2)}, u32[]{:S(2)}) async-start(bf16[128,32,256]{2,1,0:T(8,128)(2,1)} %get-tuple-element.34), calls=%async_computation.9 | async-start | bytes 4194304 | tf_op jit(solution)/shard_map/all_to_all | solution.py:120
  414.6 94.5 %collective-permute-start.3 = (bf16[8,16,16,512]{3,2,1,0:T(8,128)(2,1)}, bf16[8,16,16,512]{3,2,1,0:T(8,128)(2,1)}, u32[]{:S(2)}, u32[]{:S(2)}) collective-permute-start(bf16[8,16,16,512]{3,2,1,0:T(8,128)(2,1)} %grad_b.5), channel_id=1, source_target_pairs={{0,8},{1,9},{2,10},{3,11},{4,12},{5,13},{6,14},{7,15},{8,0},{9,1},... | collective-permute-start | bytes 6291464 | tf_op jit(solution)/shard_map/ppermute | solution.py:125
  441.2 71.9 %all-to-all-start.7 = ((bf16[128,32,128]{2,1,0:T(8,128)(2,1)}), bf16[128,32,128]{2,1,0:T(8,128)(2,1)S(1)}, u32[]{:S(2)}, u32[]{:S(2)}) async-start(bf16[128,32,128]{2,1,0:T(8,128)(2,1)} %get-tuple-element.32), calls=%async_computation.7 | async-start | bytes 2097152 | tf_op jit(solution)/shard_map/all_to_all | solution.py:120
  513.0 30.1 %all-to-all-start.12 = ((bf16[128,16,512]{2,1,0:T(8,128)(2,1)}), bf16[128,16,512]{2,1,0:T(8,128)(2,1)}, u32[]{:S(2)}, u32[]{:S(2)}) async-start(bf16[128,16,512]{2,1,0:T(8,128)(2,1)} %bitcast.99), calls=%async_computation.12 | async-start | bytes 4194304 | tf_op jit(solution)/shard_map/all_to_all | solution.py:120
  543.1 111.0 %all-to-all-start.10 = ((bf16[128,32,512]{2,1,0:T(8,128)(2,1)}), bf16[128,32,512]{2,1,0:T(8,128)(2,1)}, u32[]{:S(2)}, u32[]{:S(2)}) async-start(bf16[128,32,512]{2,1,0:T(8,128)(2,1)} %bitcast.97), calls=%async_computation.10 | async-start | bytes 8388608 | tf_op jit(solution)/shard_map/all_to_all | solution.py:120
  547.6 104.1 %copy-start.10 = (bf16[8,16,16,512]{3,2,1,0:T(8,128)(2,1)S(1)}, bf16[8,16,16,512]{3,2,1,0:T(8,128)(2,1)}, u32[]{:S(2)}) copy-start(bf16[8,16,16,512]{3,2,1,0:T(8,128)(2,1)} %get-tuple-element.35) | copy-start | bytes 6291460
  557.9 93.8 %collective-permute-start.2 = (bf16[8,16,16,512]{3,2,1,0:T(8,128)(2,1)S(1)}, bf16[8,16,16,512]{3,2,1,0:T(8,128)(2,1)S(1)}, u32[]{:S(2)}, u32[]{:S(2)}) collective-permute-start(bf16[8,16,16,512]{3,2,1,0:T(8,128)(2,1)S(1)} %grad_b.4), channel_id=1, source_target_pairs={{0,8},{1,9},{2,10},{3,11},{4,12},{5,13},{6,14},{7,15},{8,0},{9,1},... | collective-permute-start | bytes 6291464 | tf_op jit(solution)/shard_map/ppermute | solution.py:125
  654.1 3.7 copy-start.13
  654.1 29.4 %all-to-all-start.11 = ((bf16[128,16,512]{2,1,0:T(8,128)(2,1)}), bf16[128,16,512]{2,1,0:T(8,128)(2,1)S(1)}, u32[]{:S(2)}, u32[]{:S(2)}) async-start(bf16[128,16,512]{2,1,0:T(8,128)(2,1)} %bitcast.98), calls=%async_computation.11 | async-start | bytes 4194304 | tf_op jit(solution)/shard_map/all_to_all | solution.py:120
  683.4 25.1 %all-to-all-start.15 = ((bf16[16,8,256]{2,1,0:T(8,128)(2,1)}), bf16[16,8,256]{2,1,0:T(8,128)(2,1)S(1)}, u32[]{:S(2)}, u32[]{:S(2)}) async-start(bf16[16,8,256]{2,1,0:T(8,128)(2,1)} %fusion.2), calls=%async_computation.15 | async-start | bytes 131072 | tf_op jit(solution)/shard_map/all_to_all | solution.py:396
  708.6 14.0 %all-to-all-start.13 = ((bf16[16,8,512]{2,1,0:T(8,128)(2,1)}), bf16[16,8,512]{2,1,0:T(8,128)(2,1)S(1)}, u32[]{:S(2)}, u32[]{:S(2)}) async-start(bf16[16,8,512]{2,1,0:T(8,128)(2,1)} %fusion), calls=%async_computation.13 | async-start | bytes 262144 | tf_op jit(solution)/shard_map/all_to_all | solution.py:396
  723.2 10.4 %all-to-all-start.16 = ((bf16[16,8,256]{2,1,0:T(8,128)(2,1)}), bf16[16,8,256]{2,1,0:T(8,128)(2,1)S(1)}, u32[]{:S(2)}, u32[]{:S(2)}) async-start(bf16[16,8,256]{2,1,0:T(8,128)(2,1)} %broadcast_in_dim.30), calls=%async_computation.16 | async-start | bytes 131072 | tf_op jit(solution)/shard_map/all_to_all | solution.py:396
  734.2 11.4 %all-to-all-start.14 = ((bf16[16,8,512]{2,1,0:T(8,128)(2,1)}), bf16[16,8,512]{2,1,0:T(8,128)(2,1)S(1)}, u32[]{:S(2)}, u32[]{:S(2)}) async-start(bf16[16,8,512]{2,1,0:T(8,128)(2,1)} %broadcast_in_dim.29), calls=%async_computation.14 | async-start | bytes 262144 | tf_op jit(solution)/shard_map/all_to_all | solution.py:396

commit v3 on v2

--- a/solution.py
+++ b/solution.py
@@ -8,6 +8,7 @@
 from jax.sharding import PartitionSpec as P
 
 EPS = 1e-05
+CHANS = 4
 F32 = jnp.float32
 BF16 = jnp.bfloat16
 NN = (((1,), (0,)), ((), ()))
@@ -18,6 +19,12 @@
 def params(steps):
     return pltpu.CompilerParams(
         dimension_semantics=("arbitrary",) * steps, vmem_limit_bytes=50 * 1024 * 1024
+    )
+
+
+def cost(micros):
+    return pl.CostEstimate(
+        flops=int(micros * 1.0e9), bytes_accessed=int(micros * 3.0e6), transcendentals=0
     )
 
 
@@ -164,40 +171,43 @@
         out_shape=[out, out],
         scratch_shapes=[plan.scratch(hidden)] * 2,
         compiler_params=params(1),
+        cost_estimate=cost(12),
         name="factors",
     )(x, mask, gain, bias, w_t)
 
 
-def matrix(refs):
-    parts = [ref[...].reshape(-1, ref.shape[-1]) for ref in refs]
+def matrix(refs, chan):
+    parts = [ref[:, chan].reshape(-1, ref.shape[-1]) for ref in refs]
     return jnp.concatenate(parts, axis=0) if len(parts) > 1 else parts[0]
 
 
-def by_sub(ref, subs):
+def by_sub(ref, chan, subs):
     rows = ref.shape[2] // subs
     parts = [
-        ref[:, 0, sub * rows : (sub + 1) * rows, :].reshape(-1, ref.shape[3]) for sub in range(subs)
+        ref[:, chan, sub * rows : (sub + 1) * rows, :].reshape(-1, ref.shape[3])
+        for sub in range(subs)
     ]
     return jnp.concatenate(parts, axis=0) if subs > 1 else parts[0]
 
 
-def to_subs(ref, value, subs):
+def to_subs(ref, chan, value, subs):
     tiles, _, rows, cols = ref.shape
     part = value.shape[0] // subs
     for sub in range(subs):
-        ref[:, 0, sub * (rows // subs) : (sub + 1) * (rows // subs), :] = value[
+        ref[:, chan, sub * (rows // subs) : (sub + 1) * (rows // subs), :] = value[
             sub * part : (sub + 1) * part
         ].astype(BF16).reshape(tiles, rows // subs, cols)
 
 
 def own_spec(array):
     src, _, rows, cols = array.shape
-    return pl.BlockSpec((src, 1, rows, cols), lambda h: (0, h, 0, 0))
+    return pl.BlockSpec((src, CHANS, rows, cols), lambda h: (0, h, 0, 0))
 
 
 def product_kernel(subs, count, *refs):
     a, b, p_ref = refs[:subs], refs[subs : subs + count], refs[subs + count]
-    to_subs(p_ref, dot(matrix(a), matrix(b), NT), subs)
+    for chan in range(CHANS):
+        to_subs(p_ref, chan, dot(matrix(a, chan), matrix(b, chan), NT), subs)
 
 
 def make_product(plan, a, b):
@@ -205,40 +215,45 @@
     out = jax.ShapeDtypeStruct((tiles, chans, plan.count, len(b) * plan.width), BF16)
     return pl.pallas_call(
         functools.partial(product_kernel, plan.subs, len(b)),
-        grid=(chans,),
+        grid=(chans // CHANS,),
         in_specs=[own_spec(value) for value in (*a, *b)],
         out_specs=own_spec(out),
         out_shape=out,
         compiler_params=params(1),
+        cost_estimate=cost(6),
         name="product",
     )(*a, *b)
 
 
 def grad_b_kernel(subs, g_ref, *refs):
     a, outs = refs[:subs], refs[subs:]
-    grad = dot(by_sub(g_ref, subs), matrix(a), TN).astype(BF16)
-    size = grad.shape[0] // len(outs)
-    for at, out in enumerate(outs):
-        out[...] = grad[at * size : (at + 1) * size].reshape(out.shape)
+    for chan in range(CHANS):
+        grad = dot(by_sub(g_ref, chan, subs), matrix(a, chan), TN).astype(BF16)
+        size = grad.shape[0] // len(outs)
+        for at, out in enumerate(outs):
+            part = grad[at * size : (at + 1) * size]
+            out[:, chan] = part.reshape(out.shape[0], *out.shape[2:])
 
 
 def make_grad_b(plan, g, a):
     outs = g.shape[-1] // plan.width
     return pl.pallas_call(
         functools.partial(grad_b_kernel, plan.subs),
-        grid=(g.shape[1],),
+        grid=(g.shape[1] // CHANS,),
         in_specs=[own_spec(value) for value in (g, *a)],
         out_specs=[own_spec(a[0])] * outs,
         out_shape=[jax.ShapeDtypeStruct(a[0].shape, BF16)] * outs,
         compiler_params=params(1),
+        cost_estimate=cost(8),
         name="grad_b",
     )(g, *a)
 
 
 def grad_a_kernel(subs, count, *refs):
     g, b, out = refs[:count], refs[count:-1], refs[-1]
-    rows = jnp.concatenate([by_sub(ref, subs) for ref in g], axis=1)
-    to_subs(out, dot(rows, matrix(b)), subs)
+    for chan in range(CHANS):
+        rows = jnp.concatenate([by_sub(ref, chan, subs) for ref in g], axis=1)
+        to_subs(out, chan, dot(rows, matrix(b, chan)), subs)
 
 
 def make_grad_a(plan, g, b):
@@ -246,11 +261,12 @@
     out = jax.ShapeDtypeStruct((tiles, chans, plan.count, plan.crop), BF16)
     return pl.pallas_call(
         functools.partial(grad_a_kernel, plan.subs, len(g)),
-        grid=(chans,),
+        grid=(chans // CHANS,),
         in_specs=[own_spec(value) for value in (*g, *b)],
         out_specs=own_spec(out),
         out_shape=out,
         compiler_params=params(1),
+        cost_estimate=cost(10),
         name="grad_a",
     )(*g, *b)
 
@@ -298,7 +314,7 @@
     grads = [jax.ShapeDtypeStruct((hidden, chans), F32), jax.ShapeDtypeStruct((chans, chans), F32)]
     pairs = plan.pair_spec(chans, lambda i, j, at: (i, at[j, 0], at[j, 1], 0, 0))
     channel = pl.BlockSpec((hidden, plan.rows, plan.width), lambda i, j, at: (0, i, j))
-    kept = [] if before is None else [before]
+    kept = list(before)
     return pl.pallas_call(
         functools.partial(middle_kernel, plan.step),
         grid_spec=pltpu.PrefetchScalarGridSpec(
@@ -324,6 +340,7 @@
         + grads,
         input_output_aliases={4 + len(small): 1} if kept else {},
         compiler_params=params(2),
+        cost_estimate=cost(10 * cut),
         name="middle",
     )(table, x, d, p, *small, *kept)
 
@@ -364,13 +381,13 @@
         gw_ref[...] += dot(normed, grad_proj, NT)
 
 
-def make_last(plan, sub, before, x, mask, grad_a, grad_b, gate_back, small):
+def make_last(plan, sub, before, ready, x, mask, grad_a, grad_b, gate_back, small):
     chans = x.shape[-1]
     hidden = grad_a.shape[0]
     grad = jax.ShapeDtypeStruct((chans, 4 * hidden), F32)
     pairs = plan.pair_spec(chans, lambda j: (sub, j % 2, j // 2, 0, 0))
     channel = (hidden, plan.rows, plan.width)
-    kept = [] if before is None else [before]
+    kept = [ready] if before is None else [before]
     return pl.pallas_call(
         functools.partial(last_kernel, plan.step),
         grid=(plan.blocks,),
@@ -386,8 +403,9 @@
         out_specs=[pairs, whole(grad)],
         out_shape=[jax.ShapeDtypeStruct(x.shape, BF16), grad],
         scratch_shapes=[plan.scratch(hidden)] * 2,
-        input_output_aliases={5 + len(small): 0} if kept else {},
+        input_output_aliases={} if before is None else {5 + len(small): 0},
         compiler_params=params(1),
+        cost_estimate=cost(20),
         name="last",
     )(x, mask, grad_a, grad_b, gate_back, *small, *kept)
 
@@ -429,19 +447,20 @@
     for sub in every:
         factor_a, factor_b = make_factors(plan, sub, x, mask, gain, bias, w_t)
         own_b.append(owned(plan.swap(factor_b)))
-        other_b.append(plan.exchange(own_b[sub]))
+        other_b.append(owned(plan.swap(plan.exchange(factor_b))))
         own_a.append(owned(plan.swap(factor_a)))
 
-    gate_back, local_mid, owner_g, grad_own, grad_other = None, [], [], [], []
+    before, local_mid, owner_g, grad_own, grad_other = (), [], [], [], []
     turns = [([sub], [(1 - side, sub)], [other_b[sub]]) for sub in every]
     turns += [(list(every), [(side, sub) for sub in every], own_b)]
     for which, (subs, at, b) in enumerate(turns):
         table = jnp.stack([jnp.stack([half, jnp.int32(sub)]) for half, sub in at])
         product = plan.swap(joined(make_product(plan, own_a, b)))
-        grad_prod, gate_back, *local = make_middle(plan, table, gate_back, x, d, product, mid)
+        grad_prod, gate_back, *local = make_middle(plan, table, before, x, d, product, mid)
         local_mid.append(jnp.concatenate(local[::-1], axis=1))
         owner_g.append(owned(plan.swap(grad_prod)))
         grads = make_grad_b(plan, owner_g[which], own_a)
+        before = (gate_back, grads[0])
         if which < plan.subs:
             grad_other.append(plan.exchange(grads[0]))
         else:
@@ -453,7 +472,7 @@
         whole_b = (grad_own[sub].astype(F32) + grad_other[sub].astype(F32)).astype(BF16)
         grad_b = plan.swap(joined(whole_b))
         pair_grad, local = make_last(
-            plan, sub, pair_grad, x, mask, grad_a, grad_b, gate_back, [gain, bias, w_t, w_cat]
+            plan, sub, pair_grad, sum_mid, x, mask, grad_a, grad_b, gate_back, [gain, bias, w_t, w_cat]
         )
         local_ab.append(local)
     sum_ab = tile_sum(sum(local_ab), tiles) / crop

time: 750 us -> 779 us (1.039)
  waiting for transfers between devices: 387 us -> 474 us
  Pallas kernels: 179 us -> 134 us
  blocking collectives: 89.1 us -> 70.1 us
    all_to_all x10 -> x13, waiting for transfers between devices: 56.5 us -> 152 us  [swap(): lax.all_to_all(array, 'tile', split_axis=0, concat_axis=0, axis_index_gro...]
    all_to_all x3 -> x2, blocking collectives: 89.1 us -> 48.8 us  [swap(): lax.all_to_all(array, 'tile', split_axis=0, concat_axis=0, axis_index_gro...]
    all_to_all x0 -> x2, blocking collectives: none -> 21.3 us  [swap_all(): lax.all_to_all(array, 'tile', split_axis=0, concat_axis=0, tiled=True)]
    pallas_call x3, Pallas kernels: 33.7 us -> 12.8 us  [make_grad_b(): pl.pallas_call(functools.partial(grad_b_kernel, plan.subs), grid=(g.shape...]
    pallas_call x3, Pallas kernels: 31.9 us -> 13.9 us  [make_product(): pl.pallas_call(functools.partial(product_kernel, plan.subs, len(b)), grid...]
    all_to_all x4 -> x2, waiting for transfers between devices: 22 us -> 7.24 us  [swap_all(): lax.all_to_all(array, 'tile', split_axis=0, concat_axis=0, tiled=True)]
    all_to_all x10 -> x13, starting transfers between devices: 41.1 us -> 55 us  [swap(): lax.all_to_all(array, 'tile', split_axis=0, concat_axis=0, axis_index_gro...]
    all_to_all x4 -> x2, starting transfers between devices: 17.9 us -> 7.27 us  [swap_all(): lax.all_to_all(array, 'tile', split_axis=0, concat_axis=0, tiled=True)]
  transfers between devices with their start and end apart: 18 -> 19, of which waited for: 12 -> 14; matrix products, arithmetic and copies ran while one was open for 1% -> 2% of each run, Pallas kernels for 21% -> 11%
where the time goes in v3:
time: 779 us; the launch traced here: 777 us
  waiting for transfers between devices  474 us (61%)
  Pallas kernels  134 us (17%)
  blocking collectives  70.1 us (9%)
  starting transfers between devices  68 us (9%)
  local copies, waits for them, and re-layouts  20.1 us (3%)
  other arithmetic  9.73 us (1%)
    ppermute x4, waiting for transfers between devices, exchange(): return lax.ppermute(array, 'tile', self.partner)  315 us
    all_to_all x13, waiting for transfers between devices, swap(): lax.all_to_all(array, 'tile', split_axis=0, concat_axis=0, axis_index_gro...  152 us
    all_to_all x13, starting transfers between devices, swap(): lax.all_to_all(array, 'tile', split_axis=0, concat_axis=0, axis_index_gro...  55 us
    all_to_all x2, blocking collectives, swap(): lax.all_to_all(array, 'tile', split_axis=0, concat_axis=0, axis_index_gro...  48.8 us
    pallas_call x2, Pallas kernels, make_last(): pl.pallas_call(functools.partial(last_kernel, plan.step), grid=(plan.bloc...  39.1 us
    pallas_call x3, Pallas kernels, make_middle(): pl.pallas_call(functools.partial(middle_kernel, plan.step), grid_spec=plt...  36.8 us
    pallas_call x2, Pallas kernels, make_factors(): pl.pallas_call(functools.partial(factors_kernel, plan.step), grid=(plan.b...  24.1 us
    all_to_all x2, blocking collectives, swap_all(): lax.all_to_all(array, 'tile', split_axis=0, concat_axis=0, tiled=True)  21.3 us
  transfers between devices with their start and end apart: 19, of which 14 were waited for; matrix products, arithmetic and copies ran while one was open for 2% of the time, Pallas kernels for 11%

profile of v3, /device:TPU:0, one launch (start us, length us, event | category | flops | bytes accessed | tf_op | source)
XLA Modules:
  0.0 777.1 jit_solution(4106176468862023028)
XLA Ops:
  4.2 12.0 %factors.2 = (bf16[128,16,512]{2,1,0:T(8,128)(2,1)S(1)}, bf16[128,16,512]{2,1,0:T(8,128)(2,1)}) custom-call(bf16[32,16,2,16,128]{4,3,2,1,0:T(8,128)(2,1)} %bitcast.93, f32[32,512]{1,0:T(8,128)S(1)} %broadcast_multiply_fusion.mask_ref, f32[128,1]{1,0:T(8,128)S(1)} %copy.65.gain_ref, f32[128,1]{1,0:T(8,128)S(1)} %copy.66.bias_ref, bf16[512,128]{1,0:T(8,128)(2,1)S(1)} %bitcast.60), custom_call_target="tpu_custom_call" | custom-call | flops 12000000000 | bytes 36000000 | tf_op jit(solution)/shard_map/factors/pallas_call | solution.py:160
  17.5 5.3 all-to-all-start
  22.8 12.1 %factors.3 = (bf16[128,16,512]{2,1,0:T(8,128)(2,1)S(1)}, bf16[128,16,512]{2,1,0:T(8,128)(2,1)}) custom-call(bf16[32,16,2,16,128]{4,3,2,1,0:T(8,128)(2,1)} %bitcast.94, f32[32,512]{1,0:T(8,128)S(1)} %broadcast_multiply_fusion.mask_ref, f32[128,1]{1,0:T(8,128)S(1)} %copy.65.gain_ref, f32[128,1]{1,0:T(8,128)S(1)} %copy.66.bias_ref, bf16[512,128]{1,0:T(8,128)(2,1)S(1)} %bitcast.61), custom_call_target="tpu_custom_call" | custom-call | flops 12000000000 | bytes 36000000 | tf_op jit(solution)/shard_map/factors/pallas_call | solution.py:160
  36.2 12.3 %all-to-all-done = bf16[128,16,512]{2,1,0:T(8,128)(2,1)S(1)} async-done(((bf16[128,16,512]{2,1,0:T(8,128)(2,1)}), bf16[128,16,512]{2,1,0:T(8,128)(2,1)S(1)}, u32[]{:S(2)}, u32[]{:S(2)}) %all-to-all-start) | async-done | bytes 2097184 | tf_op jit(solution)/shard_map/all_to_all | solution.py:127
  48.5 30.3 %all_to_all.102 = bf16[128,16,512]{2,1,0:T(8,128)(2,1)} all-to-all(bf16[128,16,512]{2,1,0:T(8,128)(2,1)} %copy-done.2), channel_id=1, replica_groups={{0,1,2,3,4,5,6,7},{8,9,10,11,12,13,14,15},{16,17,18,19,20,21,22,23},{24..., dimensions={0} | all-to-all | bytes 4194304 | tf_op jit(solution)/shard_map/all_to_all | solution.py:127
  78.8 4.4 all-to-all-start.8
  85.8 91.5 %collective-permute-done = bf16[128,16,512]{2,1,0:T(8,128)(2,1)} collective-permute-done((bf16[128,16,512]{2,1,0:T(8,128)(2,1)}, bf16[128,16,512]{2,1,0:T(8,128)(2,1)}, u32[]{:S(2)}, u32[]{:S(2)}) %collective-permute-start) | collective-permute-done | bytes 2097184 | tf_op jit(solution)/shard_map/ppermute | solution.py:132
  177.3 4.3 all-to-all-start.2
  183.8 92.0 %collective-permute-done.1 = bf16[128,16,512]{2,1,0:T(8,128)(2,1)} collective-permute-done((bf16[128,16,512]{2,1,0:T(8,128)(2,1)}, bf16[128,16,512]{2,1,0:T(8,128)(2,1)}, u32[]{:S(2)}, u32[]{:S(2)}) %collective-permute-start.1) | collective-permute-done | bytes 2097184 | tf_op jit(solution)/shard_map/ppermute | solution.py:132
  275.8 4.4 all-to-all-start.5
  280.2 4.0 product.3
  285.1 20.7 %all-to-all-done.5 = bf16[128,16,512]{2,1,0:T(8,128)(2,1)} async-done(((bf16[128,16,512]{2,1,0:T(8,128)(2,1)}), bf16[128,16,512]{2,1,0:T(8,128)(2,1)}, u32[]{:S(2)}, u32[]{:S(2)}) %all-to-all-start.5) | async-done | bytes 2097184 | tf_op jit(solution)/shard_map/all_to_all | solution.py:127
  305.8 3.6 all-to-all-start.3
  309.4 4.0 product.4
  314.4 9.4 %all-to-all-done.3.p_ref = bf16[128,32,128]{2,1,0:T(8,128)(2,1)S(1)} async-done(((bf16[128,32,128]{2,1,0:T(8,128)(2,1)}), bf16[128,32,128]{2,1,0:T(8,128)(2,1)S(1)}, u32[]{:S(2)}, u32[]{:S(2)}) %all-to-all-start.3) | async-done | bytes 1048608 | tf_op jit(solution)/shard_map/all_to_all | solution.py:127
  323.8 3.6 all-to-all-start.6
  334.3 9.7 %middle.3 = (bf16[128,32,128]{2,1,0:T(8,128)(2,1)S(1)}, bf16[32,128,512]{2,1,0:T(8,128)(2,1)}, f32[128,128]{1,0:T(8,128)S(1)}, f32[128,128]{1,0:T(8,128)S(1)}) custom-call(s32[1,2]{1,0:T(1,128)S(1)} %fusion.5._, bf16[32,16,2,16,128]{4,3,2,1,0:T(8,128)(2,1)} %bitcast.95, bf16[32,16,2,16,128]{4,3,2,1,0:T(8,128)(2,1)} %bitcast.90, ...), custom_call_target="tpu_custom_call" | custom-call | flops 10000000000 | bytes 30000000 | tf_op jit(solution)/shard_map/middle/pallas_call | solution.py:318
  344.1 18.5 %all_to_all.103 = bf16[128,32,128]{2,1,0:T(8,128)(2,1)S(1)} all-to-all(bf16[128,32,128]{2,1,0:T(8,128)(2,1)S(1)} %get-tuple-element.29), channel_id=1, replica_groups={{0,1,2,3,4,5,6,7},{8,9,10,11,12,13,14,15},{16,17,18,19,20,21,22,23},{24..., dimensions={0} | all-to-all | bytes 2097152 | tf_op jit(solution)/shard_map/all_to_all | solution.py:127
  362.6 4.4 all-to-all-start.9
  367.0 3.7 grad_b.3.refs_1_
  372.1 9.8 %middle.4 = (bf16[128,32,128]{2,1,0:T(8,128)(2,1)}, bf16[32,128,512]{2,1,0:T(8,128)(2,1)}, f32[128,128]{1,0:T(8,128)S(1)}, f32[128,128]{1,0:T(8,128)S(1)}) custom-call(s32[1,2]{1,0:T(1,128)S(1)} %fusion.3._, bf16[32,16,2,16,128]{4,3,2,1,0:T(8,128)(2,1)} %bitcast.96, bf16[32,16,2,16,128]{4,3,2,1,0:T(8,128)(2,1)} %bitcast.91, ...), custom_call_target="tpu_custom_call", output_to_operand_aliasing={{1}: (11, {})} | custom-call | flops 10000000000 | bytes 30000000 | tf_op jit(solution)/shard_map/middle/pallas_call | solution.py:318
  381.9 10.7 %all-to-all-done.9 = bf16[128,16,512]{2,1,0:T(8,128)(2,1)} async-done(((bf16[128,16,512]{2,1,0:T(8,128)(2,1)}), bf16[128,16,512]{2,1,0:T(8,128)(2,1)}, u32[]{:S(2)}, u32[]{:S(2)}) %all-to-all-start.9) | async-done | bytes 2097184 | tf_op jit(solution)/shard_map/all_to_all | solution.py:127
  392.6 3.6 all-to-all-start.7
  396.2 6.0 product.5
  402.1 8.4 %all-to-all-done.7 = bf16[128,32,128]{2,1,0:T(8,128)(2,1)S(1)} async-done(((bf16[128,32,128]{2,1,0:T(8,128)(2,1)}), bf16[128,32,128]{2,1,0:T(8,128)(2,1)S(1)}, u32[]{:S(2)}, u32[]{:S(2)}) %all-to-all-start.7) | async-done | bytes 1048608 | tf_op jit(solution)/shard_map/all_to_all | solution.py:127
  410.6 4.3 all-to-all-start.10
  415.0 3.6 grad_b.4.refs_1_
  420.0 20.6 %all-to-all-done.10.p_ref = bf16[128,32,256]{2,1,0:T(8,128)(2,1)} async-done(((bf16[128,32,256]{2,1,0:T(8,128)(2,1)}), bf16[128,32,256]{2,1,0:T(8,128)(2,1)}, u32[]{:S(2)}, u32[]{:S(2)}) %all-to-all-start.10) | async-done | bytes 2097184 | tf_op jit(solution)/shard_map/all_to_all | solution.py:127
  440.6 17.3 %middle.5 = (bf16[128,32,256]{2,1,0:T(8,128)(2,1)}, bf16[32,128,512]{2,1,0:T(8,128)(2,1)}, f32[128,128]{1,0:T(8,128)S(1)}, f32[128,128]{1,0:T(8,128)S(1)}) custom-call(s32[2,2]{1,0:T(2,128)S(1)} %pad_add_fusion._, bf16[32,16,2,16,128]{4,3,2,1,0:T(8,128)(2,1)} %bitcast.97, bf16[32,16,2,16,128]{4,3,2,1,0:T(8,128)(2,1)} %bitcast.92, ...), custom_call_target="tpu_custom_call", output_to_operand_aliasing={{1}: (11, {})} | custom-call | flops 20000000000 | bytes 60000000 | tf_op jit(solution)/shard_map/middle/pallas_call | solution.py:318
  457.9 10.7 %all_to_all.104 = bf16[16,8,256]{2,1,0:T(8,128)(2,1)S(1)} all-to-all(bf16[16,8,256]{2,1,0:T(8,128)(2,1)S(1)} %fusion.2), channel_id=1, replica_groups=mesh['crops'=2,'tile'=16] {'tile'}, dimensions={0} | all-to-all | bytes 131072 | tf_op jit(solution)/shard_map/all_to_all | solution.py:414
  468.6 4.5 all-to-all-start.11
  473.4 46.8 %all-to-all-done.11 = bf16[128,32,256]{2,1,0:T(8,128)(2,1)} async-done(((bf16[128,32,256]{2,1,0:T(8,128)(2,1)}), bf16[128,32,256]{2,1,0:T(8,128)(2,1)}, u32[]{:S(2)}, u32[]{:S(2)}) %all-to-all-start.11) | async-done | bytes 2097184 | tf_op jit(solution)/shard_map/all_to_all | solution.py:127
  520.8 3.8 all-to-all-start.16
  524.6 5.5 grad_b.5
  530.0 38.0 %collective-permute-done.3 = bf16[8,16,16,512]{3,2,1,0:T(8,128)(2,1)} collective-permute-done((bf16[8,16,16,512]{3,2,1,0:T(8,128)(2,1)S(1)}, bf16[8,16,16,512]{3,2,1,0:T(8,128)(2,1)}, u32[]{:S(2)}, u32[]{:S(2)}) %collective-permute-start.3) | collective-permute-done | bytes 2097184 | tf_op jit(solution)/shard_map/ppermute | solution.py:132
  568.0 3.9 add_convert_fusion
  571.9 3.6 all-to-all-start.14
  576.8 7.5 grad_a.1
  584.3 16.9 %all-to-all-done.14.gb_ref = bf16[128,16,512]{2,1,0:T(8,128)(2,1)S(1)} async-done(((bf16[128,16,512]{2,1,0:T(8,128)(2,1)}), bf16[128,16,512]{2,1,0:T(8,128)(2,1)S(1)}, u32[]{:S(2)}, u32[]{:S(2)}) %all-to-all-start.14) | async-done | bytes 2097184 | tf_op jit(solution)/shard_map/all_to_all | solution.py:127
  601.2 4.7 all-to-all-start.12
  606.6 93.3 %collective-permute-done.2 = bf16[8,16,16,512]{3,2,1,0:T(8,128)(2,1)S(1)} collective-permute-done((bf16[8,16,16,512]{3,2,1,0:T(8,128)(2,1)}, bf16[8,16,16,512]{3,2,1,0:T(8,128)(2,1)S(1)}, u32[]{:S(2)}, u32[]{:S(2)}) %collective-permute-start.2) | collective-permute-done | bytes 2097184 | tf_op jit(solution)/shard_map/ppermute | solution.py:132
  699.9 4.0 add_convert_fusion.1
  703.9 4.5 all-to-all-start.13
  708.5 19.6 %last.2 = (bf16[32,16,2,16,128]{4,3,2,1,0:T(8,128)(2,1)}, f32[128,512]{1,0:T(8,128)S(1)}) custom-call(bf16[32,16,2,16,128]{4,3,2,1,0:T(8,128)(2,1)} %bitcast.98, f32[32,512]{1,0:T(8,128)S(1)} %copy-done.8, bf16[128,32,512]{2,1,0:T(8,128)(2,1)} %all-to-all-done.12.ga_ref, bf16[128,16,512]{2,1,0:T(8,128)(2,1)S(1)} %all-to-all-done.14.gb_ref, ...), custom_call_target="tpu_custom_call" | custom-call | flops 20000000000 | bytes 60000000 | tf_op jit(solution)/shard_map/last/pallas_call | solution.py:391
  728.0 6.0 all-to-all-done.13.gb_ref
  734.1 19.5 %last.3 = (bf16[32,16,2,16,128]{4,3,2,1,0:T(8,128)(2,1)}, f32[128,512]{1,0:T(8,128)S(1)}) custom-call(bf16[32,16,2,16,128]{4,3,2,1,0:T(8,128)(2,1)} %bitcast.99, f32[32,512]{1,0:T(8,128)S(1)} %copy-done.8, bf16[128,32,512]{2,1,0:T(8,128)(2,1)} %all-to-all-done.12.ga_ref, ...), custom_call_target="tpu_custom_call", output_to_operand_aliasing={{0}: (9, {})} | custom-call | flops 20000000000 | bytes 60000000 | tf_op jit(solution)/shard_map/last/pallas_call | solution.py:391
  753.6 10.6 %all_to_all.105 = bf16[16,8,512]{2,1,0:T(8,128)(2,1)S(1)} all-to-all(bf16[16,8,512]{2,1,0:T(8,128)(2,1)S(1)} %fusion), channel_id=1, replica_groups=mesh['crops'=2,'tile'=16] {'tile'}, dimensions={0} | all-to-all | bytes 262144 | tf_op jit(solution)/shard_map/all_to_all | solution.py:414
  769.1 7.2 all-to-all-done.18
  (94 shorter events, 31.2 us)
Async XLA Ops:
  4.2 18.6 %copy-start.7 = (f32[32,512]{1,0:T(8,128)}, f32[32,512]{1,0:T(8,128)S(1)}, u32[]{:S(2)}) copy-start(f32[32,512]{1,0:T(8,128)S(1)} %broadcast_multiply_fusion.mask_ref) | copy-start | bytes 196612
  16.2 1.3 copy-start.1
  17.5 31.0 %all-to-all-start = ((bf16[128,16,512]{2,1,0:T(8,128)(2,1)}), bf16[128,16,512]{2,1,0:T(8,128)(2,1)S(1)}, u32[]{:S(2)}, u32[]{:S(2)}) async-start(bf16[128,16,512]{2,1,0:T(8,128)(2,1)} %copy-done.1), calls=%async_computation | async-start | bytes 4194304 | tf_op jit(solution)/shard_map/all_to_all | solution.py:127
  34.9 1.3 copy-start.2
  48.5 260.9 %copy-start = (bf16[128,16,512]{2,1,0:T(8,128)(2,1)}, bf16[128,16,512]{2,1,0:T(8,128)(2,1)S(1)}, u32[]{:S(2)}) copy-start(bf16[128,16,512]{2,1,0:T(8,128)(2,1)S(1)} %all-to-all-done) | copy-start | bytes 6291460
  78.8 98.5 %all-to-all-start.8 = ((bf16[128,16,512]{2,1,0:T(8,128)(2,1)}), bf16[128,16,512]{2,1,0:T(8,128)(2,1)}, u32[]{:S(2)}, u32[]{:S(2)}) async-start(bf16[128,16,512]{2,1,0:T(8,128)(2,1)} %get-tuple-element.28), calls=%async_computation.8 | async-start | bytes 4194304 | tf_op jit(solution)/shard_map/all_to_all | solution.py:127
  83.2 94.1 %collective-permute-start = (bf16[128,16,512]{2,1,0:T(8,128)(2,1)}, bf16[128,16,512]{2,1,0:T(8,128)(2,1)}, u32[]{:S(2)}, u32[]{:S(2)}) collective-permute-start(bf16[128,16,512]{2,1,0:T(8,128)(2,1)} %get-tuple-element.28), channel_id=1, source_target_pairs={{0,8},{1,9},{2,10},{3,11},{4,12},{5,13},{6,14},{7,15},{8,0},{9,1},... | collective-permute-start | bytes 6291464 | tf_op jit(solution)/shard_map/ppermute | solution.py:132
  177.3 98.5 %all-to-all-start.2 = ((bf16[128,16,512]{2,1,0:T(8,128)(2,1)}), bf16[128,16,512]{2,1,0:T(8,128)(2,1)}, u32[]{:S(2)}, u32[]{:S(2)}) async-start(bf16[128,16,512]{2,1,0:T(8,128)(2,1)} %collective-permute-done), calls=%async_computation.2 | async-start | bytes 4194304 | tf_op jit(solution)/shard_map/all_to_all | solution.py:127
  181.7 94.1 %collective-permute-start.1 = (bf16[128,16,512]{2,1,0:T(8,128)(2,1)}, bf16[128,16,512]{2,1,0:T(8,128)(2,1)}, u32[]{:S(2)}, u32[]{:S(2)}) collective-permute-start(bf16[128,16,512]{2,1,0:T(8,128)(2,1)} %get-tuple-element.30), channel_id=1, source_target_pairs={{0,8},{1,9},{2,10},{3,11},{4,12},{5,13},{6,14},{7,15},{8,0},{9,1},... | collective-permute-start | bytes 6291464 | tf_op jit(solution)/shard_map/ppermute | solution.py:132
  275.8 30.1 %all-to-all-start.5 = ((bf16[128,16,512]{2,1,0:T(8,128)(2,1)}), bf16[128,16,512]{2,1,0:T(8,128)(2,1)}, u32[]{:S(2)}, u32[]{:S(2)}) async-start(bf16[128,16,512]{2,1,0:T(8,128)(2,1)} %collective-permute-done.1), calls=%async_computation.5 | async-start | bytes 4194304 | tf_op jit(solution)/shard_map/all_to_all | solution.py:127
  284.1 1.0 copy-start.6
  305.8 17.9 %all-to-all-start.3 = ((bf16[128,32,128]{2,1,0:T(8,128)(2,1)}), bf16[128,32,128]{2,1,0:T(8,128)(2,1)S(1)}, u32[]{:S(2)}, u32[]{:S(2)}) async-start(bf16[128,32,128]{2,1,0:T(8,128)(2,1)} %bitcast.59), calls=%async_computation.3 | async-start | bytes 2097152 | tf_op jit(solution)/shard_map/all_to_all | solution.py:127
  313.4 1.0 copy-start.5
  314.4 13.0 %copy-start.26 = (f32[128]{0:T(128)S(1)}, f32[128]{0:T(128)}, u32[]{:S(2)}) copy-start(f32[128]{0:T(128)} %param.17) | copy-start | bytes 1540
  314.4 13.7 %copy-start.27 = (f32[128]{0:T(128)S(1)}, f32[128]{0:T(128)}, u32[]{:S(2)}) copy-start(f32[128]{0:T(128)} %param.18) | copy-start | bytes 1540
  314.4 14.5 %copy-start.24 = (bf16[128,128]{1,0:T(8,128)(2,1)S(1)}, bf16[128,128]{1,0:T(8,128)(2,1)}, u32[]{:S(2)}) copy-start(bf16[128,128]{1,0:T(8,128)(2,1)} %param.16) | copy-start | bytes 98308
  314.4 15.2 %copy-start.13 = (bf16[128,128]{1,0:T(8,128)(2,1)S(1)}, bf16[128,128]{1,0:T(8,128)(2,1)}, u32[]{:S(2)}) copy-start(bf16[128,128]{1,0:T(8,128)(2,1)} %wo_ref.5) | copy-start | bytes 98308
  323.8 20.3 %all-to-all-start.6 = ((bf16[128,32,128]{2,1,0:T(8,128)(2,1)}), bf16[128,32,128]{2,1,0:T(8,128)(2,1)S(1)}, u32[]{:S(2)}, u32[]{:S(2)}) async-start(bf16[128,32,128]{2,1,0:T(8,128)(2,1)} %bitcast.58), calls=%async_computation.6 | async-start | bytes 2097152 | tf_op jit(solution)/shard_map/all_to_all | solution.py:127
  330.4 0.8 copy-start.9
  331.2 0.8 copy-start.11
  332.1 0.8 copy-start.14
  332.8 0.8 copy-start.16
  333.6 0.8 copy-start.18
  362.6 30.1 %all-to-all-start.9 = ((bf16[128,16,512]{2,1,0:T(8,128)(2,1)}), bf16[128,16,512]{2,1,0:T(8,128)(2,1)}, u32[]{:S(2)}, u32[]{:S(2)}) async-start(bf16[128,16,512]{2,1,0:T(8,128)(2,1)} %get-tuple-element.30), calls=%async_computation.9 | async-start | bytes 4194304 | tf_op jit(solution)/shard_map/all_to_all | solution.py:127
  367.0 5.0 copy-start.10
  367.0 5.0 copy-start.12
  367.0 5.0 copy-start.15
  367.0 5.1 copy-start.17
  367.0 5.1 copy-start.19
  370.7 1.3 copy-start.20
  392.6 17.9 %all-to-all-start.7 = ((bf16[128,32,128]{2,1,0:T(8,128)(2,1)}), bf16[128,32,128]{2,1,0:T(8,128)(2,1)S(1)}, u32[]{:S(2)}, u32[]{:S(2)}) async-start(bf16[128,32,128]{2,1,0:T(8,128)(2,1)} %get-tuple-element.32), calls=%async_computation.7 | async-start | bytes 2097152 | tf_op jit(solution)/shard_map/all_to_all | solution.py:127
  410.6 4.4 copy-start.3
  410.6 30.0 %all-to-all-start.10 = ((bf16[128,32,256]{2,1,0:T(8,128)(2,1)}), bf16[128,32,256]{2,1,0:T(8,128)(2,1)}, u32[]{:S(2)}, u32[]{:S(2)}) async-start(bf16[128,32,256]{2,1,0:T(8,128)(2,1)} %bitcast.26), calls=%async_computation.10 | async-start | bytes 4194304 | tf_op jit(solution)/shard_map/all_to_all | solution.py:127
  418.7 1.3 copy-start.22
  468.6 4.5 copy-start.21
  468.6 51.6 %all-to-all-start.11 = ((bf16[128,32,256]{2,1,0:T(8,128)(2,1)}), bf16[128,32,256]{2,1,0:T(8,128)(2,1)}, u32[]{:S(2)}, u32[]{:S(2)}) async-start(bf16[128,32,256]{2,1,0:T(8,128)(2,1)} %get-tuple-element.34), calls=%async_computation.11 | async-start | bytes 4194304 | tf_op jit(solution)/shard_map/all_to_all | solution.py:127
  473.1 94.9 %collective-permute-start.3 = (bf16[8,16,16,512]{3,2,1,0:T(8,128)(2,1)S(1)}, bf16[8,16,16,512]{3,2,1,0:T(8,128)(2,1)}, u32[]{:S(2)}, u32[]{:S(2)}) collective-permute-start(bf16[8,16,16,512]{3,2,1,0:T(8,128)(2,1)S(1)} %copy-done.21), channel_id=1, source_target_pairs={{0,8},{1,9},{2,10},{3,11},{4,12},{5,13},{6,14},{7,15},{8,0},{9,1},... | collective-permute-start | bytes 6291464 | tf_op jit(solution)/shard_map/ppermute | solution.py:132
  520.8 51.1 %all-to-all-start.16 = ((bf16[16,8,256]{2,1,0:T(8,128)(2,1)}), bf16[16,8,256]{2,1,0:T(8,128)(2,1)S(1)}, u32[]{:S(2)}, u32[]{:S(2)}) async-start(bf16[16,8,256]{2,1,0:T(8,128)(2,1)} %broadcast_in_dim.29), calls=%async_computation.16 | async-start | bytes 131072 | tf_op jit(solution)/shard_map/all_to_all | solution.py:414
  571.9 29.2 %all-to-all-start.14 = ((bf16[128,16,512]{2,1,0:T(8,128)(2,1)}), bf16[128,16,512]{2,1,0:T(8,128)(2,1)S(1)}, u32[]{:S(2)}, u32[]{:S(2)}) async-start(bf16[128,16,512]{2,1,0:T(8,128)(2,1)} %bitcast.77), calls=%async_computation.14 | async-start | bytes 4194304 | tf_op jit(solution)/shard_map/all_to_all | solution.py:127
  575.6 1.2 copy-start.4
  601.2 102.7 %all-to-all-start.12 = ((bf16[128,32,512]{2,1,0:T(8,128)(2,1)}), bf16[128,32,512]{2,1,0:T(8,128)(2,1)}, u32[]{:S(2)}, u32[]{:S(2)}) async-start(bf16[128,32,512]{2,1,0:T(8,128)(2,1)} %bitcast.78), calls=%async_computation.12 | async-start | bytes 8388608 | tf_op jit(solution)/shard_map/all_to_all | solution.py:127
  605.9 94.0 %collective-permute-start.2 = (bf16[8,16,16,512]{3,2,1,0:T(8,128)(2,1)}, bf16[8,16,16,512]{3,2,1,0:T(8,128)(2,1)S(1)}, u32[]{:S(2)}, u32[]{:S(2)}) collective-permute-start(bf16[8,16,16,512]{3,2,1,0:T(8,128)(2,1)} %copy-done.22), channel_id=1, source_target_pairs={{0,8},{1,9},{2,10},{3,11},{4,12},{5,13},{6,14},{7,15},{8,0},{9,1},... | collective-permute-start | bytes 6291464 | tf_op jit(solution)/shard_map/ppermute | solution.py:132
  703.9 4.5 copy-start.23
  703.9 4.5 copy-start.25
  703.9 4.6 copy-start.8
  703.9 30.2 %all-to-all-start.13 = ((bf16[128,16,512]{2,1,0:T(8,128)(2,1)}), bf16[128,16,512]{2,1,0:T(8,128)(2,1)}, u32[]{:S(2)}, u32[]{:S(2)}) async-start(bf16[128,16,512]{2,1,0:T(8,128)(2,1)} %bitcast.76), calls=%async_computation.13 | async-start | bytes 4194304 | tf_op jit(solution)/shard_map/all_to_all | solution.py:127
  764.9 11.4 %all-to-all-start.18 = ((bf16[16,8,512]{2,1,0:T(8,128)(2,1)}), bf16[16,8,512]{2,1,0:T(8,128)(2,1)S(1)}, u32[]{:S(2)}, u32[]{:S(2)}) async-start(bf16[16,8,512]{2,1,0:T(8,128)(2,1)} %broadcast_in_dim.30), calls=%async_computation.18 | async-start | bytes 262144 | tf_op jit(solution)/shard_map/all_to_all | solution.py:414

commit v4 on v3

--- a/solution.py
+++ b/solution.py
@@ -7,6 +7,7 @@
 from jax.experimental.pallas import tpu as pltpu
 from jax.sharding import PartitionSpec as P
 
+HELD = pl.BlockSpec(memory_space=pl.ANY)
 EPS = 1e-05
 CHANS = 4
 F32 = jnp.float32
@@ -128,11 +129,36 @@
             array, "tile", split_axis=0, concat_axis=0, axis_index_groups=self.groups, tiled=True
         )
 
+    def cut(self, *eighths):
+        return [max(1, self.half * share // 8) for share in eighths]
+
+    def pieces(self, array, counts):
+        ends = [sum(counts[: at + 1]) for at in range(len(counts))]
+        return [array[end - size : end] for size, end in zip(counts, ends)]
+
     def exchange(self, array):
         return lax.ppermute(array, "tile", self.partner)
 
 
-def factors_kernel(step, x_ref, mask_ref, gain_ref, bias_ref, w_ref, fa_ref, fb_ref, sa_ref, sb_ref):
+def after_kernel(*refs):
+    del refs
+
+
+def after(value, *others):
+    return pl.pallas_call(
+        after_kernel,
+        in_specs=[HELD] * (1 + len(others)),
+        out_specs=HELD,
+        out_shape=jax.ShapeDtypeStruct(value.shape, value.dtype),
+        input_output_aliases={0: 0},
+        compiler_params=params(0),
+        cost_estimate=cost(0.1),
+        name="after",
+    )(value, *others)
+
+
+def factors_kernel(step, x_ref, mask_ref, gain_ref, bias_ref, w_ref, *refs):
+    fa_ref, fb_ref, sa_ref, sb_ref = refs[-4:]
     rows = x_ref.shape[0]
     hidden = fa_ref.shape[0]
 
@@ -152,11 +178,10 @@
     gather_out(sb_ref, fb_ref)
 
 
-def make_factors(plan, sub, x, mask, gain, bias, w_t):
+def make_factors(plan, sub, before, x, mask, gain, bias, w_t):
     chans = x.shape[-1]
     hidden = w_t.shape[0] // 4
-    out = jax.ShapeDtypeStruct((hidden, plan.rows, plan.crop), BF16)
-    out_spec = pl.BlockSpec((hidden, plan.rows, plan.width), lambda j: (0, 0, j))
+    block = (hidden, plan.rows, plan.width)
     return pl.pallas_call(
         functools.partial(factors_kernel, plan.step),
         grid=(plan.blocks,),
@@ -166,14 +191,22 @@
             whole(gain),
             whole(bias),
             whole(w_t),
+        ]
+        + [HELD for _ in before],
+        out_specs=[
+            pl.BlockSpec(block, lambda j: (0, sub, j)),
+            pl.BlockSpec(block, lambda j: (0, 0, j)),
         ],
-        out_specs=[out_spec] * 2,
-        out_shape=[out, out],
+        out_shape=[
+            jax.ShapeDtypeStruct((hidden, plan.count, plan.crop), BF16),
+            jax.ShapeDtypeStruct((hidden, plan.rows, plan.crop), BF16),
+        ],
+        input_output_aliases={5: 0} if before else {},
         scratch_shapes=[plan.scratch(hidden)] * 2,
         compiler_params=params(1),
-        cost_estimate=cost(12),
+        cost_estimate=cost(0.2),
         name="factors",
-    )(x, mask, gain, bias, w_t)
+    )(x, mask, gain, bias, w_t, *before)
 
 
 def matrix(refs, chan):
@@ -204,49 +237,52 @@
     return pl.BlockSpec((src, CHANS, rows, cols), lambda h: (0, h, 0, 0))
 
 
-def product_kernel(subs, count, *refs):
-    a, b, p_ref = refs[:subs], refs[subs : subs + count], refs[subs + count]
+def product_kernel(subs, a_ref, *refs):
+    b, p_ref = refs[:-1], refs[-1]
     for chan in range(CHANS):
-        to_subs(p_ref, chan, dot(matrix(a, chan), matrix(b, chan), NT), subs)
+        to_subs(p_ref, chan, dot(by_sub(a_ref, chan, subs), matrix(b, chan), NT), subs)
 
 
 def make_product(plan, a, b):
-    tiles, chans, rows, _ = a[0].shape
-    out = jax.ShapeDtypeStruct((tiles, chans, plan.count, len(b) * plan.width), BF16)
-    return pl.pallas_call(
-        functools.partial(product_kernel, plan.subs, len(b)),
+    tiles, chans, _, _ = a.shape
+    cols = sum(value.shape[0] for value in b) * plan.rows
+    out = jax.ShapeDtypeStruct((tiles, chans, plan.count, cols), BF16)
+    return pl.pallas_call(
+        functools.partial(product_kernel, plan.subs),
         grid=(chans // CHANS,),
-        in_specs=[own_spec(value) for value in (*a, *b)],
+        in_specs=[own_spec(value) for value in (a, *b)],
         out_specs=own_spec(out),
         out_shape=out,
         compiler_params=params(1),
-        cost_estimate=cost(6),
+        cost_estimate=cost(0.2),
         name="product",
-    )(*a, *b)
-
-
-def grad_b_kernel(subs, g_ref, *refs):
-    a, outs = refs[:subs], refs[subs:]
+    )(a, *b)
+
+
+def grad_b_kernel(subs, g_ref, a_ref, *outs):
     for chan in range(CHANS):
-        grad = dot(by_sub(g_ref, chan, subs), matrix(a, chan), TN).astype(BF16)
-        size = grad.shape[0] // len(outs)
-        for at, out in enumerate(outs):
-            part = grad[at * size : (at + 1) * size]
-            out[:, chan] = part.reshape(out.shape[0], *out.shape[2:])
-
-
-def make_grad_b(plan, g, a):
-    outs = g.shape[-1] // plan.width
+        grad = dot(by_sub(g_ref, chan, subs), by_sub(a_ref, chan, subs), TN).astype(BF16)
+        at = 0
+        for out in outs:
+            size = out.shape[0] * out.shape[2]
+            out[:, chan] = grad[at : at + size].reshape(out.shape[0], *out.shape[2:])
+            at += size
+
+
+def make_grad_b(plan, g, a, tiles):
+    outs = [
+        jax.ShapeDtypeStruct((count, a.shape[1], plan.rows, plan.crop), BF16) for count in tiles
+    ]
     return pl.pallas_call(
         functools.partial(grad_b_kernel, plan.subs),
         grid=(g.shape[1] // CHANS,),
-        in_specs=[own_spec(value) for value in (g, *a)],
-        out_specs=[own_spec(a[0])] * outs,
-        out_shape=[jax.ShapeDtypeStruct(a[0].shape, BF16)] * outs,
+        in_specs=[own_spec(value) for value in (g, a)],
+        out_specs=[own_spec(value) for value in outs],
+        out_shape=outs,
         compiler_params=params(1),
-        cost_estimate=cost(8),
+        cost_estimate=cost(0.2),
         name="grad_b",
-    )(g, *a)
+    )(g, a)
 
 
 def grad_a_kernel(subs, count, *refs):
@@ -257,8 +293,8 @@
 
 
 def make_grad_a(plan, g, b):
-    tiles, chans, _, _ = b[0].shape
-    out = jax.ShapeDtypeStruct((tiles, chans, plan.count, plan.crop), BF16)
+    chans = b[0].shape[1]
+    out = jax.ShapeDtypeStruct((plan.half, chans, plan.count, plan.crop), BF16)
     return pl.pallas_call(
         functools.partial(grad_a_kernel, plan.subs, len(g)),
         grid=(chans // CHANS,),
@@ -266,7 +302,7 @@
         out_specs=own_spec(out),
         out_shape=out,
         compiler_params=params(1),
-        cost_estimate=cost(10),
+        cost_estimate=cost(0.2),
         name="grad_a",
     )(*g, *b)
 
@@ -322,7 +358,7 @@
             grid=(plan.subs, cut),
             in_specs=[pairs, pairs, channel]
             + [whole(value) for value in small]
-            + [pl.BlockSpec(memory_space=pl.ANY) for _ in kept],
+            + [HELD for _ in kept],
             out_specs=[
                 channel,
                 pl.BlockSpec(
@@ -340,7 +376,7 @@
         + grads,
         input_output_aliases={4 + len(small): 1} if kept else {},
         compiler_params=params(2),
-        cost_estimate=cost(10 * cut),
+        cost_estimate=cost(0.2),
         name="middle",
     )(table, x, d, p, *small, *kept)
 
@@ -387,7 +423,7 @@
     grad = jax.ShapeDtypeStruct((chans, 4 * hidden), F32)
     pairs = plan.pair_spec(chans, lambda j: (sub, j % 2, j // 2, 0, 0))
     channel = (hidden, plan.rows, plan.width)
-    kept = [ready] if before is None else [before]
+    kept = list(ready) if before is None else [before]
     return pl.pallas_call(
         functools.partial(last_kernel, plan.step),
         grid=(plan.blocks,),
@@ -399,13 +435,13 @@
             pl.BlockSpec((plan.rows, chans, plan.width), lambda j: (sub, 0, j)),
         ]
         + [whole(value) for value in small]
-        + [pl.BlockSpec(memory_space=pl.ANY) for _ in kept],
+        + [HELD for _ in kept],
         out_specs=[pairs, whole(grad)],
         out_shape=[jax.ShapeDtypeStruct(x.shape, BF16), grad],
         scratch_shapes=[plan.scratch(hidden)] * 2,
         input_output_aliases={} if before is None else {5 + len(small): 0},
         compiler_params=params(1),
-        cost_estimate=cost(20),
+        cost_estimate=cost(0.2),
         name="last",
     )(x, mask, grad_a, grad_b, gate_back, *small, *kept)
 
@@ -443,39 +479,74 @@
     joined = lambda array: array.reshape(hidden, *array.shape[2:])
     every = range(plan.subs)
 
-    own_a, own_b, other_b = [], [], []
-    for sub in every:
-        factor_a, factor_b = make_factors(plan, sub, x, mask, gain, bias, w_t)
-        own_b.append(owned(plan.swap(factor_b)))
-        other_b.append(owned(plan.swap(plan.exchange(factor_b))))
-        own_a.append(owned(plan.swap(factor_a)))
-
-    before, local_mid, owner_g, grad_own, grad_other = (), [], [], [], []
-    turns = [([sub], [(1 - side, sub)], [other_b[sub]]) for sub in every]
-    turns += [(list(every), [(side, sub) for sub in every], own_b)]
-    for which, (subs, at, b) in enumerate(turns):
+    plan_cut = plan.cut
+    two = plan.subs == 2
+    cut_a, cut_b = plan_cut(5, 3), plan_cut(2, 2, 2, 2)
+    back_a, back_b = plan_cut(2, 1, 2, 3), plan_cut(2, 3, 3)
+
+    def middle(at, before, product):
         table = jnp.stack([jnp.stack([half, jnp.int32(sub)]) for half, sub in at])
-        product = plan.swap(joined(make_product(plan, own_a, b)))
-        grad_prod, gate_back, *local = make_middle(plan, table, before, x, d, product, mid)
-        local_mid.append(jnp.concatenate(local[::-1], axis=1))
-        owner_g.append(owned(plan.swap(grad_prod)))
-        grads = make_grad_b(plan, owner_g[which], own_a)
-        before = (gate_back, grads[0])
-        if which < plan.subs:
-            grad_other.append(plan.exchange(grads[0]))
-        else:
-            grad_own = grads
-    sum_mid = tile_sum(sum(local_mid), tiles) / crop
-    grad_a = plan.swap(joined(make_grad_a(plan, owner_g, other_b + own_b)))
-    pair_grad, local_ab = None, []
-    for sub in every:
-        whole_b = (grad_own[sub].astype(F32) + grad_other[sub].astype(F32)).astype(BF16)
-        grad_b = plan.swap(joined(whole_b))
-        pair_grad, local = make_last(
-            plan, sub, pair_grad, sum_mid, x, mask, grad_a, grad_b, gate_back, [gain, bias, w_t, w_cat]
+        g, kept, *local = make_middle(plan, table, before, x, d, product, mid)
+        return g, kept, jnp.concatenate(local[::-1], axis=1)
+
+    def product_of(b):
+        return joined(make_product(plan, own_a, b))
+
+    factor_a, factor_b0 = make_factors(plan, 0, (), x, mask, gain, bias, w_t)
+    own_b = [owned(plan.swap(factor_b0))]
+    if two:
+        factor_a, factor_b1 = make_factors(plan, 1, (factor_a,), x, mask, gain, bias, w_t)
+    sent = plan.pieces(own_b[0], cut_a)
+    got_a = [plan.exchange(sent[0])]
+    own_a = owned(plan.swap(after(factor_a, own_b[0])))
+    got_a.append(plan.exchange(sent[1]))
+    if two:
+        own_b.append(owned(plan.swap(after(factor_b1, own_a, got_a[0]))))
+        sent = plan.pieces(own_b[1], cut_b)
+        got_b = [plan.exchange(piece) for piece in sent]
+    else:
+        got_b = [own_a] * 4
+    product = plan.swap(after(product_of(got_a), own_b[-1]))
+    grad, kept, local_0 = middle([(1 - side, 0)], (), product)
+    product_own = plan.swap(after(product_of(own_b), product, got_b[0]))
+    owner_g = [owned(plan.swap(after(grad, product_own, got_b[1])))]
+    grad_own, kept, local_own = middle([(side, sub) for sub in every], (kept, grad), product_own)
+    grad_b0 = make_grad_b(plan, owner_g[0], own_a, back_a)
+    owner_own = owned(plan.swap(after(grad_own, owner_g[0], got_b[2], grad_b0[0])))
+    grad_b_own = make_grad_b(plan, owner_own, own_a, [plan.half] * plan.subs)
+    back_0 = [plan.exchange(piece) for piece in grad_b0]
+    local_mid = local_0 + local_own
+    back_1, b_other = [], [got_a]
+    if two:
+        product = plan.swap(after(product_of(got_b), owner_own, grad_b_own[0]))
+        grad, kept, local_1 = middle([(1 - side, 1)], (kept, back_0[0]), product)
+        local_mid += local_1
+        owner_g.append(owned(plan.swap(after(grad, back_0[1]))))
+        grad_b1 = make_grad_b(plan, owner_g[1], own_a, back_b)
+        back_1 = [plan.exchange(piece) for piece in grad_b1]
+        b_other.append(got_b)
+    grad_a = joined(
+        make_grad_a(plan, owner_g + [owner_own], [v for got in b_other for v in got] + own_b)
+    )
+    grad_a = plan.swap(after(grad_a, back_0[2], *(grad_b1[:1] if two else [])))
+
+    def summed(own, back):
+        return joined(
+            (own.astype(F32) + jnp.concatenate(back, axis=0).astype(F32)).astype(BF16)
         )
-        local_ab.append(local)
-    sum_ab = tile_sum(sum(local_ab), tiles) / crop
+
+    waits = (grad_a, *back_1[:1])
+    grad_b = plan.swap(after(summed(grad_b_own[0], back_0), *waits))
+    sum_mid = tile_sum(after(local_mid, grad_b, *back_1[1:2]), tiles) / crop
+    small = [gain, bias, w_t, w_cat]
+    pair_grad, local_ab = make_last(
+        plan, 0, None, (grad_b,), x, mask, grad_a, grad_b, kept, small
+    )
+    if two:
+        grad_b = plan.swap(after(summed(grad_b_own[1], back_1), sum_mid))
+        pair_grad, local = make_last(plan, 1, pair_grad, (), x, mask, grad_a, grad_b, kept, small)
+        local_ab += local
+    sum_ab = tile_sum(local_ab, tiles) / crop
     return (pair_grad.reshape(count, crop, chans), sum_ab, sum_mid[:, :chans], sum_mid[:, chans:])
 
 

time: 779 us -> 699 us (0.90)
  waiting for transfers between devices: 474 us -> 383 us
  blocking collectives: 70.1 us -> 35.8 us
  local copies, waits for them, and re-layouts: 20.1 us -> 43.1 us
  starting transfers between devices: 68 us -> 86.2 us
    all_to_all x13 -> x12, waiting for transfers between devices: 152 us -> 59.8 us  [swap(): lax.all_to_all(array, 'tile', split_axis=0, concat_axis=0, axis_index_gro...]
    all_to_all x2 -> x0, blocking collectives: 48.8 us -> none  [swap(): lax.all_to_all(array, 'tile', split_axis=0, concat_axis=0, axis_index_gro...]
    unnamed x60 -> x121, local copies, waits for them, and re-layouts: 14.9 us -> 36.2 us
    ppermute x4 -> x13, starting transfers between devices: 5.72 us -> 20.5 us  [exchange(): return lax.ppermute(array, 'tile', self.partner)]
    all_to_all x2, blocking collectives: 21.3 us -> 35.8 us  [swap_all(): lax.all_to_all(array, 'tile', split_axis=0, concat_axis=0, tiled=True)]
    all_to_all x13 -> x12, starting transfers between devices: 55 us -> 58.1 us  [swap(): lax.all_to_all(array, 'tile', split_axis=0, concat_axis=0, axis_index_gro...]
    ppermute x4 -> x13, waiting for transfers between devices: 315 us -> 313 us  [exchange(): return lax.ppermute(array, 'tile', self.partner)]
  transfers between devices with their start and end apart: 19 -> 27, of which waited for: 14 -> 21; matrix products, arithmetic and copies ran while one was open for 2% -> 2% of each run, Pallas kernels for 11% -> 14%
where the time goes in v4:
time: 699 us; the launch traced here: 697 us
  waiting for transfers between devices  383 us (55%)
  Pallas kernels  136 us (19%)
  starting transfers between devices  86.2 us (12%)
  local copies, waits for them, and re-layouts  43.1 us (6%)
  blocking collectives  35.8 us (5%)
  other arithmetic  11.9 us (2%)
    ppermute x13, waiting for transfers between devices, exchange(): return lax.ppermute(array, 'tile', self.partner)  313 us
    all_to_all x12, waiting for transfers between devices, swap(): lax.all_to_all(array, 'tile', split_axis=0, concat_axis=0, axis_index_gro...  59.8 us
    all_to_all x12, starting transfers between devices, swap(): lax.all_to_all(array, 'tile', split_axis=0, concat_axis=0, axis_index_gro...  58.1 us
    pallas_call x2, Pallas kernels, make_last(): pl.pallas_call(functools.partial(last_kernel, plan.step), grid=(plan.bloc...  39.1 us
    pallas_call x3, Pallas kernels, make_middle(): pl.pallas_call(functools.partial(middle_kernel, plan.step), grid_spec=plt...  36.7 us
    unnamed x121, local copies, waits for them, and re-layouts  36.2 us
    all_to_all x2, blocking collectives, swap_all(): lax.all_to_all(array, 'tile', split_axis=0, concat_axis=0, tiled=True)  35.8 us
    pallas_call x2, Pallas kernels, make_factors(): pl.pallas_call(functools.partial(factors_kernel, plan.step), grid=(plan.b...  23.8 us
  transfers between devices with their start and end apart: 27, of which 21 were waited for; matrix products, arithmetic and copies ran while one was open for 2% of the time, Pallas kernels for 14%

profile of v4, /device:TPU:0, one launch (start us, length us, event | category | flops | bytes accessed | tf_op | source)
XLA Modules:
  0.0 697.0 jit_solution(6423909938387937758)
XLA Ops:
  4.2 11.9 %factors.2 = (bf16[128,32,512]{2,1,0:T(8,128)(2,1)}, bf16[128,16,512]{2,1,0:T(8,128)(2,1)S(1)}) custom-call(bf16[32,16,2,16,128]{4,3,2,1,0:T(8,128)(2,1)} %bitcast.72, f32[32,512]{1,0:T(8,128)S(1)} %broadcast_multiply_fusion.mask_ref, f32[128,1]{1,0:T(8,128)S(1)} %copy.80.gain_ref, f32[128,1]{1,0:T(8,128)S(1)} %copy.81.bias_ref, bf16[512,128]{1,0:T(8,128)(2,1)S(1)} %bitcast.62), custom_call_target="tpu_custom_call" | custom-call | flops 200000000 | bytes 600000 | tf_op jit(solution)/shard_map/factors/pallas_call | solution.py:185
  17.5 5.3 all-to-all-start
  22.7 11.9 %factors.3 = (bf16[128,32,512]{2,1,0:T(8,128)(2,1)}, bf16[128,16,512]{2,1,0:T(8,128)(2,1)S(1)}) custom-call(bf16[32,16,2,16,128]{4,3,2,1,0:T(8,128)(2,1)} %bitcast.73, f32[32,512]{1,0:T(8,128)S(1)} %broadcast_multiply_fusion.mask_ref, f32[128,1]{1,0:T(8,128)S(1)} %copy.80.gain_ref, f32[128,1]{1,0:T(8,128)S(1)} %copy.81.bias_ref, ...), custom_call_target="tpu_custom_call", output_to_operand_aliasing={{0}: (5, {})} | custom-call | flops 200000000 | bytes 600000 | tf_op jit(solution)/shard_map/factors/pallas_call | solution.py:185
  36.0 12.5 %all-to-all-done = bf16[128,16,512]{2,1,0:T(8,128)(2,1)S(1)} async-done(((bf16[128,16,512]{2,1,0:T(8,128)(2,1)}), bf16[128,16,512]{2,1,0:T(8,128)(2,1)S(1)}, u32[]{:S(2)}, u32[]{:S(2)}) %all-to-all-start) | async-done | bytes 2097184 | tf_op jit(solution)/shard_map/all_to_all | solution.py:128
  48.4 4.5 all-to-all-start.1
  55.7 71.3 %collective-permute-done.refs_0_.refs_2_.refs_3_ = bf16[5,16,16,512]{3,2,1,0:T(8,128)(2,1)S(1)} collective-permute-done((bf16[5,16,16,512]{3,2,1,0:T(8,128)(2,1)S(1)}, bf16[5,16,16,512]{3,2,1,0:T(8,128)(2,1)S(1)}, u32[]{:S(2)}, u32[]{:S(2)}) %collective-permute-start) | collective-permute-done | bytes 1310752 | tf_op jit(solution)/shard_map/ppermute | solution.py:140
  132.1 5.1 all-to-all-start.2
  138.3 39.4 %collective-permute-done.1.refs_1_.refs_4_ = bf16[3,16,16,512]{3,2,1,0:T(8,128)(2,1)S(1)} collective-permute-done((bf16[3,16,16,512]{3,2,1,0:T(8,128)(2,1)S(1)}, bf16[3,16,16,512]{3,2,1,0:T(8,128)(2,1)S(1)}, u32[]{:S(2)}, u32[]{:S(2)}) %collective-permute-start.1) | collective-permute-done | bytes 786464 | tf_op jit(solution)/shard_map/ppermute | solution.py:140
  177.7 4.8 product.3
  183.4 5.0 all-to-all-start.3
  193.1 4.8 product.4
  198.0 19.8 %collective-permute-done.2.refs_2_.refs_0_.refs_5_ = bf16[2,16,16,512]{3,2,1,0:T(8,128)(2,1)S(1)} collective-permute-done((bf16[2,16,16,512]{3,2,1,0:T(8,128)(2,1)S(1)}, bf16[2,16,16,512]{3,2,1,0:T(8,128)(2,1)S(1)}, u32[]{:S(2)}, u32[]{:S(2)}) %collective-permute-start.2) | collective-permute-done | bytes 524320 | tf_op jit(solution)/shard_map/ppermute | solution.py:140
  220.9 3.7 all-to-all-start.4
  227.3 9.6 %middle.3 = (bf16[128,32,128]{2,1,0:T(8,128)(2,1)S(1)}, bf16[32,128,512]{2,1,0:T(8,128)(2,1)}, f32[128,128]{1,0:T(8,128)S(1)}, f32[128,128]{1,0:T(8,128)S(1)}) custom-call(s32[1,2]{1,0:T(1,128)S(1)} %fusion.4._, bf16[32,16,2,16,128]{4,3,2,1,0:T(8,128)(2,1)} %bitcast.74, bf16[32,16,2,16,128]{4,3,2,1,0:T(8,128)(2,1)} %bitcast.79, ...), custom_call_target="tpu_custom_call" | custom-call | flops 200000000 | bytes 600000 | tf_op jit(solution)/shard_map/middle/pallas_call | solution.py:354
  237.9 21.6 %collective-permute-done.3.refs_2_.refs_1_.refs_6_ = bf16[2,16,16,512]{3,2,1,0:T(8,128)(2,1)} collective-permute-done((bf16[2,16,16,512]{3,2,1,0:T(8,128)(2,1)}, bf16[2,16,16,512]{3,2,1,0:T(8,128)(2,1)}, u32[]{:S(2)}, u32[]{:S(2)}) %collective-permute-start.3) | collective-permute-done | bytes 524320 | tf_op jit(solution)/shard_map/ppermute | solution.py:140
  263.8 4.4 all-to-all-start.5
  270.2 17.3 %middle.4 = (bf16[128,32,256]{2,1,0:T(8,128)(2,1)S(1)}, bf16[32,128,512]{2,1,0:T(8,128)(2,1)}, f32[128,128]{1,0:T(8,128)S(1)}, f32[128,128]{1,0:T(8,128)S(1)}) custom-call(s32[2,2]{1,0:T(2,128)S(1)} %pad_add_fusion._, bf16[32,16,2,16,128]{4,3,2,1,0:T(8,128)(2,1)} %bitcast.75, ...), custom_call_target="tpu_custom_call", output_to_operand_aliasing={{1}: (11, {})} | custom-call | flops 200000000 | bytes 600000 | tf_op jit(solution)/shard_map/middle/pallas_call | solution.py:354
  290.1 2.9 all-to-all-done.5
  292.9 4.7 grad_b.3
  299.3 3.6 all-to-all-start.6
  303.4 34.4 %collective-permute-done.5.refs_3_.refs_8_ = bf16[2,16,16,512]{3,2,1,0:T(8,128)(2,1)S(1)} collective-permute-done((bf16[2,16,16,512]{3,2,1,0:T(8,128)(2,1)}, bf16[2,16,16,512]{3,2,1,0:T(8,128)(2,1)S(1)}, u32[]{:S(2)}, u32[]{:S(2)}) %collective-permute-start.5) | collective-permute-done | bytes 524320 | tf_op jit(solution)/shard_map/ppermute | solution.py:140
  339.8 4.0 product.5
  347.0 5.7 grad_b.4
  356.6 4.7 all-to-all-start.7
  364.3 21.0 %collective-permute-done.6.refs_1_ = bf16[2,16,16,512]{3,2,1,0:T(8,128)(2,1)S(1)} collective-permute-done((bf16[2,16,16,512]{3,2,1,0:T(8,128)(2,1)}, bf16[2,16,16,512]{3,2,1,0:T(8,128)(2,1)S(1)}, u32[]{:S(2)}, u32[]{:S(2)}) %collective-permute-start.6) | collective-permute-done | bytes 524320 | tf_op jit(solution)/shard_map/ppermute | solution.py:140
  387.5 9.8 %middle.5 = (bf16[128,32,128]{2,1,0:T(8,128)(2,1)}, bf16[32,128,512]{2,1,0:T(8,128)(2,1)}, f32[128,128]{1,0:T(8,128)S(1)}, f32[128,128]{1,0:T(8,128)S(1)}) custom-call(s32[1,2]{1,0:T(1,128)S(1)} %fusion.2._, bf16[32,16,2,16,128]{4,3,2,1,0:T(8,128)(2,1)} %bitcast.76, bf16[32,16,2,16,128]{4,3,2,1,0:T(8,128)(2,1)} %bitcast.81, ...), custom_call_target="tpu_custom_call", output_to_operand_aliasing={{1}: (11, {})} | custom-call | flops 200000000 | bytes 600000 | tf_op jit(solution)/shard_map/middle/pallas_call | solution.py:354
  400.0 8.6 %all-to-all-start.8 = ((bf16[128,32,128]{2,1,0:T(8,128)(2,1)}), bf16[128,32,128]{2,1,0:T(8,128)(2,1)S(1)}, u32[]{:S(2)}, u32[]{:S(2)}) async-start(bf16[128,32,128]{2,1,0:T(8,128)(2,1)} %after.19), calls=%async_computation.8 | async-start | bytes 2097152 | tf_op jit(solution)/shard_map/all_to_all | solution.py:128
  408.5 2.9 collective-permute-start.8
  411.5 22.8 %all-to-all-done.8 = bf16[128,32,128]{2,1,0:T(8,128)(2,1)S(1)} async-done(((bf16[128,32,128]{2,1,0:T(8,128)(2,1)}), bf16[128,32,128]{2,1,0:T(8,128)(2,1)S(1)}, u32[]{:S(2)}, u32[]{:S(2)}) %all-to-all-start.8) | async-done | bytes 1048608 | tf_op jit(solution)/shard_map/all_to_all | solution.py:128
  434.3 5.0 grad_b.5
  440.1 7.4 %grad_a.1 = bf16[8,16,32,512]{3,2,1,0:T(8,128)(2,1)} custom-call(bf16[8,16,32,128]{3,2,1,0:T(8,128)(2,1)S(1)} %bitcast.58, bf16[8,16,32,128]{3,2,1,0:T(8,128)(2,1)} %bitcast.60, bf16[8,16,32,256]{3,2,1,0:T(8,128)(2,1)} %bitcast.51, bf16[5,16,16,512]{3,2,1,0:T(8,128)(2,1)} %copy-done.8, bf16[3,16,16,512]{3,2,1,0:T(8,128)(2,1)S(1)} %copy-done.31, ...), custom_call_target="tpu_custom_call" | custom-call | flops 200000000 | bytes 600000 | tf_op jit(solution)/shard_map/grad_a/pallas_call | solution.py:298
  447.6 4.9 all-to-all-start.9
  452.6 2.9 collective-permute-start.9
  455.5 59.9 %collective-permute-done.12 = bf16[3,16,16,512]{3,2,1,0:T(8,128)(2,1)S(1)} collective-permute-done((bf16[3,16,16,512]{3,2,1,0:T(8,128)(2,1)S(1)}, bf16[3,16,16,512]{3,2,1,0:T(8,128)(2,1)S(1)}, u32[]{:S(2)}, u32[]{:S(2)}) %collective-permute-start.12) | collective-permute-done | bytes 786464 | tf_op jit(solution)/shard_map/ppermute | solution.py:140
  518.1 8.4 %collective-permute-done.9.refs_2_ = bf16[2,16,16,512]{3,2,1,0:T(8,128)(2,1)S(1)} collective-permute-done((bf16[2,16,16,512]{3,2,1,0:T(8,128)(2,1)}, bf16[2,16,16,512]{3,2,1,0:T(8,128)(2,1)S(1)}, u32[]{:S(2)}, u32[]{:S(2)}) %collective-permute-start.9) | collective-permute-done | bytes 524320 | tf_op jit(solution)/shard_map/ppermute | solution.py:140
  529.9 3.6 all-to-all-start.10
  538.2 36.1 %collective-permute-done.10.refs_2_ = bf16[3,16,16,512]{3,2,1,0:T(8,128)(2,1)S(1)} collective-permute-done((bf16[3,16,16,512]{3,2,1,0:T(8,128)(2,1)}, bf16[3,16,16,512]{3,2,1,0:T(8,128)(2,1)S(1)}, u32[]{:S(2)}, u32[]{:S(2)}) %collective-permute-start.10) | collective-permute-done | bytes 786464 | tf_op jit(solution)/shard_map/ppermute | solution.py:140
  574.3 7.0 %all-to-all-done.10.refs_1_.gb_ref.refs_0_ = bf16[128,16,512]{2,1,0:T(8,128)(2,1)S(1)} async-done(((bf16[128,16,512]{2,1,0:T(8,128)(2,1)}), bf16[128,16,512]{2,1,0:T(8,128)(2,1)S(1)}, u32[]{:S(2)}, u32[]{:S(2)}) %all-to-all-start.10) | async-done | bytes 2097184 | tf_op jit(solution)/shard_map/all_to_all | solution.py:128
  582.2 25.2 %all_to_all.90 = bf16[16,8,256]{2,1,0:T(8,128)(2,1)} all-to-all(bf16[16,8,256]{2,1,0:T(8,128)(2,1)S(1)} %convert_bitcast_fusion), channel_id=1, replica_groups=mesh['crops'=2,'tile'=16] {'tile'}, dimensions={0} | all-to-all | bytes 131072 | tf_op jit(solution)/shard_map/all_to_all | solution.py:450
  608.9 4.2 all-to-all-start.12
  613.1 4.0 add_convert_fusion.1
  623.8 4.5 all-to-all-start.13
  628.4 19.6 %last.2 = (bf16[32,16,2,16,128]{4,3,2,1,0:T(8,128)(2,1)}, f32[128,512]{1,0:T(8,128)S(1)}) custom-call(bf16[32,16,2,16,128]{4,3,2,1,0:T(8,128)(2,1)} %bitcast.77, f32[32,512]{1,0:T(8,128)S(1)} %copy-done.38, bf16[128,32,512]{2,1,0:T(8,128)(2,1)} %all-to-all-done.9.refs_1_.ga_ref, bf16[128,16,512]{2,1,0:T(8,128)(2,1)S(1)} %all-to-all-done.10.refs_1_.gb_ref.refs_0_, ...), custom_call_target="tpu_custom_call" | custom-call | flops 200000000 | bytes 600000 | tf_op jit(solution)/shard_map/last/pallas_call | solution.py:427
  648.0 6.1 all-to-all-done.13.gb_ref
  654.1 19.5 %last.3 = (bf16[32,16,2,16,128]{4,3,2,1,0:T(8,128)(2,1)}, f32[128,512]{1,0:T(8,128)S(1)}) custom-call(bf16[32,16,2,16,128]{4,3,2,1,0:T(8,128)(2,1)} %bitcast.78, f32[32,512]{1,0:T(8,128)S(1)} %copy-done.38, bf16[128,32,512]{2,1,0:T(8,128)(2,1)} %all-to-all-done.9.refs_1_.ga_ref, ...), custom_call_target="tpu_custom_call", output_to_operand_aliasing={{0}: (9, {})} | custom-call | flops 200000000 | bytes 600000 | tf_op jit(solution)/shard_map/last/pallas_call | solution.py:427
  673.6 10.6 %all_to_all.91 = bf16[16,8,512]{2,1,0:T(8,128)(2,1)S(1)} all-to-all(bf16[16,8,512]{2,1,0:T(8,128)(2,1)S(1)} %fusion), channel_id=1, replica_groups=mesh['crops'=2,'tile'=16] {'tile'}, dimensions={0} | all-to-all | bytes 262144 | tf_op jit(solution)/shard_map/all_to_all | solution.py:450
  684.9 3.5 all-to-all-start.15
  689.1 7.2 %all-to-all-done.15 = bf16[16,8,512]{2,1,0:T(8,128)(2,1)S(1)} async-done(((bf16[16,8,512]{2,1,0:T(8,128)(2,1)}), bf16[16,8,512]{2,1,0:T(8,128)(2,1)S(1)}, u32[]{:S(2)}, u32[]{:S(2)}) %all-to-all-start.15) | async-done | bytes 131104 | tf_op jit(solution)/shard_map/all_to_all | solution.py:450
  (185 shorter events, 78.3 us)
Async XLA Ops:
  4.1 18.6 %copy-start.28 = (bf16[128,512]{0,1:T(8,128)(2,1)}, bf16[128,512]{0,1:T(8,128)(2,1)S(1)}, u32[]{:S(2)}) copy-start(bf16[128,512]{0,1:T(8,128)(2,1)S(1)} %copy.77) | copy-start | bytes 393220
  4.2 18.5 %copy-start.37 = (f32[32,512]{1,0:T(8,128)}, f32[32,512]{1,0:T(8,128)S(1)}, u32[]{:S(2)}) copy-start(f32[32,512]{1,0:T(8,128)S(1)} %broadcast_multiply_fusion.mask_ref) | copy-start | bytes 196612
  17.5 31.0 %all-to-all-start = ((bf16[128,16,512]{2,1,0:T(8,128)(2,1)}), bf16[128,16,512]{2,1,0:T(8,128)(2,1)S(1)}, u32[]{:S(2)}, u32[]{:S(2)}) async-start(bf16[128,16,512]{2,1,0:T(8,128)(2,1)} %copy-done.36), calls=%async_computation | async-start | bytes 4194304 | tf_op jit(solution)/shard_map/all_to_all | solution.py:128
  48.4 88.8 %copy-start = (bf16[128,16,512]{2,1,0:T(8,128)(2,1)}, bf16[128,16,512]{2,1,0:T(8,128)(2,1)S(1)}, u32[]{:S(2)}) copy-start(bf16[128,16,512]{2,1,0:T(8,128)(2,1)S(1)} %all-to-all-done) | copy-start | bytes 6291460
  48.4 80.8 %all-to-all-start.1 = ((bf16[128,32,512]{2,1,0:T(8,128)(2,1)}), bf16[128,32,512]{2,1,0:T(8,128)(2,1)}, u32[]{:S(2)}, u32[]{:S(2)}) async-start(bf16[128,32,512]{2,1,0:T(8,128)(2,1)} %after.12), calls=%async_computation.1 | async-start | bytes 8388608 | tf_op jit(solution)/shard_map/all_to_all | solution.py:128
  53.1 74.0 %collective-permute-start = (bf16[5,16,16,512]{3,2,1,0:T(8,128)(2,1)S(1)}, bf16[5,16,16,512]{3,2,1,0:T(8,128)(2,1)S(1)}, u32[]{:S(2)}, u32[]{:S(2)}) collective-permute-start(bf16[5,16,16,512]{3,2,1,0:T(8,128)(2,1)S(1)} %bitcast.84), channel_id=1, source_target_pairs={{0,8},{1,9},{2,10},{3,11},{4,12},{5,13},{6,14},{7,15},{8,0},{9,1},... | collective-permute-start | bytes 3932168 | tf_op jit(solution)/shard_map/ppermute | solution.py:140
  127.0 50.7 %copy-start.8 = (bf16[5,16,16,512]{3,2,1,0:T(8,128)(2,1)}, bf16[5,16,16,512]{3,2,1,0:T(8,128)(2,1)S(1)}, u32[]{:S(2)}) copy-start(bf16[5,16,16,512]{3,2,1,0:T(8,128)(2,1)S(1)} %collective-permute-done.refs_0_.refs_2_.refs_3_) | copy-start | bytes 3932164
  132.1 51.3 %all-to-all-start.2 = ((bf16[128,16,512]{2,1,0:T(8,128)(2,1)}), bf16[128,16,512]{2,1,0:T(8,128)(2,1)}, u32[]{:S(2)}, u32[]{:S(2)}) async-start(bf16[128,16,512]{2,1,0:T(8,128)(2,1)} %copy-done.17), calls=%async_computation.2 | async-start | bytes 4194304 | tf_op jit(solution)/shard_map/all_to_all | solution.py:128
  137.3 40.4 %collective-permute-start.1 = (bf16[3,16,16,512]{3,2,1,0:T(8,128)(2,1)S(1)}, bf16[3,16,16,512]{3,2,1,0:T(8,128)(2,1)S(1)}, u32[]{:S(2)}, u32[]{:S(2)}) collective-permute-start(bf16[3,16,16,512]{3,2,1,0:T(8,128)(2,1)S(1)} %bitcast.85), channel_id=1, source_target_pairs={{0,8},{1,9},{2,10},{3,11},{4,12},{5,13},{6,14},{7,15},{8,0},{9,1},... | collective-permute-start | bytes 2359304 | tf_op jit(solution)/shard_map/ppermute | solution.py:140
  183.4 35.1 %all-to-all-start.3 = ((bf16[128,32,128]{2,1,0:T(8,128)(2,1)}), bf16[128,32,128]{2,1,0:T(8,128)(2,1)S(1)}, u32[]{:S(2)}, u32[]{:S(2)}) async-start(bf16[128,32,128]{2,1,0:T(8,128)(2,1)} %after.14), calls=%async_computation.3 | async-start | bytes 2097152 | tf_op jit(solution)/shard_map/all_to_all | solution.py:128
  191.2 26.5 %collective-permute-start.2 = (bf16[2,16,16,512]{3,2,1,0:T(8,128)(2,1)S(1)}, bf16[2,16,16,512]{3,2,1,0:T(8,128)(2,1)S(1)}, u32[]{:S(2)}, u32[]{:S(2)}) collective-permute-start(bf16[2,16,16,512]{3,2,1,0:T(8,128)(2,1)S(1)} %bitcast.89), channel_id=1, source_target_pairs={{0,8},{1,9},{2,10},{3,11},{4,12},{5,13},{6,14},{7,15},{8,0},{9,1},... | collective-permute-start | bytes 1572872 | tf_op jit(solution)/shard_map/ppermute | solution.py:140
  220.9 5.8 copy-start.56
  220.9 5.9 copy-start.57
  220.9 6.1 copy-start.54
  220.9 6.2 copy-start.42
  220.9 40.6 %all-to-all-start.4 = ((bf16[128,32,256]{2,1,0:T(8,128)(2,1)}), bf16[128,32,256]{2,1,0:T(8,128)(2,1)S(1)}, u32[]{:S(2)}, u32[]{:S(2)}) async-start(bf16[128,32,256]{2,1,0:T(8,128)(2,1)} %copy-done.7), calls=%async_computation.4 | async-start | bytes 4194304 | tf_op jit(solution)/shard_map/all_to_all | solution.py:128
  224.7 34.9 %collective-permute-start.3 = (bf16[2,16,16,512]{3,2,1,0:T(8,128)(2,1)}, bf16[2,16,16,512]{3,2,1,0:T(8,128)(2,1)}, u32[]{:S(2)}, u32[]{:S(2)}) collective-permute-start(bf16[2,16,16,512]{3,2,1,0:T(8,128)(2,1)} %bitcast.88), channel_id=1, source_target_pairs={{0,8},{1,9},{2,10},{3,11},{4,12},{5,13},{6,14},{7,15},{8,0},{9,1},... | collective-permute-start | bytes 1572872 | tf_op jit(solution)/shard_map/ppermute | solution.py:140
  263.8 29.1 %all-to-all-start.5 = ((bf16[128,32,128]{2,1,0:T(8,128)(2,1)}), bf16[128,32,128]{2,1,0:T(8,128)(2,1)S(1)}, u32[]{:S(2)}, u32[]{:S(2)}) async-start(bf16[128,32,128]{2,1,0:T(8,128)(2,1)} %copy-done.13), calls=%async_computation.5 | async-start | bytes 2097152 | tf_op jit(solution)/shard_map/all_to_all | solution.py:128
  268.3 30.2 %collective-permute-start.4 = (bf16[2,16,16,512]{3,2,1,0:T(8,128)(2,1)}, bf16[2,16,16,512]{3,2,1,0:T(8,128)(2,1)S(1)}, u32[]{:S(2)}, u32[]{:S(2)}) collective-permute-start(bf16[2,16,16,512]{3,2,1,0:T(8,128)(2,1)} %bitcast.87), channel_id=1, source_target_pairs={{0,8},{1,9},{2,10},{3,11},{4,12},{5,13},{6,14},{7,15},{8,0},{9,1},... | collective-permute-start | bytes 1572872 | tf_op jit(solution)/shard_map/ppermute | solution.py:140
  299.3 46.3 %all-to-all-start.6 = ((bf16[128,32,256]{2,1,0:T(8,128)(2,1)}), bf16[128,32,256]{2,1,0:T(8,128)(2,1)S(1)}, u32[]{:S(2)}, u32[]{:S(2)}) async-start(bf16[128,32,256]{2,1,0:T(8,128)(2,1)} %after.17), calls=%async_computation.6 | async-start | bytes 4194304 | tf_op jit(solution)/shard_map/all_to_all | solution.py:128
  302.9 34.9 %collective-permute-start.5 = (bf16[2,16,16,512]{3,2,1,0:T(8,128)(2,1)}, bf16[2,16,16,512]{3,2,1,0:T(8,128)(2,1)S(1)}, u32[]{:S(2)}, u32[]{:S(2)}) collective-permute-start(bf16[2,16,16,512]{3,2,1,0:T(8,128)(2,1)} %bitcast.86), channel_id=1, source_target_pairs={{0,8},{1,9},{2,10},{3,11},{4,12},{5,13},{6,14},{7,15},{8,0},{9,1},... | collective-permute-start | bytes 1572872 | tf_op jit(solution)/shard_map/ppermute | solution.py:140
  347.0 7.1 %copy-start.11 = (bf16[8,16,32,128]{3,2,1,0:T(8,128)(2,1)S(1)}, bf16[8,16,32,128]{3,2,1,0:T(8,128)(2,1)}, u32[]{:S(2)}) copy-start(bf16[8,16,32,128]{3,2,1,0:T(8,128)(2,1)} %copy-done.10) | copy-start | bytes 3145732
  356.6 31.0 %all-to-all-start.7 = ((bf16[128,32,128]{2,1,0:T(8,128)(2,1)}), bf16[128,32,128]{2,1,0:T(8,128)(2,1)S(1)}, u32[]{:S(2)}, u32[]{:S(2)}) async-start(bf16[128,32,128]{2,1,0:T(8,128)(2,1)} %copy-done.12), calls=%async_computation.7 | async-start | bytes 2097152 | tf_op jit(solution)/shard_map/all_to_all | solution.py:128
  361.3 24.0 %collective-permute-start.6 = (bf16[2,16,16,512]{3,2,1,0:T(8,128)(2,1)}, bf16[2,16,16,512]{3,2,1,0:T(8,128)(2,1)S(1)}, u32[]{:S(2)}, u32[]{:S(2)}) collective-permute-start(bf16[2,16,16,512]{3,2,1,0:T(8,128)(2,1)} %get-tuple-element.40.refs_3_), channel_id=1, source_target_pairs={{0,8},{1,9},{2,10},{3,11},{4,12},{5,13},{6,14},{7,15},{8,0},{9,1},... | collective-permute-start | bytes 1572872 | tf_op jit(solution)/shard_map/ppermute | solution.py:140
  363.5 35.8 %collective-permute-start.7 = (bf16[1,16,16,512]{3,2,1,0:T(8,128)(2,1)}, bf16[1,16,16,512]{3,2,1,0:T(8,128)(2,1)S(1)}, u32[]{:S(2)}, u32[]{:S(2)}) collective-permute-start(bf16[1,16,16,512]{3,2,1,0:T(8,128)(2,1)} %get-tuple-element.44), channel_id=1, source_target_pairs={{0,8},{1,9},{2,10},{3,11},{4,12},{5,13},{6,14},{7,15},{8,0},{9,1},... | collective-permute-start | bytes 786440 | tf_op jit(solution)/shard_map/ppermute | solution.py:140
  385.3 12.1 %copy-start.34 = (bf16[2,16,16,512]{3,2,1,0:T(8,128)(2,1)}, bf16[2,16,16,512]{3,2,1,0:T(8,128)(2,1)S(1)}, u32[]{:S(2)}) copy-start(bf16[2,16,16,512]{3,2,1,0:T(8,128)(2,1)S(1)} %collective-permute-done.6.refs_1_) | copy-start | bytes 1572868
  400.0 34.3 %all-to-all-start.8 = ((bf16[128,32,128]{2,1,0:T(8,128)(2,1)}), bf16[128,32,128]{2,1,0:T(8,128)(2,1)S(1)}, u32[]{:S(2)}, u32[]{:S(2)}) async-start(bf16[128,32,128]{2,1,0:T(8,128)(2,1)} %after.19), calls=%async_computation.8 | async-start | bytes 2097152 | tf_op jit(solution)/shard_map/all_to_all | solution.py:128
  408.5 39.0 %collective-permute-start.8 = (bf16[2,16,16,512]{3,2,1,0:T(8,128)(2,1)}, bf16[2,16,16,512]{3,2,1,0:T(8,128)(2,1)}, u32[]{:S(2)}, u32[]{:S(2)}) collective-permute-start(bf16[2,16,16,512]{3,2,1,0:T(8,128)(2,1)} %get-tuple-element.45), channel_id=1, source_target_pairs={{0,8},{1,9},{2,10},{3,11},{4,12},{5,13},{6,14},{7,15},{8,0},{9,1},... | collective-permute-start | bytes 1572872 | tf_op jit(solution)/shard_map/ppermute | solution.py:140
  434.2 5.0 copy-start.9
  434.2 5.9 copy-start.21
  434.2 5.9 copy-start.25
  434.2 5.9 copy-start.31
  434.3 5.9 copy-start.33
  440.1 7.4 %copy-start.52 = (bf16[3,16,16,512]{3,2,1,0:T(8,128)(2,1)}, bf16[3,16,16,512]{3,2,1,0:T(8,128)(2,1)S(1)}, u32[]{:S(2)}) copy-start(bf16[3,16,16,512]{3,2,1,0:T(8,128)(2,1)S(1)} %get-tuple-element.48) | copy-start | bytes 2359300
  447.6 5.0 copy-start.50
  447.6 67.9 %copy-start.35 = (bf16[2,16,16,512]{3,2,1,0:T(8,128)(2,1)S(1)}, bf16[2,16,16,512]{3,2,1,0:T(8,128)(2,1)}, u32[]{:S(2)}) copy-start(bf16[2,16,16,512]{3,2,1,0:T(8,128)(2,1)} %copy-done.34) | copy-start | bytes 1572868
  447.6 67.9 %copy-start.41 = (bf16[1,16,16,512]{3,2,1,0:T(8,128)(2,1)S(1)}, bf16[1,16,16,512]{3,2,1,0:T(8,128)(2,1)}, u32[]{:S(2)}) copy-start(bf16[1,16,16,512]{3,2,1,0:T(8,128)(2,1)} %copy-done.40) | copy-start | bytes 786436
  447.6 81.0 %all-to-all-start.9 = ((bf16[128,32,512]{2,1,0:T(8,128)(2,1)}), bf16[128,32,512]{2,1,0:T(8,128)(2,1)}, u32[]{:S(2)}, u32[]{:S(2)}) async-start(bf16[128,32,512]{2,1,0:T(8,128)(2,1)} %after.20), calls=%async_computation.9 | async-start | bytes 8388608 | tf_op jit(solution)/shard_map/all_to_all | solution.py:128
  452.5 62.9 %collective-permute-start.12 = (bf16[3,16,16,512]{3,2,1,0:T(8,128)(2,1)S(1)}, bf16[3,16,16,512]{3,2,1,0:T(8,128)(2,1)S(1)}, u32[]{:S(2)}, u32[]{:S(2)}) collective-permute-start(bf16[3,16,16,512]{3,2,1,0:T(8,128)(2,1)S(1)} %copy-done.50), channel_id=1, source_target_pairs={{0,8},{1,9},{2,10},{3,11},{4,12},{5,13},{6,14},{7,15},{8,0},{9,1},... | collective-permute-start | bytes 2359304 | tf_op jit(solution)/shard_map/ppermute | solution.py:140
  452.6 73.8 %collective-permute-start.9 = (bf16[2,16,16,512]{3,2,1,0:T(8,128)(2,1)}, bf16[2,16,16,512]{3,2,1,0:T(8,128)(2,1)S(1)}, u32[]{:S(2)}, u32[]{:S(2)}) collective-permute-start(bf16[2,16,16,512]{3,2,1,0:T(8,128)(2,1)} %get-tuple-element.46.refs_2_), channel_id=1, source_target_pairs={{0,8},{1,9},{2,10},{3,11},{4,12},{5,13},{6,14},{7,15},{8,0},{9,1},... | collective-permute-start | bytes 1572872 | tf_op jit(solution)/shard_map/ppermute | solution.py:140
  529.9 51.4 %all-to-all-start.10 = ((bf16[128,16,512]{2,1,0:T(8,128)(2,1)}), bf16[128,16,512]{2,1,0:T(8,128)(2,1)S(1)}, u32[]{:S(2)}, u32[]{:S(2)}) async-start(bf16[128,16,512]{2,1,0:T(8,128)(2,1)} %copy-done.3), calls=%async_computation.10 | async-start | bytes 4194304 | tf_op jit(solution)/shard_map/all_to_all | solution.py:128
  533.5 40.8 %collective-permute-start.10 = (bf16[3,16,16,512]{3,2,1,0:T(8,128)(2,1)}, bf16[3,16,16,512]{3,2,1,0:T(8,128)(2,1)S(1)}, u32[]{:S(2)}, u32[]{:S(2)}) collective-permute-start(bf16[3,16,16,512]{3,2,1,0:T(8,128)(2,1)} %copy-done.52), channel_id=1, source_target_pairs={{0,8},{1,9},{2,10},{3,11},{4,12},{5,13},{6,14},{7,15},{8,0},{9,1},... | collective-permute-start | bytes 2359304 | tf_op jit(solution)/shard_map/ppermute | solution.py:140
  534.7 78.3 %collective-permute-start.11 = (bf16[3,16,16,512]{3,2,1,0:T(8,128)(2,1)}, bf16[3,16,16,512]{3,2,1,0:T(8,128)(2,1)}, u32[]{:S(2)}, u32[]{:S(2)}) collective-permute-start(bf16[3,16,16,512]{3,2,1,0:T(8,128)(2,1)} %copy-done.51), channel_id=1, source_target_pairs={{0,8},{1,9},{2,10},{3,11},{4,12},{5,13},{6,14},{7,15},{8,0},{9,1},... | collective-permute-start | bytes 2359304 | tf_op jit(solution)/shard_map/ppermute | solution.py:140
  608.9 11.1 %all-to-all-start.12 = ((bf16[16,8,256]{2,1,0:T(8,128)(2,1)}), bf16[16,8,256]{2,1,0:T(8,128)(2,1)}, u32[]{:S(2)}, u32[]{:S(2)}) async-start(bf16[16,8,256]{2,1,0:T(8,128)(2,1)} %broadcast_in_dim.29), calls=%async_computation.12 | async-start | bytes 131072 | tf_op jit(solution)/shard_map/all_to_all | solution.py:450
  623.8 4.6 copy-start.29
  623.8 4.6 copy-start.38
  623.8 30.2 %all-to-all-start.13 = ((bf16[128,16,512]{2,1,0:T(8,128)(2,1)}), bf16[128,16,512]{2,1,0:T(8,128)(2,1)}, u32[]{:S(2)}, u32[]{:S(2)}) async-start(bf16[128,16,512]{2,1,0:T(8,128)(2,1)} %copy-done.6), calls=%async_computation.13 | async-start | bytes 4194304 | tf_op jit(solution)/shard_map/all_to_all | solution.py:128
  684.9 11.4 %all-to-all-start.15 = ((bf16[16,8,512]{2,1,0:T(8,128)(2,1)}), bf16[16,8,512]{2,1,0:T(8,128)(2,1)S(1)}, u32[]{:S(2)}, u32[]{:S(2)}) async-start(bf16[16,8,512]{2,1,0:T(8,128)(2,1)} %broadcast_in_dim.30), calls=%async_computation.15 | async-start | bytes 262144 | tf_op jit(solution)/shard_map/all_to_all | solution.py:450
  (37 other events, 47.3 us)

commit v5 on v4

--- a/solution.py
+++ b/solution.py
@@ -162,7 +162,7 @@
     rows = x_ref.shape[0]
     hidden = fa_ref.shape[0]
 
-    @pl.loop(0, rows // step)
+    @pl.loop(0, rows // step, unroll=min(2, rows // step))
     def _(turn):
         row = pl.multiple_of(turn * step, step)
         z_hat, _ = stats(turned(x_ref, row, step))
@@ -321,7 +321,7 @@
 
     spread_in(p_ref, s_ref)
 
-    @pl.loop(0, rows // step)
+    @pl.loop(0, rows // step, unroll=min(2, rows // step))
     def _(turn):
         row = pl.multiple_of(turn * step, step)
         z_hat, _ = stats(turned(x_ref, row, step))
@@ -343,14 +343,14 @@
     gather_out(s_ref, g_ref)
 
 
-def make_middle(plan, table, before, x, d, p, small):
+def make_middle(plan, table, before, ready, x, d, p, small):
     chans = x.shape[-1]
     hidden = p.shape[0]
     cut = table.shape[0]
     grads = [jax.ShapeDtypeStruct((hidden, chans), F32), jax.ShapeDtypeStruct((chans, chans), F32)]
     pairs = plan.pair_spec(chans, lambda i, j, at: (i, at[j, 0], at[j, 1], 0, 0))
     channel = pl.BlockSpec((hidden, plan.rows, plan.width), lambda i, j, at: (0, i, j))
-    kept = list(before)
+    kept = [*before, *ready]
     return pl.pallas_call(
         functools.partial(middle_kernel, plan.step),
         grid_spec=pltpu.PrefetchScalarGridSpec(
@@ -374,7 +374,7 @@
             jax.ShapeDtypeStruct((plan.count, chans, plan.crop), BF16),
         ]
         + grads,
-        input_output_aliases={4 + len(small): 1} if kept else {},
+        input_output_aliases={4 + len(small): 1} if before else {},
         compiler_params=params(2),
         cost_estimate=cost(0.2),
         name="middle",
@@ -395,7 +395,7 @@
     spread_in(ga_ref, sa_ref)
     spread_in(gb_ref, sb_ref)
 
-    @pl.loop(0, rows // step)
+    @pl.loop(0, rows // step, unroll=min(2, rows // step))
     def _(turn):
         row = pl.multiple_of(turn * step, step)
         z_hat, inv_in = stats(turned(x_ref, row, step))
@@ -481,16 +481,22 @@
 
     plan_cut = plan.cut
     two = plan.subs == 2
-    cut_a, cut_b = plan_cut(5, 3), plan_cut(2, 2, 2, 2)
-    back_a, back_b = plan_cut(2, 1, 2, 3), plan_cut(2, 3, 3)
-
-    def middle(at, before, product):
+    cut_a, cut_b = plan_cut(5, 3), plan_cut(3, 2, 3)
+    back_a, back_b = plan_cut(3, 1, 4), plan_cut(2, 4, 2)
+    small = [gain, bias, w_t, w_cat]
+
+    def middle(at, before, ready, product):
         table = jnp.stack([jnp.stack([half, jnp.int32(sub)]) for half, sub in at])
-        g, kept, *local = make_middle(plan, table, before, x, d, product, mid)
+        g, kept, *local = make_middle(plan, table, before, ready, x, d, product, mid)
         return g, kept, jnp.concatenate(local[::-1], axis=1)
 
-    def product_of(b):
-        return joined(make_product(plan, own_a, b))
+    def summed(own, back):
+        return joined(
+            (own.astype(F32) + jnp.concatenate(back, axis=0).astype(F32)).astype(BF16)
+        )
+
+    def last(sub, before, ready, grad_b):
+        return make_last(plan, sub, before, ready, x, mask, grad_a, grad_b, kept, small)
 
     factor_a, factor_b0 = make_factors(plan, 0, (), x, mask, gain, bias, w_t)
     own_b = [owned(plan.swap(factor_b0))]
@@ -500,54 +506,45 @@
     got_a = [plan.exchange(sent[0])]
     own_a = owned(plan.swap(after(factor_a, own_b[0])))
     got_a.append(plan.exchange(sent[1]))
+    got_b = []
     if two:
         own_b.append(owned(plan.swap(after(factor_b1, own_a, got_a[0]))))
         sent = plan.pieces(own_b[1], cut_b)
         got_b = [plan.exchange(piece) for piece in sent]
-    else:
-        got_b = [own_a] * 4
-    product = plan.swap(after(product_of(got_a), own_b[-1]))
-    grad, kept, local_0 = middle([(1 - side, 0)], (), product)
-    product_own = plan.swap(after(product_of(own_b), product, got_b[0]))
-    owner_g = [owned(plan.swap(after(grad, product_own, got_b[1])))]
-    grad_own, kept, local_own = middle([(side, sub) for sub in every], (kept, grad), product_own)
-    grad_b0 = make_grad_b(plan, owner_g[0], own_a, back_a)
-    owner_own = owned(plan.swap(after(grad_own, owner_g[0], got_b[2], grad_b0[0])))
-    grad_b_own = make_grad_b(plan, owner_own, own_a, [plan.half] * plan.subs)
+    product = plan.swap(joined(make_product(plan, own_a, got_a + own_b)))
+    places = [(1 - side, 0)] + [(side, sub) for sub in every]
+    grad, kept, local_mid = middle(places, (), got_b[:1], product)
+    owner_g = [owned(plan.swap(after(grad, *got_b[1:2])))]
+    parts = make_grad_b(plan, owner_g[0], own_a, back_a + [plan.half] * plan.subs)
+    grad_b0, grad_b_own = parts[: len(back_a)], parts[len(back_a) :]
     back_0 = [plan.exchange(piece) for piece in grad_b0]
-    local_mid = local_0 + local_own
-    back_1, b_other = [], [got_a]
+    other_b, held = got_a + own_b, ()
     if two:
-        product = plan.swap(after(product_of(got_b), owner_own, grad_b_own[0]))
-        grad, kept, local_1 = middle([(1 - side, 1)], (kept, back_0[0]), product)
+        product = plan.swap(after(joined(make_product(plan, own_a, got_b)), grad_b0[0]))
+        grad, kept, local_1 = middle([(1 - side, 1)], (kept,), back_0[:1], product)
         local_mid += local_1
         owner_g.append(owned(plan.swap(after(grad, back_0[1]))))
+        held = (owner_g[1],)
+    grad_b = plan.swap(after(summed(grad_b_own[0], back_0), *held))
+    if two:
         grad_b1 = make_grad_b(plan, owner_g[1], own_a, back_b)
         back_1 = [plan.exchange(piece) for piece in grad_b1]
-        b_other.append(got_b)
-    grad_a = joined(
-        make_grad_a(plan, owner_g + [owner_own], [v for got in b_other for v in got] + own_b)
+        other_b, held = other_b + got_b, (grad_b1[0], back_1[0])
+    grad_a = joined(make_grad_a(plan, owner_g, other_b))
+    grad_a = plan.swap(after(grad_a, grad_b, *held))
+    pair_grad, local_ab = last(0, None, (back_1[1],) if two else (grad_b,), grad_b)
+    if two:
+        grad_b = plan.swap(after(summed(grad_b_own[1], back_1), local_ab))
+        pair_grad, local = last(1, pair_grad, (), grad_b)
+        local_ab += local
+    total = tile_sum(jnp.concatenate([local_ab, local_mid], axis=1), tiles) / crop
+    wide = 4 * hidden
+    return (
+        pair_grad.reshape(count, crop, chans),
+        total[:, :wide],
+        total[:, wide : wide + chans],
+        total[:, wide + chans :],
     )
-    grad_a = plan.swap(after(grad_a, back_0[2], *(grad_b1[:1] if two else [])))
-
-    def summed(own, back):
-        return joined(
-            (own.astype(F32) + jnp.concatenate(back, axis=0).astype(F32)).astype(BF16)
-        )
-
-    waits = (grad_a, *back_1[:1])
-    grad_b = plan.swap(after(summed(grad_b_own[0], back_0), *waits))
-    sum_mid = tile_sum(after(local_mid, grad_b, *back_1[1:2]), tiles) / crop
-    small = [gain, bias, w_t, w_cat]
-    pair_grad, local_ab = make_last(
-        plan, 0, None, (grad_b,), x, mask, grad_a, grad_b, kept, small
-    )
-    if two:
-        grad_b = plan.swap(after(summed(grad_b_own[1], back_1), sum_mid))
-        pair_grad, local = make_last(plan, 1, pair_grad, (), x, mask, grad_a, grad_b, kept, small)
-        local_ab += local
-    sum_ab = tile_sum(local_ab, tiles) / crop
-    return (pair_grad.reshape(count, crop, chans), sum_ab, sum_mid[:, :chans], sum_mid[:, chans:])
 
 
 def solution(mesh):

time: 699 us -> 692 us (0.990)
  waiting for transfers between devices: 383 us -> 449 us
  Pallas kernels: 136 us -> 113 us
  starting transfers between devices: 86.2 us -> 65.1 us
  local copies, waits for them, and re-layouts: 43.1 us -> 28.6 us
  blocking collectives: 35.8 us -> 24.8 us
    ppermute x13 -> x11, waiting for transfers between devices: 313 us -> 389 us  [exchange(): return lax.ppermute(array, 'tile', self.partner)]
    unnamed x121 -> x98, local copies, waits for them, and re-layouts: 36.2 us -> 21.6 us
    all_to_all x12 -> x10, starting transfers between devices: 58.1 us -> 46.3 us  [swap(): lax.all_to_all(array, 'tile', split_axis=0, concat_axis=0, axis_index_gro...]
    all_to_all x2, blocking collectives: 35.8 us -> 24.8 us  [swap_all(): lax.all_to_all(array, 'tile', split_axis=0, concat_axis=0, tiled=True)]
    all_to_all x2 -> x0, waiting for transfers between devices: 10.1 us -> none  [swap_all(): lax.all_to_all(array, 'tile', split_axis=0, concat_axis=0, tiled=True)]
    all_to_all x2 -> x0, starting transfers between devices: 7.67 us -> none  [swap_all(): lax.all_to_all(array, 'tile', split_axis=0, concat_axis=0, tiled=True)]
    pallas_call x3 -> x2, Pallas kernels: 36.7 us -> 30.7 us  [make_middle(): pl.pallas_call(functools.partial(middle_kernel, plan.step), grid_spec=plt...]
    pallas_call x3 -> x2, Pallas kernels: 15.3 us -> 10.4 us  [make_grad_b(): pl.pallas_call(functools.partial(grad_b_kernel, plan.subs), grid=(g.shape...]
  transfers between devices with their start and end apart: 27 -> 21, of which waited for: 21 -> 14; matrix products, arithmetic and copies ran while one was open for 2% -> 2% of each run, Pallas kernels for 14% -> 8%
where the time goes in v5:
time: 692 us; the launch traced here: 691 us
  waiting for transfers between devices  449 us (65%)
  Pallas kernels  113 us (16%)
  starting transfers between devices  65.1 us (9%)
  local copies, waits for them, and re-layouts  28.6 us (4%)
  blocking collectives  24.8 us (4%)
  other arithmetic  9.05 us (1%)
    ppermute x11, waiting for transfers between devices, exchange(): return lax.ppermute(array, 'tile', self.partner)  389 us
    all_to_all x10, waiting for transfers between devices, swap(): lax.all_to_all(array, 'tile', split_axis=0, concat_axis=0, axis_index_gro...  59.5 us
    all_to_all x10, starting transfers between devices, swap(): lax.all_to_all(array, 'tile', split_axis=0, concat_axis=0, axis_index_gro...  46.3 us
    pallas_call x2, Pallas kernels, make_last(): pl.pallas_call(functools.partial(last_kernel, plan.step), grid=(plan.bloc...  34.7 us
    pallas_call x2, Pallas kernels, make_middle(): pl.pallas_call(functools.partial(middle_kernel, plan.step), grid_spec=plt...  30.7 us
    all_to_all x2, blocking collectives, swap_all(): lax.all_to_all(array, 'tile', split_axis=0, concat_axis=0, tiled=True)  24.8 us
    unnamed x98, local copies, waits for them, and re-layouts  21.6 us
    pallas_call x2, Pallas kernels, make_factors(): pl.pallas_call(functools.partial(factors_kernel, plan.step), grid=(plan.b...  19 us
  transfers between devices with their start and end apart: 21, of which 14 were waited for; matrix products, arithmetic and copies ran while one was open for 2% of the time, Pallas kernels for 8%

profile of v5, /device:TPU:0, one launch (start us, length us, event | category | flops | bytes accessed | tf_op | source)
XLA Modules:
  0.0 690.6 jit_solution(7794082487738651037)
XLA Ops:
  4.3 9.5 %factors.2 = (bf16[128,32,512]{2,1,0:T(8,128)(2,1)}, bf16[128,16,512]{2,1,0:T(8,128)(2,1)S(1)}) custom-call(bf16[32,16,2,16,128]{4,3,2,1,0:T(8,128)(2,1)} %bitcast.62, f32[32,512]{1,0:T(8,128)S(1)} %broadcast_multiply_fusion.mask_ref, f32[128,1]{1,0:T(8,128)S(1)} %copy.67.gain_ref, f32[128,1]{1,0:T(8,128)S(1)} %copy.68.bias_ref, bf16[512,128]{1,0:T(8,128)(2,1)S(1)} %bitcast.50), custom_call_target="tpu_custom_call" | custom-call | flops 200000000 | bytes 600000 | tf_op jit(solution)/shard_map/factors/pallas_call | solution.py:185
  15.1 5.3 all-to-all-start
  20.4 9.5 %factors.3 = (bf16[128,32,512]{2,1,0:T(8,128)(2,1)}, bf16[128,16,512]{2,1,0:T(8,128)(2,1)S(1)}) custom-call(bf16[32,16,2,16,128]{4,3,2,1,0:T(8,128)(2,1)} %bitcast.63, f32[32,512]{1,0:T(8,128)S(1)} %broadcast_multiply_fusion.mask_ref, f32[128,1]{1,0:T(8,128)S(1)} %copy.67.gain_ref, f32[128,1]{1,0:T(8,128)S(1)} %copy.68.bias_ref, ...), custom_call_target="tpu_custom_call", output_to_operand_aliasing={{0}: (5, {})} | custom-call | flops 200000000 | bytes 600000 | tf_op jit(solution)/shard_map/factors/pallas_call | solution.py:185
  31.2 14.9 %all-to-all-done = bf16[128,16,512]{2,1,0:T(8,128)(2,1)S(1)} async-done(((bf16[128,16,512]{2,1,0:T(8,128)(2,1)}), bf16[128,16,512]{2,1,0:T(8,128)(2,1)S(1)}, u32[]{:S(2)}, u32[]{:S(2)}) %all-to-all-start) | async-done | bytes 2097184 | tf_op jit(solution)/shard_map/all_to_all | solution.py:128
  46.1 4.6 all-to-all-start.1
  50.8 2.7 collective-permute-start
  53.4 71.3 %collective-permute-done.refs_2_.refs_0_ = bf16[5,16,16,512]{3,2,1,0:T(8,128)(2,1)S(1)} collective-permute-done((bf16[5,16,16,512]{3,2,1,0:T(8,128)(2,1)S(1)}, bf16[5,16,16,512]{3,2,1,0:T(8,128)(2,1)S(1)}, u32[]{:S(2)}, u32[]{:S(2)}) %collective-permute-start) | collective-permute-done | bytes 1310752 | tf_op jit(solution)/shard_map/ppermute | solution.py:140
  124.7 2.2 all-to-all-done.1
  126.9 1.6 copy-done.5
  129.8 5.2 all-to-all-start.2
  136.0 39.4 %collective-permute-done.1.refs_1_.refs_3_ = bf16[3,16,16,512]{3,2,1,0:T(8,128)(2,1)S(1)} collective-permute-done((bf16[3,16,16,512]{3,2,1,0:T(8,128)(2,1)S(1)}, bf16[3,16,16,512]{3,2,1,0:T(8,128)(2,1)S(1)}, u32[]{:S(2)}, u32[]{:S(2)}) %collective-permute-start.1) | collective-permute-done | bytes 786464 | tf_op jit(solution)/shard_map/ppermute | solution.py:140
  175.5 2.2 all-to-all-done.2
  177.6 6.7 product.2
  184.3 4.5 all-to-all-start.3
  190.4 1.6 collective-permute-start.2
  192.0 1.9 slice.55
  196.0 44.7 %collective-permute-done.2.refs_0_.refs_6_ = bf16[3,16,16,512]{3,2,1,0:T(8,128)(2,1)S(1)} collective-permute-done((bf16[3,16,16,512]{3,2,1,0:T(8,128)(2,1)S(1)}, bf16[3,16,16,512]{3,2,1,0:T(8,128)(2,1)S(1)}, u32[]{:S(2)}, u32[]{:S(2)}) %collective-permute-start.2) | collective-permute-done | bytes 786464 | tf_op jit(solution)/shard_map/ppermute | solution.py:140
  240.6 13.2 %all-to-all-done.3.p_ref = bf16[128,32,384]{2,1,0:T(8,128)(2,1)} async-done(((bf16[128,32,384]{2,1,0:T(8,128)(2,1)}), bf16[128,32,384]{2,1,0:T(8,128)(2,1)}, u32[]{:S(2)}, u32[]{:S(2)}) %all-to-all-start.3) | async-done | bytes 3145760 | tf_op jit(solution)/shard_map/all_to_all | solution.py:128
  253.8 21.7 %middle.2 = (bf16[128,32,384]{2,1,0:T(8,128)(2,1)}, bf16[32,128,512]{2,1,0:T(8,128)(2,1)}, f32[128,128]{1,0:T(8,128)S(1)}, f32[128,128]{1,0:T(8,128)S(1)}) custom-call(s32[3,2]{1,0:T(4,128)S(1)} %pad_add_fusion._, bf16[32,16,2,16,128]{4,3,2,1,0:T(8,128)(2,1)} %bitcast.64, bf16[32,16,2,16,128]{4,3,2,1,0:T(8,128)(2,1)} %bitcast.69, ...), custom_call_target="tpu_custom_call" | custom-call | flops 200000000 | bytes 600000 | tf_op jit(solution)/shard_map/middle/pallas_call | solution.py:354
  275.6 2.1 copy-done.1
  277.7 1.7 copy-done.2
  279.4 4.5 all-to-all-start.4
  283.9 51.5 %collective-permute-done.4.refs_2_.refs_8_ = bf16[3,16,16,512]{3,2,1,0:T(8,128)(2,1)S(1)} collective-permute-done((bf16[3,16,16,512]{3,2,1,0:T(8,128)(2,1)S(1)}, bf16[3,16,16,512]{3,2,1,0:T(8,128)(2,1)S(1)}, u32[]{:S(2)}, u32[]{:S(2)}) %collective-permute-start.4) | collective-permute-done | bytes 786464 | tf_op jit(solution)/shard_map/ppermute | solution.py:140
  335.4 4.9 product.3
  341.2 6.6 grad_b.2
  349.5 4.2 all-to-all-start.5
  353.6 2.9 collective-permute-start.5
  356.6 40.7 %collective-permute-done.5.refs_1_ = bf16[3,16,16,512]{3,2,1,0:T(8,128)(2,1)S(1)} collective-permute-done((bf16[3,16,16,512]{3,2,1,0:T(8,128)(2,1)S(1)}, bf16[3,16,16,512]{3,2,1,0:T(8,128)(2,1)S(1)}, u32[]{:S(2)}, u32[]{:S(2)}) %collective-permute-start.5) | collective-permute-done | bytes 786464 | tf_op jit(solution)/shard_map/ppermute | solution.py:140
  397.4 8.9 %middle.3 = (bf16[128,32,128]{2,1,0:T(8,128)(2,1)}, bf16[32,128,512]{2,1,0:T(8,128)(2,1)}, f32[128,128]{1,0:T(8,128)S(1)}, f32[128,128]{1,0:T(8,128)S(1)}) custom-call(s32[1,2]{1,0:T(1,128)S(1)} %fusion.3._, bf16[32,16,2,16,128]{4,3,2,1,0:T(8,128)(2,1)} %bitcast.65, bf16[32,16,2,16,128]{4,3,2,1,0:T(8,128)(2,1)} %bitcast.70, ...), custom_call_target="tpu_custom_call", output_to_operand_aliasing={{1}: (11, {})} | custom-call | flops 200000000 | bytes 600000 | tf_op jit(solution)/shard_map/middle/pallas_call | solution.py:354
  407.6 3.6 all-to-all-start.6
  411.2 3.5 collective-permute-start.7
  414.7 46.3 %collective-permute-done.7 = bf16[4,16,16,512]{3,2,1,0:T(8,128)(2,1)S(1)} collective-permute-done((bf16[4,16,16,512]{3,2,1,0:T(8,128)(2,1)S(1)}, bf16[4,16,16,512]{3,2,1,0:T(8,128)(2,1)S(1)}, u32[]{:S(2)}, u32[]{:S(2)}) %collective-permute-start.7) | collective-permute-done | bytes 1048608 | tf_op jit(solution)/shard_map/ppermute | solution.py:140
  460.9 3.9 add_convert_fusion.1
  464.9 3.8 all-to-all-start.7
  468.7 3.9 grad_b.3
  473.6 2.7 collective-permute-start.8
  476.3 7.0 %grad_a.1 = bf16[8,16,32,512]{3,2,1,0:T(8,128)(2,1)} custom-call(bf16[8,16,32,384]{3,2,1,0:T(8,128)(2,1)} %bitcast.23.g_ref.refs_0_, bf16[8,16,32,128]{3,2,1,0:T(8,128)(2,1)S(1)} %bitcast.49, bf16[5,16,16,512]{3,2,1,0:T(8,128)(2,1)} %copy-done.3, bf16[3,16,16,512]{3,2,1,0:T(8,128)(2,1)S(1)} %copy-done.18, bf16[8,16,16,512]{3,2,1,0:T(8,128)(2,1)} %bitcast.46, ...), custom_call_target="tpu_custom_call" | custom-call | flops 200000000 | bytes 600000 | tf_op jit(solution)/shard_map/grad_a/pallas_call | solution.py:298
  483.4 19.9 %collective-permute-done.8.refs_3_ = bf16[2,16,16,512]{3,2,1,0:T(8,128)(2,1)S(1)} collective-permute-done((bf16[2,16,16,512]{3,2,1,0:T(8,128)(2,1)S(1)}, bf16[2,16,16,512]{3,2,1,0:T(8,128)(2,1)S(1)}, u32[]{:S(2)}, u32[]{:S(2)}) %collective-permute-start.8) | collective-permute-done | bytes 524320 | tf_op jit(solution)/shard_map/ppermute | solution.py:140
  507.4 6.1 all-to-all-start.8
  514.2 2.2 collective-permute-start.10
  518.1 75.3 %collective-permute-done.10 = bf16[2,16,16,512]{3,2,1,0:T(8,128)(2,1)S(1)} collective-permute-done((bf16[2,16,16,512]{3,2,1,0:T(8,128)(2,1)}, bf16[2,16,16,512]{3,2,1,0:T(8,128)(2,1)S(1)}, u32[]{:S(2)}, u32[]{:S(2)}) %collective-permute-start.10) | collective-permute-done | bytes 524320 | tf_op jit(solution)/shard_map/ppermute | solution.py:140
  593.4 4.0 add_convert_fusion
  598.3 17.3 %last.2 = (bf16[32,16,2,16,128]{4,3,2,1,0:T(8,128)(2,1)}, f32[128,512]{1,0:T(8,128)S(1)}) custom-call(bf16[32,16,2,16,128]{4,3,2,1,0:T(8,128)(2,1)} %bitcast.66, f32[32,512]{1,0:T(8,128)S(1)} %copy-done.23, bf16[128,32,512]{2,1,0:T(8,128)(2,1)} %all-to-all-done.8.ga_ref, bf16[128,16,512]{2,1,0:T(8,128)(2,1)S(1)} %all-to-all-done.7.refs_1_.gb_ref, ...), custom_call_target="tpu_custom_call" | custom-call | flops 200000000 | bytes 600000 | tf_op jit(solution)/shard_map/last/pallas_call | solution.py:427
  616.4 4.9 all-to-all-start.9
  621.3 25.6 %all-to-all-done.9.gb_ref = bf16[128,16,512]{2,1,0:T(8,128)(2,1)S(1)} async-done(((bf16[128,16,512]{2,1,0:T(8,128)(2,1)}), bf16[128,16,512]{2,1,0:T(8,128)(2,1)S(1)}, u32[]{:S(2)}, u32[]{:S(2)}) %all-to-all-start.9) | async-done | bytes 2097184 | tf_op jit(solution)/shard_map/all_to_all | solution.py:128
  646.9 17.4 %last.3 = (bf16[32,16,2,16,128]{4,3,2,1,0:T(8,128)(2,1)}, f32[128,512]{1,0:T(8,128)S(1)}) custom-call(bf16[32,16,2,16,128]{4,3,2,1,0:T(8,128)(2,1)} %bitcast.67, f32[32,512]{1,0:T(8,128)S(1)} %copy-done.23, bf16[128,32,512]{2,1,0:T(8,128)(2,1)} %all-to-all-done.8.ga_ref, ...), custom_call_target="tpu_custom_call", output_to_operand_aliasing={{0}: (9, {})} | custom-call | flops 200000000 | bytes 600000 | tf_op jit(solution)/shard_map/last/pallas_call | solution.py:427
  664.4 13.2 %all_to_all.62 = bf16[16,8,768]{2,1,0:T(8,128)(2,1)S(1)} all-to-all(bf16[16,8,768]{2,1,0:T(8,128)(2,1)S(1)} %pad_maximum_fusion), channel_id=1, replica_groups=mesh['crops'=2,'tile'=16] {'tile'}, dimensions={0} | all-to-all | bytes 393216 | tf_op jit(solution)/shard_map/all_to_all | solution.py:450
  677.6 11.6 %all_to_all.63 = bf16[16,8,768]{2,1,0:T(8,128)(2,1)S(1)} all-to-all(bf16[16,8,768]{2,1,0:T(8,128)(2,1)S(1)} %broadcast_in_dim.23), channel_id=1, replica_groups=mesh['crops'=2,'tile'=16] {'tile'}, dimensions={0} | all-to-all | bytes 393216 | tf_op jit(solution)/shard_map/all_to_all | solution.py:450
  (142 shorter events, 27.2 us)
Async XLA Ops:
  2.3 18.1 %copy-start.11 = (f32[128,1]{1,0:T(8,128)}, f32[128,1]{1,0:T(8,128)S(1)}, u32[]{:S(2)}) copy-start(f32[128,1]{1,0:T(8,128)S(1)} %copy.67.gain_ref) | copy-start | bytes 1540
  3.1 17.3 %copy-start.13 = (f32[128,1]{1,0:T(8,128)}, f32[128,1]{1,0:T(8,128)S(1)}, u32[]{:S(2)}) copy-start(f32[128,1]{1,0:T(8,128)S(1)} %copy.68.bias_ref) | copy-start | bytes 1540
  4.3 16.1 %copy-start.22 = (f32[32,512]{1,0:T(8,128)}, f32[32,512]{1,0:T(8,128)S(1)}, u32[]{:S(2)}) copy-start(f32[32,512]{1,0:T(8,128)S(1)} %broadcast_multiply_fusion.mask_ref) | copy-start | bytes 196612
  15.1 31.0 %all-to-all-start = ((bf16[128,16,512]{2,1,0:T(8,128)(2,1)}), bf16[128,16,512]{2,1,0:T(8,128)(2,1)S(1)}, u32[]{:S(2)}, u32[]{:S(2)}) async-start(bf16[128,16,512]{2,1,0:T(8,128)(2,1)} %copy-done.21), calls=%async_computation | async-start | bytes 4194304 | tf_op jit(solution)/shard_map/all_to_all | solution.py:128
  46.1 88.9 %copy-start = (bf16[128,16,512]{2,1,0:T(8,128)(2,1)}, bf16[128,16,512]{2,1,0:T(8,128)(2,1)S(1)}, u32[]{:S(2)}) copy-start(bf16[128,16,512]{2,1,0:T(8,128)(2,1)S(1)} %all-to-all-done) | copy-start | bytes 6291460
  46.1 80.8 %all-to-all-start.1 = ((bf16[128,32,512]{2,1,0:T(8,128)(2,1)}), bf16[128,32,512]{2,1,0:T(8,128)(2,1)}, u32[]{:S(2)}, u32[]{:S(2)}) async-start(bf16[128,32,512]{2,1,0:T(8,128)(2,1)} %after.8), calls=%async_computation.1 | async-start | bytes 8388608 | tf_op jit(solution)/shard_map/all_to_all | solution.py:128
  50.8 74.0 %collective-permute-start = (bf16[5,16,16,512]{3,2,1,0:T(8,128)(2,1)S(1)}, bf16[5,16,16,512]{3,2,1,0:T(8,128)(2,1)S(1)}, u32[]{:S(2)}, u32[]{:S(2)}) collective-permute-start(bf16[5,16,16,512]{3,2,1,0:T(8,128)(2,1)S(1)} %bitcast.73), channel_id=1, source_target_pairs={{0,8},{1,9},{2,10},{3,11},{4,12},{5,13},{6,14},{7,15},{8,0},{9,1},... | collective-permute-start | bytes 3932168 | tf_op jit(solution)/shard_map/ppermute | solution.py:140
  124.7 52.9 %copy-start.3 = (bf16[5,16,16,512]{3,2,1,0:T(8,128)(2,1)}, bf16[5,16,16,512]{3,2,1,0:T(8,128)(2,1)S(1)}, u32[]{:S(2)}) copy-start(bf16[5,16,16,512]{3,2,1,0:T(8,128)(2,1)S(1)} %collective-permute-done.refs_2_.refs_0_) | copy-start | bytes 3932164
  129.8 47.8 %all-to-all-start.2 = ((bf16[128,16,512]{2,1,0:T(8,128)(2,1)}), bf16[128,16,512]{2,1,0:T(8,128)(2,1)}, u32[]{:S(2)}, u32[]{:S(2)}) async-start(bf16[128,16,512]{2,1,0:T(8,128)(2,1)} %copy-done.6), calls=%async_computation.2 | async-start | bytes 4194304 | tf_op jit(solution)/shard_map/all_to_all | solution.py:128
  135.0 40.4 %collective-permute-start.1 = (bf16[3,16,16,512]{3,2,1,0:T(8,128)(2,1)S(1)}, bf16[3,16,16,512]{3,2,1,0:T(8,128)(2,1)S(1)}, u32[]{:S(2)}, u32[]{:S(2)}) collective-permute-start(bf16[3,16,16,512]{3,2,1,0:T(8,128)(2,1)S(1)} %bitcast.74), channel_id=1, source_target_pairs={{0,8},{1,9},{2,10},{3,11},{4,12},{5,13},{6,14},{7,15},{8,0},{9,1},... | collective-permute-start | bytes 2359304 | tf_op jit(solution)/shard_map/ppermute | solution.py:140
  175.5 8.9 %copy-start.17 = (bf16[3,16,16,512]{3,2,1,0:T(8,128)(2,1)}, bf16[3,16,16,512]{3,2,1,0:T(8,128)(2,1)S(1)}, u32[]{:S(2)}) copy-start(bf16[3,16,16,512]{3,2,1,0:T(8,128)(2,1)S(1)} %collective-permute-done.1.refs_1_.refs_3_) | copy-start | bytes 2359300
  184.3 69.5 %all-to-all-start.3 = ((bf16[128,32,384]{2,1,0:T(8,128)(2,1)}), bf16[128,32,384]{2,1,0:T(8,128)(2,1)}, u32[]{:S(2)}, u32[]{:S(2)}) async-start(bf16[128,32,384]{2,1,0:T(8,128)(2,1)} %bitcast.71), calls=%async_computation.3 | async-start | bytes 6291456 | tf_op jit(solution)/shard_map/all_to_all | solution.py:128
  188.8 6.5 copy-start.45
  188.8 6.6 copy-start.46
  188.8 6.7 copy-start.43
  188.8 6.8 copy-start.31
  188.8 65.0 %copy-start.12 = (f32[128,1]{1,0:T(8,128)S(1)}, f32[128,1]{1,0:T(8,128)}, u32[]{:S(2)}) copy-start(f32[128,1]{1,0:T(8,128)} %copy-done.11) | copy-start | bytes 1540
  188.9 65.0 %copy-start.14 = (f32[128,1]{1,0:T(8,128)S(1)}, f32[128,1]{1,0:T(8,128)}, u32[]{:S(2)}) copy-start(f32[128,1]{1,0:T(8,128)} %copy-done.13) | copy-start | bytes 1540
  190.4 50.2 %collective-permute-start.2 = (bf16[3,16,16,512]{3,2,1,0:T(8,128)(2,1)S(1)}, bf16[3,16,16,512]{3,2,1,0:T(8,128)(2,1)S(1)}, u32[]{:S(2)}, u32[]{:S(2)}) collective-permute-start(bf16[3,16,16,512]{3,2,1,0:T(8,128)(2,1)S(1)} %bitcast.76), channel_id=1, source_target_pairs={{0,8},{1,9},{2,10},{3,11},{4,12},{5,13},{6,14},{7,15},{8,0},{9,1},... | collective-permute-start | bytes 2359304 | tf_op jit(solution)/shard_map/ppermute | solution.py:140
  193.9 81.7 %collective-permute-start.3 = (bf16[2,16,16,512]{3,2,1,0:T(8,128)(2,1)}, bf16[2,16,16,512]{3,2,1,0:T(8,128)(2,1)S(1)}, u32[]{:S(2)}, u32[]{:S(2)}) collective-permute-start(bf16[2,16,16,512]{3,2,1,0:T(8,128)(2,1)} %bitcast.22), channel_id=1, source_target_pairs={{0,8},{1,9},{2,10},{3,11},{4,12},{5,13},{6,14},{7,15},{8,0},{9,1},... | collective-permute-start | bytes 1572872 | tf_op jit(solution)/shard_map/ppermute | solution.py:140
  240.6 94.8 %copy-start.7 = (bf16[3,16,16,512]{3,2,1,0:T(8,128)(2,1)}, bf16[3,16,16,512]{3,2,1,0:T(8,128)(2,1)S(1)}, u32[]{:S(2)}) copy-start(bf16[3,16,16,512]{3,2,1,0:T(8,128)(2,1)S(1)} %collective-permute-done.2.refs_0_.refs_6_) | copy-start | bytes 2359300
  275.6 59.8 %copy-start.9 = (bf16[2,16,16,512]{3,2,1,0:T(8,128)(2,1)}, bf16[2,16,16,512]{3,2,1,0:T(8,128)(2,1)S(1)}, u32[]{:S(2)}) copy-start(bf16[2,16,16,512]{3,2,1,0:T(8,128)(2,1)S(1)} %collective-permute-done.3.refs_1_.refs_7_) | copy-start | bytes 1572868
  279.4 61.9 %all-to-all-start.4 = ((bf16[128,32,384]{2,1,0:T(8,128)(2,1)}), bf16[128,32,384]{2,1,0:T(8,128)(2,1)}, u32[]{:S(2)}, u32[]{:S(2)}) async-start(bf16[128,32,384]{2,1,0:T(8,128)(2,1)} %copy-done.2), calls=%async_computation.4 | async-start | bytes 6291456 | tf_op jit(solution)/shard_map/all_to_all | solution.py:128
  283.8 51.6 %collective-permute-start.4 = (bf16[3,16,16,512]{3,2,1,0:T(8,128)(2,1)S(1)}, bf16[3,16,16,512]{3,2,1,0:T(8,128)(2,1)S(1)}, u32[]{:S(2)}, u32[]{:S(2)}) collective-permute-start(bf16[3,16,16,512]{3,2,1,0:T(8,128)(2,1)S(1)} %bitcast.75), channel_id=1, source_target_pairs={{0,8},{1,9},{2,10},{3,11},{4,12},{5,13},{6,14},{7,15},{8,0},{9,1},... | collective-permute-start | bytes 2359304 | tf_op jit(solution)/shard_map/ppermute | solution.py:140
  349.5 47.9 %all-to-all-start.5 = ((bf16[128,32,128]{2,1,0:T(8,128)(2,1)}), bf16[128,32,128]{2,1,0:T(8,128)(2,1)S(1)}, u32[]{:S(2)}, u32[]{:S(2)}) async-start(bf16[128,32,128]{2,1,0:T(8,128)(2,1)} %after.11), calls=%async_computation.5 | async-start | bytes 2097152 | tf_op jit(solution)/shard_map/all_to_all | solution.py:128
  353.6 43.7 %collective-permute-start.5 = (bf16[3,16,16,512]{3,2,1,0:T(8,128)(2,1)S(1)}, bf16[3,16,16,512]{3,2,1,0:T(8,128)(2,1)S(1)}, u32[]{:S(2)}, u32[]{:S(2)}) collective-permute-start(bf16[3,16,16,512]{3,2,1,0:T(8,128)(2,1)S(1)} %get-tuple-element.33.refs_1_), channel_id=1, source_target_pairs={{0,8},{1,9},{2,10},{3,11},{4,12},{5,13},{6,14},{7,15},{8,0},{9,1},... | collective-permute-start | bytes 2359304 | tf_op jit(solution)/shard_map/ppermute | solution.py:140
  356.5 50.5 %collective-permute-start.6 = (bf16[1,16,16,512]{3,2,1,0:T(8,128)(2,1)}, bf16[1,16,16,512]{3,2,1,0:T(8,128)(2,1)S(1)}, u32[]{:S(2)}, u32[]{:S(2)}) collective-permute-start(bf16[1,16,16,512]{3,2,1,0:T(8,128)(2,1)} %copy-done.42), channel_id=1, source_target_pairs={{0,8},{1,9},{2,10},{3,11},{4,12},{5,13},{6,14},{7,15},{8,0},{9,1},... | collective-permute-start | bytes 786440 | tf_op jit(solution)/shard_map/ppermute | solution.py:140
  407.0 4.2 copy-start.39
  407.6 57.3 %all-to-all-start.6 = ((bf16[128,32,128]{2,1,0:T(8,128)(2,1)}), bf16[128,32,128]{2,1,0:T(8,128)(2,1)S(1)}, u32[]{:S(2)}, u32[]{:S(2)}) async-start(bf16[128,32,128]{2,1,0:T(8,128)(2,1)} %after.12), calls=%async_computation.6 | async-start | bytes 2097152 | tf_op jit(solution)/shard_map/all_to_all | solution.py:128
  411.2 49.8 %collective-permute-start.7 = (bf16[4,16,16,512]{3,2,1,0:T(8,128)(2,1)S(1)}, bf16[4,16,16,512]{3,2,1,0:T(8,128)(2,1)S(1)}, u32[]{:S(2)}, u32[]{:S(2)}) collective-permute-start(bf16[4,16,16,512]{3,2,1,0:T(8,128)(2,1)S(1)} %copy-done.39), channel_id=1, source_target_pairs={{0,8},{1,9},{2,10},{3,11},{4,12},{5,13},{6,14},{7,15},{8,0},{9,1},... | collective-permute-start | bytes 3145736 | tf_op jit(solution)/shard_map/ppermute | solution.py:140
  464.9 40.5 %all-to-all-start.7 = ((bf16[128,16,512]{2,1,0:T(8,128)(2,1)}), bf16[128,16,512]{2,1,0:T(8,128)(2,1)S(1)}, u32[]{:S(2)}, u32[]{:S(2)}) async-start(bf16[128,16,512]{2,1,0:T(8,128)(2,1)} %after.13), calls=%async_computation.7 | async-start | bytes 4194304 | tf_op jit(solution)/shard_map/all_to_all | solution.py:128
  468.7 7.6 %copy-start.8 = (bf16[3,16,16,512]{3,2,1,0:T(8,128)(2,1)S(1)}, bf16[3,16,16,512]{3,2,1,0:T(8,128)(2,1)}, u32[]{:S(2)}) copy-start(bf16[3,16,16,512]{3,2,1,0:T(8,128)(2,1)} %copy-done.7) | copy-start | bytes 2359300
  468.7 7.6 %copy-start.10 = (bf16[2,16,16,512]{3,2,1,0:T(8,128)(2,1)S(1)}, bf16[2,16,16,512]{3,2,1,0:T(8,128)(2,1)}, u32[]{:S(2)}) copy-start(bf16[2,16,16,512]{3,2,1,0:T(8,128)(2,1)} %copy-done.9) | copy-start | bytes 1572868
  468.7 7.6 %copy-start.16 = (bf16[3,16,16,512]{3,2,1,0:T(8,128)(2,1)S(1)}, bf16[3,16,16,512]{3,2,1,0:T(8,128)(2,1)}, u32[]{:S(2)}) copy-start(bf16[3,16,16,512]{3,2,1,0:T(8,128)(2,1)} %copy-done.15) | copy-start | bytes 2359300
  468.7 7.6 %copy-start.18 = (bf16[3,16,16,512]{3,2,1,0:T(8,128)(2,1)S(1)}, bf16[3,16,16,512]{3,2,1,0:T(8,128)(2,1)}, u32[]{:S(2)}) copy-start(bf16[3,16,16,512]{3,2,1,0:T(8,128)(2,1)} %copy-done.17) | copy-start | bytes 2359300
  473.6 9.8 %copy-start.29 = (bf16[2,16,16,512]{3,2,1,0:T(8,128)(2,1)}, bf16[2,16,16,512]{3,2,1,0:T(8,128)(2,1)S(1)}, u32[]{:S(2)}) copy-start(bf16[2,16,16,512]{3,2,1,0:T(8,128)(2,1)S(1)} %get-tuple-element.39.refs_2_) | copy-start | bytes 1572868
  473.6 9.8 %copy-start.41 = (bf16[2,16,16,512]{3,2,1,0:T(8,128)(2,1)}, bf16[2,16,16,512]{3,2,1,0:T(8,128)(2,1)S(1)}, u32[]{:S(2)}) copy-start(bf16[2,16,16,512]{3,2,1,0:T(8,128)(2,1)S(1)} %get-tuple-element.42) | copy-start | bytes 1572868
  473.6 29.6 %collective-permute-start.8 = (bf16[2,16,16,512]{3,2,1,0:T(8,128)(2,1)S(1)}, bf16[2,16,16,512]{3,2,1,0:T(8,128)(2,1)S(1)}, u32[]{:S(2)}, u32[]{:S(2)}) collective-permute-start(bf16[2,16,16,512]{3,2,1,0:T(8,128)(2,1)S(1)} %get-tuple-element.39.refs_2_), channel_id=1, source_target_pairs={{0,8},{1,9},{2,10},{3,11},{4,12},{5,13},{6,14},{7,15},{8,0},{9,1},... | collective-permute-start | bytes 1572872 | tf_op jit(solution)/shard_map/ppermute | solution.py:140
  507.4 9.9 %copy-start.44 = (bf16[128,128]{1,0:T(8,128)(2,1)S(1)}, bf16[128,128]{1,0:T(8,128)(2,1)}, u32[]{:S(2)}) copy-start(bf16[128,128]{1,0:T(8,128)(2,1)} %param.16) | copy-start | bytes 98308
  507.4 89.9 %all-to-all-start.8 = ((bf16[128,32,512]{2,1,0:T(8,128)(2,1)}), bf16[128,32,512]{2,1,0:T(8,128)(2,1)}, u32[]{:S(2)}, u32[]{:S(2)}) async-start(bf16[128,32,512]{2,1,0:T(8,128)(2,1)} %after.14), calls=%async_computation.8 | async-start | bytes 8388608 | tf_op jit(solution)/shard_map/all_to_all | solution.py:128
  513.5 79.9 %collective-permute-start.9 = (bf16[4,16,16,512]{3,2,1,0:T(8,128)(2,1)}, bf16[4,16,16,512]{3,2,1,0:T(8,128)(2,1)S(1)}, u32[]{:S(2)}, u32[]{:S(2)}) collective-permute-start(bf16[4,16,16,512]{3,2,1,0:T(8,128)(2,1)} %copy-done.40), channel_id=1, source_target_pairs={{0,8},{1,9},{2,10},{3,11},{4,12},{5,13},{6,14},{7,15},{8,0},{9,1},... | collective-permute-start | bytes 3145736 | tf_op jit(solution)/shard_map/ppermute | solution.py:140
  514.2 79.2 %collective-permute-start.10 = (bf16[2,16,16,512]{3,2,1,0:T(8,128)(2,1)}, bf16[2,16,16,512]{3,2,1,0:T(8,128)(2,1)S(1)}, u32[]{:S(2)}, u32[]{:S(2)}) collective-permute-start(bf16[2,16,16,512]{3,2,1,0:T(8,128)(2,1)} %copy-done.41), channel_id=1, source_target_pairs={{0,8},{1,9},{2,10},{3,11},{4,12},{5,13},{6,14},{7,15},{8,0},{9,1},... | collective-permute-start | bytes 1572872 | tf_op jit(solution)/shard_map/ppermute | solution.py:140
  616.3 4.9 copy-start.33
  616.3 4.9 copy-start.35
  616.3 4.9 copy-start.37
  616.3 30.6 %copy-start.26 = (bf16[128,640]{1,0:T(8,128)(2,1)S(1)}, bf16[128,640]{1,0:T(8,128)(2,1)}, u32[]{:S(2)}) copy-start(bf16[128,640]{1,0:T(8,128)(2,1)} %copy-done.24) | copy-start | bytes 491524
  616.4 30.6 %all-to-all-start.9 = ((bf16[128,16,512]{2,1,0:T(8,128)(2,1)}), bf16[128,16,512]{2,1,0:T(8,128)(2,1)S(1)}, u32[]{:S(2)}, u32[]{:S(2)}) async-start(bf16[128,16,512]{2,1,0:T(8,128)(2,1)} %after.15), calls=%async_computation.9 | async-start | bytes 4194304 | tf_op jit(solution)/shard_map/all_to_all | solution.py:128
  646.9 17.4 %copy-start.28 = (f32[128,512]{1,0:T(8,128)S(1)}, f32[128,512]{1,0:T(8,128)}, u32[]{:S(2)}) copy-start(f32[128,512]{1,0:T(8,128)} %copy-done.27) | copy-start | bytes 786436
  (20 other events, 25.4 us)

commit v6 on v5

--- a/solution.py
+++ b/solution.py
@@ -162,7 +162,7 @@
     rows = x_ref.shape[0]
     hidden = fa_ref.shape[0]
 
-    @pl.loop(0, rows // step, unroll=min(2, rows // step))
+    @pl.loop(0, rows // step, unroll=min(4, rows // step))
     def _(turn):
         row = pl.multiple_of(turn * step, step)
         z_hat, _ = stats(turned(x_ref, row, step))
@@ -321,7 +321,7 @@
 
     spread_in(p_ref, s_ref)
 
-    @pl.loop(0, rows // step, unroll=min(2, rows // step))
+    @pl.loop(0, rows // step, unroll=min(4, rows // step))
     def _(turn):
         row = pl.multiple_of(turn * step, step)
         z_hat, _ = stats(turned(x_ref, row, step))
@@ -395,7 +395,7 @@
     spread_in(ga_ref, sa_ref)
     spread_in(gb_ref, sb_ref)
 
-    @pl.loop(0, rows // step, unroll=min(2, rows // step))
+    @pl.loop(0, rows // step, unroll=min(4, rows // step))
     def _(turn):
         row = pl.multiple_of(turn * step, step)
         z_hat, inv_in = stats(turned(x_ref, row, step))
@@ -481,8 +481,8 @@
 
     plan_cut = plan.cut
     two = plan.subs == 2
-    cut_a, cut_b = plan_cut(5, 3), plan_cut(3, 2, 3)
-    back_a, back_b = plan_cut(3, 1, 4), plan_cut(2, 4, 2)
+    cut_a, cut_b = plan_cut(5, 3), plan_cut(4, 4)
+    back_a, back_b = plan_cut(3, 2, 3), plan_cut(2, 3, 3)
     small = [gain, bias, w_t, w_cat]
 
     def middle(at, before, ready, product):
@@ -520,18 +520,18 @@
     back_0 = [plan.exchange(piece) for piece in grad_b0]
     other_b, held = got_a + own_b, ()
     if two:
-        product = plan.swap(after(joined(make_product(plan, own_a, got_b)), grad_b0[0]))
-        grad, kept, local_1 = middle([(1 - side, 1)], (kept,), back_0[:1], product)
+        got_b[0] = after(got_b[0], grad_b0[0])
+        product = plan.swap(joined(make_product(plan, own_a, got_b)))
+        grad, kept, local_1 = middle([(1 - side, 1)], (kept,), (), product)
         local_mid += local_1
-        owner_g.append(owned(plan.swap(after(grad, back_0[1]))))
-        held = (owner_g[1],)
-    grad_b = plan.swap(after(summed(grad_b_own[0], back_0), *held))
-    if two:
+        owner_g.append(after(owned(plan.swap(after(grad, back_0[0]))), back_0[1]))
         grad_b1 = make_grad_b(plan, owner_g[1], own_a, back_b)
         back_1 = [plan.exchange(piece) for piece in grad_b1]
-        other_b, held = other_b + got_b, (grad_b1[0], back_1[0])
+        other_b, held = other_b + got_b, (grad_b1[0],)
     grad_a = joined(make_grad_a(plan, owner_g, other_b))
-    grad_a = plan.swap(after(grad_a, grad_b, *held))
+    grad_a = plan.swap(after(grad_a, *held))
+    held = (grad_a, back_1[0]) if two else (grad_a,)
+    grad_b = plan.swap(after(summed(grad_b_own[0], back_0), *held))
     pair_grad, local_ab = last(0, None, (back_1[1],) if two else (grad_b,), grad_b)
     if two:
         grad_b = plan.swap(after(summed(grad_b_own[1], back_1), local_ab))

time: 692 us -> 679 us (0.981)
  blocking collectives: 24.8 us -> 66.7 us
  waiting for transfers between devices: 449 us -> 414 us
  starting transfers between devices: 65.1 us -> 52.7 us
    ppermute x11 -> x10, waiting for transfers between devices: 389 us -> 332 us  [exchange(): return lax.ppermute(array, 'tile', self.partner)]
    all_to_all x0 -> x1, blocking collectives: none -> 41.8 us  [swap(): lax.all_to_all(array, 'tile', split_axis=0, concat_axis=0, axis_index_gro...]
    all_to_all x10 -> x9, waiting for transfers between devices: 59.5 us -> 81.4 us  [swap(): lax.all_to_all(array, 'tile', split_axis=0, concat_axis=0, axis_index_gro...]
    all_to_all x10 -> x9, starting transfers between devices: 46.3 us -> 39.1 us  [swap(): lax.all_to_all(array, 'tile', split_axis=0, concat_axis=0, axis_index_gro...]
    ppermute x11 -> x10, starting transfers between devices: 18.8 us -> 13.6 us  [exchange(): return lax.ppermute(array, 'tile', self.partner)]
    unnamed x98 -> x104, local copies, waits for them, and re-layouts: 21.6 us -> 18.1 us
  transfers between devices with their start and end apart: 21 -> 19, of which waited for: 14 -> 16; matrix products, arithmetic and copies ran while one was open for 2% -> 2% of each run, Pallas kernels for 8% -> 6%
where the time goes in v6:
time: 679 us; the launch traced here: 677 us
  waiting for transfers between devices  414 us (61%)
  Pallas kernels  109 us (16%)
  blocking collectives  66.7 us (10%)
  starting transfers between devices  52.7 us (8%)
  local copies, waits for them, and re-layouts  24.8 us (4%)
  other arithmetic  9.3 us (1%)
    ppermute x10, waiting for transfers between devices, exchange(): return lax.ppermute(array, 'tile', self.partner)  332 us
    all_to_all x9, waiting for transfers between devices, swap(): lax.all_to_all(array, 'tile', split_axis=0, concat_axis=0, axis_index_gro...  81.4 us
    all_to_all x1, blocking collectives, swap(): lax.all_to_all(array, 'tile', split_axis=0, concat_axis=0, axis_index_gro...  41.8 us
    all_to_all x9, starting transfers between devices, swap(): lax.all_to_all(array, 'tile', split_axis=0, concat_axis=0, axis_index_gro...  39.1 us
    pallas_call x2, Pallas kernels, make_last(): pl.pallas_call(functools.partial(last_kernel, plan.step), grid=(plan.bloc...  32.6 us
    pallas_call x2, Pallas kernels, make_middle(): pl.pallas_call(functools.partial(middle_kernel, plan.step), grid_spec=plt...  29.2 us
    all_to_all x2, blocking collectives, swap_all(): lax.all_to_all(array, 'tile', split_axis=0, concat_axis=0, tiled=True)  24.8 us
    unnamed x104, local copies, waits for them, and re-layouts  18.1 us
  transfers between devices with their start and end apart: 19, of which 16 were waited for; matrix products, arithmetic and copies ran while one was open for 2% of the time, Pallas kernels for 6%

profile of v6, /device:TPU:0, one launch (start us, length us, event | category | flops | bytes accessed | tf_op | source)
XLA Modules:
  0.0 676.7 jit_solution(16242159623297051555)
XLA Ops:
  4.3 8.6 %factors.2 = (bf16[128,32,512]{2,1,0:T(8,128)(2,1)}, bf16[128,16,512]{2,1,0:T(8,128)(2,1)S(1)}) custom-call(bf16[32,16,2,16,128]{4,3,2,1,0:T(8,128)(2,1)} %bitcast.59, f32[32,512]{1,0:T(8,128)S(1)} %broadcast_multiply_fusion.mask_ref, f32[128,1]{1,0:T(8,128)S(1)} %copy.68.gain_ref, f32[128,1]{1,0:T(8,128)S(1)} %copy.69.bias_ref, bf16[512,128]{1,0:T(8,128)(2,1)S(1)} %bitcast.47), custom_call_target="tpu_custom_call" | custom-call | flops 200000000 | bytes 600000 | tf_op jit(solution)/shard_map/factors/pallas_call | solution.py:185
  14.2 5.2 all-to-all-start
  19.4 8.6 %factors.3 = (bf16[128,32,512]{2,1,0:T(8,128)(2,1)}, bf16[128,16,512]{2,1,0:T(8,128)(2,1)S(1)}) custom-call(bf16[32,16,2,16,128]{4,3,2,1,0:T(8,128)(2,1)} %bitcast.60, f32[32,512]{1,0:T(8,128)S(1)} %broadcast_multiply_fusion.mask_ref, f32[128,1]{1,0:T(8,128)S(1)} %copy.68.gain_ref, f32[128,1]{1,0:T(8,128)S(1)} %copy.69.bias_ref, ...), custom_call_target="tpu_custom_call", output_to_operand_aliasing={{0}: (5, {})} | custom-call | flops 200000000 | bytes 600000 | tf_op jit(solution)/shard_map/factors/pallas_call | solution.py:185
  29.4 15.8 %all-to-all-done = bf16[128,16,512]{2,1,0:T(8,128)(2,1)S(1)} async-done(((bf16[128,16,512]{2,1,0:T(8,128)(2,1)}), bf16[128,16,512]{2,1,0:T(8,128)(2,1)S(1)}, u32[]{:S(2)}, u32[]{:S(2)}) %all-to-all-start) | async-done | bytes 2097184 | tf_op jit(solution)/shard_map/all_to_all | solution.py:128
  45.1 4.5 all-to-all-start.1
  49.8 2.7 collective-permute-start
  52.5 71.3 %collective-permute-done.refs_2_.refs_0_ = bf16[5,16,16,512]{3,2,1,0:T(8,128)(2,1)S(1)} collective-permute-done((bf16[5,16,16,512]{3,2,1,0:T(8,128)(2,1)S(1)}, bf16[5,16,16,512]{3,2,1,0:T(8,128)(2,1)S(1)}, u32[]{:S(2)}, u32[]{:S(2)}) %collective-permute-start) | collective-permute-done | bytes 1310752 | tf_op jit(solution)/shard_map/ppermute | solution.py:140
  123.7 2.2 all-to-all-done.1
  125.9 1.6 copy-done.3
  128.8 5.2 all-to-all-start.2
  135.0 39.5 %collective-permute-done.1.refs_1_.refs_3_ = bf16[3,16,16,512]{3,2,1,0:T(8,128)(2,1)S(1)} collective-permute-done((bf16[3,16,16,512]{3,2,1,0:T(8,128)(2,1)S(1)}, bf16[3,16,16,512]{3,2,1,0:T(8,128)(2,1)S(1)}, u32[]{:S(2)}, u32[]{:S(2)}) %collective-permute-start.1) | collective-permute-done | bytes 786464 | tf_op jit(solution)/shard_map/ppermute | solution.py:140
  174.5 2.2 all-to-all-done.2
  176.7 6.7 product.2
  183.3 4.5 all-to-all-start.3
  187.9 3.1 fusion.6
  191.0 1.5 collective-permute-start.2
  192.5 1.4 collective-permute-start.3
  194.6 50.8 %collective-permute-done.2.refs_0_ = bf16[4,16,16,512]{3,2,1,0:T(8,128)(2,1)S(1)} collective-permute-done((bf16[4,16,16,512]{3,2,1,0:T(8,128)(2,1)}, bf16[4,16,16,512]{3,2,1,0:T(8,128)(2,1)S(1)}, u32[]{:S(2)}, u32[]{:S(2)}) %collective-permute-start.2) | collective-permute-done | bytes 1048608 | tf_op jit(solution)/shard_map/ppermute | solution.py:140
  245.4 9.9 %all-to-all-done.3.p_ref = bf16[128,32,384]{2,1,0:T(8,128)(2,1)} async-done(((bf16[128,32,384]{2,1,0:T(8,128)(2,1)}), bf16[128,32,384]{2,1,0:T(8,128)(2,1)}, u32[]{:S(2)}, u32[]{:S(2)}) %all-to-all-start.3) | async-done | bytes 3145760 | tf_op jit(solution)/shard_map/all_to_all | solution.py:128
  255.3 20.7 %middle.2 = (bf16[128,32,384]{2,1,0:T(8,128)(2,1)}, bf16[32,128,512]{2,1,0:T(8,128)(2,1)}, f32[128,128]{1,0:T(8,128)S(1)}, f32[128,128]{1,0:T(8,128)S(1)}) custom-call(s32[3,2]{1,0:T(4,128)S(1)} %pad_add_fusion._, bf16[32,16,2,16,128]{4,3,2,1,0:T(8,128)(2,1)} %bitcast.61, bf16[32,16,2,16,128]{4,3,2,1,0:T(8,128)(2,1)} %bitcast.68, ...), custom_call_target="tpu_custom_call" | custom-call | flops 200000000 | bytes 600000 | tf_op jit(solution)/shard_map/middle/pallas_call | solution.py:354
  276.1 8.9 %collective-permute-done.3.refs_1_.refs_7_ = bf16[4,16,16,512]{3,2,1,0:T(8,128)(2,1)S(1)} collective-permute-done((bf16[4,16,16,512]{3,2,1,0:T(8,128)(2,1)}, bf16[4,16,16,512]{3,2,1,0:T(8,128)(2,1)S(1)}, u32[]{:S(2)}, u32[]{:S(2)}) %collective-permute-start.3) | collective-permute-done | bytes 1048608 | tf_op jit(solution)/shard_map/ppermute | solution.py:140
  285.0 41.8 %all_to_all.62 = bf16[128,32,384]{2,1,0:T(8,128)(2,1)} all-to-all(bf16[128,32,384]{2,1,0:T(8,128)(2,1)} %after.11), channel_id=1, replica_groups={{0,1,2,3,4,5,6,7},{8,9,10,11,12,13,14,15},{16,17,18,19,20,21,22,23},{24..., dimensions={0} | all-to-all | bytes 6291456 | tf_op jit(solution)/shard_map/all_to_all | solution.py:128
  326.8 6.6 grad_b.2
  335.3 4.8 product.3
  340.1 3.7 all-to-all-start.5
  344.8 23.8 %all-to-all-done.5.p_ref = bf16[128,32,128]{2,1,0:T(8,128)(2,1)S(1)} async-done(((bf16[128,32,128]{2,1,0:T(8,128)(2,1)}), bf16[128,32,128]{2,1,0:T(8,128)(2,1)S(1)}, u32[]{:S(2)}, u32[]{:S(2)}) %all-to-all-start.5) | async-done | bytes 1048608 | tf_op jit(solution)/shard_map/all_to_all | solution.py:128
  373.1 8.4 %middle.3 = (bf16[128,32,128]{2,1,0:T(8,128)(2,1)S(1)}, bf16[32,128,512]{2,1,0:T(8,128)(2,1)}, f32[128,128]{1,0:T(8,128)S(1)}, f32[128,128]{1,0:T(8,128)S(1)}) custom-call(s32[1,2]{1,0:T(1,128)S(1)} %fusion.3._, bf16[32,16,2,16,128]{4,3,2,1,0:T(8,128)(2,1)} %bitcast.62, bf16[32,16,2,16,128]{4,3,2,1,0:T(8,128)(2,1)} %bitcast.69, ...), custom_call_target="tpu_custom_call", output_to_operand_aliasing={{1}: (11, {})} | custom-call | flops 200000000 | bytes 600000 | tf_op jit(solution)/shard_map/middle/pallas_call | solution.py:354
  383.7 3.6 all-to-all-start.6
  387.5 26.4 %collective-permute-done.5.refs_1_ = bf16[2,16,16,512]{3,2,1,0:T(8,128)(2,1)S(1)} collective-permute-done((bf16[2,16,16,512]{3,2,1,0:T(8,128)(2,1)}, bf16[2,16,16,512]{3,2,1,0:T(8,128)(2,1)S(1)}, u32[]{:S(2)}, u32[]{:S(2)}) %collective-permute-start.5) | collective-permute-done | bytes 524320 | tf_op jit(solution)/shard_map/ppermute | solution.py:140
  415.8 3.8 grad_b.3
  419.6 7.8 %grad_a.1 = bf16[8,16,32,512]{3,2,1,0:T(8,128)(2,1)} custom-call(bf16[8,16,32,384]{3,2,1,0:T(8,128)(2,1)} %bitcast.67, bf16[8,16,32,128]{3,2,1,0:T(8,128)(2,1)S(1)} %after.14.refs_1_.g_ref, bf16[5,16,16,512]{3,2,1,0:T(8,128)(2,1)} %copy-done.1, bf16[3,16,16,512]{3,2,1,0:T(8,128)(2,1)S(1)} %copy-done.13, bf16[8,16,16,512]{3,2,1,0:T(8,128)(2,1)} %bitcast.45, ...), custom_call_target="tpu_custom_call" | custom-call | flops 200000000 | bytes 600000 | tf_op jit(solution)/shard_map/grad_a/pallas_call | solution.py:298
  427.4 4.7 all-to-all-start.7
  432.6 2.5 collective-permute-start.6
  435.1 60.0 %collective-permute-done.9 = bf16[3,16,16,512]{3,2,1,0:T(8,128)(2,1)S(1)} collective-permute-done((bf16[3,16,16,512]{3,2,1,0:T(8,128)(2,1)S(1)}, bf16[3,16,16,512]{3,2,1,0:T(8,128)(2,1)S(1)}, u32[]{:S(2)}, u32[]{:S(2)}) %collective-permute-start.9) | collective-permute-done | bytes 786464 | tf_op jit(solution)/shard_map/ppermute | solution.py:140
  495.2 4.2 add_convert_fusion
  499.4 6.8 %collective-permute-done.6.refs_2_ = bf16[2,16,16,512]{3,2,1,0:T(8,128)(2,1)S(1)} collective-permute-done((bf16[2,16,16,512]{3,2,1,0:T(8,128)(2,1)S(1)}, bf16[2,16,16,512]{3,2,1,0:T(8,128)(2,1)S(1)}, u32[]{:S(2)}, u32[]{:S(2)}) %collective-permute-start.6) | collective-permute-done | bytes 524320 | tf_op jit(solution)/shard_map/ppermute | solution.py:140
  506.2 2.2 all-to-all-done.7.refs_1_.ga_ref
  508.4 3.7 all-to-all-start.8
  512.2 1.9 collective-permute-start.7
  515.2 37.7 %collective-permute-done.7.refs_0_ = bf16[3,16,16,512]{3,2,1,0:T(8,128)(2,1)S(1)} collective-permute-done((bf16[3,16,16,512]{3,2,1,0:T(8,128)(2,1)}, bf16[3,16,16,512]{3,2,1,0:T(8,128)(2,1)S(1)}, u32[]{:S(2)}, u32[]{:S(2)}) %collective-permute-start.7) | collective-permute-done | bytes 786464 | tf_op jit(solution)/shard_map/ppermute | solution.py:140
  552.9 30.8 %collective-permute-done.8 = bf16[3,16,16,512]{3,2,1,0:T(8,128)(2,1)S(1)} collective-permute-done((bf16[3,16,16,512]{3,2,1,0:T(8,128)(2,1)}, bf16[3,16,16,512]{3,2,1,0:T(8,128)(2,1)S(1)}, u32[]{:S(2)}, u32[]{:S(2)}) %collective-permute-start.8) | collective-permute-done | bytes 786464 | tf_op jit(solution)/shard_map/ppermute | solution.py:140
  583.7 4.0 add_convert_fusion.1
  587.7 16.3 %last.2 = (bf16[32,16,2,16,128]{4,3,2,1,0:T(8,128)(2,1)}, f32[128,512]{1,0:T(8,128)S(1)}) custom-call(bf16[32,16,2,16,128]{4,3,2,1,0:T(8,128)(2,1)} %bitcast.63, f32[32,512]{1,0:T(8,128)S(1)} %copy-done.20, bf16[128,32,512]{2,1,0:T(8,128)(2,1)} %all-to-all-done.7.refs_1_.ga_ref, bf16[128,16,512]{2,1,0:T(8,128)(2,1)S(1)} %all-to-all-done.8.gb_ref, ...), custom_call_target="tpu_custom_call" | custom-call | flops 200000000 | bytes 600000 | tf_op jit(solution)/shard_map/last/pallas_call | solution.py:427
  604.7 4.0 all-to-all-start.9
  608.7 25.3 %all-to-all-done.9.gb_ref = bf16[128,16,512]{2,1,0:T(8,128)(2,1)S(1)} async-done(((bf16[128,16,512]{2,1,0:T(8,128)(2,1)}), bf16[128,16,512]{2,1,0:T(8,128)(2,1)S(1)}, u32[]{:S(2)}, u32[]{:S(2)}) %all-to-all-start.9) | async-done | bytes 2097184 | tf_op jit(solution)/shard_map/all_to_all | solution.py:128
  634.1 16.3 %last.3 = (bf16[32,16,2,16,128]{4,3,2,1,0:T(8,128)(2,1)}, f32[128,512]{1,0:T(8,128)S(1)}) custom-call(bf16[32,16,2,16,128]{4,3,2,1,0:T(8,128)(2,1)} %bitcast.64, f32[32,512]{1,0:T(8,128)S(1)} %copy-done.20, bf16[128,32,512]{2,1,0:T(8,128)(2,1)} %all-to-all-done.7.refs_1_.ga_ref, ...), custom_call_target="tpu_custom_call", output_to_operand_aliasing={{0}: (9, {})} | custom-call | flops 200000000 | bytes 600000 | tf_op jit(solution)/shard_map/last/pallas_call | solution.py:427
  650.4 13.2 %all_to_all.63 = bf16[16,8,768]{2,1,0:T(8,128)(2,1)S(1)} all-to-all(bf16[16,8,768]{2,1,0:T(8,128)(2,1)S(1)} %pad_maximum_fusion), channel_id=1, replica_groups=mesh['crops'=2,'tile'=16] {'tile'}, dimensions={0} | all-to-all | bytes 393216 | tf_op jit(solution)/shard_map/all_to_all | solution.py:450
  663.7 11.6 %all_to_all.64 = bf16[16,8,768]{2,1,0:T(8,128)(2,1)S(1)} all-to-all(bf16[16,8,768]{2,1,0:T(8,128)(2,1)S(1)} %broadcast_in_dim.23), channel_id=1, replica_groups=mesh['crops'=2,'tile'=16] {'tile'}, dimensions={0} | all-to-all | bytes 393216 | tf_op jit(solution)/shard_map/all_to_all | solution.py:450
  (145 shorter events, 24.8 us)
Async XLA Ops:
  2.3 17.1 %copy-start.8 = (f32[128,1]{1,0:T(8,128)}, f32[128,1]{1,0:T(8,128)S(1)}, u32[]{:S(2)}) copy-start(f32[128,1]{1,0:T(8,128)S(1)} %copy.68.gain_ref) | copy-start | bytes 1540
  3.1 16.3 %copy-start.10 = (f32[128,1]{1,0:T(8,128)}, f32[128,1]{1,0:T(8,128)S(1)}, u32[]{:S(2)}) copy-start(f32[128,1]{1,0:T(8,128)S(1)} %copy.69.bias_ref) | copy-start | bytes 1540
  4.3 15.2 %copy-start.19 = (f32[32,512]{1,0:T(8,128)}, f32[32,512]{1,0:T(8,128)S(1)}, u32[]{:S(2)}) copy-start(f32[32,512]{1,0:T(8,128)S(1)} %broadcast_multiply_fusion.mask_ref) | copy-start | bytes 196612
  14.2 30.9 %all-to-all-start = ((bf16[128,16,512]{2,1,0:T(8,128)(2,1)}), bf16[128,16,512]{2,1,0:T(8,128)(2,1)S(1)}, u32[]{:S(2)}, u32[]{:S(2)}) async-start(bf16[128,16,512]{2,1,0:T(8,128)(2,1)} %copy-done.18), calls=%async_computation | async-start | bytes 4194304 | tf_op jit(solution)/shard_map/all_to_all | solution.py:128
  45.1 88.9 %copy-start = (bf16[128,16,512]{2,1,0:T(8,128)(2,1)}, bf16[128,16,512]{2,1,0:T(8,128)(2,1)S(1)}, u32[]{:S(2)}) copy-start(bf16[128,16,512]{2,1,0:T(8,128)(2,1)S(1)} %all-to-all-done) | copy-start | bytes 6291460
  45.1 80.8 %all-to-all-start.1 = ((bf16[128,32,512]{2,1,0:T(8,128)(2,1)}), bf16[128,32,512]{2,1,0:T(8,128)(2,1)}, u32[]{:S(2)}, u32[]{:S(2)}) async-start(bf16[128,32,512]{2,1,0:T(8,128)(2,1)} %after.9), calls=%async_computation.1 | async-start | bytes 8388608 | tf_op jit(solution)/shard_map/all_to_all | solution.py:128
  49.8 74.0 %collective-permute-start = (bf16[5,16,16,512]{3,2,1,0:T(8,128)(2,1)S(1)}, bf16[5,16,16,512]{3,2,1,0:T(8,128)(2,1)S(1)}, u32[]{:S(2)}, u32[]{:S(2)}) collective-permute-start(bf16[5,16,16,512]{3,2,1,0:T(8,128)(2,1)S(1)} %bitcast.72), channel_id=1, source_target_pairs={{0,8},{1,9},{2,10},{3,11},{4,12},{5,13},{6,14},{7,15},{8,0},{9,1},... | collective-permute-start | bytes 3932168 | tf_op jit(solution)/shard_map/ppermute | solution.py:140
  123.7 52.9 %copy-start.1 = (bf16[5,16,16,512]{3,2,1,0:T(8,128)(2,1)}, bf16[5,16,16,512]{3,2,1,0:T(8,128)(2,1)S(1)}, u32[]{:S(2)}) copy-start(bf16[5,16,16,512]{3,2,1,0:T(8,128)(2,1)S(1)} %collective-permute-done.refs_2_.refs_0_) | copy-start | bytes 3932164
  128.8 47.8 %all-to-all-start.2 = ((bf16[128,16,512]{2,1,0:T(8,128)(2,1)}), bf16[128,16,512]{2,1,0:T(8,128)(2,1)}, u32[]{:S(2)}, u32[]{:S(2)}) async-start(bf16[128,16,512]{2,1,0:T(8,128)(2,1)} %copy-done.4), calls=%async_computation.2 | async-start | bytes 4194304 | tf_op jit(solution)/shard_map/all_to_all | solution.py:128
  134.1 40.4 %collective-permute-start.1 = (bf16[3,16,16,512]{3,2,1,0:T(8,128)(2,1)S(1)}, bf16[3,16,16,512]{3,2,1,0:T(8,128)(2,1)S(1)}, u32[]{:S(2)}, u32[]{:S(2)}) collective-permute-start(bf16[3,16,16,512]{3,2,1,0:T(8,128)(2,1)S(1)} %bitcast.73), channel_id=1, source_target_pairs={{0,8},{1,9},{2,10},{3,11},{4,12},{5,13},{6,14},{7,15},{8,0},{9,1},... | collective-permute-start | bytes 2359304 | tf_op jit(solution)/shard_map/ppermute | solution.py:140
  174.5 8.9 %copy-start.12 = (bf16[3,16,16,512]{3,2,1,0:T(8,128)(2,1)}, bf16[3,16,16,512]{3,2,1,0:T(8,128)(2,1)S(1)}, u32[]{:S(2)}) copy-start(bf16[3,16,16,512]{3,2,1,0:T(8,128)(2,1)S(1)} %collective-permute-done.1.refs_1_.refs_3_) | copy-start | bytes 2359300
  183.3 72.0 %all-to-all-start.3 = ((bf16[128,32,384]{2,1,0:T(8,128)(2,1)}), bf16[128,32,384]{2,1,0:T(8,128)(2,1)}, u32[]{:S(2)}, u32[]{:S(2)}) async-start(bf16[128,32,384]{2,1,0:T(8,128)(2,1)} %bitcast.70), calls=%async_computation.3 | async-start | bytes 6291456 | tf_op jit(solution)/shard_map/all_to_all | solution.py:128
  187.8 6.1 copy-start.48
  187.8 6.2 copy-start.49
  187.8 6.3 copy-start.46
  187.8 6.4 copy-start.26
  187.9 67.4 %copy-start.9 = (f32[128,1]{1,0:T(8,128)S(1)}, f32[128,1]{1,0:T(8,128)}, u32[]{:S(2)}) copy-start(f32[128,1]{1,0:T(8,128)} %copy-done.8) | copy-start | bytes 1540
  187.9 67.4 %copy-start.11 = (f32[128,1]{1,0:T(8,128)S(1)}, f32[128,1]{1,0:T(8,128)}, u32[]{:S(2)}) copy-start(f32[128,1]{1,0:T(8,128)} %copy-done.10) | copy-start | bytes 1540
  191.0 54.4 %collective-permute-start.2 = (bf16[4,16,16,512]{3,2,1,0:T(8,128)(2,1)}, bf16[4,16,16,512]{3,2,1,0:T(8,128)(2,1)S(1)}, u32[]{:S(2)}, u32[]{:S(2)}) collective-permute-start(bf16[4,16,16,512]{3,2,1,0:T(8,128)(2,1)} %bitcast.21), channel_id=1, source_target_pairs={{0,8},{1,9},{2,10},{3,11},{4,12},{5,13},{6,14},{7,15},{8,0},{9,1},... | collective-permute-start | bytes 3145736 | tf_op jit(solution)/shard_map/ppermute | solution.py:140
  192.5 92.5 %collective-permute-start.3 = (bf16[4,16,16,512]{3,2,1,0:T(8,128)(2,1)}, bf16[4,16,16,512]{3,2,1,0:T(8,128)(2,1)S(1)}, u32[]{:S(2)}, u32[]{:S(2)}) collective-permute-start(bf16[4,16,16,512]{3,2,1,0:T(8,128)(2,1)} %bitcast.22), channel_id=1, source_target_pairs={{0,8},{1,9},{2,10},{3,11},{4,12},{5,13},{6,14},{7,15},{8,0},{9,1},... | collective-permute-start | bytes 3145736 | tf_op jit(solution)/shard_map/ppermute | solution.py:140
  194.3 81.8 %copy-start.28 = (bf16[128,128]{0,1:T(8,128)(2,1)}, bf16[128,128]{0,1:T(8,128)(2,1)S(1)}, u32[]{:S(2)}) copy-start(bf16[128,128]{0,1:T(8,128)(2,1)S(1)} %copy.70) | copy-start | bytes 98308
  194.4 81.6 %copy-start.30 = (bf16[128,128]{0,1:T(8,128)(2,1)}, bf16[128,128]{0,1:T(8,128)(2,1)S(1)}, u32[]{:S(2)}) copy-start(bf16[128,128]{0,1:T(8,128)(2,1)S(1)} %copy.71) | copy-start | bytes 98308
  276.0 8.9 %copy-start.32 = (f32[128,128]{1,0:T(8,128)}, f32[128,128]{1,0:T(8,128)S(1)}, u32[]{:S(2)}) copy-start(f32[128,128]{1,0:T(8,128)S(1)} %get-tuple-element.49) | copy-start | bytes 196612
  276.1 8.9 %copy-start.34 = (f32[128,128]{1,0:T(8,128)}, f32[128,128]{1,0:T(8,128)S(1)}, u32[]{:S(2)}) copy-start(f32[128,128]{1,0:T(8,128)S(1)} %get-tuple-element.48) | copy-start | bytes 196612
  334.4 5.8 copy-start.44
  340.1 28.4 %all-to-all-start.5 = ((bf16[128,32,128]{2,1,0:T(8,128)(2,1)}), bf16[128,32,128]{2,1,0:T(8,128)(2,1)S(1)}, u32[]{:S(2)}, u32[]{:S(2)}) async-start(bf16[128,32,128]{2,1,0:T(8,128)(2,1)} %bitcast.25), calls=%async_computation.5 | async-start | bytes 2097152 | tf_op jit(solution)/shard_map/all_to_all | solution.py:128
  343.9 38.9 %collective-permute-start.4 = (bf16[3,16,16,512]{3,2,1,0:T(8,128)(2,1)}, bf16[3,16,16,512]{3,2,1,0:T(8,128)(2,1)}, u32[]{:S(2)}, u32[]{:S(2)}) collective-permute-start(bf16[3,16,16,512]{3,2,1,0:T(8,128)(2,1)} %copy-done.23), channel_id=1, source_target_pairs={{0,8},{1,9},{2,10},{3,11},{4,12},{5,13},{6,14},{7,15},{8,0},{9,1},... | collective-permute-start | bytes 2359304 | tf_op jit(solution)/shard_map/ppermute | solution.py:140
  383.7 31.0 %all-to-all-start.6 = ((bf16[128,32,128]{2,1,0:T(8,128)(2,1)}), bf16[128,32,128]{2,1,0:T(8,128)(2,1)S(1)}, u32[]{:S(2)}, u32[]{:S(2)}) async-start(bf16[128,32,128]{2,1,0:T(8,128)(2,1)} %copy-done.5), calls=%async_computation.6 | async-start | bytes 2097152 | tf_op jit(solution)/shard_map/all_to_all | solution.py:128
  387.3 26.6 %collective-permute-start.5 = (bf16[2,16,16,512]{3,2,1,0:T(8,128)(2,1)}, bf16[2,16,16,512]{3,2,1,0:T(8,128)(2,1)S(1)}, u32[]{:S(2)}, u32[]{:S(2)}) collective-permute-start(bf16[2,16,16,512]{3,2,1,0:T(8,128)(2,1)} %copy-done.44), channel_id=1, source_target_pairs={{0,8},{1,9},{2,10},{3,11},{4,12},{5,13},{6,14},{7,15},{8,0},{9,1},... | collective-permute-start | bytes 1572872 | tf_op jit(solution)/shard_map/ppermute | solution.py:140
  419.6 7.8 %copy-start.42 = (bf16[3,16,16,512]{3,2,1,0:T(8,128)(2,1)}, bf16[3,16,16,512]{3,2,1,0:T(8,128)(2,1)S(1)}, u32[]{:S(2)}) copy-start(bf16[3,16,16,512]{3,2,1,0:T(8,128)(2,1)S(1)} %get-tuple-element.40) | copy-start | bytes 2359300
  419.6 7.8 %copy-start.43 = (bf16[3,16,16,512]{3,2,1,0:T(8,128)(2,1)}, bf16[3,16,16,512]{3,2,1,0:T(8,128)(2,1)S(1)}, u32[]{:S(2)}) copy-start(bf16[3,16,16,512]{3,2,1,0:T(8,128)(2,1)S(1)} %get-tuple-element.39) | copy-start | bytes 2359300
  419.6 7.8 %copy-start.24 = (bf16[2,16,16,512]{3,2,1,0:T(8,128)(2,1)}, bf16[2,16,16,512]{3,2,1,0:T(8,128)(2,1)S(1)}, u32[]{:S(2)}) copy-start(bf16[2,16,16,512]{3,2,1,0:T(8,128)(2,1)S(1)} %get-tuple-element.37.refs_1_) | copy-start | bytes 1572868
  427.4 4.7 copy-start.41
  427.4 5.2 copy-start.25
  427.4 67.8 %copy-start.17 = (bf16[2,16,16,512]{3,2,1,0:T(8,128)(2,1)S(1)}, bf16[2,16,16,512]{3,2,1,0:T(8,128)(2,1)}, u32[]{:S(2)}) copy-start(bf16[2,16,16,512]{3,2,1,0:T(8,128)(2,1)} %copy-done.15) | copy-start | bytes 1572868
  427.4 81.0 %all-to-all-start.7 = ((bf16[128,32,512]{2,1,0:T(8,128)(2,1)}), bf16[128,32,512]{2,1,0:T(8,128)(2,1)}, u32[]{:S(2)}, u32[]{:S(2)}) async-start(bf16[128,32,512]{2,1,0:T(8,128)(2,1)} %after.15), calls=%async_computation.7 | async-start | bytes 8388608 | tf_op jit(solution)/shard_map/all_to_all | solution.py:128
  432.2 63.0 %collective-permute-start.9 = (bf16[3,16,16,512]{3,2,1,0:T(8,128)(2,1)S(1)}, bf16[3,16,16,512]{3,2,1,0:T(8,128)(2,1)S(1)}, u32[]{:S(2)}, u32[]{:S(2)}) collective-permute-start(bf16[3,16,16,512]{3,2,1,0:T(8,128)(2,1)S(1)} %copy-done.41), channel_id=1, source_target_pairs={{0,8},{1,9},{2,10},{3,11},{4,12},{5,13},{6,14},{7,15},{8,0},{9,1},... | collective-permute-start | bytes 2359304 | tf_op jit(solution)/shard_map/ppermute | solution.py:140
  432.6 73.6 %collective-permute-start.6 = (bf16[2,16,16,512]{3,2,1,0:T(8,128)(2,1)S(1)}, bf16[2,16,16,512]{3,2,1,0:T(8,128)(2,1)S(1)}, u32[]{:S(2)}, u32[]{:S(2)}) collective-permute-start(bf16[2,16,16,512]{3,2,1,0:T(8,128)(2,1)S(1)} %copy-done.25), channel_id=1, source_target_pairs={{0,8},{1,9},{2,10},{3,11},{4,12},{5,13},{6,14},{7,15},{8,0},{9,1},... | collective-permute-start | bytes 1572872 | tf_op jit(solution)/shard_map/ppermute | solution.py:140
  508.4 6.8 copy-start.45
  508.4 6.8 %copy-start.47 = (bf16[128,128]{1,0:T(8,128)(2,1)S(1)}, bf16[128,128]{1,0:T(8,128)(2,1)}, u32[]{:S(2)}) copy-start(bf16[128,128]{1,0:T(8,128)(2,1)} %param.16) | copy-start | bytes 98308
  508.4 79.3 %all-to-all-start.8 = ((bf16[128,16,512]{2,1,0:T(8,128)(2,1)}), bf16[128,16,512]{2,1,0:T(8,128)(2,1)S(1)}, u32[]{:S(2)}, u32[]{:S(2)}) async-start(bf16[128,16,512]{2,1,0:T(8,128)(2,1)} %after.16), calls=%async_computation.8 | async-start | bytes 4194304 | tf_op jit(solution)/shard_map/all_to_all | solution.py:128
  512.2 40.8 %collective-permute-start.7 = (bf16[3,16,16,512]{3,2,1,0:T(8,128)(2,1)}, bf16[3,16,16,512]{3,2,1,0:T(8,128)(2,1)S(1)}, u32[]{:S(2)}, u32[]{:S(2)}) collective-permute-start(bf16[3,16,16,512]{3,2,1,0:T(8,128)(2,1)} %copy-done.43), channel_id=1, source_target_pairs={{0,8},{1,9},{2,10},{3,11},{4,12},{5,13},{6,14},{7,15},{8,0},{9,1},... | collective-permute-start | bytes 2359304 | tf_op jit(solution)/shard_map/ppermute | solution.py:140
  514.0 69.7 %collective-permute-start.8 = (bf16[3,16,16,512]{3,2,1,0:T(8,128)(2,1)}, bf16[3,16,16,512]{3,2,1,0:T(8,128)(2,1)S(1)}, u32[]{:S(2)}, u32[]{:S(2)}) collective-permute-start(bf16[3,16,16,512]{3,2,1,0:T(8,128)(2,1)} %copy-done.42), channel_id=1, source_target_pairs={{0,8},{1,9},{2,10},{3,11},{4,12},{5,13},{6,14},{7,15},{8,0},{9,1},... | collective-permute-start | bytes 2359304 | tf_op jit(solution)/shard_map/ppermute | solution.py:140
  604.7 4.0 copy-start.35
  604.7 4.0 copy-start.37
  604.7 4.0 copy-start.39
  604.7 29.4 %all-to-all-start.9 = ((bf16[128,16,512]{2,1,0:T(8,128)(2,1)}), bf16[128,16,512]{2,1,0:T(8,128)(2,1)S(1)}, u32[]{:S(2)}, u32[]{:S(2)}) async-start(bf16[128,16,512]{2,1,0:T(8,128)(2,1)} %after.17), calls=%async_computation.9 | async-start | bytes 4194304 | tf_op jit(solution)/shard_map/all_to_all | solution.py:128
  634.1 16.3 %copy-start.22 = (f32[128,512]{1,0:T(8,128)S(1)}, f32[128,512]{1,0:T(8,128)}, u32[]{:S(2)}) copy-start(f32[128,512]{1,0:T(8,128)} %copy-done.21) | copy-start | bytes 786436
  (21 other events, 30.6 us)

commit v7 on v6

--- a/solution.py
+++ b/solution.py
@@ -77,10 +77,10 @@
     )
 
 
-def gather_out(scratch, out_ref):
-    hidden, rows, cols = out_ref.shape
+def gather_out(scratch, out_ref, rows, at=0):
+    hidden = out_ref.shape[0]
     for lane in range(scratch.shape[0]):
-        out_ref[:, :, lane * 128 : (lane + 1) * 128] = (
+        out_ref[:, at : at + rows, lane * 128 : (lane + 1) * 128] = (
             scratch[lane].reshape(hidden, rows, 128).astype(BF16)
         )
 
@@ -157,10 +157,10 @@
     )(value, *others)
 
 
-def factors_kernel(step, x_ref, mask_ref, gain_ref, bias_ref, w_ref, *refs):
-    fa_ref, fb_ref, sa_ref, sb_ref = refs[-4:]
+def factors_kernel(step, joint, x_ref, mask_ref, gain_ref, bias_ref, w_ref, *refs):
+    sa_ref, sb_ref = refs[-2:]
     rows = x_ref.shape[0]
-    hidden = fa_ref.shape[0]
+    hidden = w_ref.shape[0] // 4
 
     @pl.loop(0, rows // step, unroll=min(4, rows // step))
     def _(turn):
@@ -174,16 +174,32 @@
         store_rows(sb_ref, row, step, rows, mask * sigmoid(gate_b) * value_b)
         store_rows(sa_ref, row, step, rows, mask * sigmoid(gate_a) * value_a)
 
-    gather_out(sa_ref, fa_ref)
-    gather_out(sb_ref, fb_ref)
+    if joint:
+        gather_out(sa_ref, refs[-3], rows)
+        gather_out(sb_ref, refs[-3], rows, rows)
+    else:
+        gather_out(sa_ref, refs[-4], rows)
+        gather_out(sb_ref, refs[-3], rows)
 
 
 def make_factors(plan, sub, before, x, mask, gain, bias, w_t):
     chans = x.shape[-1]
     hidden = w_t.shape[0] // 4
     block = (hidden, plan.rows, plan.width)
-    return pl.pallas_call(
-        functools.partial(factors_kernel, plan.step),
+    held = plan.rows * (3 if plan.subs == 2 else 1)
+    out_specs = [
+        pl.BlockSpec(block, lambda j: (0, 2 * (plan.subs - 1), j)),
+        pl.BlockSpec(block, lambda j: (0, 0, j)),
+    ]
+    out_shape = [
+        jax.ShapeDtypeStruct((hidden, held, plan.crop), BF16),
+        jax.ShapeDtypeStruct((hidden, plan.rows, plan.crop), BF16),
+    ]
+    if before:
+        out_specs = [pl.BlockSpec((hidden, 2 * plan.rows, plan.width), lambda j: (0, 0, j))]
+        out_shape = out_shape[:1]
+    return pl.pallas_call(
+        functools.partial(factors_kernel, plan.step, bool(before)),
         grid=(plan.blocks,),
         in_specs=[
             plan.pair_spec(chans, lambda j: (sub, j % 2, j // 2, 0, 0)),
@@ -193,14 +209,8 @@
             whole(w_t),
         ]
         + [HELD for _ in before],
-        out_specs=[
-            pl.BlockSpec(block, lambda j: (0, sub, j)),
-            pl.BlockSpec(block, lambda j: (0, 0, j)),
-        ],
-        out_shape=[
-            jax.ShapeDtypeStruct((hidden, plan.count, plan.crop), BF16),
-            jax.ShapeDtypeStruct((hidden, plan.rows, plan.crop), BF16),
-        ],
+        out_specs=out_specs,
+        out_shape=out_shape,
         input_output_aliases={5: 0} if before else {},
         scratch_shapes=[plan.scratch(hidden)] * 2,
         compiler_params=params(1),
@@ -223,13 +233,12 @@
     return jnp.concatenate(parts, axis=0) if subs > 1 else parts[0]
 
 
-def to_subs(ref, chan, value, subs):
-    tiles, _, rows, cols = ref.shape
+def to_subs(ref, chan, value, subs, rows):
     part = value.shape[0] // subs
     for sub in range(subs):
-        ref[:, chan, sub * (rows // subs) : (sub + 1) * (rows // subs), :] = value[
+        ref[:, chan, sub * rows : (sub + 1) * rows, :] = value[
             sub * part : (sub + 1) * part
-        ].astype(BF16).reshape(tiles, rows // subs, cols)
+        ].astype(BF16).reshape(ref.shape[0], rows, ref.shape[3])
 
 
 def own_spec(array):
@@ -237,31 +246,41 @@
     return pl.BlockSpec((src, CHANS, rows, cols), lambda h: (0, h, 0, 0))
 
 
-def product_kernel(subs, a_ref, *refs):
-    b, p_ref = refs[:-1], refs[-1]
+def view_spec(plan, view):
+    array, at = view
+    return pl.BlockSpec((array.shape[0], CHANS, plan.rows, array.shape[3]), lambda h: (0, h, at, 0))
+
+
+def arrays(views):
+    return [array for array, _ in views]
+
+
+def product_kernel(subs, rows, *refs):
+    a, b, p_ref = refs[:subs], refs[subs:-1], refs[-1]
     for chan in range(CHANS):
-        to_subs(p_ref, chan, dot(by_sub(a_ref, chan, subs), matrix(b, chan), NT), subs)
+        to_subs(p_ref, chan, dot(matrix(a, chan), matrix(b, chan), NT), subs, rows)
 
 
 def make_product(plan, a, b):
-    tiles, chans, _, _ = a.shape
-    cols = sum(value.shape[0] for value in b) * plan.rows
+    tiles, chans = a[0][0].shape[:2]
+    cols = sum(array.shape[0] for array in arrays(b)) * plan.rows
     out = jax.ShapeDtypeStruct((tiles, chans, plan.count, cols), BF16)
     return pl.pallas_call(
-        functools.partial(product_kernel, plan.subs),
+        functools.partial(product_kernel, plan.subs, plan.rows),
         grid=(chans // CHANS,),
-        in_specs=[own_spec(value) for value in (a, *b)],
+        in_specs=[view_spec(plan, view) for view in (*a, *b)],
         out_specs=own_spec(out),
         out_shape=out,
         compiler_params=params(1),
         cost_estimate=cost(0.2),
         name="product",
-    )(a, *b)
-
-
-def grad_b_kernel(subs, g_ref, a_ref, *outs):
+    )(*arrays(a), *arrays(b))
+
+
+def grad_b_kernel(subs, g_ref, *refs):
+    a, outs = refs[:subs], refs[subs:]
     for chan in range(CHANS):
-        grad = dot(by_sub(g_ref, chan, subs), by_sub(a_ref, chan, subs), TN).astype(BF16)
+        grad = dot(by_sub(g_ref, chan, subs), matrix(a, chan), TN).astype(BF16)
         at = 0
         for out in outs:
             size = out.shape[0] * out.shape[2]
@@ -271,40 +290,49 @@
 
 def make_grad_b(plan, g, a, tiles):
     outs = [
-        jax.ShapeDtypeStruct((count, a.shape[1], plan.rows, plan.crop), BF16) for count in tiles
+        jax.ShapeDtypeStruct((count, g.shape[1], plan.rows, plan.crop), BF16) for count in tiles
     ]
     return pl.pallas_call(
         functools.partial(grad_b_kernel, plan.subs),
         grid=(g.shape[1] // CHANS,),
-        in_specs=[own_spec(value) for value in (g, a)],
+        in_specs=[own_spec(g)] + [view_spec(plan, view) for view in a],
         out_specs=[own_spec(value) for value in outs],
         out_shape=outs,
         compiler_params=params(1),
         cost_estimate=cost(0.2),
         name="grad_b",
-    )(g, a)
-
-
-def grad_a_kernel(subs, count, *refs):
-    g, b, out = refs[:count], refs[count:-1], refs[-1]
+    )(g, *arrays(a))
+
+
+def grad_a_kernel(subs, rows, counts, *refs):
+    g, b = refs[: counts[0]], refs[counts[0] : counts[0] + counts[1]]
+    own, back, out = refs[counts[0] + counts[1]], refs[counts[0] + counts[1] + 1 : -1], refs[-1]
     for chan in range(CHANS):
-        rows = jnp.concatenate([by_sub(ref, chan, subs) for ref in g], axis=1)
-        to_subs(out, chan, dot(rows, matrix(b, chan)), subs)
-
-
-def make_grad_a(plan, g, b):
-    chans = b[0].shape[1]
-    out = jax.ShapeDtypeStruct((plan.half, chans, plan.count, plan.crop), BF16)
-    return pl.pallas_call(
-        functools.partial(grad_a_kernel, plan.subs, len(g)),
+        left = jnp.concatenate([by_sub(ref, chan, subs) for ref in g], axis=1)
+        to_subs(out, chan, dot(left, matrix(b, chan)), subs, rows)
+        at = 0
+        for piece in back:
+            end = at + piece.shape[0]
+            added = own[at:end, chan].astype(F32) + piece[:, chan].astype(F32)
+            out[at:end, chan, subs * rows :, :] = added.astype(BF16)
+            at = end
+
+
+def make_grad_a(plan, g, b, own, back):
+    chans = own.shape[1]
+    out = jax.ShapeDtypeStruct((plan.half, chans, plan.count + plan.rows, plan.crop), BF16)
+    return pl.pallas_call(
+        functools.partial(grad_a_kernel, plan.subs, plan.rows, (len(g), len(b))),
         grid=(chans // CHANS,),
-        in_specs=[own_spec(value) for value in (*g, *b)],
+        in_specs=[own_spec(value) for value in g]
+        + [view_spec(plan, view) for view in b]
+        + [own_spec(value) for value in (own, *back)],
         out_specs=own_spec(out),
         out_shape=out,
         compiler_params=params(1),
         cost_estimate=cost(0.2),
         name="grad_a",
-    )(*g, *b)
+    )(*g, *arrays(b), own, *back)
 
 
 def middle_kernel(
@@ -340,7 +368,7 @@
         gwo_ref[...] += dot(x_norm, grad_lin, NT)
         gwg_ref[...] += dot(normed, gate_back, NT)
 
-    gather_out(s_ref, g_ref)
+    gather_out(s_ref, g_ref, rows)
 
 
 def make_middle(plan, table, before, ready, x, d, p, small):
@@ -417,13 +445,13 @@
         gw_ref[...] += dot(normed, grad_proj, NT)
 
 
-def make_last(plan, sub, before, ready, x, mask, grad_a, grad_b, gate_back, small):
+def make_last(plan, sub, before, x, mask, grad_a, grad_b, at, gate_back, small):
     chans = x.shape[-1]
     hidden = grad_a.shape[0]
     grad = jax.ShapeDtypeStruct((chans, 4 * hidden), F32)
     pairs = plan.pair_spec(chans, lambda j: (sub, j % 2, j // 2, 0, 0))
     channel = (hidden, plan.rows, plan.width)
-    kept = list(ready) if before is None else [before]
+    kept = [] if before is None else [before]
     return pl.pallas_call(
         functools.partial(last_kernel, plan.step),
         grid=(plan.blocks,),
@@ -431,7 +459,7 @@
             pairs,
             pl.BlockSpec((plan.rows, plan.width), lambda j: (sub, j)),
             pl.BlockSpec(channel, lambda j: (0, sub, j)),
-            pl.BlockSpec(channel, lambda j: (0, 0, j)),
+            pl.BlockSpec(channel, lambda j: (0, at, j)),
             pl.BlockSpec((plan.rows, chans, plan.width), lambda j: (sub, 0, j)),
         ]
         + [whole(value) for value in small]
@@ -481,8 +509,7 @@
 
     plan_cut = plan.cut
     two = plan.subs == 2
-    cut_a, cut_b = plan_cut(5, 3), plan_cut(4, 4)
-    back_a, back_b = plan_cut(3, 2, 3), plan_cut(2, 3, 3)
+    cut_b, back_a = plan_cut(4, 2, 2), plan_cut(4, 4)
     small = [gain, bias, w_t, w_cat]
 
     def middle(at, before, ready, product):
@@ -490,52 +517,52 @@
         g, kept, *local = make_middle(plan, table, before, ready, x, d, product, mid)
         return g, kept, jnp.concatenate(local[::-1], axis=1)
 
-    def summed(own, back):
-        return joined(
-            (own.astype(F32) + jnp.concatenate(back, axis=0).astype(F32)).astype(BF16)
-        )
-
-    def last(sub, before, ready, grad_b):
-        return make_last(plan, sub, before, ready, x, mask, grad_a, grad_b, kept, small)
-
-    factor_a, factor_b0 = make_factors(plan, 0, (), x, mask, gain, bias, w_t)
-    own_b = [owned(plan.swap(factor_b0))]
+    def product_of(b):
+        return plan.swap(joined(make_product(plan, own_a, b)))
+
+    held, factor_b0 = make_factors(plan, 0, (), x, mask, gain, bias, w_t)
+    own_b0 = owned(plan.swap(factor_b0))
     if two:
-        factor_a, factor_b1 = make_factors(plan, 1, (factor_a,), x, mask, gain, bias, w_t)
-    sent = plan.pieces(own_b[0], cut_a)
-    got_a = [plan.exchange(sent[0])]
-    own_a = owned(plan.swap(after(factor_a, own_b[0])))
-    got_a.append(plan.exchange(sent[1]))
-    got_b = []
+        (held,) = make_factors(plan, 1, (held,), x, mask, gain, bias, w_t)
+    other_0 = plan.exchange(own_b0)
+    own_ab = owned(plan.swap(after(held, own_b0)))
+    own_a, own_b, got_b = [(own_ab, 0)], [(own_b0, 0)], []
     if two:
-        own_b.append(owned(plan.swap(after(factor_b1, own_a, got_a[0]))))
-        sent = plan.pieces(own_b[1], cut_b)
-        got_b = [plan.exchange(piece) for piece in sent]
-    product = plan.swap(joined(make_product(plan, own_a, got_a + own_b)))
+        own_a, own_b = [(own_ab, 2), (own_ab, 0)], [(own_b0, 0), (own_ab, 1)]
+        sent = plan.pieces(own_ab[:, :, plan.rows : 2 * plan.rows], cut_b)
+        got_b = [plan.exchange(sent[0])]
+    b_first = [(other_0, 0)] + own_b
+    product = product_of(b_first)
+    if two:
+        got_b.append(plan.exchange(after(sent[1], product)))
+        got_b.append(plan.exchange(sent[2]))
     places = [(1 - side, 0)] + [(side, sub) for sub in every]
     grad, kept, local_mid = middle(places, (), got_b[:1], product)
     owner_g = [owned(plan.swap(after(grad, *got_b[1:2])))]
     parts = make_grad_b(plan, owner_g[0], own_a, back_a + [plan.half] * plan.subs)
     grad_b0, grad_b_own = parts[: len(back_a)], parts[len(back_a) :]
     back_0 = [plan.exchange(piece) for piece in grad_b0]
-    other_b, held = got_a + own_b, ()
     if two:
-        got_b[0] = after(got_b[0], grad_b0[0])
-        product = plan.swap(joined(make_product(plan, own_a, got_b)))
+        b_second = [(after(got_b[0], grad_b0[0]), 0)] + [(piece, 0) for piece in got_b[1:]]
+        product = product_of(b_second)
+        b_first = b_first + b_second
         grad, kept, local_1 = middle([(1 - side, 1)], (kept,), (), product)
         local_mid += local_1
-        owner_g.append(after(owned(plan.swap(after(grad, back_0[0]))), back_0[1]))
-        grad_b1 = make_grad_b(plan, owner_g[1], own_a, back_b)
-        back_1 = [plan.exchange(piece) for piece in grad_b1]
-        other_b, held = other_b + got_b, (grad_b1[0],)
-    grad_a = joined(make_grad_a(plan, owner_g, other_b))
-    grad_a = plan.swap(after(grad_a, *held))
-    held = (grad_a, back_1[0]) if two else (grad_a,)
-    grad_b = plan.swap(after(summed(grad_b_own[0], back_0), *held))
-    pair_grad, local_ab = last(0, None, (back_1[1],) if two else (grad_b,), grad_b)
+        owner_g.append(owned(plan.swap(after(grad, back_0[0]))))
+        (grad_b1,) = make_grad_b(plan, owner_g[1], own_a, [plan.half])
+        back_1 = plan.exchange(grad_b1)
+        back_0[1] = after(back_0[1], grad_b1)
+    grads = plan.swap(joined(make_grad_a(plan, owner_g, b_first, grad_b_own[0], back_0)))
+    pair_grad, local_ab = make_last(
+        plan, 0, None, x, mask, grads, grads, plan.subs, kept, small
+    )
     if two:
-        grad_b = plan.swap(after(summed(grad_b_own[1], back_1), local_ab))
-        pair_grad, local = last(1, pair_grad, (), grad_b)
+        grad_b = plan.swap(
+            joined((grad_b_own[1].astype(F32) + back_1.astype(F32)).astype(BF16))
+        )
+        pair_grad, local = make_last(
+            plan, 1, pair_grad, x, mask, grads, grad_b, 0, kept, small
+        )
         local_ab += local
     total = tile_sum(jnp.concatenate([local_ab, local_mid], axis=1), tiles) / crop
     wide = 4 * hidden

time: 679 us -> 647 us (0.953)
  blocking collectives: 66.7 us -> 23.8 us
  waiting for transfers between devices: 414 us -> 427 us
    all_to_all x9 -> x8, waiting for transfers between devices: 81.4 us -> 176 us  [swap(): lax.all_to_all(array, 'tile', split_axis=0, concat_axis=0, axis_index_gro...]
    ppermute x10 -> x7, waiting for transfers between devices: 332 us -> 251 us  [exchange(): return lax.ppermute(array, 'tile', self.partner)]
    all_to_all x1 -> x0, blocking collectives: 41.8 us -> none  [swap(): lax.all_to_all(array, 'tile', split_axis=0, concat_axis=0, axis_index_gro...]
    ppermute x10 -> x7, starting transfers between devices: 13.6 us -> 11 us  [exchange(): return lax.ppermute(array, 'tile', self.partner)]
    unnamed x104 -> x70, local copies, waits for them, and re-layouts: 18.1 us -> 19.3 us
    all_to_all x9 -> x8, starting transfers between devices: 39.1 us -> 38.6 us  [swap(): lax.all_to_all(array, 'tile', split_axis=0, concat_axis=0, axis_index_gro...]
  transfers between devices with their start and end apart: 19 -> 15, of which waited for: 16 -> 11; matrix products, arithmetic and copies ran while one was open for 2% -> 2% of each run, Pallas kernels for 6% -> 10%
where the time goes in v7:
time: 647 us; the launch traced here: 645 us
  waiting for transfers between devices  427 us (66%)
  Pallas kernels  111 us (17%)
  starting transfers between devices  49.6 us (8%)
  local copies, waits for them, and re-layouts  28 us (4%)
  blocking collectives  23.8 us (4%)
    ppermute x7, waiting for transfers between devices, exchange(): return lax.ppermute(array, 'tile', self.partner)  251 us
    all_to_all x8, waiting for transfers between devices, swap(): lax.all_to_all(array, 'tile', split_axis=0, concat_axis=0, axis_index_gro...  176 us
    all_to_all x8, starting transfers between devices, swap(): lax.all_to_all(array, 'tile', split_axis=0, concat_axis=0, axis_index_gro...  38.6 us
    pallas_call x2, Pallas kernels, make_last(): pl.pallas_call(functools.partial(last_kernel, plan.step), grid=(plan.bloc...  32.6 us
    pallas_call x2, Pallas kernels, make_middle(): pl.pallas_call(functools.partial(middle_kernel, plan.step), grid_spec=plt...  29.5 us
    all_to_all x2, blocking collectives, swap_all(): lax.all_to_all(array, 'tile', split_axis=0, concat_axis=0, tiled=True)  23.8 us
    unnamed x70, local copies, waits for them, and re-layouts  19.3 us
    pallas_call x2, Pallas kernels, make_factors(): pl.pallas_call(functools.partial(factors_kernel, plan.step, bool(before))...  17.2 us
  transfers between devices with their start and end apart: 15, of which 11 were waited for; matrix products, arithmetic and copies ran while one was open for 2% of the time, Pallas kernels for 10%

profile of v7, /device:TPU:0, one launch (start us, length us, event | category | flops | bytes accessed | tf_op | source)
XLA Modules:
  0.0 645.4 jit_solution(411080777326940549)
XLA Ops:
  3.1 1.0 copy.62
  4.2 8.6 %factors.2 = (bf16[128,48,512]{2,1,0:T(8,128)(2,1)}, bf16[128,16,512]{2,1,0:T(8,128)(2,1)S(1)}) custom-call(bf16[32,16,2,16,128]{4,3,2,1,0:T(8,128)(2,1)} %bitcast.55, f32[32,512]{1,0:T(8,128)S(1)} %broadcast_multiply_fusion.mask_ref, f32[128,1]{1,0:T(8,128)S(1)} %copy.65.gain_ref, f32[128,1]{1,0:T(8,128)S(1)} %copy.66.bias_ref, bf16[512,128]{1,0:T(8,128)(2,1)S(1)} %bitcast.43), custom_call_target="tpu_custom_call" | custom-call | flops 200000000 | bytes 600000 | tf_op jit(solution)/shard_map/factors/pallas_call | solution.py:201
  12.8 1.3 copy-done.7
  14.1 5.3 all-to-all-start
  19.4 8.5 %factors.3.refs_0_ = bf16[128,48,512]{2,1,0:T(8,128)(2,1)} custom-call(bf16[32,16,2,16,128]{4,3,2,1,0:T(8,128)(2,1)} %bitcast.56, f32[32,512]{1,0:T(8,128)S(1)} %broadcast_multiply_fusion.mask_ref, f32[128,1]{1,0:T(8,128)S(1)} %copy.65.gain_ref, f32[128,1]{1,0:T(8,128)S(1)} %copy.66.bias_ref, ...), custom_call_target="tpu_custom_call", output_to_operand_aliasing={{}: (5, {})} | custom-call | flops 200000000 | bytes 600000 | tf_op jit(solution)/shard_map/factors/pallas_call | solution.py:201
  27.9 17.2 %all-to-all-done = bf16[128,16,512]{2,1,0:T(8,128)(2,1)S(1)} async-done(((bf16[128,16,512]{2,1,0:T(8,128)(2,1)}), bf16[128,16,512]{2,1,0:T(8,128)(2,1)S(1)}, u32[]{:S(2)}, u32[]{:S(2)}) %all-to-all-start) | async-done | bytes 2097184 | tf_op jit(solution)/shard_map/all_to_all | solution.py:128
  45.1 4.8 all-to-all-start.1
  49.9 2.7 collective-permute-start
  52.6 110.7 %collective-permute-done.refs_2_ = bf16[8,16,16,512]{3,2,1,0:T(8,128)(2,1)S(1)} collective-permute-done((bf16[8,16,16,512]{3,2,1,0:T(8,128)(2,1)S(1)}, bf16[8,16,16,512]{3,2,1,0:T(8,128)(2,1)S(1)}, u32[]{:S(2)}, u32[]{:S(2)}) %collective-permute-start) | collective-permute-done | bytes 2097184 | tf_op jit(solution)/shard_map/ppermute | solution.py:140
  163.3 1.3 copy-done.4
  164.6 0.9 all-to-all-done.1
  165.5 1.6 copy-done.5
  167.1 6.7 %product.2 = bf16[8,16,32,384]{3,2,1,0:T(8,128)(2,1)} custom-call(bf16[8,16,48,512]{3,2,1,0:T(8,128)(2,1)} %bitcast.12.refs_0_.refs_1_.refs_4_, bf16[8,16,48,512]{3,2,1,0:T(8,128)(2,1)} %bitcast.12.refs_0_.refs_1_.refs_4_, bf16[8,16,16,512]{3,2,1,0:T(8,128)(2,1)S(1)} %copy-done.5, bf16[8,16,16,512]{3,2,1,0:T(8,128)(2,1)} %bitcast.39, ...), custom_call_target="tpu_custom_call" | custom-call | flops 200000000 | bytes 600000 | tf_op jit(solution)/shard_map/product/pallas_call | solution.py:268
  173.8 6.0 all-to-all-start.2
  179.8 2.4 slice.28
  182.4 2.3 fusion.6
  184.7 54.5 %all-to-all-done.2.p_ref.refs_1_ = bf16[128,32,384]{2,1,0:T(8,128)(2,1)S(1)} async-done(((bf16[128,32,384]{2,1,0:T(8,128)(2,1)}), bf16[128,32,384]{2,1,0:T(8,128)(2,1)S(1)}, u32[]{:S(2)}, u32[]{:S(2)}) %all-to-all-start.2) | async-done | bytes 3145760 | tf_op jit(solution)/shard_map/all_to_all | solution.py:128
  239.2 0.9 copy.67
  245.0 20.9 %middle.2 = (bf16[128,32,384]{2,1,0:T(8,128)(2,1)}, bf16[32,128,512]{2,1,0:T(8,128)(2,1)}, f32[128,128]{1,0:T(8,128)S(1)}, f32[128,128]{1,0:T(8,128)S(1)}) custom-call(s32[3,2]{1,0:T(4,128)S(1)} %pad_add_fusion._, bf16[32,16,2,16,128]{4,3,2,1,0:T(8,128)(2,1)} %bitcast.57, bf16[32,16,2,16,128]{4,3,2,1,0:T(8,128)(2,1)} %bitcast.62, ...), custom_call_target="tpu_custom_call" | custom-call | flops 200000000 | bytes 600000 | tf_op jit(solution)/shard_map/middle/pallas_call | solution.py:382
  267.2 1.9 copy-done.2
  269.1 1.7 copy-done.3
  270.8 4.6 all-to-all-start.3
  275.4 2.8 collective-permute-start.3
  278.1 45.4 %all-to-all-done.3 = bf16[128,32,384]{2,1,0:T(8,128)(2,1)} async-done(((bf16[128,32,384]{2,1,0:T(8,128)(2,1)}), bf16[128,32,384]{2,1,0:T(8,128)(2,1)}, u32[]{:S(2)}, u32[]{:S(2)}) %all-to-all-start.3) | async-done | bytes 3145760 | tf_op jit(solution)/shard_map/all_to_all | solution.py:128
  323.6 6.8 %grad_b.2 = (bf16[4,16,16,512]{3,2,1,0:T(8,128)(2,1)S(1)}, bf16[4,16,16,512]{3,2,1,0:T(8,128)(2,1)}, bf16[8,16,16,512]{3,2,1,0:T(8,128)(2,1)}, bf16[8,16,16,512]{3,2,1,0:T(8,128)(2,1)}) custom-call(bf16[8,16,32,384]{3,2,1,0:T(8,128)(2,1)} %bitcast.18.g_ref.refs_0_, bf16[8,16,48,512]{3,2,1,0:T(8,128)(2,1)} %bitcast.12.refs_0_.refs_1_.refs_4_, ...), custom_call_target="tpu_custom_call" | custom-call | flops 200000000 | bytes 600000 | tf_op jit(solution)/shard_map/grad_b/pallas_call | solution.py:295
  330.4 5.3 product.3
  335.7 3.7 all-to-all-start.4
  339.4 1.7 collective-permute-start.4
  341.2 24.4 %all-to-all-done.4.p_ref = bf16[128,32,128]{2,1,0:T(8,128)(2,1)S(1)} async-done(((bf16[128,32,128]{2,1,0:T(8,128)(2,1)}), bf16[128,32,128]{2,1,0:T(8,128)(2,1)S(1)}, u32[]{:S(2)}, u32[]{:S(2)}) %all-to-all-start.4) | async-done | bytes 1048608 | tf_op jit(solution)/shard_map/all_to_all | solution.py:128
  365.5 0.8 copy-done.11
  368.6 8.6 %middle.3 = (bf16[128,32,128]{2,1,0:T(8,128)(2,1)}, bf16[32,128,512]{2,1,0:T(8,128)(2,1)}, f32[128,128]{1,0:T(8,128)S(1)}, f32[128,128]{1,0:T(8,128)S(1)}) custom-call(s32[1,2]{1,0:T(1,128)S(1)} %fusion.3._, bf16[32,16,2,16,128]{4,3,2,1,0:T(8,128)(2,1)} %bitcast.58, bf16[32,16,2,16,128]{4,3,2,1,0:T(8,128)(2,1)} %bitcast.63, ...), custom_call_target="tpu_custom_call", output_to_operand_aliasing={{1}: (11, {})} | custom-call | flops 200000000 | bytes 600000 | tf_op jit(solution)/shard_map/middle/pallas_call | solution.py:382
  378.5 9.6 %collective-permute-done.4.refs_1_.refs_9_ = bf16[4,16,16,512]{3,2,1,0:T(8,128)(2,1)S(1)} collective-permute-done((bf16[4,16,16,512]{3,2,1,0:T(8,128)(2,1)S(1)}, bf16[4,16,16,512]{3,2,1,0:T(8,128)(2,1)S(1)}, u32[]{:S(2)}, u32[]{:S(2)}) %collective-permute-start.4) | collective-permute-done | bytes 1048608 | tf_op jit(solution)/shard_map/ppermute | solution.py:140
  388.1 3.6 all-to-all-start.5
  391.7 2.2 collective-permute-start.5
  393.9 24.2 %all-to-all-done.5 = bf16[128,32,128]{2,1,0:T(8,128)(2,1)S(1)} async-done(((bf16[128,32,128]{2,1,0:T(8,128)(2,1)}), bf16[128,32,128]{2,1,0:T(8,128)(2,1)S(1)}, u32[]{:S(2)}, u32[]{:S(2)}) %all-to-all-start.5) | async-done | bytes 1048608 | tf_op jit(solution)/shard_map/all_to_all | solution.py:128
  418.2 3.6 grad_b.3.refs_1_
  421.8 19.1 %collective-permute-done.5.refs_0_ = bf16[4,16,16,512]{3,2,1,0:T(8,128)(2,1)} collective-permute-done((bf16[4,16,16,512]{3,2,1,0:T(8,128)(2,1)}, bf16[4,16,16,512]{3,2,1,0:T(8,128)(2,1)}, u32[]{:S(2)}, u32[]{:S(2)}) %collective-permute-start.5) | collective-permute-done | bytes 1048608 | tf_op jit(solution)/shard_map/ppermute | solution.py:140
  440.9 9.2 %grad_a.1 = bf16[8,16,48,512]{3,2,1,0:T(8,128)(2,1)} custom-call(bf16[8,16,32,384]{3,2,1,0:T(8,128)(2,1)} %bitcast.18.g_ref.refs_0_, bf16[8,16,32,128]{3,2,1,0:T(8,128)(2,1)S(1)} %bitcast.42, bf16[8,16,16,512]{3,2,1,0:T(8,128)(2,1)} %copy-done.4, bf16[8,16,16,512]{3,2,1,0:T(8,128)(2,1)} %bitcast.40, ...), custom_call_target="tpu_custom_call" | custom-call | flops 200000000 | bytes 600000 | tf_op jit(solution)/shard_map/grad_a/pallas_call | solution.py:324
  450.1 4.8 all-to-all-start.6
  454.9 1.4 collective-permute-start.6
  456.3 112.0 %collective-permute-done.6 = bf16[8,16,16,512]{3,2,1,0:T(8,128)(2,1)S(1)} collective-permute-done((bf16[8,16,16,512]{3,2,1,0:T(8,128)(2,1)S(1)}, bf16[8,16,16,512]{3,2,1,0:T(8,128)(2,1)S(1)}, u32[]{:S(2)}, u32[]{:S(2)}) %collective-permute-start.6) | collective-permute-done | bytes 2097184 | tf_op jit(solution)/shard_map/ppermute | solution.py:140
  568.3 3.9 add_convert_fusion
  572.2 5.9 all-to-all-start.7
  578.2 16.3 %last.2 = (bf16[32,16,2,16,128]{4,3,2,1,0:T(8,128)(2,1)}, f32[128,512]{1,0:T(8,128)S(1)}) custom-call(bf16[32,16,2,16,128]{4,3,2,1,0:T(8,128)(2,1)} %bitcast.59, f32[32,512]{1,0:T(8,128)S(1)} %broadcast_multiply_fusion.mask_ref, bf16[128,48,512]{2,1,0:T(8,128)(2,1)} %all-to-all-done.6.ga_ref.gb_ref, bf16[128,48,512]{2,1,0:T(8,128)(2,1)} %all-to-all-done.6.ga_ref.gb_ref, ...), custom_call_target="tpu_custom_call" | custom-call | flops 200000000 | bytes 600000 | tf_op jit(solution)/shard_map/last/pallas_call | solution.py:455
  594.5 9.3 %all-to-all-done.7.gb_ref = bf16[128,16,512]{2,1,0:T(8,128)(2,1)S(1)} async-done(((bf16[128,16,512]{2,1,0:T(8,128)(2,1)}), bf16[128,16,512]{2,1,0:T(8,128)(2,1)S(1)}, u32[]{:S(2)}, u32[]{:S(2)}) %all-to-all-start.7) | async-done | bytes 2097184 | tf_op jit(solution)/shard_map/all_to_all | solution.py:128
  603.8 16.3 %last.3 = (bf16[32,16,2,16,128]{4,3,2,1,0:T(8,128)(2,1)}, f32[128,512]{1,0:T(8,128)S(1)}) custom-call(bf16[32,16,2,16,128]{4,3,2,1,0:T(8,128)(2,1)} %bitcast.60, f32[32,512]{1,0:T(8,128)S(1)} %broadcast_multiply_fusion.mask_ref, bf16[128,48,512]{2,1,0:T(8,128)(2,1)} %all-to-all-done.6.ga_ref.gb_ref, ...), custom_call_target="tpu_custom_call", output_to_operand_aliasing={{0}: (9, {})} | custom-call | flops 200000000 | bytes 600000 | tf_op jit(solution)/shard_map/last/pallas_call | solution.py:455
  620.1 12.2 %all_to_all.52 = bf16[16,8,768]{2,1,0:T(8,128)(2,1)S(1)} all-to-all(bf16[16,8,768]{2,1,0:T(8,128)(2,1)S(1)} %pad_maximum_fusion), channel_id=1, replica_groups=mesh['crops'=2,'tile'=16] {'tile'}, dimensions={0} | all-to-all | bytes 393216 | tf_op jit(solution)/shard_map/all_to_all | solution.py:478
  632.4 11.6 %all_to_all.53 = bf16[16,8,768]{2,1,0:T(8,128)(2,1)S(1)} all-to-all(bf16[16,8,768]{2,1,0:T(8,128)(2,1)S(1)} %broadcast_in_dim.23), channel_id=1, replica_groups=mesh['crops'=2,'tile'=16] {'tile'}, dimensions={0} | all-to-all | bytes 393216 | tf_op jit(solution)/shard_map/all_to_all | solution.py:478
  (97 shorter events, 14.2 us)
Async XLA Ops:
  12.8 1.3 copy-start.7
  14.1 31.0 %all-to-all-start = ((bf16[128,16,512]{2,1,0:T(8,128)(2,1)}), bf16[128,16,512]{2,1,0:T(8,128)(2,1)S(1)}, u32[]{:S(2)}, u32[]{:S(2)}) async-start(bf16[128,16,512]{2,1,0:T(8,128)(2,1)} %copy-done.7), calls=%async_computation | async-start | bytes 4194304 | tf_op jit(solution)/shard_map/all_to_all | solution.py:128
  45.1 4.8 copy-start
  45.1 120.4 %all-to-all-start.1 = ((bf16[128,48,512]{2,1,0:T(8,128)(2,1)}), bf16[128,48,512]{2,1,0:T(8,128)(2,1)}, u32[]{:S(2)}, u32[]{:S(2)}) async-start(bf16[128,48,512]{2,1,0:T(8,128)(2,1)} %after.6), calls=%async_computation.1 | async-start | bytes 12582912 | tf_op jit(solution)/shard_map/all_to_all | solution.py:128
  49.9 113.4 %collective-permute-start = (bf16[8,16,16,512]{3,2,1,0:T(8,128)(2,1)S(1)}, bf16[8,16,16,512]{3,2,1,0:T(8,128)(2,1)S(1)}, u32[]{:S(2)}, u32[]{:S(2)}) collective-permute-start(bf16[8,16,16,512]{3,2,1,0:T(8,128)(2,1)S(1)} %bitcast.38), channel_id=1, source_target_pairs={{0,8},{1,9},{2,10},{3,11},{4,12},{5,13},{6,14},{7,15},{8,0},{9,1},... | collective-permute-start | bytes 6291464 | tf_op jit(solution)/shard_map/ppermute | solution.py:140
  163.3 1.3 copy-start.4
  165.5 1.6 copy-start.5
  173.8 65.4 %all-to-all-start.2 = ((bf16[128,32,384]{2,1,0:T(8,128)(2,1)}), bf16[128,32,384]{2,1,0:T(8,128)(2,1)S(1)}, u32[]{:S(2)}, u32[]{:S(2)}) async-start(bf16[128,32,384]{2,1,0:T(8,128)(2,1)} %bitcast.64), calls=%async_computation.2 | async-start | bytes 6291456 | tf_op jit(solution)/shard_map/all_to_all | solution.py:128
  182.2 57.0 %copy-start.29 = (bf16[128,128]{1,0:T(8,128)(2,1)S(1)}, bf16[128,128]{1,0:T(8,128)(2,1)}, u32[]{:S(2)}) copy-start(bf16[128,128]{1,0:T(8,128)(2,1)} %param.16) | copy-start | bytes 98308
  182.2 57.9 %copy-start.12 = (bf16[128,128]{1,0:T(8,128)(2,1)S(1)}, bf16[128,128]{1,0:T(8,128)(2,1)}, u32[]{:S(2)}) copy-start(bf16[128,128]{1,0:T(8,128)(2,1)} %wo_ref.3) | copy-start | bytes 98308
  182.2 58.7 %copy-start.31 = (f32[128]{0:T(128)S(1)}, f32[128]{0:T(128)}, u32[]{:S(2)}) copy-start(f32[128]{0:T(128)} %param.17) | copy-start | bytes 1540
  182.2 58.8 %copy-start.32 = (f32[128]{0:T(128)S(1)}, f32[128]{0:T(128)}, u32[]{:S(2)}) copy-start(f32[128]{0:T(128)} %param.18) | copy-start | bytes 1540
  182.2 59.7 %collective-permute-start.1 = (bf16[4,16,16,512]{3,2,1,0:T(8,128)(2,1)}, bf16[4,16,16,512]{3,2,1,0:T(8,128)(2,1)}, u32[]{:S(2)}, u32[]{:S(2)}) collective-permute-start(bf16[4,16,16,512]{3,2,1,0:T(8,128)(2,1)} %slice.28), channel_id=1, source_target_pairs={{0,8},{1,9},{2,10},{3,11},{4,12},{5,13},{6,14},{7,15},{8,0},{9,1},... | collective-permute-start | bytes 3145736 | tf_op jit(solution)/shard_map/ppermute | solution.py:140
  239.2 2.7 copy-start.1
  239.2 28.0 %collective-permute-start.2 = (bf16[2,16,16,512]{3,2,1,0:T(8,128)(2,1)}, bf16[2,16,16,512]{3,2,1,0:T(8,128)(2,1)}, u32[]{:S(2)}, u32[]{:S(2)}) collective-permute-start(bf16[2,16,16,512]{3,2,1,0:T(8,128)(2,1)} %after.7), channel_id=1, source_target_pairs={{0,8},{1,9},{2,10},{3,11},{4,12},{5,13},{6,14},{7,15},{8,0},{9,1},... | collective-permute-start | bytes 1572872 | tf_op jit(solution)/shard_map/ppermute | solution.py:140
  241.9 0.8 copy-start.10
  242.8 0.8 copy-start.13
  243.5 0.8 copy-start.15
  244.3 0.8 copy-start.17
  266.0 0.6 copy-start.19
  266.6 0.6 copy-start.21
  267.2 1.9 copy-start.2
  269.1 1.7 copy-start.3
  270.8 4.6 copy-start.28
  270.8 52.8 %all-to-all-start.3 = ((bf16[128,32,384]{2,1,0:T(8,128)(2,1)}), bf16[128,32,384]{2,1,0:T(8,128)(2,1)}, u32[]{:S(2)}, u32[]{:S(2)}) async-start(bf16[128,32,384]{2,1,0:T(8,128)(2,1)} %copy-done.3), calls=%async_computation.3 | async-start | bytes 6291456 | tf_op jit(solution)/shard_map/all_to_all | solution.py:128
  275.4 55.0 %collective-permute-start.3 = (bf16[2,16,16,512]{3,2,1,0:T(8,128)(2,1)S(1)}, bf16[2,16,16,512]{3,2,1,0:T(8,128)(2,1)S(1)}, u32[]{:S(2)}, u32[]{:S(2)}) collective-permute-start(bf16[2,16,16,512]{3,2,1,0:T(8,128)(2,1)S(1)} %copy-done.28), channel_id=1, source_target_pairs={{0,8},{1,9},{2,10},{3,11},{4,12},{5,13},{6,14},{7,15},{8,0},{9,1},... | collective-permute-start | bytes 1572872 | tf_op jit(solution)/shard_map/ppermute | solution.py:140
  330.4 5.3 copy-start.8
  335.7 29.9 %all-to-all-start.4 = ((bf16[128,32,128]{2,1,0:T(8,128)(2,1)}), bf16[128,32,128]{2,1,0:T(8,128)(2,1)S(1)}, u32[]{:S(2)}, u32[]{:S(2)}) async-start(bf16[128,32,128]{2,1,0:T(8,128)(2,1)} %bitcast.20), calls=%async_computation.4 | async-start | bytes 2097152 | tf_op jit(solution)/shard_map/all_to_all | solution.py:128
  339.4 48.7 %collective-permute-start.4 = (bf16[4,16,16,512]{3,2,1,0:T(8,128)(2,1)S(1)}, bf16[4,16,16,512]{3,2,1,0:T(8,128)(2,1)S(1)}, u32[]{:S(2)}, u32[]{:S(2)}) collective-permute-start(bf16[4,16,16,512]{3,2,1,0:T(8,128)(2,1)S(1)} %get-tuple-element.25.refs_1_), channel_id=1, source_target_pairs={{0,8},{1,9},{2,10},{3,11},{4,12},{5,13},{6,14},{7,15},{8,0},{9,1},... | collective-permute-start | bytes 3145736 | tf_op jit(solution)/shard_map/ppermute | solution.py:140
  365.5 0.8 copy-start.11
  366.4 0.8 copy-start.14
  367.1 0.8 copy-start.16
  367.9 0.8 copy-start.18
  377.2 0.6 copy-start.23
  377.8 0.6 copy-start.25
  388.1 30.0 %copy-start.6 = (bf16[4,16,16,512]{3,2,1,0:T(8,128)(2,1)}, bf16[4,16,16,512]{3,2,1,0:T(8,128)(2,1)S(1)}, u32[]{:S(2)}) copy-start(bf16[4,16,16,512]{3,2,1,0:T(8,128)(2,1)S(1)} %collective-permute-done.4.refs_1_.refs_9_) | copy-start | bytes 3145732
  388.1 30.0 %all-to-all-start.5 = ((bf16[128,32,128]{2,1,0:T(8,128)(2,1)}), bf16[128,32,128]{2,1,0:T(8,128)(2,1)S(1)}, u32[]{:S(2)}, u32[]{:S(2)}) async-start(bf16[128,32,128]{2,1,0:T(8,128)(2,1)} %after.10), calls=%async_computation.5 | async-start | bytes 2097152 | tf_op jit(solution)/shard_map/all_to_all | solution.py:128
  391.7 49.2 %collective-permute-start.5 = (bf16[4,16,16,512]{3,2,1,0:T(8,128)(2,1)}, bf16[4,16,16,512]{3,2,1,0:T(8,128)(2,1)}, u32[]{:S(2)}, u32[]{:S(2)}) collective-permute-start(bf16[4,16,16,512]{3,2,1,0:T(8,128)(2,1)} %get-tuple-element.29), channel_id=1, source_target_pairs={{0,8},{1,9},{2,10},{3,11},{4,12},{5,13},{6,14},{7,15},{8,0},{9,1},... | collective-permute-start | bytes 3145736 | tf_op jit(solution)/shard_map/ppermute | solution.py:140
  421.8 19.1 %copy-start.9 = (bf16[2,16,16,512]{3,2,1,0:T(8,128)(2,1)S(1)}, bf16[2,16,16,512]{3,2,1,0:T(8,128)(2,1)}, u32[]{:S(2)}) copy-start(bf16[2,16,16,512]{3,2,1,0:T(8,128)(2,1)} %copy-done.8) | copy-start | bytes 1572868
  450.1 122.1 %all-to-all-start.6 = ((bf16[128,48,512]{2,1,0:T(8,128)(2,1)}), bf16[128,48,512]{2,1,0:T(8,128)(2,1)}, u32[]{:S(2)}, u32[]{:S(2)}) async-start(bf16[128,48,512]{2,1,0:T(8,128)(2,1)} %bitcast.61), calls=%async_computation.6 | async-start | bytes 12582912 | tf_op jit(solution)/shard_map/all_to_all | solution.py:128
  454.9 113.4 %collective-permute-start.6 = (bf16[8,16,16,512]{3,2,1,0:T(8,128)(2,1)S(1)}, bf16[8,16,16,512]{3,2,1,0:T(8,128)(2,1)S(1)}, u32[]{:S(2)}, u32[]{:S(2)}) collective-permute-start(bf16[8,16,16,512]{3,2,1,0:T(8,128)(2,1)S(1)} %grad_b.3.refs_1_), channel_id=1, source_target_pairs={{0,8},{1,9},{2,10},{3,11},{4,12},{5,13},{6,14},{7,15},{8,0},{9,1},... | collective-permute-start | bytes 6291464 | tf_op jit(solution)/shard_map/ppermute | solution.py:140
  572.2 5.9 copy-start.27
  572.2 6.0 copy-start.30
  572.2 6.0 copy-start.20
  572.2 6.0 copy-start.22
  572.2 6.0 copy-start.24
  572.2 6.0 copy-start.26
  572.2 31.6 %all-to-all-start.7 = ((bf16[128,16,512]{2,1,0:T(8,128)(2,1)}), bf16[128,16,512]{2,1,0:T(8,128)(2,1)S(1)}, u32[]{:S(2)}, u32[]{:S(2)}) async-start(bf16[128,16,512]{2,1,0:T(8,128)(2,1)} %bitcast.65), calls=%async_computation.7 | async-start | bytes 4194304 | tf_op jit(solution)/shard_map/all_to_all | solution.py:128

commit v8 on v7

--- a/solution.py
+++ b/solution.py
@@ -371,24 +371,24 @@
     gather_out(s_ref, g_ref, rows)
 
 
-def make_middle(plan, table, before, ready, x, d, p, small):
+def make_middle(plan, table, first, before, ready, x, d, p, small):
     chans = x.shape[-1]
     hidden = p.shape[0]
     cut = table.shape[0]
     grads = [jax.ShapeDtypeStruct((hidden, chans), F32), jax.ShapeDtypeStruct((chans, chans), F32)]
     pairs = plan.pair_spec(chans, lambda i, j, at: (i, at[j, 0], at[j, 1], 0, 0))
-    channel = pl.BlockSpec((hidden, plan.rows, plan.width), lambda i, j, at: (0, i, j))
+    channel = (hidden, plan.rows, plan.width)
     kept = [*before, *ready]
     return pl.pallas_call(
         functools.partial(middle_kernel, plan.step),
         grid_spec=pltpu.PrefetchScalarGridSpec(
             num_scalar_prefetch=1,
             grid=(plan.subs, cut),
-            in_specs=[pairs, pairs, channel]
+            in_specs=[pairs, pairs, pl.BlockSpec(channel, lambda i, j, at: (0, i, first + j))]
             + [whole(value) for value in small]
             + [HELD for _ in kept],
             out_specs=[
-                channel,
+                pl.BlockSpec(channel, lambda i, j, at: (0, i, j)),
                 pl.BlockSpec(
                     (plan.rows, chans, plan.width),
                     lambda i, j, at: (i, 0, at[j, 1] * 2 + at[j, 0]),
@@ -398,7 +398,7 @@
             scratch_shapes=[plan.scratch(hidden)],
         ),
         out_shape=[
-            jax.ShapeDtypeStruct(p.shape, BF16),
+            jax.ShapeDtypeStruct((hidden, plan.count, cut * plan.width), BF16),
             jax.ShapeDtypeStruct((plan.count, chans, plan.crop), BF16),
         ]
         + grads,
@@ -509,12 +509,12 @@
 
     plan_cut = plan.cut
     two = plan.subs == 2
-    cut_b, back_a = plan_cut(4, 2, 2), plan_cut(4, 4)
+    cut_b, back_a = plan_cut(4, 2, 2), plan_cut(3, 3, 2)
     small = [gain, bias, w_t, w_cat]
 
-    def middle(at, before, ready, product):
+    def middle(at, first, before, ready, product):
         table = jnp.stack([jnp.stack([half, jnp.int32(sub)]) for half, sub in at])
-        g, kept, *local = make_middle(plan, table, before, ready, x, d, product, mid)
+        g, kept, *local = make_middle(plan, table, first, before, ready, x, d, product, mid)
         return g, kept, jnp.concatenate(local[::-1], axis=1)
 
     def product_of(b):
@@ -536,22 +536,26 @@
     if two:
         got_b.append(plan.exchange(after(sent[1], product)))
         got_b.append(plan.exchange(sent[2]))
-    places = [(1 - side, 0)] + [(side, sub) for sub in every]
-    grad, kept, local_mid = middle(places, (), got_b[:1], product)
-    owner_g = [owned(plan.swap(after(grad, *got_b[1:2])))]
-    parts = make_grad_b(plan, owner_g[0], own_a, back_a + [plan.half] * plan.subs)
-    grad_b0, grad_b_own = parts[: len(back_a)], parts[len(back_a) :]
+    grad, kept, local_mid = middle([(1 - side, 0)], 0, (), got_b[:1], product)
+    owner_g = [owned(plan.swap(grad))]
+    grad, kept, local = middle([(side, sub) for sub in every], 1, (kept,), (), product)
+    local_mid += local
+    grad_b0 = make_grad_b(plan, owner_g[0], own_a, back_a)
     back_0 = [plan.exchange(piece) for piece in grad_b0]
+    waits = (owner_g[0], grad_b0[0], *got_b[1:2])
+    owner_g.append(owned(plan.swap(after(grad, *waits))))
+    grad_b_own = make_grad_b(plan, owner_g[1], own_a, [plan.half] * plan.subs)
     if two:
-        b_second = [(after(got_b[0], grad_b0[0]), 0)] + [(piece, 0) for piece in got_b[1:]]
-        product = product_of(b_second)
+        b_second = [(piece, 0) for piece in got_b]
         b_first = b_first + b_second
-        grad, kept, local_1 = middle([(1 - side, 1)], (kept,), (), product)
-        local_mid += local_1
-        owner_g.append(owned(plan.swap(after(grad, back_0[0]))))
-        (grad_b1,) = make_grad_b(plan, owner_g[1], own_a, [plan.half])
+        product = joined(make_product(plan, own_a, b_second))
+        product = plan.swap(after(product, owner_g[1], back_0[0]))
+        grad, kept, local = middle([(1 - side, 1)], 0, (kept,), grad_b_own[:1], product)
+        local_mid += local
+        owner_g.append(owned(plan.swap(after(grad, back_0[1]))))
+        (grad_b1,) = make_grad_b(plan, owner_g[2], own_a, [plan.half])
         back_1 = plan.exchange(grad_b1)
-        back_0[1] = after(back_0[1], grad_b1)
+        back_0[2] = after(back_0[2], grad_b1)
     grads = plan.swap(joined(make_grad_a(plan, owner_g, b_first, grad_b_own[0], back_0)))
     pair_grad, local_ab = make_last(
         plan, 0, None, x, mask, grads, grads, plan.subs, kept, small

time: 647 us -> 643 us (level)
  waiting for transfers between devices: 427 us -> 406 us
  local copies, waits for them, and re-layouts: 28 us -> 35.1 us
    all_to_all x8 -> x9, waiting for transfers between devices: 176 us -> 72.2 us  [swap(): lax.all_to_all(array, 'tile', split_axis=0, concat_axis=0, axis_index_gro...]
    ppermute x7 -> x8, waiting for transfers between devices: 251 us -> 334 us  [exchange(): return lax.ppermute(array, 'tile', self.partner)]
    unnamed x70 -> x106, local copies, waits for them, and re-layouts: 19.3 us -> 26.4 us
    pallas_call x2 -> x3, Pallas kernels: 10.4 us -> 14.2 us  [make_grad_b(): pl.pallas_call(functools.partial(grad_b_kernel, plan.subs), grid=(g.shape...]
    pallas_call x2 -> x3, Pallas kernels: 29.5 us -> 32.1 us  [make_middle(): pl.pallas_call(functools.partial(middle_kernel, plan.step), grid_spec=plt...]
    all_to_all x8 -> x9, starting transfers between devices: 38.6 us -> 40.3 us  [swap(): lax.all_to_all(array, 'tile', split_axis=0, concat_axis=0, axis_index_gro...]
  transfers between devices with their start and end apart: 15 -> 17, of which waited for: 11 -> 12; matrix products, arithmetic and copies ran while one was open for 2% -> 2% of each run, Pallas kernels for 10% -> 11%
where the time goes in v8:
time: 643 us; the launch traced here: 641 us
  waiting for transfers between devices  406 us (63%)
  Pallas kernels  117 us (18%)
  starting transfers between devices  50.2 us (8%)
  local copies, waits for them, and re-layouts  35.1 us (5%)
  blocking collectives  26.1 us (4%)
    ppermute x8, waiting for transfers between devices, exchange(): return lax.ppermute(array, 'tile', self.partner)  334 us
    all_to_all x9, waiting for transfers between devices, swap(): lax.all_to_all(array, 'tile', split_axis=0, concat_axis=0, axis_index_gro...  72.2 us
    all_to_all x9, starting transfers between devices, swap(): lax.all_to_all(array, 'tile', split_axis=0, concat_axis=0, axis_index_gro...  40.3 us
    pallas_call x2, Pallas kernels, make_last(): pl.pallas_call(functools.partial(last_kernel, plan.step), grid=(plan.bloc...  32.5 us
    pallas_call x3, Pallas kernels, make_middle(): pl.pallas_call(functools.partial(middle_kernel, plan.step), grid_spec=plt...  32.1 us
    unnamed x106, local copies, waits for them, and re-layouts  26.4 us
    all_to_all x2, blocking collectives, swap_all(): lax.all_to_all(array, 'tile', split_axis=0, concat_axis=0, tiled=True)  26.1 us
    pallas_call x2, Pallas kernels, make_factors(): pl.pallas_call(functools.partial(factors_kernel, plan.step, bool(before))...  17.2 us
  transfers between devices with their start and end apart: 17, of which 12 were waited for; matrix products, arithmetic and copies ran while one was open for 2% of the time, Pallas kernels for 11%

profile of v8, /device:TPU:0, one launch (start us, length us, event | category | flops | bytes accessed | tf_op | source)
XLA Modules:
  0.0 640.7 jit_solution(2104087162445759854)
XLA Ops:
  4.2 8.6 %factors.2 = (bf16[128,48,512]{2,1,0:T(8,128)(2,1)}, bf16[128,16,512]{2,1,0:T(8,128)(2,1)S(1)}) custom-call(bf16[32,16,2,16,128]{4,3,2,1,0:T(8,128)(2,1)} %bitcast.65, f32[32,512]{1,0:T(8,128)S(1)} %broadcast_multiply_fusion.mask_ref, f32[128,1]{1,0:T(8,128)S(1)} %copy.74.gain_ref, f32[128,1]{1,0:T(8,128)S(1)} %copy.75.bias_ref, bf16[512,128]{1,0:T(8,128)(2,1)S(1)} %bitcast.49), custom_call_target="tpu_custom_call" | custom-call | flops 200000000 | bytes 600000 | tf_op jit(solution)/shard_map/factors/pallas_call | solution.py:201
  12.8 1.3 copy-done.14
  14.1 5.3 all-to-all-start
  19.4 8.6 %factors.3.refs_0_ = bf16[128,48,512]{2,1,0:T(8,128)(2,1)} custom-call(bf16[32,16,2,16,128]{4,3,2,1,0:T(8,128)(2,1)} %bitcast.66, f32[32,512]{1,0:T(8,128)S(1)} %broadcast_multiply_fusion.mask_ref, f32[128,1]{1,0:T(8,128)S(1)} %copy.74.gain_ref, f32[128,1]{1,0:T(8,128)S(1)} %copy.75.bias_ref, ...), custom_call_target="tpu_custom_call", output_to_operand_aliasing={{}: (5, {})} | custom-call | flops 200000000 | bytes 600000 | tf_op jit(solution)/shard_map/factors/pallas_call | solution.py:201
  27.9 17.1 %all-to-all-done = bf16[128,16,512]{2,1,0:T(8,128)(2,1)S(1)} async-done(((bf16[128,16,512]{2,1,0:T(8,128)(2,1)}), bf16[128,16,512]{2,1,0:T(8,128)(2,1)S(1)}, u32[]{:S(2)}, u32[]{:S(2)}) %all-to-all-start) | async-done | bytes 2097184 | tf_op jit(solution)/shard_map/all_to_all | solution.py:128
  45.1 4.8 all-to-all-start.1
  49.9 2.7 collective-permute-start
  52.5 110.7 %collective-permute-done.refs_2_.refs_3_ = bf16[8,16,16,512]{3,2,1,0:T(8,128)(2,1)S(1)} collective-permute-done((bf16[8,16,16,512]{3,2,1,0:T(8,128)(2,1)S(1)}, bf16[8,16,16,512]{3,2,1,0:T(8,128)(2,1)S(1)}, u32[]{:S(2)}, u32[]{:S(2)}) %collective-permute-start) | collective-permute-done | bytes 2097184 | tf_op jit(solution)/shard_map/ppermute | solution.py:140
  163.3 1.4 copy-done.6
  165.5 1.6 copy-done.7
  167.0 6.7 %product.2 = bf16[8,16,32,384]{3,2,1,0:T(8,128)(2,1)} custom-call(bf16[8,16,48,512]{3,2,1,0:T(8,128)(2,1)} %bitcast.9.refs_0_.refs_1_.refs_4_.refs_5_, bf16[8,16,48,512]{3,2,1,0:T(8,128)(2,1)} %bitcast.9.refs_0_.refs_1_.refs_4_.refs_5_, bf16[8,16,16,512]{3,2,1,0:T(8,128)(2,1)S(1)} %copy-done.7, bf16[8,16,16,512]{3,2,1,0:T(8,128)(2,1)} %bitcast.42, ...), custom_call_target="tpu_custom_call" | custom-call | flops 200000000 | bytes 600000 | tf_op jit(solution)/shard_map/product/pallas_call | solution.py:268
  173.8 6.2 all-to-all-start.2
  180.0 2.3 slice.28
  184.8 52.6 %collective-permute-done.1.refs_0_.refs_2_.refs_6_ = bf16[4,16,16,512]{3,2,1,0:T(8,128)(2,1)} collective-permute-done((bf16[4,16,16,512]{3,2,1,0:T(8,128)(2,1)}, bf16[4,16,16,512]{3,2,1,0:T(8,128)(2,1)}, u32[]{:S(2)}, u32[]{:S(2)}) %collective-permute-start.1) | collective-permute-done | bytes 1048608 | tf_op jit(solution)/shard_map/ppermute | solution.py:140
  237.4 2.0 all-to-all-done.2.p_ref.refs_1_
  239.4 1.7 copy-done
  244.1 8.7 %middle.3 = (bf16[128,32,128]{2,1,0:T(8,128)(2,1)S(1)}, bf16[32,128,512]{2,1,0:T(8,128)(2,1)}, f32[128,128]{1,0:T(8,128)S(1)}, f32[128,128]{1,0:T(8,128)S(1)}) custom-call(s32[1,2]{1,0:T(1,128)S(1)} %fusion.5._, bf16[32,16,2,16,128]{4,3,2,1,0:T(8,128)(2,1)} %bitcast.67, bf16[32,16,2,16,128]{4,3,2,1,0:T(8,128)(2,1)} %bitcast.72, ...), custom_call_target="tpu_custom_call" | custom-call | flops 200000000 | bytes 600000 | tf_op jit(solution)/shard_map/middle/pallas_call | solution.py:382
  255.1 4.5 all-to-all-start.3
  259.6 2.4 fusion.7
  262.0 1.4 collective-permute-start.2
  263.5 14.9 %middle.4 = (bf16[128,32,256]{2,1,0:T(8,128)(2,1)S(1)}, bf16[32,128,512]{2,1,0:T(8,128)(2,1)}, f32[128,128]{1,0:T(8,128)S(1)}, f32[128,128]{1,0:T(8,128)S(1)}) custom-call(s32[2,2]{1,0:T(2,128)S(1)} %pad_add_fusion._, bf16[32,16,2,16,128]{4,3,2,1,0:T(8,128)(2,1)} %bitcast.68, ...), custom_call_target="tpu_custom_call", output_to_operand_aliasing={{1}: (11, {})} | custom-call | flops 200000000 | bytes 600000 | tf_op jit(solution)/shard_map/middle/pallas_call | solution.py:382
  278.4 1.3 copy-done.5
  281.0 1.8 all-to-all-done.3
  282.8 4.7 grad_b.3
  289.2 3.9 all-to-all-start.4
  294.0 2.2 collective-permute-start.3
  296.1 57.2 %collective-permute-done.3.refs_4_.refs_8_ = bf16[2,16,16,512]{3,2,1,0:T(8,128)(2,1)S(1)} collective-permute-done((bf16[2,16,16,512]{3,2,1,0:T(8,128)(2,1)S(1)}, bf16[2,16,16,512]{3,2,1,0:T(8,128)(2,1)S(1)}, u32[]{:S(2)}, u32[]{:S(2)}) %collective-permute-start.3) | collective-permute-done | bytes 524320 | tf_op jit(solution)/shard_map/ppermute | solution.py:140
  353.3 5.1 product.3
  359.4 1.7 copy-done.12
  361.1 3.6 all-to-all-start.5
  364.7 1.4 collective-permute-start.5
  366.1 5.5 grad_b.4
  371.6 1.4 copy-done.8
  373.0 17.3 %all-to-all-done.5.p_ref = bf16[128,32,128]{2,1,0:T(8,128)(2,1)S(1)} async-done(((bf16[128,32,128]{2,1,0:T(8,128)(2,1)}), bf16[128,32,128]{2,1,0:T(8,128)(2,1)S(1)}, u32[]{:S(2)}, u32[]{:S(2)}) %all-to-all-start.5) | async-done | bytes 1048608 | tf_op jit(solution)/shard_map/all_to_all | solution.py:128
  393.4 8.6 %middle.5 = (bf16[128,32,128]{2,1,0:T(8,128)(2,1)}, bf16[32,128,512]{2,1,0:T(8,128)(2,1)}, f32[128,128]{1,0:T(8,128)S(1)}, f32[128,128]{1,0:T(8,128)S(1)}) custom-call(s32[1,2]{1,0:T(1,128)S(1)} %fusion.4._, bf16[32,16,2,16,128]{4,3,2,1,0:T(8,128)(2,1)} %bitcast.69, bf16[32,16,2,16,128]{4,3,2,1,0:T(8,128)(2,1)} %bitcast.74, ...), custom_call_target="tpu_custom_call", output_to_operand_aliasing={{1}: (11, {})} | custom-call | flops 200000000 | bytes 600000 | tf_op jit(solution)/shard_map/middle/pallas_call | solution.py:382
  403.2 3.6 all-to-all-start.6
  407.9 24.2 %all-to-all-done.6 = bf16[128,32,128]{2,1,0:T(8,128)(2,1)S(1)} async-done(((bf16[128,32,128]{2,1,0:T(8,128)(2,1)}), bf16[128,32,128]{2,1,0:T(8,128)(2,1)S(1)}, u32[]{:S(2)}, u32[]{:S(2)}) %all-to-all-start.6) | async-done | bytes 1048608 | tf_op jit(solution)/shard_map/all_to_all | solution.py:128
  432.2 4.1 grad_b.5.refs_1_
  436.3 9.1 %grad_a.1 = bf16[8,16,48,512]{3,2,1,0:T(8,128)(2,1)} custom-call(bf16[8,16,32,128]{3,2,1,0:T(8,128)(2,1)} %bitcast.15.g_ref.refs_1_.refs_0_, bf16[8,16,32,256]{3,2,1,0:T(8,128)(2,1)} %bitcast.46, bf16[8,16,32,128]{3,2,1,0:T(8,128)(2,1)} %bitcast.48, bf16[8,16,16,512]{3,2,1,0:T(8,128)(2,1)} %copy-done.6, bf16[8,16,16,512]{3,2,1,0:T(8,128)(2,1)} %bitcast.43, ...), custom_call_target="tpu_custom_call" | custom-call | flops 200000000 | bytes 600000 | tf_op jit(solution)/shard_map/grad_a/pallas_call | solution.py:324
  445.5 4.8 all-to-all-start.7
  450.3 113.3 %collective-permute-done.7 = bf16[8,16,16,512]{3,2,1,0:T(8,128)(2,1)S(1)} collective-permute-done((bf16[8,16,16,512]{3,2,1,0:T(8,128)(2,1)S(1)}, bf16[8,16,16,512]{3,2,1,0:T(8,128)(2,1)S(1)}, u32[]{:S(2)}, u32[]{:S(2)}) %collective-permute-start.7) | collective-permute-done | bytes 2097184 | tf_op jit(solution)/shard_map/ppermute | solution.py:140
  563.7 3.9 add_convert_fusion
  567.6 3.8 all-to-all-start.8
  571.5 16.3 %last.2 = (bf16[32,16,2,16,128]{4,3,2,1,0:T(8,128)(2,1)}, f32[128,512]{1,0:T(8,128)S(1)}) custom-call(bf16[32,16,2,16,128]{4,3,2,1,0:T(8,128)(2,1)} %bitcast.70, f32[32,512]{1,0:T(8,128)S(1)} %broadcast_multiply_fusion.mask_ref, bf16[128,48,512]{2,1,0:T(8,128)(2,1)} %all-to-all-done.7.ga_ref.gb_ref, bf16[128,48,512]{2,1,0:T(8,128)(2,1)} %all-to-all-done.7.ga_ref.gb_ref, ...), custom_call_target="tpu_custom_call" | custom-call | flops 200000000 | bytes 600000 | tf_op jit(solution)/shard_map/last/pallas_call | solution.py:455
  587.8 9.0 %all-to-all-done.8.gb_ref = bf16[128,16,512]{2,1,0:T(8,128)(2,1)S(1)} async-done(((bf16[128,16,512]{2,1,0:T(8,128)(2,1)}), bf16[128,16,512]{2,1,0:T(8,128)(2,1)S(1)}, u32[]{:S(2)}, u32[]{:S(2)}) %all-to-all-start.8) | async-done | bytes 2097184 | tf_op jit(solution)/shard_map/all_to_all | solution.py:128
  596.8 16.3 %last.3 = (bf16[32,16,2,16,128]{4,3,2,1,0:T(8,128)(2,1)}, f32[128,512]{1,0:T(8,128)S(1)}) custom-call(bf16[32,16,2,16,128]{4,3,2,1,0:T(8,128)(2,1)} %bitcast.71, f32[32,512]{1,0:T(8,128)S(1)} %broadcast_multiply_fusion.mask_ref, bf16[128,48,512]{2,1,0:T(8,128)(2,1)} %all-to-all-done.7.ga_ref.gb_ref, ...), custom_call_target="tpu_custom_call", output_to_operand_aliasing={{0}: (9, {})} | custom-call | flops 200000000 | bytes 600000 | tf_op jit(solution)/shard_map/last/pallas_call | solution.py:455
  613.1 14.5 %all_to_all.57 = bf16[16,8,768]{2,1,0:T(8,128)(2,1)S(1)} all-to-all(bf16[16,8,768]{2,1,0:T(8,128)(2,1)S(1)} %pad_maximum_fusion), channel_id=1, replica_groups=mesh['crops'=2,'tile'=16] {'tile'}, dimensions={0} | all-to-all | bytes 393216 | tf_op jit(solution)/shard_map/all_to_all | solution.py:478
  627.6 11.6 %all_to_all.58 = bf16[16,8,768]{2,1,0:T(8,128)(2,1)S(1)} all-to-all(bf16[16,8,768]{2,1,0:T(8,128)(2,1)S(1)} %broadcast_in_dim.23), channel_id=1, replica_groups=mesh['crops'=2,'tile'=16] {'tile'}, dimensions={0} | all-to-all | bytes 393216 | tf_op jit(solution)/shard_map/all_to_all | solution.py:478
  (139 shorter events, 24.5 us)
Async XLA Ops:
  14.1 31.0 %all-to-all-start = ((bf16[128,16,512]{2,1,0:T(8,128)(2,1)}), bf16[128,16,512]{2,1,0:T(8,128)(2,1)S(1)}, u32[]{:S(2)}, u32[]{:S(2)}) async-start(bf16[128,16,512]{2,1,0:T(8,128)(2,1)} %copy-done.14), calls=%async_computation | async-start | bytes 4194304 | tf_op jit(solution)/shard_map/all_to_all | solution.py:128
  45.1 4.8 copy-start.2
  45.1 120.4 %all-to-all-start.1 = ((bf16[128,48,512]{2,1,0:T(8,128)(2,1)}), bf16[128,48,512]{2,1,0:T(8,128)(2,1)}, u32[]{:S(2)}, u32[]{:S(2)}) async-start(bf16[128,48,512]{2,1,0:T(8,128)(2,1)} %after.6), calls=%async_computation.1 | async-start | bytes 12582912 | tf_op jit(solution)/shard_map/all_to_all | solution.py:128
  49.9 113.4 %collective-permute-start = (bf16[8,16,16,512]{3,2,1,0:T(8,128)(2,1)S(1)}, bf16[8,16,16,512]{3,2,1,0:T(8,128)(2,1)S(1)}, u32[]{:S(2)}, u32[]{:S(2)}) collective-permute-start(bf16[8,16,16,512]{3,2,1,0:T(8,128)(2,1)S(1)} %bitcast.41), channel_id=1, source_target_pairs={{0,8},{1,9},{2,10},{3,11},{4,12},{5,13},{6,14},{7,15},{8,0},{9,1},... | collective-permute-start | bytes 6291464 | tf_op jit(solution)/shard_map/ppermute | solution.py:140
  163.3 1.4 copy-start.6
  165.4 1.6 copy-start.7
  173.7 8.7 %copy-start.47 = (bf16[128,128]{1,0:T(8,128)(2,1)S(1)}, bf16[128,128]{1,0:T(8,128)(2,1)}, u32[]{:S(2)}) copy-start(bf16[128,128]{1,0:T(8,128)(2,1)} %param.16) | copy-start | bytes 98308
  173.8 9.4 %copy-start.22 = (bf16[128,128]{1,0:T(8,128)(2,1)S(1)}, bf16[128,128]{1,0:T(8,128)(2,1)}, u32[]{:S(2)}) copy-start(bf16[128,128]{1,0:T(8,128)(2,1)} %wo_ref.5) | copy-start | bytes 98308
  173.8 10.1 %copy-start.49 = (f32[128]{0:T(128)S(1)}, f32[128]{0:T(128)}, u32[]{:S(2)}) copy-start(f32[128]{0:T(128)} %param.17) | copy-start | bytes 1540
  173.8 10.2 %copy-start.50 = (f32[128]{0:T(128)S(1)}, f32[128]{0:T(128)}, u32[]{:S(2)}) copy-start(f32[128]{0:T(128)} %param.18) | copy-start | bytes 1540
  173.8 65.6 %all-to-all-start.2 = ((bf16[128,32,384]{2,1,0:T(8,128)(2,1)}), bf16[128,32,384]{2,1,0:T(8,128)(2,1)S(1)}, u32[]{:S(2)}, u32[]{:S(2)}) async-start(bf16[128,32,384]{2,1,0:T(8,128)(2,1)} %bitcast.76), calls=%async_computation.2 | async-start | bytes 6291456 | tf_op jit(solution)/shard_map/all_to_all | solution.py:128
  182.3 55.1 %collective-permute-start.1 = (bf16[4,16,16,512]{3,2,1,0:T(8,128)(2,1)}, bf16[4,16,16,512]{3,2,1,0:T(8,128)(2,1)}, u32[]{:S(2)}, u32[]{:S(2)}) collective-permute-start(bf16[4,16,16,512]{3,2,1,0:T(8,128)(2,1)} %slice.28), channel_id=1, source_target_pairs={{0,8},{1,9},{2,10},{3,11},{4,12},{5,13},{6,14},{7,15},{8,0},{9,1},... | collective-permute-start | bytes 3145736 | tf_op jit(solution)/shard_map/ppermute | solution.py:140
  239.4 1.7 copy-start
  255.1 6.9 %copy-start.1 = (bf16[128,32,384]{2,1,0:T(8,128)(2,1)S(1)}, bf16[128,32,384]{2,1,0:T(8,128)(2,1)}, u32[]{:S(2)}) copy-start(bf16[128,32,384]{2,1,0:T(8,128)(2,1)} %copy-done) | copy-start | bytes 9437188
  255.1 27.7 %all-to-all-start.3 = ((bf16[128,32,128]{2,1,0:T(8,128)(2,1)}), bf16[128,32,128]{2,1,0:T(8,128)(2,1)}, u32[]{:S(2)}, u32[]{:S(2)}) async-start(bf16[128,32,128]{2,1,0:T(8,128)(2,1)} %copy-done.20), calls=%async_computation.3 | async-start | bytes 2097152 | tf_op jit(solution)/shard_map/all_to_all | solution.py:128
  259.6 3.9 copy-start.18
  259.6 3.9 copy-start.24
  259.6 3.9 copy-start.27
  259.6 3.9 copy-start.30
  262.0 26.6 %collective-permute-start.2 = (bf16[2,16,16,512]{3,2,1,0:T(8,128)(2,1)}, bf16[2,16,16,512]{3,2,1,0:T(8,128)(2,1)S(1)}, u32[]{:S(2)}, u32[]{:S(2)}) collective-permute-start(bf16[2,16,16,512]{3,2,1,0:T(8,128)(2,1)} %after.7), channel_id=1, source_target_pairs={{0,8},{1,9},{2,10},{3,11},{4,12},{5,13},{6,14},{7,15},{8,0},{9,1},... | collective-permute-start | bytes 1572872 | tf_op jit(solution)/shard_map/ppermute | solution.py:140
  288.6 64.7 %copy-start.9 = (bf16[2,16,16,512]{3,2,1,0:T(8,128)(2,1)}, bf16[2,16,16,512]{3,2,1,0:T(8,128)(2,1)S(1)}, u32[]{:S(2)}) copy-start(bf16[2,16,16,512]{3,2,1,0:T(8,128)(2,1)S(1)} %collective-permute-done.2.refs_3_.refs_7_) | copy-start | bytes 1572868
  289.2 4.8 copy-start.46
  289.2 70.2 %all-to-all-start.4 = ((bf16[128,32,256]{2,1,0:T(8,128)(2,1)}), bf16[128,32,256]{2,1,0:T(8,128)(2,1)S(1)}, u32[]{:S(2)}, u32[]{:S(2)}) async-start(bf16[128,32,256]{2,1,0:T(8,128)(2,1)} %after.8), calls=%async_computation.4 | async-start | bytes 4194304 | tf_op jit(solution)/shard_map/all_to_all | solution.py:128
  293.2 65.3 %collective-permute-start.4 = (bf16[3,16,16,512]{3,2,1,0:T(8,128)(2,1)}, bf16[3,16,16,512]{3,2,1,0:T(8,128)(2,1)S(1)}, u32[]{:S(2)}, u32[]{:S(2)}) collective-permute-start(bf16[3,16,16,512]{3,2,1,0:T(8,128)(2,1)} %copy-done.21), channel_id=1, source_target_pairs={{0,8},{1,9},{2,10},{3,11},{4,12},{5,13},{6,14},{7,15},{8,0},{9,1},... | collective-permute-start | bytes 2359304 | tf_op jit(solution)/shard_map/ppermute | solution.py:140
  294.0 59.3 %collective-permute-start.3 = (bf16[2,16,16,512]{3,2,1,0:T(8,128)(2,1)S(1)}, bf16[2,16,16,512]{3,2,1,0:T(8,128)(2,1)S(1)}, u32[]{:S(2)}, u32[]{:S(2)}) collective-permute-start(bf16[2,16,16,512]{3,2,1,0:T(8,128)(2,1)S(1)} %copy-done.46), channel_id=1, source_target_pairs={{0,8},{1,9},{2,10},{3,11},{4,12},{5,13},{6,14},{7,15},{8,0},{9,1},... | collective-permute-start | bytes 1572872 | tf_op jit(solution)/shard_map/ppermute | solution.py:140
  353.3 5.1 copy-start.15
  359.4 6.7 %copy-start.3 = (bf16[128,32,256]{2,1,0:T(8,128)(2,1)}, bf16[128,32,256]{2,1,0:T(8,128)(2,1)S(1)}, u32[]{:S(2)}) copy-start(bf16[128,32,256]{2,1,0:T(8,128)(2,1)S(1)} %all-to-all-done.4) | copy-start | bytes 6291460
  359.4 1.7 copy-start.12
  361.1 29.2 %all-to-all-start.5 = ((bf16[128,32,128]{2,1,0:T(8,128)(2,1)}), bf16[128,32,128]{2,1,0:T(8,128)(2,1)S(1)}, u32[]{:S(2)}, u32[]{:S(2)}) async-start(bf16[128,32,128]{2,1,0:T(8,128)(2,1)} %after.9), calls=%async_computation.5 | async-start | bytes 2097152 | tf_op jit(solution)/shard_map/all_to_all | solution.py:128
  364.7 38.6 %collective-permute-start.5 = (bf16[3,16,16,512]{3,2,1,0:T(8,128)(2,1)}, bf16[3,16,16,512]{3,2,1,0:T(8,128)(2,1)}, u32[]{:S(2)}, u32[]{:S(2)}) collective-permute-start(bf16[3,16,16,512]{3,2,1,0:T(8,128)(2,1)} %copy-done.44), channel_id=1, source_target_pairs={{0,8},{1,9},{2,10},{3,11},{4,12},{5,13},{6,14},{7,15},{8,0},{9,1},... | collective-permute-start | bytes 2359304 | tf_op jit(solution)/shard_map/ppermute | solution.py:140
  371.6 1.4 copy-start.8
  403.2 29.0 %all-to-all-start.6 = ((bf16[128,32,128]{2,1,0:T(8,128)(2,1)}), bf16[128,32,128]{2,1,0:T(8,128)(2,1)S(1)}, u32[]{:S(2)}, u32[]{:S(2)}) async-start(bf16[128,32,128]{2,1,0:T(8,128)(2,1)} %after.10), calls=%async_computation.6 | async-start | bytes 2097152 | tf_op jit(solution)/shard_map/all_to_all | solution.py:128
  406.8 29.5 %collective-permute-start.6 = (bf16[2,16,16,512]{3,2,1,0:T(8,128)(2,1)}, bf16[2,16,16,512]{3,2,1,0:T(8,128)(2,1)}, u32[]{:S(2)}, u32[]{:S(2)}) collective-permute-start(bf16[2,16,16,512]{3,2,1,0:T(8,128)(2,1)} %get-tuple-element.37), channel_id=1, source_target_pairs={{0,8},{1,9},{2,10},{3,11},{4,12},{5,13},{6,14},{7,15},{8,0},{9,1},... | collective-permute-start | bytes 1572872 | tf_op jit(solution)/shard_map/ppermute | solution.py:140
  432.2 4.1 copy-start.4
  432.2 4.1 copy-start.10
  432.2 4.1 copy-start.13
  432.2 4.1 copy-start.16
  445.5 122.1 %all-to-all-start.7 = ((bf16[128,48,512]{2,1,0:T(8,128)(2,1)}), bf16[128,48,512]{2,1,0:T(8,128)(2,1)}, u32[]{:S(2)}, u32[]{:S(2)}) async-start(bf16[128,48,512]{2,1,0:T(8,128)(2,1)} %bitcast.75), calls=%async_computation.7 | async-start | bytes 12582912 | tf_op jit(solution)/shard_map/all_to_all | solution.py:128
  450.2 113.4 %collective-permute-start.7 = (bf16[8,16,16,512]{3,2,1,0:T(8,128)(2,1)S(1)}, bf16[8,16,16,512]{3,2,1,0:T(8,128)(2,1)S(1)}, u32[]{:S(2)}, u32[]{:S(2)}) collective-permute-start(bf16[8,16,16,512]{3,2,1,0:T(8,128)(2,1)S(1)} %grad_b.5.refs_1_), channel_id=1, source_target_pairs={{0,8},{1,9},{2,10},{3,11},{4,12},{5,13},{6,14},{7,15},{8,0},{9,1},... | collective-permute-start | bytes 6291464 | tf_op jit(solution)/shard_map/ppermute | solution.py:140
  563.6 7.8 %copy-start.45 = (bf16[128,512]{1,0:T(8,128)(2,1)S(1)}, bf16[128,512]{1,0:T(8,128)(2,1)}, u32[]{:S(2)}) copy-start(bf16[128,512]{1,0:T(8,128)(2,1)} %param.15) | copy-start | bytes 393220
  563.6 7.8 %copy-start.48 = (bf16[128,128]{1,0:T(8,128)(2,1)S(1)}, bf16[128,128]{1,0:T(8,128)(2,1)}, u32[]{:S(2)}) copy-start(bf16[128,128]{1,0:T(8,128)(2,1)} %param.16) | copy-start | bytes 98308
  563.6 7.8 %copy-start.33 = (f32[128,128]{1,0:T(8,128)S(1)}, f32[128,128]{1,0:T(8,128)}, u32[]{:S(2)}) copy-start(f32[128,128]{1,0:T(8,128)} %copy-done.32) | copy-start | bytes 196612
  563.6 7.8 %copy-start.35 = (f32[128,128]{1,0:T(8,128)S(1)}, f32[128,128]{1,0:T(8,128)}, u32[]{:S(2)}) copy-start(f32[128,128]{1,0:T(8,128)} %copy-done.34) | copy-start | bytes 196612
  563.6 7.8 %copy-start.37 = (f32[128,128]{1,0:T(8,128)S(1)}, f32[128,128]{1,0:T(8,128)}, u32[]{:S(2)}) copy-start(f32[128,128]{1,0:T(8,128)} %copy-done.36) | copy-start | bytes 196612
  563.6 7.9 %copy-start.39 = (f32[128,128]{1,0:T(8,128)S(1)}, f32[128,128]{1,0:T(8,128)}, u32[]{:S(2)}) copy-start(f32[128,128]{1,0:T(8,128)} %copy-done.38) | copy-start | bytes 196612
  563.6 7.9 %copy-start.41 = (f32[128,128]{1,0:T(8,128)S(1)}, f32[128,128]{1,0:T(8,128)}, u32[]{:S(2)}) copy-start(f32[128,128]{1,0:T(8,128)} %copy-done.40) | copy-start | bytes 196612
  563.7 7.8 %copy-start.43 = (f32[128,128]{1,0:T(8,128)S(1)}, f32[128,128]{1,0:T(8,128)}, u32[]{:S(2)}) copy-start(f32[128,128]{1,0:T(8,128)} %copy-done.42) | copy-start | bytes 196612
  567.6 29.2 %all-to-all-start.8 = ((bf16[128,16,512]{2,1,0:T(8,128)(2,1)}), bf16[128,16,512]{2,1,0:T(8,128)(2,1)S(1)}, u32[]{:S(2)}, u32[]{:S(2)}) async-start(bf16[128,16,512]{2,1,0:T(8,128)(2,1)} %bitcast.77), calls=%async_computation.8 | async-start | bytes 4194304 | tf_op jit(solution)/shard_map/all_to_all | solution.py:128
  (20 other events, 16.3 us)

commit v9 on v8

--- a/solution.py
+++ b/solution.py
@@ -409,19 +409,28 @@
     )(table, x, d, p, *small, *kept)
 
 
-def last_kernel(
-    step, x_ref, mask_ref, ga_ref, gb_ref, gate_ref, gain_ref, bias_ref, wt_ref, wcat_ref, *refs
-):
-    out_ref, gw_ref, sa_ref, sb_ref = refs[-4:]
-    rows = x_ref.shape[0]
-    hidden = ga_ref.shape[0]
-
-    @pl.when(pl.program_id(0) == 0)
-    def _():
-        gw_ref[...] = jnp.zeros_like(gw_ref)
-
-    spread_in(ga_ref, sa_ref)
-    spread_in(gb_ref, sb_ref)
+def last_kernel(step, mode, *refs):
+    sides, gated, based, out_kind, summed = MODES[mode]
+    scratches, rest = refs[-len(sides) :], iter(refs[: -len(sides)])
+    x_ref, mask_ref = next(rest), next(rest)
+    grads = [next(rest) for _ in sides]
+    gate_ref = next(rest) if gated else None
+    base_ref = next(rest) if based else None
+    gain_ref, bias_ref, wt_ref, wcat_ref, *outs = rest
+    gw_ref = outs[-1]
+    out_ref = outs[-1 - summed] if out_kind else None
+    rows, _, _, _, _ = x_ref.shape
+    hidden = grads[0].shape[0]
+    width = mask_ref.shape[1]
+
+    if summed:
+
+        @pl.when(pl.program_id(0) == 0)
+        def _():
+            gw_ref[...] = jnp.zeros_like(gw_ref)
+
+    for ref, scratch in zip(grads, scratches):
+        spread_in(ref, scratch)
 
     @pl.loop(0, rows // step, unroll=min(4, rows // step))
     def _(turn):
@@ -430,48 +439,81 @@
         normed = (z_hat * gain_ref[...] + bias_ref[...]).astype(BF16)
         mask = flat_rows(mask_ref, row, step)
         proj = dot(wt_ref[...], normed)
-        sides = []
-        for side, ref in enumerate((sa_ref, sb_ref)):
+        parts = []
+        for side, scratch in enumerate(scratches):
             value = proj[2 * side * hidden : (2 * side + 1) * hidden]
             sig = sigmoid(proj[(2 * side + 1) * hidden : (2 * side + 2) * hidden])
-            to_value = load_rows(ref, row, step, rows) * mask * sig
-            sides += [to_value.astype(BF16), (to_value * value * (1.0 - sig)).astype(BF16)]
-        grad_proj = jnp.concatenate(sides, axis=0)
-        gate_back = jnp.concatenate([gate_ref[row + at] for at in range(step)], axis=1)
-        every = jnp.concatenate([grad_proj, gate_back], axis=0)
-        upstream = dot(wcat_ref[...], every) * gain_ref[...]
-        grad = norm_back(upstream, z_hat, inv_in).T.astype(BF16)
-        out_ref[pl.ds(row, step)] = grad.reshape((step,) + out_ref.shape[1:])
-        gw_ref[...] += dot(normed, grad_proj, NT)
-
-
-def make_last(plan, sub, before, x, mask, grad_a, grad_b, at, gate_back, small):
+            to_value = load_rows(scratch, row, step, rows) * mask * sig
+            parts += [to_value.astype(BF16), (to_value * value * (1.0 - sig)).astype(BF16)]
+        grad_proj = jnp.concatenate(parts, axis=0)
+        if summed:
+            gw_ref[...] += dot(normed, grad_proj, NT)
+        if out_kind:
+            every = grad_proj
+            if gated:
+                gate_back = jnp.concatenate([gate_ref[row + at] for at in range(step)], axis=1)
+                every = jnp.concatenate([grad_proj, gate_back], axis=0)
+            upstream = dot(wcat_ref[...], every)
+            if based:
+                upstream += jnp.concatenate(
+                    [base_ref[row + at].astype(F32) for at in range(step)], axis=1
+                )
+            if out_kind == "pair":
+                grad = norm_back(upstream * gain_ref[...], z_hat, inv_in).T.astype(BF16)
+                out_ref[pl.ds(row, step)] = grad.reshape((step,) + out_ref.shape[1:])
+            else:
+                for at in range(step):
+                    out_ref[row + at] = upstream[:, at * width : (at + 1) * width].astype(BF16)
+
+
+MODES = {
+    "both": ((0, 1), True, False, "pair", True),
+    "a": ((0,), True, False, "base", True),
+    "b_sum": ((1,), False, False, "", True),
+    "b": ((1,), False, True, "pair", False),
+}
+
+
+def make_last(plan, mode, sub, before, x, mask, grads, extra, small):
+    sides, gated, based, out_kind, summed = MODES[mode]
     chans = x.shape[-1]
-    hidden = grad_a.shape[0]
-    grad = jax.ShapeDtypeStruct((chans, 4 * hidden), F32)
+    hidden = grads[0][0].shape[0]
+    grad = jax.ShapeDtypeStruct((chans, 2 * len(sides) * hidden), F32)
     pairs = plan.pair_spec(chans, lambda j: (sub, j % 2, j // 2, 0, 0))
     channel = (hidden, plan.rows, plan.width)
+    lines = (plan.rows, chans, plan.width)
     kept = [] if before is None else [before]
+    in_specs = [pairs, pl.BlockSpec((plan.rows, plan.width), lambda j: (sub, j))]
+    for _, at in grads:
+        in_specs.append(pl.BlockSpec(channel, lambda j, at=at: (0, at, j)))
+    if gated:
+        in_specs.append(pl.BlockSpec(lines, lambda j: (sub, 0, j)))
+    if based:
+        in_specs.append(pl.BlockSpec(lines, lambda j: (0, 0, j)))
+    out_specs, out_shape = [], []
+    if out_kind == "pair":
+        out_specs.append(pairs)
+        out_shape.append(jax.ShapeDtypeStruct(x.shape, BF16))
+    if out_kind == "base":
+        out_specs.append(pl.BlockSpec(lines, lambda j: (0, 0, j)))
+        out_shape.append(jax.ShapeDtypeStruct((plan.rows, chans, plan.crop), BF16))
+    if summed:
+        out_specs.append(whole(grad))
+        out_shape.append(grad)
+    operands = [x, mask, *arrays(grads), *extra, *small]
+    in_specs += [whole(value) for value in small]
     return pl.pallas_call(
-        functools.partial(last_kernel, plan.step),
+        functools.partial(last_kernel, plan.step, mode),
         grid=(plan.blocks,),
-        in_specs=[
-            pairs,
-            pl.BlockSpec((plan.rows, plan.width), lambda j: (sub, j)),
-            pl.BlockSpec(channel, lambda j: (0, sub, j)),
-            pl.BlockSpec(channel, lambda j: (0, at, j)),
-            pl.BlockSpec((plan.rows, chans, plan.width), lambda j: (sub, 0, j)),
-        ]
-        + [whole(value) for value in small]
-        + [HELD for _ in kept],
-        out_specs=[pairs, whole(grad)],
-        out_shape=[jax.ShapeDtypeStruct(x.shape, BF16), grad],
-        scratch_shapes=[plan.scratch(hidden)] * 2,
-        input_output_aliases={} if before is None else {5 + len(small): 0},
+        in_specs=in_specs + [HELD for _ in kept],
+        out_specs=out_specs,
+        out_shape=out_shape,
+        scratch_shapes=[plan.scratch(hidden)] * len(sides),
+        input_output_aliases={len(operands): 0} if kept else {},
         compiler_params=params(1),
         cost_estimate=cost(0.2),
-        name="last",
-    )(x, mask, grad_a, grad_b, gate_back, *small, *kept)
+        name="last_" + mode,
+    )(*operands, *kept)
 
 
 def swap_all(array):
@@ -509,7 +551,7 @@
 
     plan_cut = plan.cut
     two = plan.subs == 2
-    cut_b, back_a = plan_cut(4, 2, 2), plan_cut(3, 3, 2)
+    cut_b, back_a = plan_cut(6, 2), plan_cut(3, 3, 2)
     small = [gain, bias, w_t, w_cat]
 
     def middle(at, first, before, ready, product):
@@ -535,9 +577,8 @@
     product = product_of(b_first)
     if two:
         got_b.append(plan.exchange(after(sent[1], product)))
-        got_b.append(plan.exchange(sent[2]))
-    grad, kept, local_mid = middle([(1 - side, 0)], 0, (), got_b[:1], product)
-    owner_g = [owned(plan.swap(grad))]
+    grad, kept, local_mid = middle([(1 - side, 0)], 0, (), (), product)
+    owner_g = [owned(plan.swap(after(grad, *got_b[:1])))]
     grad, kept, local = middle([(side, sub) for sub in every], 1, (kept,), (), product)
     local_mid += local
     grad_b0 = make_grad_b(plan, owner_g[0], own_a, back_a)
@@ -557,17 +598,22 @@
         back_1 = plan.exchange(grad_b1)
         back_0[2] = after(back_0[2], grad_b1)
     grads = plan.swap(joined(make_grad_a(plan, owner_g, b_first, grad_b_own[0], back_0)))
+    first, second = w_ab[:, : 2 * hidden], w_ab[:, 2 * hidden :]
     pair_grad, local_ab = make_last(
-        plan, 0, None, x, mask, grads, grads, plan.subs, kept, small
+        plan, "both", 0, None, x, mask, [(grads, 0), (grads, plan.subs)], [kept], small
     )
     if two:
         grad_b = plan.swap(
             joined((grad_b_own[1].astype(F32) + back_1.astype(F32)).astype(BF16))
         )
-        pair_grad, local = make_last(
-            plan, 1, pair_grad, x, mask, grads, grad_b, 0, kept, small
+        side_a = [gain, bias, w_t[: 2 * hidden], jnp.concatenate([first, w_gate], axis=1)]
+        side_b = [gain, bias, w_t[2 * hidden :], second]
+        base, local_a = make_last(plan, "a", 1, None, x, mask, [(grads, 1)], [kept], side_a)
+        (local_b,) = make_last(plan, "b_sum", 1, None, x, mask, [(grad_b, 0)], [], side_b)
+        (pair_grad,) = make_last(
+            plan, "b", 1, pair_grad, x, mask, [(grad_b, 0)], [base], side_b
         )
-        local_ab += local
+        local_ab += jnp.concatenate([local_a, local_b], axis=1)
     total = tile_sum(jnp.concatenate([local_ab, local_mid], axis=1), tiles) / crop
     wide = 4 * hidden
     return (

time: 643 us -> 687 us (1.068)
  waiting for transfers between devices: 406 us -> 437 us
  Pallas kernels: 117 us -> 126 us
    all_to_all x9 -> x8, waiting for transfers between devices: 72.2 us -> 164 us  [swap(): lax.all_to_all(array, 'tile', split_axis=0, concat_axis=0, axis_index_gro...]
    ppermute x8 -> x7, waiting for transfers between devices: 334 us -> 273 us  [exchange(): return lax.ppermute(array, 'tile', self.partner)]
    all_to_all x0 -> x1, blocking collectives: none -> 17.3 us  [swap(): lax.all_to_all(array, 'tile', split_axis=0, concat_axis=0, axis_index_gro...]
    all_to_all x2 -> x1, blocking collectives: 26.1 us -> 12.8 us  [swap_all(): lax.all_to_all(array, 'tile', split_axis=0, concat_axis=0, tiled=True)]
    pallas_call x2 -> x4, Pallas kernels: 32.5 us -> 42.5 us  [make_last(): pl.pallas_call(functools.partial(last_kernel, plan.step, mode), grid=(pla...]
    all_to_all x9 -> x8, starting transfers between devices: 40.3 us -> 38.3 us  [swap(): lax.all_to_all(array, 'tile', split_axis=0, concat_axis=0, axis_index_gro...]
    unnamed x106 -> x91, local copies, waits for them, and re-layouts: 26.4 us -> 25.1 us
  transfers between devices with their start and end apart: 17 -> 16, of which waited for: 12 -> 13; matrix products, arithmetic and copies ran while one was open for 2% -> 1% of each run, Pallas kernels for 11% -> 12%
where the time goes in v9:
time: 687 us; the launch traced here: 685 us
  waiting for transfers between devices  437 us (64%)
  Pallas kernels  126 us (18%)
  starting transfers between devices  52.2 us (8%)
  local copies, waits for them, and re-layouts  34.6 us (5%)
  blocking collectives  30.1 us (4%)
    ppermute x7, waiting for transfers between devices, exchange(): return lax.ppermute(array, 'tile', self.partner)  273 us
    all_to_all x8, waiting for transfers between devices, swap(): lax.all_to_all(array, 'tile', split_axis=0, concat_axis=0, axis_index_gro...  164 us
    pallas_call x4, Pallas kernels, make_last(): pl.pallas_call(functools.partial(last_kernel, plan.step, mode), grid=(pla...  42.5 us
    all_to_all x8, starting transfers between devices, swap(): lax.all_to_all(array, 'tile', split_axis=0, concat_axis=0, axis_index_gro...  38.3 us
    pallas_call x3, Pallas kernels, make_middle(): pl.pallas_call(functools.partial(middle_kernel, plan.step), grid_spec=plt...  32.2 us
    unnamed x91, local copies, waits for them, and re-layouts  25.1 us
    all_to_all x1, blocking collectives, swap(): lax.all_to_all(array, 'tile', split_axis=0, concat_axis=0, axis_index_gro...  17.3 us
    pallas_call x2, Pallas kernels, make_factors(): pl.pallas_call(functools.partial(factors_kernel, plan.step, bool(before))...  17.1 us
  transfers between devices with their start and end apart: 16, of which 13 were waited for; matrix products, arithmetic and copies ran while one was open for 1% of the time, Pallas kernels for 12%

profile of v9, /device:TPU:0, one launch (start us, length us, event | category | flops | bytes accessed | tf_op | source)
XLA Modules:
  0.0 684.9 jit_solution(4287303405790608995)
XLA Ops:
  4.2 8.6 %factors.2 = (bf16[128,48,512]{2,1,0:T(8,128)(2,1)}, bf16[128,16,512]{2,1,0:T(8,128)(2,1)S(1)}) custom-call(bf16[32,16,2,16,128]{4,3,2,1,0:T(8,128)(2,1)} %bitcast.65, f32[32,512]{1,0:T(8,128)S(1)} %broadcast_multiply_fusion.mask_ref.refs_1_, f32[128,1]{1,0:T(8,128)S(1)} %copy.83.gain_ref.refs_4_.refs_5_.refs_3_, ...), custom_call_target="tpu_custom_call" | custom-call | flops 200000000 | bytes 600000 | tf_op jit(solution)/shard_map/factors/pallas_call | solution.py:201
  14.1 5.2 all-to-all-start
  19.4 8.5 %factors.3.refs_0_ = bf16[128,48,512]{2,1,0:T(8,128)(2,1)} custom-call(bf16[32,16,2,16,128]{4,3,2,1,0:T(8,128)(2,1)} %bitcast.66, f32[32,512]{1,0:T(8,128)S(1)} %broadcast_multiply_fusion.mask_ref.refs_1_, f32[128,1]{1,0:T(8,128)S(1)} %copy.83.gain_ref.refs_4_.refs_5_.refs_3_, ...), custom_call_target="tpu_custom_call", output_to_operand_aliasing={{}: (5, {})} | custom-call | flops 200000000 | bytes 600000 | tf_op jit(solution)/shard_map/factors/pallas_call | solution.py:201
  27.9 17.2 %all-to-all-done = bf16[128,16,512]{2,1,0:T(8,128)(2,1)S(1)} async-done(((bf16[128,16,512]{2,1,0:T(8,128)(2,1)}), bf16[128,16,512]{2,1,0:T(8,128)(2,1)S(1)}, u32[]{:S(2)}, u32[]{:S(2)}) %all-to-all-start) | async-done | bytes 2097184 | tf_op jit(solution)/shard_map/all_to_all | solution.py:128
  45.1 4.8 all-to-all-start.1
  49.9 2.7 collective-permute-start
  52.5 110.7 %collective-permute-done.refs_2_.refs_3_ = bf16[8,16,16,512]{3,2,1,0:T(8,128)(2,1)S(1)} collective-permute-done((bf16[8,16,16,512]{3,2,1,0:T(8,128)(2,1)S(1)}, bf16[8,16,16,512]{3,2,1,0:T(8,128)(2,1)S(1)}, u32[]{:S(2)}, u32[]{:S(2)}) %collective-permute-start) | collective-permute-done | bytes 2097184 | tf_op jit(solution)/shard_map/ppermute | solution.py:140
  165.5 1.6 copy-done.9
  167.0 6.7 product.2
  173.8 6.0 all-to-all-start.2
  179.8 2.8 slice.39
  184.4 1.5 copy.86
  186.0 60.2 %all-to-all-done.2.p_ref.refs_1_ = bf16[128,32,384]{2,1,0:T(8,128)(2,1)S(1)} async-done(((bf16[128,32,384]{2,1,0:T(8,128)(2,1)}), bf16[128,32,384]{2,1,0:T(8,128)(2,1)S(1)}, u32[]{:S(2)}, u32[]{:S(2)}) %all-to-all-start.2) | async-done | bytes 3145760 | tf_op jit(solution)/shard_map/all_to_all | solution.py:128
  246.2 1.7 copy-done
  251.0 8.7 %middle.3 = (bf16[128,32,128]{2,1,0:T(8,128)(2,1)S(1)}, bf16[32,128,512]{2,1,0:T(8,128)(2,1)}, f32[128,128]{1,0:T(8,128)S(1)}, f32[128,128]{1,0:T(8,128)S(1)}) custom-call(s32[1,2]{1,0:T(1,128)S(1)} %fusion.7._, bf16[32,16,2,16,128]{4,3,2,1,0:T(8,128)(2,1)} %bitcast.67, bf16[32,16,2,16,128]{4,3,2,1,0:T(8,128)(2,1)} %bitcast.74, ...), custom_call_target="tpu_custom_call" | custom-call | flops 200000000 | bytes 600000 | tf_op jit(solution)/shard_map/middle/pallas_call | solution.py:382
  261.9 4.4 all-to-all-start.3
  266.3 1.9 slice.40.refs_0_
  268.4 14.9 %middle.4 = (bf16[128,32,256]{2,1,0:T(8,128)(2,1)S(1)}, bf16[32,128,512]{2,1,0:T(8,128)(2,1)}, f32[128,128]{1,0:T(8,128)S(1)}, f32[128,128]{1,0:T(8,128)S(1)}) custom-call(s32[2,2]{1,0:T(2,128)S(1)} %pad_add_fusion._, bf16[32,16,2,16,128]{4,3,2,1,0:T(8,128)(2,1)} %bitcast.68, ...), custom_call_target="tpu_custom_call", output_to_operand_aliasing={{1}: (11, {})} | custom-call | flops 200000000 | bytes 600000 | tf_op jit(solution)/shard_map/middle/pallas_call | solution.py:382
  284.6 4.0 all-to-all-done.3
  288.6 3.8 grad_b.3
  294.8 3.8 all-to-all-start.4
  299.0 5.1 product.3
  304.1 34.8 %collective-permute-done.3.refs_2_.refs_9_ = bf16[3,16,16,512]{3,2,1,0:T(8,128)(2,1)S(1)} collective-permute-done((bf16[3,16,16,512]{3,2,1,0:T(8,128)(2,1)}, bf16[3,16,16,512]{3,2,1,0:T(8,128)(2,1)S(1)}, u32[]{:S(2)}, u32[]{:S(2)}) %collective-permute-start.3) | collective-permute-done | bytes 786464 | tf_op jit(solution)/shard_map/ppermute | solution.py:140
  340.9 1.7 copy-done.13
  342.6 4.2 all-to-all-start.5
  346.8 2.2 collective-permute-start.4
  349.1 5.6 grad_b.4
  356.1 17.1 %all-to-all-done.5.p_ref = bf16[128,32,128]{2,1,0:T(8,128)(2,1)} async-done(((bf16[128,32,128]{2,1,0:T(8,128)(2,1)}), bf16[128,32,128]{2,1,0:T(8,128)(2,1)}, u32[]{:S(2)}, u32[]{:S(2)}) %all-to-all-start.5) | async-done | bytes 1048608 | tf_op jit(solution)/shard_map/all_to_all | solution.py:128
  373.2 8.6 %middle.5 = (bf16[128,32,128]{2,1,0:T(8,128)(2,1)S(1)}, bf16[32,128,512]{2,1,0:T(8,128)(2,1)}, f32[128,128]{1,0:T(8,128)S(1)}, f32[128,128]{1,0:T(8,128)S(1)}) custom-call(s32[1,2]{1,0:T(1,128)S(1)} %fusion.5._, bf16[32,16,2,16,128]{4,3,2,1,0:T(8,128)(2,1)} %bitcast.69, bf16[32,16,2,16,128]{4,3,2,1,0:T(8,128)(2,1)} %bitcast.76, ...), custom_call_target="tpu_custom_call", output_to_operand_aliasing={{1}: (11, {})} | custom-call | flops 200000000 | bytes 600000 | tf_op jit(solution)/shard_map/middle/pallas_call | solution.py:382
  381.8 2.8 collective-permute-done.4.refs_1_.refs_10_
  384.7 17.3 %all_to_all.57 = bf16[128,32,128]{2,1,0:T(8,128)(2,1)S(1)} all-to-all(bf16[128,32,128]{2,1,0:T(8,128)(2,1)S(1)} %after.12), channel_id=1, replica_groups={{0,1,2,3,4,5,6,7},{8,9,10,11,12,13,14,15},{16,17,18,19,20,21,22,23},{24..., dimensions={0} | all-to-all | bytes 2097152 | tf_op jit(solution)/shard_map/all_to_all | solution.py:128
  402.0 4.1 grad_b.5.refs_1_
  406.1 3.1 collective-permute-start.5
  409.2 90.5 %collective-permute-done.5 = bf16[8,16,16,512]{3,2,1,0:T(8,128)(2,1)S(1)} collective-permute-done((bf16[8,16,16,512]{3,2,1,0:T(8,128)(2,1)S(1)}, bf16[8,16,16,512]{3,2,1,0:T(8,128)(2,1)S(1)}, u32[]{:S(2)}, u32[]{:S(2)}) %collective-permute-start.5) | collective-permute-done | bytes 2097184 | tf_op jit(solution)/shard_map/ppermute | solution.py:140
  499.7 2.4 add_convert_fusion
  502.1 3.6 all-to-all-start.7
  505.8 1.8 collective-permute-start.6
  507.6 33.1 %collective-permute-done.6.refs_0_ = bf16[2,16,16,512]{3,2,1,0:T(8,128)(2,1)S(1)} collective-permute-done((bf16[2,16,16,512]{3,2,1,0:T(8,128)(2,1)}, bf16[2,16,16,512]{3,2,1,0:T(8,128)(2,1)S(1)}, u32[]{:S(2)}, u32[]{:S(2)}) %collective-permute-start.6) | collective-permute-done | bytes 524320 | tf_op jit(solution)/shard_map/ppermute | solution.py:140
  540.6 1.6 copy-done.6
  543.6 8.9 %grad_a.1 = bf16[8,16,48,512]{3,2,1,0:T(8,128)(2,1)} custom-call(bf16[8,16,32,128]{3,2,1,0:T(8,128)(2,1)} %bitcast.18.g_ref.refs_1_.refs_0_, bf16[8,16,32,256]{3,2,1,0:T(8,128)(2,1)} %bitcast.46, bf16[8,16,32,128]{3,2,1,0:T(8,128)(2,1)} %bitcast.48, bf16[8,16,16,512]{3,2,1,0:T(8,128)(2,1)} %copy-done.8, bf16[8,16,16,512]{3,2,1,0:T(8,128)(2,1)} %bitcast.43, ...), custom_call_target="tpu_custom_call" | custom-call | flops 200000000 | bytes 600000 | tf_op jit(solution)/shard_map/grad_a/pallas_call | solution.py:324
  552.6 6.2 all-to-all-start.8
  558.9 7.2 %last_b_sum.1 = f32[128,256]{1,0:T(8,128)S(1)} custom-call(bf16[32,16,2,16,128]{4,3,2,1,0:T(8,128)(2,1)} %bitcast.70, f32[32,512]{1,0:T(8,128)S(1)} %broadcast_multiply_fusion.mask_ref.refs_1_, bf16[128,16,512]{2,1,0:T(8,128)(2,1)S(1)} %all-to-all-done.7.refs_2_, f32[128,1]{1,0:T(8,128)S(1)} %copy.83.gain_ref.refs_4_.refs_5_.refs_3_, ...), custom_call_target="tpu_custom_call" | custom-call | flops 200000000 | bytes 600000 | tf_op jit(solution)/shard_map/last_b_sum/pallas_call | solution.py:505
  566.2 63.6 %all-to-all-done.8.refs_2_.refs_3_ = bf16[128,48,512]{2,1,0:T(8,128)(2,1)} async-done(((bf16[128,48,512]{2,1,0:T(8,128)(2,1)}), bf16[128,48,512]{2,1,0:T(8,128)(2,1)}, u32[]{:S(2)}, u32[]{:S(2)}) %all-to-all-start.8) | async-done | bytes 6291488 | tf_op jit(solution)/shard_map/all_to_all | solution.py:128
  629.7 14.7 %last_both.1 = (bf16[32,16,2,16,128]{4,3,2,1,0:T(8,128)(2,1)}, f32[128,512]{1,0:T(8,128)S(1)}) custom-call(bf16[32,16,2,16,128]{4,3,2,1,0:T(8,128)(2,1)} %bitcast.71, f32[32,512]{1,0:T(8,128)S(1)} %broadcast_multiply_fusion.mask_ref.refs_1_, bf16[128,48,512]{2,1,0:T(8,128)(2,1)} %all-to-all-done.8.refs_2_.refs_3_, ...), custom_call_target="tpu_custom_call" | custom-call | flops 200000000 | bytes 600000 | tf_op jit(solution)/shard_map/last_both/pallas_call | solution.py:505
  644.4 9.7 %last_a.1 = (bf16[16,128,512]{2,1,0:T(8,128)(2,1)S(1)}, f32[128,256]{1,0:T(8,128)S(1)}) custom-call(bf16[32,16,2,16,128]{4,3,2,1,0:T(8,128)(2,1)} %bitcast.72, f32[32,512]{1,0:T(8,128)S(1)} %broadcast_multiply_fusion.mask_ref.refs_1_, bf16[128,48,512]{2,1,0:T(8,128)(2,1)} %all-to-all-done.8.refs_2_.refs_3_, ...), custom_call_target="tpu_custom_call" | custom-call | flops 200000000 | bytes 600000 | tf_op jit(solution)/shard_map/last_a/pallas_call | solution.py:505
  655.5 12.8 %all_to_all.58 = bf16[16,8,768]{2,1,0:T(8,128)(2,1)S(1)} all-to-all(bf16[16,8,768]{2,1,0:T(8,128)(2,1)S(1)} %pad_maximum_fusion), channel_id=1, replica_groups=mesh['crops'=2,'tile'=16] {'tile'}, dimensions={0} | all-to-all | bytes 393216 | tf_op jit(solution)/shard_map/all_to_all | solution.py:520
  669.0 3.5 all-to-all-start.10
  672.6 10.9 %last_b.1 = bf16[32,16,2,16,128]{4,3,2,1,0:T(8,128)(2,1)} custom-call(bf16[32,16,2,16,128]{4,3,2,1,0:T(8,128)(2,1)} %bitcast.73, f32[32,512]{1,0:T(8,128)S(1)} %broadcast_multiply_fusion.mask_ref.refs_1_, bf16[128,16,512]{2,1,0:T(8,128)(2,1)S(1)} %all-to-all-done.7.refs_2_, bf16[16,128,512]{2,1,0:T(8,128)(2,1)} %copy-done.18, ...), custom_call_target="tpu_custom_call", output_to_operand_aliasing={{}: (8, {})} | custom-call | flops 200000000 | bytes 600000 | tf_op jit(solution)/shard_map/last_b/pallas_call | solution.py:505
  (128 shorter events, 26.9 us)
Async XLA Ops:
  12.8 1.3 copy-start.17
  14.1 30.9 %all-to-all-start = ((bf16[128,16,512]{2,1,0:T(8,128)(2,1)}), bf16[128,16,512]{2,1,0:T(8,128)(2,1)S(1)}, u32[]{:S(2)}, u32[]{:S(2)}) async-start(bf16[128,16,512]{2,1,0:T(8,128)(2,1)} %copy-done.17), calls=%async_computation | async-start | bytes 4194304 | tf_op jit(solution)/shard_map/all_to_all | solution.py:128
  45.1 4.8 copy-start.2
  45.1 120.4 %all-to-all-start.1 = ((bf16[128,48,512]{2,1,0:T(8,128)(2,1)}), bf16[128,48,512]{2,1,0:T(8,128)(2,1)}, u32[]{:S(2)}, u32[]{:S(2)}) async-start(bf16[128,48,512]{2,1,0:T(8,128)(2,1)} %after.7), calls=%async_computation.1 | async-start | bytes 12582912 | tf_op jit(solution)/shard_map/all_to_all | solution.py:128
  49.9 113.4 %collective-permute-start = (bf16[8,16,16,512]{3,2,1,0:T(8,128)(2,1)S(1)}, bf16[8,16,16,512]{3,2,1,0:T(8,128)(2,1)S(1)}, u32[]{:S(2)}, u32[]{:S(2)}) collective-permute-start(bf16[8,16,16,512]{3,2,1,0:T(8,128)(2,1)S(1)} %bitcast.41), channel_id=1, source_target_pairs={{0,8},{1,9},{2,10},{3,11},{4,12},{5,13},{6,14},{7,15},{8,0},{9,1},... | collective-permute-start | bytes 6291464 | tf_op jit(solution)/shard_map/ppermute | solution.py:140
  163.3 1.4 copy-start.8
  165.5 1.6 copy-start.9
  173.8 72.4 %all-to-all-start.2 = ((bf16[128,32,384]{2,1,0:T(8,128)(2,1)}), bf16[128,32,384]{2,1,0:T(8,128)(2,1)S(1)}, u32[]{:S(2)}, u32[]{:S(2)}) async-start(bf16[128,32,384]{2,1,0:T(8,128)(2,1)} %bitcast.78), calls=%async_computation.2 | async-start | bytes 6291456 | tf_op jit(solution)/shard_map/all_to_all | solution.py:128
  179.8 3.0 copy-start.40
  179.8 3.8 copy-start.42
  179.8 3.9 copy-start.43
  182.7 78.2 %collective-permute-start.1 = (bf16[6,16,16,512]{3,2,1,0:T(8,128)(2,1)}, bf16[6,16,16,512]{3,2,1,0:T(8,128)(2,1)}, u32[]{:S(2)}, u32[]{:S(2)}) collective-permute-start(bf16[6,16,16,512]{3,2,1,0:T(8,128)(2,1)} %slice.39), channel_id=1, source_target_pairs={{0,8},{1,9},{2,10},{3,11},{4,12},{5,13},{6,14},{7,15},{8,0},{9,1},... | collective-permute-start | bytes 4718600 | tf_op jit(solution)/shard_map/ppermute | solution.py:140
  246.2 1.7 copy-start
  260.9 7.4 %copy-start.1 = (bf16[128,32,384]{2,1,0:T(8,128)(2,1)S(1)}, bf16[128,32,384]{2,1,0:T(8,128)(2,1)}, u32[]{:S(2)}) copy-start(bf16[128,32,384]{2,1,0:T(8,128)(2,1)} %copy-done) | copy-start | bytes 9437188
  261.9 26.7 %all-to-all-start.3 = ((bf16[128,32,128]{2,1,0:T(8,128)(2,1)}), bf16[128,32,128]{2,1,0:T(8,128)(2,1)}, u32[]{:S(2)}, u32[]{:S(2)}) async-start(bf16[128,32,128]{2,1,0:T(8,128)(2,1)} %copy-done.11), calls=%async_computation.3 | async-start | bytes 2097152 | tf_op jit(solution)/shard_map/all_to_all | solution.py:128
  266.3 2.1 copy-start.20
  266.3 2.1 copy-start.24
  266.3 2.1 copy-start.27
  266.3 2.1 copy-start.30
  268.2 26.6 %collective-permute-start.2 = (bf16[2,16,16,512]{3,2,1,0:T(8,128)(2,1)}, bf16[2,16,16,512]{3,2,1,0:T(8,128)(2,1)S(1)}, u32[]{:S(2)}, u32[]{:S(2)}) collective-permute-start(bf16[2,16,16,512]{3,2,1,0:T(8,128)(2,1)} %after.9), channel_id=1, source_target_pairs={{0,8},{1,9},{2,10},{3,11},{4,12},{5,13},{6,14},{7,15},{8,0},{9,1},... | collective-permute-start | bytes 1572872 | tf_op jit(solution)/shard_map/ppermute | solution.py:140
  293.4 1.5 copy-start.22
  293.4 1.5 copy-start.37
  294.8 46.1 %all-to-all-start.4 = ((bf16[128,32,256]{2,1,0:T(8,128)(2,1)}), bf16[128,32,256]{2,1,0:T(8,128)(2,1)S(1)}, u32[]{:S(2)}, u32[]{:S(2)}) async-start(bf16[128,32,256]{2,1,0:T(8,128)(2,1)} %after.10), calls=%async_computation.4 | async-start | bytes 4194304 | tf_op jit(solution)/shard_map/all_to_all | solution.py:128
  298.6 40.3 %collective-permute-start.3 = (bf16[3,16,16,512]{3,2,1,0:T(8,128)(2,1)}, bf16[3,16,16,512]{3,2,1,0:T(8,128)(2,1)S(1)}, u32[]{:S(2)}, u32[]{:S(2)}) collective-permute-start(bf16[3,16,16,512]{3,2,1,0:T(8,128)(2,1)} %copy-done.22), channel_id=1, source_target_pairs={{0,8},{1,9},{2,10},{3,11},{4,12},{5,13},{6,14},{7,15},{8,0},{9,1},... | collective-permute-start | bytes 2359304 | tf_op jit(solution)/shard_map/ppermute | solution.py:140
  340.9 1.7 copy-start.3
  340.9 1.7 copy-start.13
  342.6 30.6 %all-to-all-start.5 = ((bf16[128,32,128]{2,1,0:T(8,128)(2,1)}), bf16[128,32,128]{2,1,0:T(8,128)(2,1)}, u32[]{:S(2)}, u32[]{:S(2)}) async-start(bf16[128,32,128]{2,1,0:T(8,128)(2,1)} %after.11), calls=%async_computation.5 | async-start | bytes 2097152 | tf_op jit(solution)/shard_map/all_to_all | solution.py:128
  346.8 37.8 %collective-permute-start.4 = (bf16[3,16,16,512]{3,2,1,0:T(8,128)(2,1)}, bf16[3,16,16,512]{3,2,1,0:T(8,128)(2,1)S(1)}, u32[]{:S(2)}, u32[]{:S(2)}) collective-permute-start(bf16[3,16,16,512]{3,2,1,0:T(8,128)(2,1)} %copy-done.36), channel_id=1, source_target_pairs={{0,8},{1,9},{2,10},{3,11},{4,12},{5,13},{6,14},{7,15},{8,0},{9,1},... | collective-permute-start | bytes 2359304 | tf_op jit(solution)/shard_map/ppermute | solution.py:140
  349.1 24.1 %copy-start.21 = (f32[128,1]{1,0:T(8,128)S(1)}, f32[128,1]{1,0:T(8,128)}, u32[]{:S(2)}) copy-start(f32[128,1]{1,0:T(8,128)} %copy.94.ob_ref) | copy-start | bytes 1540
  349.1 24.1 %copy-start.25 = (bf16[128,128]{1,0:T(8,128)(2,1)S(1)}, bf16[128,128]{1,0:T(8,128)(2,1)}, u32[]{:S(2)}) copy-start(bf16[128,128]{1,0:T(8,128)(2,1)} %wo_ref.5) | copy-start | bytes 98308
  349.1 24.1 %copy-start.28 = (bf16[128,128]{0,1:T(8,128)(2,1)S(1)}, bf16[128,128]{0,1:T(8,128)(2,1)}, u32[]{:S(2)}) copy-start(bf16[128,128]{0,1:T(8,128)(2,1)} %copy.85) | copy-start | bytes 98308
  349.1 24.1 %copy-start.31 = (bf16[128,128]{0,1:T(8,128)(2,1)S(1)}, bf16[128,128]{0,1:T(8,128)(2,1)}, u32[]{:S(2)}) copy-start(bf16[128,128]{0,1:T(8,128)(2,1)} %copy.86) | copy-start | bytes 98308
  354.7 1.4 copy-start.10
  384.7 21.4 %copy-start.15 = (bf16[3,16,16,512]{3,2,1,0:T(8,128)(2,1)}, bf16[3,16,16,512]{3,2,1,0:T(8,128)(2,1)S(1)}, u32[]{:S(2)}) copy-start(bf16[3,16,16,512]{3,2,1,0:T(8,128)(2,1)S(1)} %collective-permute-done.4.refs_1_.refs_10_) | copy-start | bytes 2359300
  402.0 4.1 copy-start.4
  402.0 97.7 %copy-start.38 = (bf16[8,16,16,512]{3,2,1,0:T(8,128)(2,1)S(1)}, bf16[8,16,16,512]{3,2,1,0:T(8,128)(2,1)}, u32[]{:S(2)}) copy-start(bf16[8,16,16,512]{3,2,1,0:T(8,128)(2,1)} %get-tuple-element.33) | copy-start | bytes 6291460
  406.1 96.0 %copy-start.5 = (bf16[8,16,16,512]{3,2,1,0:T(8,128)(2,1)}, bf16[8,16,16,512]{3,2,1,0:T(8,128)(2,1)S(1)}, u32[]{:S(2)}) copy-start(bf16[8,16,16,512]{3,2,1,0:T(8,128)(2,1)S(1)} %grad_b.5.refs_1_) | copy-start | bytes 6291460
  406.1 93.6 %collective-permute-start.5 = (bf16[8,16,16,512]{3,2,1,0:T(8,128)(2,1)S(1)}, bf16[8,16,16,512]{3,2,1,0:T(8,128)(2,1)S(1)}, u32[]{:S(2)}, u32[]{:S(2)}) collective-permute-start(bf16[8,16,16,512]{3,2,1,0:T(8,128)(2,1)S(1)} %grad_b.5.refs_1_), channel_id=1, source_target_pairs={{0,8},{1,9},{2,10},{3,11},{4,12},{5,13},{6,14},{7,15},{8,0},{9,1},... | collective-permute-start | bytes 6291464 | tf_op jit(solution)/shard_map/ppermute | solution.py:140
  502.1 50.4 %all-to-all-start.7 = ((bf16[128,16,512]{2,1,0:T(8,128)(2,1)}), bf16[128,16,512]{2,1,0:T(8,128)(2,1)S(1)}, u32[]{:S(2)}, u32[]{:S(2)}) async-start(bf16[128,16,512]{2,1,0:T(8,128)(2,1)} %bitcast.79), calls=%async_computation.7 | async-start | bytes 4194304 | tf_op jit(solution)/shard_map/all_to_all | solution.py:128
  505.8 34.9 %collective-permute-start.6 = (bf16[2,16,16,512]{3,2,1,0:T(8,128)(2,1)}, bf16[2,16,16,512]{3,2,1,0:T(8,128)(2,1)S(1)}, u32[]{:S(2)}, u32[]{:S(2)}) collective-permute-start(bf16[2,16,16,512]{3,2,1,0:T(8,128)(2,1)} %copy-done.37), channel_id=1, source_target_pairs={{0,8},{1,9},{2,10},{3,11},{4,12},{5,13},{6,14},{7,15},{8,0},{9,1},... | collective-permute-start | bytes 1572872 | tf_op jit(solution)/shard_map/ppermute | solution.py:140
  540.6 1.6 copy-start.6
  542.2 1.4 copy-start.16
  552.5 6.2 copy-start.39
  552.5 6.3 copy-start.41
  552.6 6.3 copy-start.33
  552.6 6.3 copy-start.35
  552.6 77.2 %all-to-all-start.8 = ((bf16[128,48,512]{2,1,0:T(8,128)(2,1)}), bf16[128,48,512]{2,1,0:T(8,128)(2,1)}, u32[]{:S(2)}, u32[]{:S(2)}) async-start(bf16[128,48,512]{2,1,0:T(8,128)(2,1)} %bitcast.77), calls=%async_computation.8 | async-start | bytes 12582912 | tf_op jit(solution)/shard_map/all_to_all | solution.py:128
  669.0 14.4 %all-to-all-start.10 = ((bf16[16,8,768]{2,1,0:T(8,128)(2,1)}), bf16[16,8,768]{2,1,0:T(8,128)(2,1)S(1)}, u32[]{:S(2)}, u32[]{:S(2)}) async-start(bf16[16,8,768]{2,1,0:T(8,128)(2,1)} %broadcast_in_dim.23), calls=%async_computation.10 | async-start | bytes 393216 | tf_op jit(solution)/shard_map/all_to_all | solution.py:520
  (12 other events, 11.0 us)

commit v10 on v9

--- a/solution.py
+++ b/solution.py
@@ -603,12 +603,14 @@
         plan, "both", 0, None, x, mask, [(grads, 0), (grads, plan.subs)], [kept], small
     )
     if two:
+        back_1 = after(back_1, grads)
         grad_b = plan.swap(
             joined((grad_b_own[1].astype(F32) + back_1.astype(F32)).astype(BF16))
         )
         side_a = [gain, bias, w_t[: 2 * hidden], jnp.concatenate([first, w_gate], axis=1)]
         side_b = [gain, bias, w_t[2 * hidden :], second]
         base, local_a = make_last(plan, "a", 1, None, x, mask, [(grads, 1)], [kept], side_a)
+        grad_b = after(grad_b, local_ab, local_a)
         (local_b,) = make_last(plan, "b_sum", 1, None, x, mask, [(grad_b, 0)], [], side_b)
         (pair_grad,) = make_last(
             plan, "b", 1, pair_grad, x, mask, [(grad_b, 0)], [base], side_b

time: 687 us -> 623 us (0.907)
  waiting for transfers between devices: 437 us -> 388 us
  blocking collectives: 30.1 us -> 13.4 us
    all_to_all x8 -> x9, waiting for transfers between devices: 164 us -> 124 us  [swap(): lax.all_to_all(array, 'tile', split_axis=0, concat_axis=0, axis_index_gro...]
    all_to_all x1 -> x0, blocking collectives: 17.3 us -> none  [swap(): lax.all_to_all(array, 'tile', split_axis=0, concat_axis=0, axis_index_gro...]
    ppermute x7, waiting for transfers between devices: 273 us -> 264 us  [exchange(): return lax.ppermute(array, 'tile', self.partner)]
    unnamed x91 -> x83, local copies, waits for them, and re-layouts: 25.1 us -> 27.5 us
    all_to_all x8 -> x9, starting transfers between devices: 38.3 us -> 40.3 us  [swap(): lax.all_to_all(array, 'tile', split_axis=0, concat_axis=0, axis_index_gro...]
  transfers between devices with their start and end apart: 16 -> 17, of which waited for: 13 -> 13; matrix products, arithmetic and copies ran while one was open for 1% -> 1% of each run, Pallas kernels for 12% -> 15%
where the time goes in v10:
time: 623 us; the launch traced here: 620 us
  waiting for transfers between devices  388 us (62%)
  Pallas kernels  126 us (20%)
  starting transfers between devices  51.4 us (8%)
  local copies, waits for them, and re-layouts  37.1 us (6%)
  blocking collectives  13.4 us (2%)
    ppermute x7, waiting for transfers between devices, exchange(): return lax.ppermute(array, 'tile', self.partner)  264 us
    all_to_all x9, waiting for transfers between devices, swap(): lax.all_to_all(array, 'tile', split_axis=0, concat_axis=0, axis_index_gro...  124 us
    pallas_call x4, Pallas kernels, make_last(): pl.pallas_call(functools.partial(last_kernel, plan.step, mode), grid=(pla...  42.5 us
    all_to_all x9, starting transfers between devices, swap(): lax.all_to_all(array, 'tile', split_axis=0, concat_axis=0, axis_index_gro...  40.3 us
    pallas_call x3, Pallas kernels, make_middle(): pl.pallas_call(functools.partial(middle_kernel, plan.step), grid_spec=plt...  32.2 us
    unnamed x83, local copies, waits for them, and re-layouts  27.5 us
    pallas_call x2, Pallas kernels, make_factors(): pl.pallas_call(functools.partial(factors_kernel, plan.step, bool(before))...  17.2 us
    all_to_all x1, blocking collectives, swap_all(): lax.all_to_all(array, 'tile', split_axis=0, concat_axis=0, tiled=True)  13.4 us
  transfers between devices with their start and end apart: 17, of which 13 were waited for; matrix products, arithmetic and copies ran while one was open for 1% of the time, Pallas kernels for 15%

profile of v10, /device:TPU:0, one launch (start us, length us, event | category | flops | bytes accessed | tf_op | source)
XLA Modules:
  0.0 620.4 jit_solution(18247882512884758662)
XLA Ops:
  4.2 8.6 %factors.2 = (bf16[128,48,512]{2,1,0:T(8,128)(2,1)}, bf16[128,16,512]{2,1,0:T(8,128)(2,1)S(1)}) custom-call(bf16[32,16,2,16,128]{4,3,2,1,0:T(8,128)(2,1)} %bitcast.65, f32[32,512]{1,0:T(8,128)S(1)} %broadcast_multiply_fusion.mask_ref.refs_1_, f32[128,1]{1,0:T(8,128)S(1)} %copy.85.gain_ref.refs_5_.refs_4_.refs_3_, ...), custom_call_target="tpu_custom_call" | custom-call | flops 200000000 | bytes 600000 | tf_op jit(solution)/shard_map/factors/pallas_call | solution.py:201
  14.1 5.3 all-to-all-start
  19.4 8.6 %factors.3.refs_0_ = bf16[128,48,512]{2,1,0:T(8,128)(2,1)} custom-call(bf16[32,16,2,16,128]{4,3,2,1,0:T(8,128)(2,1)} %bitcast.66, f32[32,512]{1,0:T(8,128)S(1)} %broadcast_multiply_fusion.mask_ref.refs_1_, f32[128,1]{1,0:T(8,128)S(1)} %copy.85.gain_ref.refs_5_.refs_4_.refs_3_, ...), custom_call_target="tpu_custom_call", output_to_operand_aliasing={{}: (5, {})} | custom-call | flops 200000000 | bytes 600000 | tf_op jit(solution)/shard_map/factors/pallas_call | solution.py:201
  28.0 17.1 %all-to-all-done = bf16[128,16,512]{2,1,0:T(8,128)(2,1)S(1)} async-done(((bf16[128,16,512]{2,1,0:T(8,128)(2,1)}), bf16[128,16,512]{2,1,0:T(8,128)(2,1)S(1)}, u32[]{:S(2)}, u32[]{:S(2)}) %all-to-all-start) | async-done | bytes 2097184 | tf_op jit(solution)/shard_map/all_to_all | solution.py:128
  45.1 4.8 all-to-all-start.1
  49.9 2.7 collective-permute-start
  52.6 110.7 %collective-permute-done.refs_2_.refs_3_ = bf16[8,16,16,512]{3,2,1,0:T(8,128)(2,1)S(1)} collective-permute-done((bf16[8,16,16,512]{3,2,1,0:T(8,128)(2,1)S(1)}, bf16[8,16,16,512]{3,2,1,0:T(8,128)(2,1)S(1)}, u32[]{:S(2)}, u32[]{:S(2)}) %collective-permute-start) | collective-permute-done | bytes 2097184 | tf_op jit(solution)/shard_map/ppermute | solution.py:140
  165.5 1.6 copy-done.8
  167.1 6.7 %product.2 = bf16[8,16,32,384]{3,2,1,0:T(8,128)(2,1)} custom-call(bf16[8,16,48,512]{3,2,1,0:T(8,128)(2,1)} %bitcast.10.refs_0_.refs_1_.refs_4_.refs_5_, bf16[8,16,48,512]{3,2,1,0:T(8,128)(2,1)} %bitcast.10.refs_0_.refs_1_.refs_4_.refs_5_, bf16[8,16,16,512]{3,2,1,0:T(8,128)(2,1)S(1)} %copy-done.8, bf16[8,16,16,512]{3,2,1,0:T(8,128)(2,1)} %bitcast.42, ...), custom_call_target="tpu_custom_call" | custom-call | flops 200000000 | bytes 600000 | tf_op jit(solution)/shard_map/product/pallas_call | solution.py:268
  173.8 6.0 all-to-all-start.2
  179.8 2.9 slice.39
  185.2 1.5 copy.88
  186.7 59.4 %all-to-all-done.2.p_ref.refs_1_ = bf16[128,32,384]{2,1,0:T(8,128)(2,1)S(1)} async-done(((bf16[128,32,384]{2,1,0:T(8,128)(2,1)}), bf16[128,32,384]{2,1,0:T(8,128)(2,1)S(1)}, u32[]{:S(2)}, u32[]{:S(2)}) %all-to-all-start.2) | async-done | bytes 3145760 | tf_op jit(solution)/shard_map/all_to_all | solution.py:128
  246.1 1.7 copy-done
  250.9 8.7 %middle.3 = (bf16[128,32,128]{2,1,0:T(8,128)(2,1)S(1)}, bf16[32,128,512]{2,1,0:T(8,128)(2,1)}, f32[128,128]{1,0:T(8,128)S(1)}, f32[128,128]{1,0:T(8,128)S(1)}) custom-call(s32[1,2]{1,0:T(1,128)S(1)} %fusion.7._, bf16[32,16,2,16,128]{4,3,2,1,0:T(8,128)(2,1)} %bitcast.67, bf16[32,16,2,16,128]{4,3,2,1,0:T(8,128)(2,1)} %bitcast.74, ...), custom_call_target="tpu_custom_call" | custom-call | flops 200000000 | bytes 600000 | tf_op jit(solution)/shard_map/middle/pallas_call | solution.py:382
  261.9 4.4 all-to-all-start.3
  266.3 2.0 slice.40.refs_0_
  269.1 14.9 %middle.4 = (bf16[128,32,256]{2,1,0:T(8,128)(2,1)S(1)}, bf16[32,128,512]{2,1,0:T(8,128)(2,1)}, f32[128,128]{1,0:T(8,128)S(1)}, f32[128,128]{1,0:T(8,128)S(1)}) custom-call(s32[2,2]{1,0:T(2,128)S(1)} %pad_add_fusion._, bf16[32,16,2,16,128]{4,3,2,1,0:T(8,128)(2,1)} %bitcast.68, ...), custom_call_target="tpu_custom_call", output_to_operand_aliasing={{1}: (11, {})} | custom-call | flops 200000000 | bytes 600000 | tf_op jit(solution)/shard_map/middle/pallas_call | solution.py:382
  285.3 3.2 all-to-all-done.3
  288.5 3.8 grad_b.3
  293.2 1.7 collective-permute-done.2.refs_3_.refs_7_
  295.8 3.8 all-to-all-start.4
  300.0 5.0 product.3
  305.0 34.8 %collective-permute-done.3.refs_2_.refs_9_ = bf16[3,16,16,512]{3,2,1,0:T(8,128)(2,1)S(1)} collective-permute-done((bf16[3,16,16,512]{3,2,1,0:T(8,128)(2,1)}, bf16[3,16,16,512]{3,2,1,0:T(8,128)(2,1)S(1)}, u32[]{:S(2)}, u32[]{:S(2)}) %collective-permute-start.3) | collective-permute-done | bytes 786464 | tf_op jit(solution)/shard_map/ppermute | solution.py:140
  341.9 1.7 copy-done.12
  343.6 3.7 all-to-all-start.5
  347.3 2.1 collective-permute-start.4
  349.4 5.5 grad_b.4
  356.4 17.0 %all-to-all-done.5.p_ref = bf16[128,32,128]{2,1,0:T(8,128)(2,1)S(1)} async-done(((bf16[128,32,128]{2,1,0:T(8,128)(2,1)}), bf16[128,32,128]{2,1,0:T(8,128)(2,1)S(1)}, u32[]{:S(2)}, u32[]{:S(2)}) %all-to-all-start.5) | async-done | bytes 1048608 | tf_op jit(solution)/shard_map/all_to_all | solution.py:128
  373.4 8.6 %middle.5 = (bf16[128,32,128]{2,1,0:T(8,128)(2,1)}, bf16[32,128,512]{2,1,0:T(8,128)(2,1)}, f32[128,128]{1,0:T(8,128)S(1)}, f32[128,128]{1,0:T(8,128)S(1)}) custom-call(s32[1,2]{1,0:T(1,128)S(1)} %fusion.5._, bf16[32,16,2,16,128]{4,3,2,1,0:T(8,128)(2,1)} %bitcast.69, bf16[32,16,2,16,128]{4,3,2,1,0:T(8,128)(2,1)} %bitcast.76, ...), custom_call_target="tpu_custom_call", output_to_operand_aliasing={{1}: (11, {})} | custom-call | flops 200000000 | bytes 600000 | tf_op jit(solution)/shard_map/middle/pallas_call | solution.py:382
  382.0 3.2 collective-permute-done.4.refs_1_.refs_10_
  385.3 3.6 all-to-all-start.6
  388.8 2.2 collective-permute-start.6
  391.0 23.4 %all-to-all-done.6 = bf16[128,32,128]{2,1,0:T(8,128)(2,1)S(1)} async-done(((bf16[128,32,128]{2,1,0:T(8,128)(2,1)}), bf16[128,32,128]{2,1,0:T(8,128)(2,1)S(1)}, u32[]{:S(2)}, u32[]{:S(2)}) %all-to-all-start.6) | async-done | bytes 1048608 | tf_op jit(solution)/shard_map/all_to_all | solution.py:128
  414.4 4.0 grad_b.5.refs_1_
  420.1 8.9 %grad_a.1 = bf16[8,16,48,512]{3,2,1,0:T(8,128)(2,1)} custom-call(bf16[8,16,32,128]{3,2,1,0:T(8,128)(2,1)} %bitcast.18.g_ref.refs_1_.refs_0_, bf16[8,16,32,256]{3,2,1,0:T(8,128)(2,1)} %bitcast.46, bf16[8,16,32,128]{3,2,1,0:T(8,128)(2,1)} %bitcast.48, bf16[8,16,16,512]{3,2,1,0:T(8,128)(2,1)} %copy-done.7, bf16[8,16,16,512]{3,2,1,0:T(8,128)(2,1)} %bitcast.43, ...), custom_call_target="tpu_custom_call" | custom-call | flops 200000000 | bytes 600000 | tf_op jit(solution)/shard_map/grad_a/pallas_call | solution.py:324
  429.0 4.8 all-to-all-start.7
  433.9 113.4 %collective-permute-done.5.refs_0_ = bf16[8,16,16,512]{3,2,1,0:T(8,128)(2,1)S(1)} collective-permute-done((bf16[8,16,16,512]{3,2,1,0:T(8,128)(2,1)}, bf16[8,16,16,512]{3,2,1,0:T(8,128)(2,1)S(1)}, u32[]{:S(2)}, u32[]{:S(2)}) %collective-permute-start.5) | collective-permute-done | bytes 2097184 | tf_op jit(solution)/shard_map/ppermute | solution.py:140
  547.3 2.1 all-to-all-done.7.refs_1_.refs_2_.refs_3_
  549.4 1.6 copy-done.35
  551.0 2.3 add_convert_fusion
  553.3 4.0 all-to-all-start.8
  557.4 14.7 %last_both.1 = (bf16[32,16,2,16,128]{4,3,2,1,0:T(8,128)(2,1)}, f32[128,512]{1,0:T(8,128)S(1)}) custom-call(bf16[32,16,2,16,128]{4,3,2,1,0:T(8,128)(2,1)} %bitcast.70, f32[32,512]{1,0:T(8,128)S(1)} %broadcast_multiply_fusion.mask_ref.refs_1_, bf16[128,48,512]{2,1,0:T(8,128)(2,1)} %all-to-all-done.7.refs_1_.refs_2_.refs_3_, ...), custom_call_target="tpu_custom_call" | custom-call | flops 200000000 | bytes 600000 | tf_op jit(solution)/shard_map/last_both/pallas_call | solution.py:505
  572.2 9.7 %last_a.1 = (bf16[16,128,512]{2,1,0:T(8,128)(2,1)S(1)}, f32[128,256]{1,0:T(8,128)S(1)}) custom-call(bf16[32,16,2,16,128]{4,3,2,1,0:T(8,128)(2,1)} %bitcast.71, f32[32,512]{1,0:T(8,128)S(1)} %broadcast_multiply_fusion.mask_ref.refs_1_, bf16[128,48,512]{2,1,0:T(8,128)(2,1)} %all-to-all-done.7.refs_1_.refs_2_.refs_3_, ...), custom_call_target="tpu_custom_call" | custom-call | flops 200000000 | bytes 600000 | tf_op jit(solution)/shard_map/last_a/pallas_call | solution.py:505
  583.2 7.2 %last_b_sum.1 = f32[128,256]{1,0:T(8,128)S(1)} custom-call(bf16[32,16,2,16,128]{4,3,2,1,0:T(8,128)(2,1)} %bitcast.72, f32[32,512]{1,0:T(8,128)S(1)} %broadcast_multiply_fusion.mask_ref.refs_1_, bf16[128,16,512]{2,1,0:T(8,128)(2,1)S(1)} %after.17.refs_2_, f32[128,1]{1,0:T(8,128)S(1)} %copy.85.gain_ref.refs_5_.refs_4_.refs_3_, ...), custom_call_target="tpu_custom_call" | custom-call | flops 200000000 | bytes 600000 | tf_op jit(solution)/shard_map/last_b_sum/pallas_call | solution.py:505
  590.5 13.4 %all_to_all.57 = bf16[16,8,768]{2,1,0:T(8,128)(2,1)S(1)} all-to-all(bf16[16,8,768]{2,1,0:T(8,128)(2,1)S(1)} %pad_maximum_fusion), channel_id=1, replica_groups=mesh['crops'=2,'tile'=16] {'tile'}, dimensions={0} | all-to-all | bytes 393216 | tf_op jit(solution)/shard_map/all_to_all | solution.py:520
  604.6 3.5 all-to-all-start.10
  608.2 10.9 %last_b.1 = bf16[32,16,2,16,128]{4,3,2,1,0:T(8,128)(2,1)} custom-call(bf16[32,16,2,16,128]{4,3,2,1,0:T(8,128)(2,1)} %bitcast.73, f32[32,512]{1,0:T(8,128)S(1)} %broadcast_multiply_fusion.mask_ref.refs_1_, bf16[128,16,512]{2,1,0:T(8,128)(2,1)S(1)} %after.17.refs_2_, bf16[16,128,512]{2,1,0:T(8,128)(2,1)} %copy-done.15, ...), custom_call_target="tpu_custom_call", output_to_operand_aliasing={{}: (8, {})} | custom-call | flops 200000000 | bytes 600000 | tf_op jit(solution)/shard_map/last_b/pallas_call | solution.py:505
  (123 shorter events, 28.1 us)
Async XLA Ops:
  12.8 1.3 copy-start.14
  14.1 31.0 %all-to-all-start = ((bf16[128,16,512]{2,1,0:T(8,128)(2,1)}), bf16[128,16,512]{2,1,0:T(8,128)(2,1)S(1)}, u32[]{:S(2)}, u32[]{:S(2)}) async-start(bf16[128,16,512]{2,1,0:T(8,128)(2,1)} %copy-done.14), calls=%async_computation | async-start | bytes 4194304 | tf_op jit(solution)/shard_map/all_to_all | solution.py:128
  45.1 4.8 copy-start.2
  45.1 120.4 %all-to-all-start.1 = ((bf16[128,48,512]{2,1,0:T(8,128)(2,1)}), bf16[128,48,512]{2,1,0:T(8,128)(2,1)}, u32[]{:S(2)}, u32[]{:S(2)}) async-start(bf16[128,48,512]{2,1,0:T(8,128)(2,1)} %after.9), calls=%async_computation.1 | async-start | bytes 12582912 | tf_op jit(solution)/shard_map/all_to_all | solution.py:128
  49.9 113.4 %collective-permute-start = (bf16[8,16,16,512]{3,2,1,0:T(8,128)(2,1)S(1)}, bf16[8,16,16,512]{3,2,1,0:T(8,128)(2,1)S(1)}, u32[]{:S(2)}, u32[]{:S(2)}) collective-permute-start(bf16[8,16,16,512]{3,2,1,0:T(8,128)(2,1)S(1)} %bitcast.41), channel_id=1, source_target_pairs={{0,8},{1,9},{2,10},{3,11},{4,12},{5,13},{6,14},{7,15},{8,0},{9,1},... | collective-permute-start | bytes 6291464 | tf_op jit(solution)/shard_map/ppermute | solution.py:140
  163.3 1.4 copy-start.7
  165.5 1.6 copy-start.8
  173.8 72.4 %all-to-all-start.2 = ((bf16[128,32,384]{2,1,0:T(8,128)(2,1)}), bf16[128,32,384]{2,1,0:T(8,128)(2,1)S(1)}, u32[]{:S(2)}, u32[]{:S(2)}) async-start(bf16[128,32,384]{2,1,0:T(8,128)(2,1)} %bitcast.78), calls=%async_computation.2 | async-start | bytes 6291456 | tf_op jit(solution)/shard_map/all_to_all | solution.py:128
  179.8 3.1 copy-start.38
  179.8 3.2 copy-start.39
  182.7 78.1 %collective-permute-start.1 = (bf16[6,16,16,512]{3,2,1,0:T(8,128)(2,1)}, bf16[6,16,16,512]{3,2,1,0:T(8,128)(2,1)}, u32[]{:S(2)}, u32[]{:S(2)}) collective-permute-start(bf16[6,16,16,512]{3,2,1,0:T(8,128)(2,1)} %slice.39), channel_id=1, source_target_pairs={{0,8},{1,9},{2,10},{3,11},{4,12},{5,13},{6,14},{7,15},{8,0},{9,1},... | collective-permute-start | bytes 4718600 | tf_op jit(solution)/shard_map/ppermute | solution.py:140
  246.1 1.7 copy-start
  260.8 7.4 %copy-start.1 = (bf16[128,32,384]{2,1,0:T(8,128)(2,1)S(1)}, bf16[128,32,384]{2,1,0:T(8,128)(2,1)}, u32[]{:S(2)}) copy-start(bf16[128,32,384]{2,1,0:T(8,128)(2,1)} %copy-done) | copy-start | bytes 9437188
  260.8 1.0 copy-start.10
  261.9 26.6 %all-to-all-start.3 = ((bf16[128,32,128]{2,1,0:T(8,128)(2,1)}), bf16[128,32,128]{2,1,0:T(8,128)(2,1)}, u32[]{:S(2)}, u32[]{:S(2)}) async-start(bf16[128,32,128]{2,1,0:T(8,128)(2,1)} %copy-done.10), calls=%async_computation.3 | async-start | bytes 2097152 | tf_op jit(solution)/shard_map/all_to_all | solution.py:128
  268.2 0.8 copy-start.24
  268.2 26.7 %collective-permute-start.2 = (bf16[2,16,16,512]{3,2,1,0:T(8,128)(2,1)}, bf16[2,16,16,512]{3,2,1,0:T(8,128)(2,1)S(1)}, u32[]{:S(2)}, u32[]{:S(2)}) collective-permute-start(bf16[2,16,16,512]{3,2,1,0:T(8,128)(2,1)} %after.11), channel_id=1, source_target_pairs={{0,8},{1,9},{2,10},{3,11},{4,12},{5,13},{6,14},{7,15},{8,0},{9,1},... | collective-permute-start | bytes 1572872 | tf_op jit(solution)/shard_map/ppermute | solution.py:140
  284.0 1.3 copy-start.6
  292.3 0.9 copy-start.33
  293.2 1.7 copy-start.34
  294.9 0.9 copy-start.19
  295.8 46.1 %all-to-all-start.4 = ((bf16[128,32,256]{2,1,0:T(8,128)(2,1)}), bf16[128,32,256]{2,1,0:T(8,128)(2,1)S(1)}, u32[]{:S(2)}, u32[]{:S(2)}) async-start(bf16[128,32,256]{2,1,0:T(8,128)(2,1)} %after.12), calls=%async_computation.4 | async-start | bytes 4194304 | tf_op jit(solution)/shard_map/all_to_all | solution.py:128
  299.6 40.3 %collective-permute-start.3 = (bf16[3,16,16,512]{3,2,1,0:T(8,128)(2,1)}, bf16[3,16,16,512]{3,2,1,0:T(8,128)(2,1)S(1)}, u32[]{:S(2)}, u32[]{:S(2)}) collective-permute-start(bf16[3,16,16,512]{3,2,1,0:T(8,128)(2,1)} %copy-done.19), channel_id=1, source_target_pairs={{0,8},{1,9},{2,10},{3,11},{4,12},{5,13},{6,14},{7,15},{8,0},{9,1},... | collective-permute-start | bytes 2359304 | tf_op jit(solution)/shard_map/ppermute | solution.py:140
  339.9 0.9 copy-start.11
  341.9 1.7 copy-start.3
  341.9 1.7 copy-start.12
  343.6 29.8 %all-to-all-start.5 = ((bf16[128,32,128]{2,1,0:T(8,128)(2,1)}), bf16[128,32,128]{2,1,0:T(8,128)(2,1)S(1)}, u32[]{:S(2)}, u32[]{:S(2)}) async-start(bf16[128,32,128]{2,1,0:T(8,128)(2,1)} %after.13), calls=%async_computation.5 | async-start | bytes 2097152 | tf_op jit(solution)/shard_map/all_to_all | solution.py:128
  347.3 38.0 %collective-permute-start.4 = (bf16[3,16,16,512]{3,2,1,0:T(8,128)(2,1)}, bf16[3,16,16,512]{3,2,1,0:T(8,128)(2,1)S(1)}, u32[]{:S(2)}, u32[]{:S(2)}) collective-permute-start(bf16[3,16,16,512]{3,2,1,0:T(8,128)(2,1)} %copy-done.33), channel_id=1, source_target_pairs={{0,8},{1,9},{2,10},{3,11},{4,12},{5,13},{6,14},{7,15},{8,0},{9,1},... | collective-permute-start | bytes 2359304 | tf_op jit(solution)/shard_map/ppermute | solution.py:140
  349.4 24.0 %copy-start.18 = (f32[128,1]{1,0:T(8,128)S(1)}, f32[128,1]{1,0:T(8,128)}, u32[]{:S(2)}) copy-start(f32[128,1]{1,0:T(8,128)} %copy.96.ob_ref) | copy-start | bytes 1540
  349.4 24.0 %copy-start.22 = (bf16[128,128]{1,0:T(8,128)(2,1)S(1)}, bf16[128,128]{1,0:T(8,128)(2,1)}, u32[]{:S(2)}) copy-start(bf16[128,128]{1,0:T(8,128)(2,1)} %wo_ref.5) | copy-start | bytes 98308
  349.4 24.0 %copy-start.25 = (bf16[128,128]{0,1:T(8,128)(2,1)S(1)}, bf16[128,128]{0,1:T(8,128)(2,1)}, u32[]{:S(2)}) copy-start(bf16[128,128]{0,1:T(8,128)(2,1)} %copy.87) | copy-start | bytes 98308
  349.4 24.0 %copy-start.28 = (bf16[128,128]{0,1:T(8,128)(2,1)S(1)}, bf16[128,128]{0,1:T(8,128)(2,1)}, u32[]{:S(2)}) copy-start(bf16[128,128]{0,1:T(8,128)(2,1)} %copy.88) | copy-start | bytes 98308
  355.0 1.4 copy-start.9
  385.3 29.2 %all-to-all-start.6 = ((bf16[128,32,128]{2,1,0:T(8,128)(2,1)}), bf16[128,32,128]{2,1,0:T(8,128)(2,1)S(1)}, u32[]{:S(2)}, u32[]{:S(2)}) async-start(bf16[128,32,128]{2,1,0:T(8,128)(2,1)} %after.14), calls=%async_computation.6 | async-start | bytes 2097152 | tf_op jit(solution)/shard_map/all_to_all | solution.py:128
  388.8 29.7 %collective-permute-start.6 = (bf16[2,16,16,512]{3,2,1,0:T(8,128)(2,1)}, bf16[2,16,16,512]{3,2,1,0:T(8,128)(2,1)S(1)}, u32[]{:S(2)}, u32[]{:S(2)}) collective-permute-start(bf16[2,16,16,512]{3,2,1,0:T(8,128)(2,1)} %copy-done.34), channel_id=1, source_target_pairs={{0,8},{1,9},{2,10},{3,11},{4,12},{5,13},{6,14},{7,15},{8,0},{9,1},... | collective-permute-start | bytes 1572872 | tf_op jit(solution)/shard_map/ppermute | solution.py:140
  414.4 4.0 copy-start.4
  418.5 1.6 copy-start.13
  418.5 1.3 copy-start.5
  429.0 120.4 %all-to-all-start.7 = ((bf16[128,48,512]{2,1,0:T(8,128)(2,1)}), bf16[128,48,512]{2,1,0:T(8,128)(2,1)}, u32[]{:S(2)}, u32[]{:S(2)}) async-start(bf16[128,48,512]{2,1,0:T(8,128)(2,1)} %bitcast.77), calls=%async_computation.7 | async-start | bytes 12582912 | tf_op jit(solution)/shard_map/all_to_all | solution.py:128
  433.8 113.5 %collective-permute-start.5 = (bf16[8,16,16,512]{3,2,1,0:T(8,128)(2,1)}, bf16[8,16,16,512]{3,2,1,0:T(8,128)(2,1)S(1)}, u32[]{:S(2)}, u32[]{:S(2)}) collective-permute-start(bf16[8,16,16,512]{3,2,1,0:T(8,128)(2,1)} %copy-done.5), channel_id=1, source_target_pairs={{0,8},{1,9},{2,10},{3,11},{4,12},{5,13},{6,14},{7,15},{8,0},{9,1},... | collective-permute-start | bytes 6291464 | tf_op jit(solution)/shard_map/ppermute | solution.py:140
  549.4 1.6 copy-start.35
  553.3 4.0 copy-start.36
  553.3 4.0 copy-start.37
  553.3 4.1 copy-start.30
  553.3 4.1 copy-start.32
  553.3 29.9 %all-to-all-start.8 = ((bf16[128,16,512]{2,1,0:T(8,128)(2,1)}), bf16[128,16,512]{2,1,0:T(8,128)(2,1)S(1)}, u32[]{:S(2)}, u32[]{:S(2)}) async-start(bf16[128,16,512]{2,1,0:T(8,128)(2,1)} %bitcast.79), calls=%async_computation.8 | async-start | bytes 4194304 | tf_op jit(solution)/shard_map/all_to_all | solution.py:128
  581.9 1.3 copy-start.15
  604.6 14.4 %all-to-all-start.10 = ((bf16[16,8,768]{2,1,0:T(8,128)(2,1)}), bf16[16,8,768]{2,1,0:T(8,128)(2,1)S(1)}, u32[]{:S(2)}, u32[]{:S(2)}) async-start(bf16[16,8,768]{2,1,0:T(8,128)(2,1)} %broadcast_in_dim.23), calls=%async_computation.10 | async-start | bytes 393216 | tf_op jit(solution)/shard_map/all_to_all | solution.py:520
  (9 other events, 6.9 us)

commit v11 on v10

--- a/solution.py
+++ b/solution.py
@@ -157,7 +157,7 @@
     )(value, *others)
 
 
-def factors_kernel(step, joint, x_ref, mask_ref, gain_ref, bias_ref, w_ref, *refs):
+def factors_kernel(step, joint, x_ref, mask_ref, norm_ref, w_ref, *refs):
     sa_ref, sb_ref = refs[-2:]
     rows = x_ref.shape[0]
     hidden = w_ref.shape[0] // 4
@@ -166,7 +166,7 @@
     def _(turn):
         row = pl.multiple_of(turn * step, step)
         z_hat, _ = stats(turned(x_ref, row, step))
-        normed = (z_hat * gain_ref[...] + bias_ref[...]).astype(BF16)
+        normed = (z_hat * norm_ref[:, 0:1] + norm_ref[:, 1:2]).astype(BF16)
         mask = flat_rows(mask_ref, row, step)
         proj = dot(w_ref[...], normed)
         value_a, gate_a = proj[:hidden], proj[hidden : 2 * hidden]
@@ -182,7 +182,7 @@
         gather_out(sb_ref, refs[-3], rows)
 
 
-def make_factors(plan, sub, before, x, mask, gain, bias, w_t):
+def make_factors(plan, sub, before, x, mask, norms, w_t):
     chans = x.shape[-1]
     hidden = w_t.shape[0] // 4
     block = (hidden, plan.rows, plan.width)
@@ -204,19 +204,18 @@
         in_specs=[
             plan.pair_spec(chans, lambda j: (sub, j % 2, j // 2, 0, 0)),
             pl.BlockSpec((plan.rows, plan.width), lambda j: (sub, j)),
-            whole(gain),
-            whole(bias),
+            whole(norms),
             whole(w_t),
         ]
         + [HELD for _ in before],
         out_specs=out_specs,
         out_shape=out_shape,
-        input_output_aliases={5: 0} if before else {},
+        input_output_aliases={4: 0} if before else {},
         scratch_shapes=[plan.scratch(hidden)] * 2,
         compiler_params=params(1),
         cost_estimate=cost(0.2),
         name="factors",
-    )(x, mask, gain, bias, w_t, *before)
+    )(x, mask, norms, w_t, *before)
 
 
 def matrix(refs, chan):
@@ -336,7 +335,7 @@
 
 
 def middle_kernel(
-    step, _, x_ref, d_ref, p_ref, gain_ref, bias_ref, wg_ref, og_ref, ob_ref, wo_ref, wot_ref, *refs
+    step, _, x_ref, d_ref, p_ref, norm_ref, wg_ref, wo_ref, wot_ref, *refs
 ):
     g_ref, gb_ref, gwo_ref, gwg_ref, s_ref = refs[-5:]
     rows = x_ref.shape[0]
@@ -353,15 +352,15 @@
     def _(turn):
         row = pl.multiple_of(turn * step, step)
         z_hat, _ = stats(turned(x_ref, row, step))
-        normed = (z_hat * gain_ref[...] + bias_ref[...]).astype(BF16)
+        normed = (z_hat * norm_ref[:, 0:1] + norm_ref[:, 1:2]).astype(BF16)
         gate = sigmoid(dot(wg_ref[...], normed))
         x_hat, inv_std = stats(load_rows(s_ref, row, step, rows))
-        x_norm = (x_hat * og_ref[...] + ob_ref[...]).astype(BF16)
+        x_norm = (x_hat * norm_ref[:, 2:3] + norm_ref[:, 3:4]).astype(BF16)
         out_lin = dot(wot_ref[...], x_norm)
         lin = turned(d_ref, row, step) * gate
         grad_lin = lin.astype(BF16)
         gate_back = (lin * out_lin * (1.0 - gate)).astype(BF16)
-        upstream = dot(wo_ref[...], grad_lin) * og_ref[...]
+        upstream = dot(wo_ref[...], grad_lin) * norm_ref[:, 2:3]
         store_rows(s_ref, row, step, rows, norm_back(upstream, x_hat, inv_std))
         for at in range(step):
             gb_ref[row + at] = gate_back[:, at * width : (at + 1) * width]
@@ -416,7 +415,7 @@
     grads = [next(rest) for _ in sides]
     gate_ref = next(rest) if gated else None
     base_ref = next(rest) if based else None
-    gain_ref, bias_ref, wt_ref, wcat_ref, *outs = rest
+    norm_ref, wt_ref, wcat_ref, *outs = rest
     gw_ref = outs[-1]
     out_ref = outs[-1 - summed] if out_kind else None
     rows, _, _, _, _ = x_ref.shape
@@ -436,7 +435,7 @@
     def _(turn):
         row = pl.multiple_of(turn * step, step)
         z_hat, inv_in = stats(turned(x_ref, row, step))
-        normed = (z_hat * gain_ref[...] + bias_ref[...]).astype(BF16)
+        normed = (z_hat * norm_ref[:, 0:1] + norm_ref[:, 1:2]).astype(BF16)
         mask = flat_rows(mask_ref, row, step)
         proj = dot(wt_ref[...], normed)
         parts = []
@@ -459,7 +458,7 @@
                     [base_ref[row + at].astype(F32) for at in range(step)], axis=1
                 )
             if out_kind == "pair":
-                grad = norm_back(upstream * gain_ref[...], z_hat, inv_in).T.astype(BF16)
+                grad = norm_back(upstream * norm_ref[:, 0:1], z_hat, inv_in).T.astype(BF16)
                 out_ref[pl.ds(row, step)] = grad.reshape((step,) + out_ref.shape[1:])
             else:
                 for at in range(step):
@@ -540,10 +539,10 @@
     own_valid = lax.dynamic_slice_in_dim(valid, me * count, count)
     turned_valid = valid.reshape(tiles, plan.subs, plan.rows).transpose(1, 0, 2).reshape(crop)
     mask = own_valid[:, None] * turned_valid[None, :]
-    gain, bias = ln_in_gain[:, None], ln_in_bias[:, None]
+    norms = jnp.stack([ln_in_gain, ln_in_bias, ln_out_gain, ln_out_bias], axis=1)
     w_t = w_ab.T
     w_cat = jnp.concatenate([w_ab, w_gate], axis=1)
-    mid = [gain, bias, w_gate.T, ln_out_gain[:, None], ln_out_bias[:, None], w_out, w_out.T]
+    mid = [norms, w_gate.T, w_out, w_out.T]
     x, d = plan.view(x), plan.view(d)
     owned = lambda array: array.reshape(plan.half, hidden // plan.half, *array.shape[1:])
     joined = lambda array: array.reshape(hidden, *array.shape[2:])
@@ -552,7 +551,7 @@
     plan_cut = plan.cut
     two = plan.subs == 2
     cut_b, back_a = plan_cut(6, 2), plan_cut(3, 3, 2)
-    small = [gain, bias, w_t, w_cat]
+    small = [norms, w_t, w_cat]
 
     def middle(at, first, before, ready, product):
         table = jnp.stack([jnp.stack([half, jnp.int32(sub)]) for half, sub in at])
@@ -562,10 +561,10 @@
     def product_of(b):
         return plan.swap(joined(make_product(plan, own_a, b)))
 
-    held, factor_b0 = make_factors(plan, 0, (), x, mask, gain, bias, w_t)
+    held, factor_b0 = make_factors(plan, 0, (), x, mask, norms, w_t)
     own_b0 = owned(plan.swap(factor_b0))
     if two:
-        (held,) = make_factors(plan, 1, (held,), x, mask, gain, bias, w_t)
+        (held,) = make_factors(plan, 1, (held,), x, mask, norms, w_t)
     other_0 = plan.exchange(own_b0)
     own_ab = owned(plan.swap(after(held, own_b0)))
     own_a, own_b, got_b = [(own_ab, 0)], [(own_b0, 0)], []
@@ -607,8 +606,8 @@
         grad_b = plan.swap(
             joined((grad_b_own[1].astype(F32) + back_1.astype(F32)).astype(BF16))
         )
-        side_a = [gain, bias, w_t[: 2 * hidden], jnp.concatenate([first, w_gate], axis=1)]
-        side_b = [gain, bias, w_t[2 * hidden :], second]
+        side_a = [norms, w_t[: 2 * hidden], jnp.concatenate([first, w_gate], axis=1)]
+        side_b = [norms, w_t[2 * hidden :], second]
         base, local_a = make_last(plan, "a", 1, None, x, mask, [(grads, 1)], [kept], side_a)
         grad_b = after(grad_b, local_ab, local_a)
         (local_b,) = make_last(plan, "b_sum", 1, None, x, mask, [(grad_b, 0)], [], side_b)

time: 623 us -> 618 us (level)
  local copies, waits for them, and re-layouts: 37.1 us -> 28.3 us
    unnamed x83 -> x57, local copies, waits for them, and re-layouts: 27.5 us -> 21 us
where the time goes in v11:
time: 618 us; the launch traced here: 616 us
  waiting for transfers between devices  393 us (64%)
  Pallas kernels  125 us (20%)
  starting transfers between devices  51.3 us (8%)
  local copies, waits for them, and re-layouts  28.3 us (5%)
  blocking collectives  13.4 us (2%)
    ppermute x7, waiting for transfers between devices, exchange(): return lax.ppermute(array, 'tile', self.partner)  264 us
    all_to_all x9, waiting for transfers between devices, swap(): lax.all_to_all(array, 'tile', split_axis=0, concat_axis=0, axis_index_gro...  129 us
    pallas_call x4, Pallas kernels, make_last(): pl.pallas_call(functools.partial(last_kernel, plan.step, mode), grid=(pla...  42.1 us
    all_to_all x9, starting transfers between devices, swap(): lax.all_to_all(array, 'tile', split_axis=0, concat_axis=0, axis_index_gro...  40.2 us
    pallas_call x3, Pallas kernels, make_middle(): pl.pallas_call(functools.partial(middle_kernel, plan.step), grid_spec=plt...  32.2 us
    unnamed x57, local copies, waits for them, and re-layouts  21 us
    pallas_call x2, Pallas kernels, make_factors(): pl.pallas_call(functools.partial(factors_kernel, plan.step, bool(before))...  17 us
    all_to_all x1, blocking collectives, swap_all(): lax.all_to_all(array, 'tile', split_axis=0, concat_axis=0, tiled=True)  13.4 us
  transfers between devices with their start and end apart: 17, of which 13 were waited for; matrix products, arithmetic and copies ran while one was open for 1% of the time, Pallas kernels for 15%

profile of v11, /device:TPU:0, one launch (start us, length us, event | category | flops | bytes accessed | tf_op | source)
XLA Modules:
  0.0 616.1 jit_solution(7464853337202677004)
XLA Ops:
  3.5 8.5 %factors.2 = (bf16[128,48,512]{2,1,0:T(8,128)(2,1)}, bf16[128,16,512]{2,1,0:T(8,128)(2,1)S(1)}) custom-call(bf16[32,16,2,16,128]{4,3,2,1,0:T(8,128)(2,1)} %bitcast.65, f32[32,512]{1,0:T(8,128)S(1)} %broadcast_multiply_fusion.mask_ref.refs_1_, f32[128,4]{1,0:T(8,128)S(1)} %copy.52.norm_ref.refs_5_.refs_4_.refs_3_, bf16[512,128]{1,0:T(8,128)(2,1)S(1)} %bitcast.49), custom_call_target="tpu_custom_call" | custom-call | flops 200000000 | bytes 600000 | tf_op jit(solution)/shard_map/factors/pallas_call | solution.py:201
  13.4 5.3 all-to-all-start
  18.6 8.5 %factors.3.refs_0_ = bf16[128,48,512]{2,1,0:T(8,128)(2,1)} custom-call(bf16[32,16,2,16,128]{4,3,2,1,0:T(8,128)(2,1)} %bitcast.66, f32[32,512]{1,0:T(8,128)S(1)} %broadcast_multiply_fusion.mask_ref.refs_1_, f32[128,4]{1,0:T(8,128)S(1)} %copy.52.norm_ref.refs_5_.refs_4_.refs_3_, bf16[512,128]{1,0:T(8,128)(2,1)S(1)} %bitcast.50, ...), custom_call_target="tpu_custom_call", output_to_operand_aliasing={{}: (4, {})} | custom-call | flops 200000000 | bytes 600000 | tf_op jit(solution)/shard_map/factors/pallas_call | solution.py:201
  27.1 17.2 %all-to-all-done = bf16[128,16,512]{2,1,0:T(8,128)(2,1)S(1)} async-done(((bf16[128,16,512]{2,1,0:T(8,128)(2,1)}), bf16[128,16,512]{2,1,0:T(8,128)(2,1)S(1)}, u32[]{:S(2)}, u32[]{:S(2)}) %all-to-all-start) | async-done | bytes 2097184 | tf_op jit(solution)/shard_map/all_to_all | solution.py:128
  44.3 4.8 all-to-all-start.1
  49.1 2.6 collective-permute-start
  51.8 110.7 %collective-permute-done.refs_2_.refs_3_ = bf16[8,16,16,512]{3,2,1,0:T(8,128)(2,1)S(1)} collective-permute-done((bf16[8,16,16,512]{3,2,1,0:T(8,128)(2,1)S(1)}, bf16[8,16,16,512]{3,2,1,0:T(8,128)(2,1)S(1)}, u32[]{:S(2)}, u32[]{:S(2)}) %collective-permute-start) | collective-permute-done | bytes 2097184 | tf_op jit(solution)/shard_map/ppermute | solution.py:140
  164.7 1.6 copy-done.8
  166.3 6.7 %product.2 = bf16[8,16,32,384]{3,2,1,0:T(8,128)(2,1)} custom-call(bf16[8,16,48,512]{3,2,1,0:T(8,128)(2,1)} %bitcast.12.refs_0_.refs_1_.refs_4_.refs_5_, bf16[8,16,48,512]{3,2,1,0:T(8,128)(2,1)} %bitcast.12.refs_0_.refs_1_.refs_4_.refs_5_, bf16[8,16,16,512]{3,2,1,0:T(8,128)(2,1)S(1)} %copy-done.8, bf16[8,16,16,512]{3,2,1,0:T(8,128)(2,1)} %bitcast.42, ...), custom_call_target="tpu_custom_call" | custom-call | flops 200000000 | bytes 600000 | tf_op jit(solution)/shard_map/product/pallas_call | solution.py:267
  173.0 6.0 all-to-all-start.2
  179.1 2.9 slice.39
  182.5 63.0 %all-to-all-done.2.p_ref.refs_1_ = bf16[128,32,384]{2,1,0:T(8,128)(2,1)S(1)} async-done(((bf16[128,32,384]{2,1,0:T(8,128)(2,1)}), bf16[128,32,384]{2,1,0:T(8,128)(2,1)S(1)}, u32[]{:S(2)}, u32[]{:S(2)}) %all-to-all-start.2) | async-done | bytes 3145760 | tf_op jit(solution)/shard_map/all_to_all | solution.py:128
  245.4 1.7 copy-done
  247.1 8.7 %middle.3 = (bf16[128,32,128]{2,1,0:T(8,128)(2,1)S(1)}, bf16[32,128,512]{2,1,0:T(8,128)(2,1)}, f32[128,128]{1,0:T(8,128)S(1)}, f32[128,128]{1,0:T(8,128)S(1)}) custom-call(s32[1,2]{1,0:T(1,128)S(1)} %fusion.7._, bf16[32,16,2,16,128]{4,3,2,1,0:T(8,128)(2,1)} %bitcast.67, bf16[32,16,2,16,128]{4,3,2,1,0:T(8,128)(2,1)} %bitcast.74, ...), custom_call_target="tpu_custom_call" | custom-call | flops 200000000 | bytes 600000 | tf_op jit(solution)/shard_map/middle/pallas_call | solution.py:381
  258.0 4.4 all-to-all-start.3
  262.4 1.9 slice.40.refs_0_
  264.4 14.9 %middle.4 = (bf16[128,32,256]{2,1,0:T(8,128)(2,1)S(1)}, bf16[32,128,512]{2,1,0:T(8,128)(2,1)}, f32[128,128]{1,0:T(8,128)S(1)}, f32[128,128]{1,0:T(8,128)S(1)}) custom-call(s32[2,2]{1,0:T(2,128)S(1)} %pad_add_fusion._, bf16[32,16,2,16,128]{4,3,2,1,0:T(8,128)(2,1)} %bitcast.68, ...), custom_call_target="tpu_custom_call", output_to_operand_aliasing={{1}: (8, {})} | custom-call | flops 200000000 | bytes 600000 | tf_op jit(solution)/shard_map/middle/pallas_call | solution.py:381
  280.7 4.1 all-to-all-done.3
  284.8 3.8 grad_b.3
  289.5 1.5 collective-permute-done.2.refs_3_.refs_7_
  291.8 3.8 all-to-all-start.4
  296.0 5.0 product.3
  301.0 34.9 %collective-permute-done.3.refs_2_.refs_9_ = bf16[3,16,16,512]{3,2,1,0:T(8,128)(2,1)S(1)} collective-permute-done((bf16[3,16,16,512]{3,2,1,0:T(8,128)(2,1)}, bf16[3,16,16,512]{3,2,1,0:T(8,128)(2,1)S(1)}, u32[]{:S(2)}, u32[]{:S(2)}) %collective-permute-start.3) | collective-permute-done | bytes 786464 | tf_op jit(solution)/shard_map/ppermute | solution.py:140
  337.9 1.7 copy-done.12
  339.6 3.7 all-to-all-start.5
  343.3 2.1 collective-permute-start.4
  345.4 5.5 grad_b.4
  350.9 1.4 copy-done.9
  352.3 17.1 %all-to-all-done.5.p_ref = bf16[128,32,128]{2,1,0:T(8,128)(2,1)S(1)} async-done(((bf16[128,32,128]{2,1,0:T(8,128)(2,1)}), bf16[128,32,128]{2,1,0:T(8,128)(2,1)S(1)}, u32[]{:S(2)}, u32[]{:S(2)}) %all-to-all-start.5) | async-done | bytes 1048608 | tf_op jit(solution)/shard_map/all_to_all | solution.py:128
  369.4 8.6 %middle.5 = (bf16[128,32,128]{2,1,0:T(8,128)(2,1)}, bf16[32,128,512]{2,1,0:T(8,128)(2,1)}, f32[128,128]{1,0:T(8,128)S(1)}, f32[128,128]{1,0:T(8,128)S(1)}) custom-call(s32[1,2]{1,0:T(1,128)S(1)} %fusion.5._, bf16[32,16,2,16,128]{4,3,2,1,0:T(8,128)(2,1)} %bitcast.69, bf16[32,16,2,16,128]{4,3,2,1,0:T(8,128)(2,1)} %bitcast.76, ...), custom_call_target="tpu_custom_call", output_to_operand_aliasing={{1}: (8, {})} | custom-call | flops 200000000 | bytes 600000 | tf_op jit(solution)/shard_map/middle/pallas_call | solution.py:381
  378.0 3.3 collective-permute-done.4.refs_1_.refs_10_
  381.2 3.6 all-to-all-start.6
  384.8 2.2 collective-permute-start.6
  387.0 23.4 %all-to-all-done.6 = bf16[128,32,128]{2,1,0:T(8,128)(2,1)S(1)} async-done(((bf16[128,32,128]{2,1,0:T(8,128)(2,1)}), bf16[128,32,128]{2,1,0:T(8,128)(2,1)S(1)}, u32[]{:S(2)}, u32[]{:S(2)}) %all-to-all-start.6) | async-done | bytes 1048608 | tf_op jit(solution)/shard_map/all_to_all | solution.py:128
  410.4 4.0 grad_b.5.refs_1_
  416.1 8.9 %grad_a.1 = bf16[8,16,48,512]{3,2,1,0:T(8,128)(2,1)} custom-call(bf16[8,16,32,128]{3,2,1,0:T(8,128)(2,1)} %bitcast.18.g_ref.refs_1_.refs_0_, bf16[8,16,32,256]{3,2,1,0:T(8,128)(2,1)} %bitcast.46, bf16[8,16,32,128]{3,2,1,0:T(8,128)(2,1)} %bitcast.48, bf16[8,16,16,512]{3,2,1,0:T(8,128)(2,1)} %copy-done.7, bf16[8,16,16,512]{3,2,1,0:T(8,128)(2,1)} %bitcast.43, ...), custom_call_target="tpu_custom_call" | custom-call | flops 200000000 | bytes 600000 | tf_op jit(solution)/shard_map/grad_a/pallas_call | solution.py:323
  425.0 4.8 all-to-all-start.7
  429.9 113.4 %collective-permute-done.5.refs_0_ = bf16[8,16,16,512]{3,2,1,0:T(8,128)(2,1)S(1)} collective-permute-done((bf16[8,16,16,512]{3,2,1,0:T(8,128)(2,1)}, bf16[8,16,16,512]{3,2,1,0:T(8,128)(2,1)S(1)}, u32[]{:S(2)}, u32[]{:S(2)}) %collective-permute-start.5) | collective-permute-done | bytes 2097184 | tf_op jit(solution)/shard_map/ppermute | solution.py:140
  543.3 2.1 all-to-all-done.7.refs_1_.refs_2_.refs_3_
  545.4 1.6 copy-done.24
  547.0 2.3 add_convert_fusion
  549.3 4.0 all-to-all-start.8
  553.4 14.5 %last_both.1 = (bf16[32,16,2,16,128]{4,3,2,1,0:T(8,128)(2,1)}, f32[128,512]{1,0:T(8,128)S(1)}) custom-call(bf16[32,16,2,16,128]{4,3,2,1,0:T(8,128)(2,1)} %bitcast.70, f32[32,512]{1,0:T(8,128)S(1)} %broadcast_multiply_fusion.mask_ref.refs_1_, bf16[128,48,512]{2,1,0:T(8,128)(2,1)} %all-to-all-done.7.refs_1_.refs_2_.refs_3_, ...), custom_call_target="tpu_custom_call" | custom-call | flops 200000000 | bytes 600000 | tf_op jit(solution)/shard_map/last_both/pallas_call | solution.py:504
  567.9 9.6 %last_a.1 = (bf16[16,128,512]{2,1,0:T(8,128)(2,1)S(1)}, f32[128,256]{1,0:T(8,128)S(1)}) custom-call(bf16[32,16,2,16,128]{4,3,2,1,0:T(8,128)(2,1)} %bitcast.71, f32[32,512]{1,0:T(8,128)S(1)} %broadcast_multiply_fusion.mask_ref.refs_1_, bf16[128,48,512]{2,1,0:T(8,128)(2,1)} %all-to-all-done.7.refs_1_.refs_2_.refs_3_, ...), custom_call_target="tpu_custom_call" | custom-call | flops 200000000 | bytes 600000 | tf_op jit(solution)/shard_map/last_a/pallas_call | solution.py:504
  578.9 7.2 %last_b_sum.1 = f32[128,256]{1,0:T(8,128)S(1)} custom-call(bf16[32,16,2,16,128]{4,3,2,1,0:T(8,128)(2,1)} %bitcast.72, f32[32,512]{1,0:T(8,128)S(1)} %broadcast_multiply_fusion.mask_ref.refs_1_, bf16[128,16,512]{2,1,0:T(8,128)(2,1)S(1)} %after.17.refs_2_, f32[128,4]{1,0:T(8,128)S(1)} %copy.52.norm_ref.refs_5_.refs_4_.refs_3_, ...), custom_call_target="tpu_custom_call" | custom-call | flops 200000000 | bytes 600000 | tf_op jit(solution)/shard_map/last_b_sum/pallas_call | solution.py:504
  586.2 13.4 %all_to_all.57 = bf16[16,8,768]{2,1,0:T(8,128)(2,1)S(1)} all-to-all(bf16[16,8,768]{2,1,0:T(8,128)(2,1)S(1)} %pad_maximum_fusion), channel_id=1, replica_groups=mesh['crops'=2,'tile'=16] {'tile'}, dimensions={0} | all-to-all | bytes 393216 | tf_op jit(solution)/shard_map/all_to_all | solution.py:519
  600.3 3.5 all-to-all-start.10
  603.9 10.8 %last_b.1 = bf16[32,16,2,16,128]{4,3,2,1,0:T(8,128)(2,1)} custom-call(bf16[32,16,2,16,128]{4,3,2,1,0:T(8,128)(2,1)} %bitcast.73, f32[32,512]{1,0:T(8,128)S(1)} %broadcast_multiply_fusion.mask_ref.refs_1_, bf16[128,16,512]{2,1,0:T(8,128)(2,1)S(1)} %after.17.refs_2_, bf16[16,128,512]{2,1,0:T(8,128)(2,1)} %copy-done.15, ...), custom_call_target="tpu_custom_call", output_to_operand_aliasing={{}: (7, {})} | custom-call | flops 200000000 | bytes 600000 | tf_op jit(solution)/shard_map/last_b/pallas_call | solution.py:504
  (95 shorter events, 20.1 us)
Async XLA Ops:
  12.1 1.3 copy-start.14
  13.4 31.0 %all-to-all-start = ((bf16[128,16,512]{2,1,0:T(8,128)(2,1)}), bf16[128,16,512]{2,1,0:T(8,128)(2,1)S(1)}, u32[]{:S(2)}, u32[]{:S(2)}) async-start(bf16[128,16,512]{2,1,0:T(8,128)(2,1)} %copy-done.14), calls=%async_computation | async-start | bytes 4194304 | tf_op jit(solution)/shard_map/all_to_all | solution.py:128
  44.3 4.8 copy-start.2
  44.3 120.4 %all-to-all-start.1 = ((bf16[128,48,512]{2,1,0:T(8,128)(2,1)}), bf16[128,48,512]{2,1,0:T(8,128)(2,1)}, u32[]{:S(2)}, u32[]{:S(2)}) async-start(bf16[128,48,512]{2,1,0:T(8,128)(2,1)} %after.9), calls=%async_computation.1 | async-start | bytes 12582912 | tf_op jit(solution)/shard_map/all_to_all | solution.py:128
  49.1 113.4 %collective-permute-start = (bf16[8,16,16,512]{3,2,1,0:T(8,128)(2,1)S(1)}, bf16[8,16,16,512]{3,2,1,0:T(8,128)(2,1)S(1)}, u32[]{:S(2)}, u32[]{:S(2)}) collective-permute-start(bf16[8,16,16,512]{3,2,1,0:T(8,128)(2,1)S(1)} %bitcast.41), channel_id=1, source_target_pairs={{0,8},{1,9},{2,10},{3,11},{4,12},{5,13},{6,14},{7,15},{8,0},{9,1},... | collective-permute-start | bytes 6291464 | tf_op jit(solution)/shard_map/ppermute | solution.py:140
  162.5 1.4 copy-start.7
  164.7 1.6 copy-start.8
  173.0 72.4 %all-to-all-start.2 = ((bf16[128,32,384]{2,1,0:T(8,128)(2,1)}), bf16[128,32,384]{2,1,0:T(8,128)(2,1)S(1)}, u32[]{:S(2)}, u32[]{:S(2)}) async-start(bf16[128,32,384]{2,1,0:T(8,128)(2,1)} %bitcast.78), calls=%async_computation.2 | async-start | bytes 6291456 | tf_op jit(solution)/shard_map/all_to_all | solution.py:128
  179.0 3.1 copy-start.26
  179.0 3.2 copy-start.17
  181.9 75.1 %collective-permute-start.1 = (bf16[6,16,16,512]{3,2,1,0:T(8,128)(2,1)}, bf16[6,16,16,512]{3,2,1,0:T(8,128)(2,1)}, u32[]{:S(2)}, u32[]{:S(2)}) collective-permute-start(bf16[6,16,16,512]{3,2,1,0:T(8,128)(2,1)} %slice.39), channel_id=1, source_target_pairs={{0,8},{1,9},{2,10},{3,11},{4,12},{5,13},{6,14},{7,15},{8,0},{9,1},... | collective-permute-start | bytes 4718600 | tf_op jit(solution)/shard_map/ppermute | solution.py:140
  245.4 1.7 copy-start
  255.8 0.6 copy-start.18
  256.4 0.6 copy-start.20
  257.0 7.3 %copy-start.1 = (bf16[128,32,384]{2,1,0:T(8,128)(2,1)S(1)}, bf16[128,32,384]{2,1,0:T(8,128)(2,1)}, u32[]{:S(2)}) copy-start(bf16[128,32,384]{2,1,0:T(8,128)(2,1)} %copy-done) | copy-start | bytes 9437188
  257.0 1.0 copy-start.10
  258.0 26.7 %all-to-all-start.3 = ((bf16[128,32,128]{2,1,0:T(8,128)(2,1)}), bf16[128,32,128]{2,1,0:T(8,128)(2,1)}, u32[]{:S(2)}, u32[]{:S(2)}) async-start(bf16[128,32,128]{2,1,0:T(8,128)(2,1)} %copy-done.10), calls=%async_computation.3 | async-start | bytes 2097152 | tf_op jit(solution)/shard_map/all_to_all | solution.py:128
  264.3 26.6 %collective-permute-start.2 = (bf16[2,16,16,512]{3,2,1,0:T(8,128)(2,1)}, bf16[2,16,16,512]{3,2,1,0:T(8,128)(2,1)S(1)}, u32[]{:S(2)}, u32[]{:S(2)}) collective-permute-start(bf16[2,16,16,512]{3,2,1,0:T(8,128)(2,1)} %after.11), channel_id=1, source_target_pairs={{0,8},{1,9},{2,10},{3,11},{4,12},{5,13},{6,14},{7,15},{8,0},{9,1},... | collective-permute-start | bytes 1572872 | tf_op jit(solution)/shard_map/ppermute | solution.py:140
  279.3 1.3 copy-start.6
  288.6 0.9 copy-start.22
  289.5 1.5 copy-start.23
  290.9 0.9 copy-start.16
  291.8 46.1 %all-to-all-start.4 = ((bf16[128,32,256]{2,1,0:T(8,128)(2,1)}), bf16[128,32,256]{2,1,0:T(8,128)(2,1)S(1)}, u32[]{:S(2)}, u32[]{:S(2)}) async-start(bf16[128,32,256]{2,1,0:T(8,128)(2,1)} %after.12), calls=%async_computation.4 | async-start | bytes 4194304 | tf_op jit(solution)/shard_map/all_to_all | solution.py:128
  295.6 40.3 %collective-permute-start.3 = (bf16[3,16,16,512]{3,2,1,0:T(8,128)(2,1)}, bf16[3,16,16,512]{3,2,1,0:T(8,128)(2,1)S(1)}, u32[]{:S(2)}, u32[]{:S(2)}) collective-permute-start(bf16[3,16,16,512]{3,2,1,0:T(8,128)(2,1)} %copy-done.16), channel_id=1, source_target_pairs={{0,8},{1,9},{2,10},{3,11},{4,12},{5,13},{6,14},{7,15},{8,0},{9,1},... | collective-permute-start | bytes 2359304 | tf_op jit(solution)/shard_map/ppermute | solution.py:140
  335.9 0.9 copy-start.11
  337.9 1.7 copy-start.3
  337.9 1.7 copy-start.12
  339.6 29.8 %all-to-all-start.5 = ((bf16[128,32,128]{2,1,0:T(8,128)(2,1)}), bf16[128,32,128]{2,1,0:T(8,128)(2,1)S(1)}, u32[]{:S(2)}, u32[]{:S(2)}) async-start(bf16[128,32,128]{2,1,0:T(8,128)(2,1)} %after.13), calls=%async_computation.5 | async-start | bytes 2097152 | tf_op jit(solution)/shard_map/all_to_all | solution.py:128
  343.3 38.0 %collective-permute-start.4 = (bf16[3,16,16,512]{3,2,1,0:T(8,128)(2,1)}, bf16[3,16,16,512]{3,2,1,0:T(8,128)(2,1)S(1)}, u32[]{:S(2)}, u32[]{:S(2)}) collective-permute-start(bf16[3,16,16,512]{3,2,1,0:T(8,128)(2,1)} %copy-done.22), channel_id=1, source_target_pairs={{0,8},{1,9},{2,10},{3,11},{4,12},{5,13},{6,14},{7,15},{8,0},{9,1},... | collective-permute-start | bytes 2359304 | tf_op jit(solution)/shard_map/ppermute | solution.py:140
  350.9 1.4 copy-start.9
  381.2 29.2 %all-to-all-start.6 = ((bf16[128,32,128]{2,1,0:T(8,128)(2,1)}), bf16[128,32,128]{2,1,0:T(8,128)(2,1)S(1)}, u32[]{:S(2)}, u32[]{:S(2)}) async-start(bf16[128,32,128]{2,1,0:T(8,128)(2,1)} %after.14), calls=%async_computation.6 | async-start | bytes 2097152 | tf_op jit(solution)/shard_map/all_to_all | solution.py:128
  384.8 29.7 %collective-permute-start.6 = (bf16[2,16,16,512]{3,2,1,0:T(8,128)(2,1)}, bf16[2,16,16,512]{3,2,1,0:T(8,128)(2,1)S(1)}, u32[]{:S(2)}, u32[]{:S(2)}) collective-permute-start(bf16[2,16,16,512]{3,2,1,0:T(8,128)(2,1)} %copy-done.23), channel_id=1, source_target_pairs={{0,8},{1,9},{2,10},{3,11},{4,12},{5,13},{6,14},{7,15},{8,0},{9,1},... | collective-permute-start | bytes 1572872 | tf_op jit(solution)/shard_map/ppermute | solution.py:140
  410.4 4.0 copy-start.4
  414.5 1.6 copy-start.13
  414.5 1.3 copy-start.5
  425.0 120.4 %all-to-all-start.7 = ((bf16[128,48,512]{2,1,0:T(8,128)(2,1)}), bf16[128,48,512]{2,1,0:T(8,128)(2,1)}, u32[]{:S(2)}, u32[]{:S(2)}) async-start(bf16[128,48,512]{2,1,0:T(8,128)(2,1)} %bitcast.77), calls=%async_computation.7 | async-start | bytes 12582912 | tf_op jit(solution)/shard_map/all_to_all | solution.py:128
  429.8 113.5 %collective-permute-start.5 = (bf16[8,16,16,512]{3,2,1,0:T(8,128)(2,1)}, bf16[8,16,16,512]{3,2,1,0:T(8,128)(2,1)S(1)}, u32[]{:S(2)}, u32[]{:S(2)}) collective-permute-start(bf16[8,16,16,512]{3,2,1,0:T(8,128)(2,1)} %copy-done.5), channel_id=1, source_target_pairs={{0,8},{1,9},{2,10},{3,11},{4,12},{5,13},{6,14},{7,15},{8,0},{9,1},... | collective-permute-start | bytes 6291464 | tf_op jit(solution)/shard_map/ppermute | solution.py:140
  545.4 1.6 copy-start.24
  549.3 4.0 copy-start.25
  549.3 4.1 copy-start.19
  549.3 4.1 copy-start.21
  549.3 29.6 %all-to-all-start.8 = ((bf16[128,16,512]{2,1,0:T(8,128)(2,1)}), bf16[128,16,512]{2,1,0:T(8,128)(2,1)S(1)}, u32[]{:S(2)}, u32[]{:S(2)}) async-start(bf16[128,16,512]{2,1,0:T(8,128)(2,1)} %bitcast.79), calls=%async_computation.8 | async-start | bytes 4194304 | tf_op jit(solution)/shard_map/all_to_all | solution.py:128
  577.5 1.4 copy-start.15
  600.3 14.3 %all-to-all-start.10 = ((bf16[16,8,768]{2,1,0:T(8,128)(2,1)}), bf16[16,8,768]{2,1,0:T(8,128)(2,1)S(1)}, u32[]{:S(2)}, u32[]{:S(2)}) async-start(bf16[16,8,768]{2,1,0:T(8,128)(2,1)} %broadcast_in_dim.2), calls=%async_computation.10 | async-start | bytes 393216 | tf_op jit(solution)/shard_map/all_to_all | solution.py:519

commit v12 on v11

--- a/solution.py
+++ b/solution.py
@@ -519,12 +519,12 @@
     return lax.all_to_all(array, "tile", split_axis=0, concat_axis=0, tiled=True)
 
 
-def tile_sum(array, tiles):
+def tile_sum(array, tiles, ready):
     chans, width = array.shape
     parts = swap_all(array.astype(BF16)).reshape(tiles, chans // tiles, width)
     part = jnp.sum(parts.astype(F32), axis=0).astype(BF16)
     spread = jnp.broadcast_to(part[None], (tiles,) + part.shape).reshape(chans, width)
-    return swap_all(spread).astype(F32)
+    return swap_all(after(spread, ready)).astype(F32)
 
 
 def body(
@@ -582,17 +582,19 @@
     local_mid += local
     grad_b0 = make_grad_b(plan, owner_g[0], own_a, back_a)
     back_0 = [plan.exchange(piece) for piece in grad_b0]
-    waits = (owner_g[0], grad_b0[0], *got_b[1:2])
+    waits = (owner_g[0], grad_b0[0])
+    if two:
+        b_second = [(piece, 0) for piece in got_b]
+        b_first = b_first + b_second
+        product = plan.swap(after(joined(make_product(plan, own_a, b_second)), *waits))
+        waits = (product, back_0[0])
     owner_g.append(owned(plan.swap(after(grad, *waits))))
     grad_b_own = make_grad_b(plan, owner_g[1], own_a, [plan.half] * plan.subs)
     if two:
-        b_second = [(piece, 0) for piece in got_b]
-        b_first = b_first + b_second
-        product = joined(make_product(plan, own_a, b_second))
-        product = plan.swap(after(product, owner_g[1], back_0[0]))
-        grad, kept, local = middle([(1 - side, 1)], 0, (kept,), grad_b_own[:1], product)
+        grad, kept, local = middle([(1 - side, 1)], 0, (kept,), (), product)
         local_mid += local
-        owner_g.append(owned(plan.swap(after(grad, back_0[1]))))
+        grad = plan.swap(after(grad, owner_g[1], back_0[1]))
+        owner_g.append(after(owned(grad), grad_b_own[0]))
         (grad_b1,) = make_grad_b(plan, owner_g[2], own_a, [plan.half])
         back_1 = plan.exchange(grad_b1)
         back_0[2] = after(back_0[2], grad_b1)
@@ -615,7 +617,7 @@
             plan, "b", 1, pair_grad, x, mask, [(grad_b, 0)], [base], side_b
         )
         local_ab += jnp.concatenate([local_a, local_b], axis=1)
-    total = tile_sum(jnp.concatenate([local_ab, local_mid], axis=1), tiles) / crop
+    total = tile_sum(jnp.concatenate([local_ab, local_mid], axis=1), tiles, pair_grad) / crop
     wide = 4 * hidden
     return (
         pair_grad.reshape(count, crop, chans),

time: 618 us -> 638 us (1.032)
  waiting for transfers between devices: 393 us -> 403 us
  local copies, waits for them, and re-layouts: 28.3 us -> 34.8 us
    ppermute x7, waiting for transfers between devices: 264 us -> 300 us  [exchange(): return lax.ppermute(array, 'tile', self.partner)]
    all_to_all x9, waiting for transfers between devices: 129 us -> 103 us  [swap(): lax.all_to_all(array, 'tile', split_axis=0, concat_axis=0, axis_index_gro...]
    unnamed x57 -> x87, local copies, waits for them, and re-layouts: 21 us -> 29.1 us
  transfers between devices with their start and end apart: 17 -> 17, of which waited for: 13 -> 11; matrix products, arithmetic and copies ran while one was open for 1% -> 1% of each run, Pallas kernels for 15% -> 14%
where the time goes in v12:
time: 638 us; the launch traced here: 636 us
  waiting for transfers between devices  403 us (63%)
  Pallas kernels  126 us (20%)
  starting transfers between devices  51.4 us (8%)
  local copies, waits for them, and re-layouts  34.8 us (5%)
  blocking collectives  14.8 us (2%)
    ppermute x7, waiting for transfers between devices, exchange(): return lax.ppermute(array, 'tile', self.partner)  300 us
    all_to_all x9, waiting for transfers between devices, swap(): lax.all_to_all(array, 'tile', split_axis=0, concat_axis=0, axis_index_gro...  103 us
    pallas_call x4, Pallas kernels, make_last(): pl.pallas_call(functools.partial(last_kernel, plan.step, mode), grid=(pla...  42.1 us
    all_to_all x9, starting transfers between devices, swap(): lax.all_to_all(array, 'tile', split_axis=0, concat_axis=0, axis_index_gro...  40.7 us
    pallas_call x3, Pallas kernels, make_middle(): pl.pallas_call(functools.partial(middle_kernel, plan.step), grid_spec=plt...  32.1 us
    unnamed x87, local copies, waits for them, and re-layouts  29.1 us
    pallas_call x2, Pallas kernels, make_factors(): pl.pallas_call(functools.partial(factors_kernel, plan.step, bool(before))...  17 us
    all_to_all x1, blocking collectives, swap_all(): lax.all_to_all(array, 'tile', split_axis=0, concat_axis=0, tiled=True)  14.8 us
  transfers between devices with their start and end apart: 17, of which 11 were waited for; matrix products, arithmetic and copies ran while one was open for 1% of the time, Pallas kernels for 14%

profile of v12, /device:TPU:0, one launch (start us, length us, event | category | flops | bytes accessed | tf_op | source)
XLA Modules:
  0.0 636.1 jit_solution(6287715405972296421)
XLA Ops:
  3.5 8.5 %factors.2 = (bf16[128,48,512]{2,1,0:T(8,128)(2,1)}, bf16[128,16,512]{2,1,0:T(8,128)(2,1)S(1)}) custom-call(bf16[32,16,2,16,128]{4,3,2,1,0:T(8,128)(2,1)} %bitcast.68, f32[32,512]{1,0:T(8,128)S(1)} %broadcast_multiply_fusion.mask_ref.refs_1_, f32[128,4]{1,0:T(8,128)S(1)} %copy.54.norm_ref.refs_5_.refs_4_.refs_3_, bf16[512,128]{1,0:T(8,128)(2,1)S(1)} %bitcast.51), custom_call_target="tpu_custom_call" | custom-call | flops 200000000 | bytes 600000 | tf_op jit(solution)/shard_map/factors/pallas_call | solution.py:201
  12.1 1.3 copy-done.20
  13.4 5.3 all-to-all-start
  18.6 8.5 %factors.3.refs_0_ = bf16[128,48,512]{2,1,0:T(8,128)(2,1)} custom-call(bf16[32,16,2,16,128]{4,3,2,1,0:T(8,128)(2,1)} %bitcast.69, f32[32,512]{1,0:T(8,128)S(1)} %broadcast_multiply_fusion.mask_ref.refs_1_, f32[128,4]{1,0:T(8,128)S(1)} %copy.54.norm_ref.refs_5_.refs_4_.refs_3_, bf16[512,128]{1,0:T(8,128)(2,1)S(1)} %bitcast.52, ...), custom_call_target="tpu_custom_call", output_to_operand_aliasing={{}: (4, {})} | custom-call | flops 200000000 | bytes 600000 | tf_op jit(solution)/shard_map/factors/pallas_call | solution.py:201
  27.1 17.2 %all-to-all-done = bf16[128,16,512]{2,1,0:T(8,128)(2,1)S(1)} async-done(((bf16[128,16,512]{2,1,0:T(8,128)(2,1)}), bf16[128,16,512]{2,1,0:T(8,128)(2,1)S(1)}, u32[]{:S(2)}, u32[]{:S(2)}) %all-to-all-start) | async-done | bytes 2097184 | tf_op jit(solution)/shard_map/all_to_all | solution.py:128
  44.3 4.8 all-to-all-start.1
  49.2 2.6 collective-permute-start
  51.8 110.7 %collective-permute-done.refs_2_.refs_3_ = bf16[8,16,16,512]{3,2,1,0:T(8,128)(2,1)S(1)} collective-permute-done((bf16[8,16,16,512]{3,2,1,0:T(8,128)(2,1)S(1)}, bf16[8,16,16,512]{3,2,1,0:T(8,128)(2,1)S(1)}, u32[]{:S(2)}, u32[]{:S(2)}) %collective-permute-start) | collective-permute-done | bytes 2097184 | tf_op jit(solution)/shard_map/ppermute | solution.py:140
  162.5 1.4 copy-done.7
  164.7 1.6 copy-done.8
  166.3 6.7 %product.2 = bf16[8,16,32,384]{3,2,1,0:T(8,128)(2,1)} custom-call(bf16[8,16,48,512]{3,2,1,0:T(8,128)(2,1)} %bitcast.12.refs_0_.refs_1_.refs_4_.refs_5_, bf16[8,16,48,512]{3,2,1,0:T(8,128)(2,1)} %bitcast.12.refs_0_.refs_1_.refs_4_.refs_5_, bf16[8,16,16,512]{3,2,1,0:T(8,128)(2,1)S(1)} %copy-done.8, bf16[8,16,16,512]{3,2,1,0:T(8,128)(2,1)} %bitcast.45, ...), custom_call_target="tpu_custom_call" | custom-call | flops 200000000 | bytes 600000 | tf_op jit(solution)/shard_map/product/pallas_call | solution.py:267
  173.0 6.0 all-to-all-start.2
  179.1 2.9 slice.39
  182.5 63.0 %all-to-all-done.2.p_ref.refs_1_ = bf16[128,32,384]{2,1,0:T(8,128)(2,1)S(1)} async-done(((bf16[128,32,384]{2,1,0:T(8,128)(2,1)}), bf16[128,32,384]{2,1,0:T(8,128)(2,1)S(1)}, u32[]{:S(2)}, u32[]{:S(2)}) %all-to-all-start.2) | async-done | bytes 3145760 | tf_op jit(solution)/shard_map/all_to_all | solution.py:128
  245.4 1.7 copy-done
  247.1 8.7 %middle.3 = (bf16[128,32,128]{2,1,0:T(8,128)(2,1)S(1)}, bf16[32,128,512]{2,1,0:T(8,128)(2,1)}, f32[128,128]{1,0:T(8,128)S(1)}, f32[128,128]{1,0:T(8,128)S(1)}) custom-call(s32[1,2]{1,0:T(1,128)S(1)} %fusion.7._, bf16[32,16,2,16,128]{4,3,2,1,0:T(8,128)(2,1)} %bitcast.70, bf16[32,16,2,16,128]{4,3,2,1,0:T(8,128)(2,1)} %bitcast.77, ...), custom_call_target="tpu_custom_call" | custom-call | flops 200000000 | bytes 600000 | tf_op jit(solution)/shard_map/middle/pallas_call | solution.py:381
  258.1 4.4 all-to-all-start.3
  263.7 26.4 %collective-permute-done.2.refs_3_.refs_7_ = bf16[2,16,16,512]{3,2,1,0:T(8,128)(2,1)S(1)} collective-permute-done((bf16[2,16,16,512]{3,2,1,0:T(8,128)(2,1)S(1)}, bf16[2,16,16,512]{3,2,1,0:T(8,128)(2,1)S(1)}, u32[]{:S(2)}, u32[]{:S(2)}) %collective-permute-start.2) | collective-permute-done | bytes 524320 | tf_op jit(solution)/shard_map/ppermute | solution.py:140
  290.1 5.1 product.3
  296.0 4.7 grad_b.3
  302.4 3.7 all-to-all-start.4
  306.6 14.9 %middle.4 = (bf16[128,32,256]{2,1,0:T(8,128)(2,1)S(1)}, bf16[32,128,512]{2,1,0:T(8,128)(2,1)}, f32[128,128]{1,0:T(8,128)S(1)}, f32[128,128]{1,0:T(8,128)S(1)}) custom-call(s32[2,2]{1,0:T(2,128)S(1)} %pad_add_fusion._, bf16[32,16,2,16,128]{4,3,2,1,0:T(8,128)(2,1)} %bitcast.71, ...), custom_call_target="tpu_custom_call", output_to_operand_aliasing={{1}: (8, {})} | custom-call | flops 200000000 | bytes 600000 | tf_op jit(solution)/shard_map/middle/pallas_call | solution.py:381
  322.8 21.0 %collective-permute-done.3.refs_2_.refs_9_ = bf16[3,16,16,512]{3,2,1,0:T(8,128)(2,1)S(1)} collective-permute-done((bf16[3,16,16,512]{3,2,1,0:T(8,128)(2,1)}, bf16[3,16,16,512]{3,2,1,0:T(8,128)(2,1)S(1)}, u32[]{:S(2)}, u32[]{:S(2)}) %collective-permute-start.3) | collective-permute-done | bytes 786464 | tf_op jit(solution)/shard_map/ppermute | solution.py:140
  345.9 1.3 copy-done.6
  347.2 3.6 all-to-all-start.5
  351.8 8.5 %middle.5 = (bf16[128,32,128]{2,1,0:T(8,128)(2,1)S(1)}, bf16[32,128,512]{2,1,0:T(8,128)(2,1)}, f32[128,128]{1,0:T(8,128)S(1)}, f32[128,128]{1,0:T(8,128)S(1)}) custom-call(s32[1,2]{1,0:T(1,128)S(1)} %fusion.5._, bf16[32,16,2,16,128]{4,3,2,1,0:T(8,128)(2,1)} %bitcast.72, bf16[32,16,2,16,128]{4,3,2,1,0:T(8,128)(2,1)} %bitcast.79, ...), custom_call_target="tpu_custom_call", output_to_operand_aliasing={{1}: (8, {})} | custom-call | flops 200000000 | bytes 600000 | tf_op jit(solution)/shard_map/middle/pallas_call | solution.py:381
  362.6 28.7 %collective-permute-done.4.refs_2_.refs_10_ = bf16[3,16,16,512]{3,2,1,0:T(8,128)(2,1)S(1)} collective-permute-done((bf16[3,16,16,512]{3,2,1,0:T(8,128)(2,1)}, bf16[3,16,16,512]{3,2,1,0:T(8,128)(2,1)S(1)}, u32[]{:S(2)}, u32[]{:S(2)}) %collective-permute-start.4) | collective-permute-done | bytes 786464 | tf_op jit(solution)/shard_map/ppermute | solution.py:140
  393.3 2.0 copy-done.11
  397.4 4.1 all-to-all-start.6
  401.5 1.7 collective-permute-start.6
  403.2 5.5 grad_b.4
  408.7 18.5 %all-to-all-done.6 = bf16[128,32,128]{2,1,0:T(8,128)(2,1)S(1)} async-done(((bf16[128,32,128]{2,1,0:T(8,128)(2,1)}), bf16[128,32,128]{2,1,0:T(8,128)(2,1)S(1)}, u32[]{:S(2)}, u32[]{:S(2)}) %all-to-all-start.6) | async-done | bytes 1048608 | tf_op jit(solution)/shard_map/all_to_all | solution.py:128
  427.2 4.0 grad_b.5.refs_1_
  431.3 1.3 copy-done.5
  433.5 9.0 %grad_a.1 = bf16[8,16,48,512]{3,2,1,0:T(8,128)(2,1)} custom-call(bf16[8,16,32,128]{3,2,1,0:T(8,128)(2,1)} %bitcast.19.g_ref.refs_1_.refs_0_, bf16[8,16,32,256]{3,2,1,0:T(8,128)(2,1)} %bitcast.49, bf16[8,16,32,128]{3,2,1,0:T(8,128)(2,1)} %copy-done.4, bf16[8,16,16,512]{3,2,1,0:T(8,128)(2,1)} %copy-done.7, bf16[8,16,16,512]{3,2,1,0:T(8,128)(2,1)} %bitcast.46, ...), custom_call_target="tpu_custom_call" | custom-call | flops 200000000 | bytes 600000 | tf_op jit(solution)/shard_map/grad_a/pallas_call | solution.py:323
  442.5 4.8 all-to-all-start.7
  447.4 113.4 %collective-permute-done.5.refs_0_ = bf16[8,16,16,512]{3,2,1,0:T(8,128)(2,1)S(1)} collective-permute-done((bf16[8,16,16,512]{3,2,1,0:T(8,128)(2,1)}, bf16[8,16,16,512]{3,2,1,0:T(8,128)(2,1)S(1)}, u32[]{:S(2)}, u32[]{:S(2)}) %collective-permute-start.5) | collective-permute-done | bytes 2097184 | tf_op jit(solution)/shard_map/ppermute | solution.py:140
  560.8 2.1 all-to-all-done.7.refs_1_.refs_2_.refs_3_
  562.9 1.6 copy-done.39
  564.5 2.3 add_convert_fusion
  566.9 4.0 all-to-all-start.8
  571.0 14.5 %last_both.1 = (bf16[32,16,2,16,128]{4,3,2,1,0:T(8,128)(2,1)}, f32[128,512]{1,0:T(8,128)S(1)}) custom-call(bf16[32,16,2,16,128]{4,3,2,1,0:T(8,128)(2,1)} %bitcast.73, f32[32,512]{1,0:T(8,128)S(1)} %broadcast_multiply_fusion.mask_ref.refs_1_, bf16[128,48,512]{2,1,0:T(8,128)(2,1)} %all-to-all-done.7.refs_1_.refs_2_.refs_3_, ...), custom_call_target="tpu_custom_call" | custom-call | flops 200000000 | bytes 600000 | tf_op jit(solution)/shard_map/last_both/pallas_call | solution.py:504
  585.5 9.6 %last_a.1 = (bf16[16,128,512]{2,1,0:T(8,128)(2,1)S(1)}, f32[128,256]{1,0:T(8,128)S(1)}) custom-call(bf16[32,16,2,16,128]{4,3,2,1,0:T(8,128)(2,1)} %bitcast.74, f32[32,512]{1,0:T(8,128)S(1)} %broadcast_multiply_fusion.mask_ref.refs_1_, bf16[128,48,512]{2,1,0:T(8,128)(2,1)} %all-to-all-done.7.refs_1_.refs_2_.refs_3_, ...), custom_call_target="tpu_custom_call" | custom-call | flops 200000000 | bytes 600000 | tf_op jit(solution)/shard_map/last_a/pallas_call | solution.py:504
  595.2 1.3 copy-done.21
  596.5 7.2 %last_b_sum.1 = f32[128,256]{1,0:T(8,128)S(1)} custom-call(bf16[32,16,2,16,128]{4,3,2,1,0:T(8,128)(2,1)} %bitcast.75, f32[32,512]{1,0:T(8,128)S(1)} %broadcast_multiply_fusion.mask_ref.refs_1_, bf16[128,16,512]{2,1,0:T(8,128)(2,1)S(1)} %after.20.refs_2_, f32[128,4]{1,0:T(8,128)S(1)} %copy.54.norm_ref.refs_5_.refs_4_.refs_3_, ...), custom_call_target="tpu_custom_call" | custom-call | flops 200000000 | bytes 600000 | tf_op jit(solution)/shard_map/last_b_sum/pallas_call | solution.py:504
  604.4 4.6 all-to-all-start.9
  609.1 10.8 %last_b.1.refs_1_ = bf16[32,16,2,16,128]{4,3,2,1,0:T(8,128)(2,1)} custom-call(bf16[32,16,2,16,128]{4,3,2,1,0:T(8,128)(2,1)} %bitcast.76, f32[32,512]{1,0:T(8,128)S(1)} %broadcast_multiply_fusion.mask_ref.refs_1_, bf16[128,16,512]{2,1,0:T(8,128)(2,1)S(1)} %after.20.refs_2_, bf16[16,128,512]{2,1,0:T(8,128)(2,1)} %copy-done.21, ...), custom_call_target="tpu_custom_call", output_to_operand_aliasing={{}: (7, {})} | custom-call | flops 200000000 | bytes 600000 | tf_op jit(solution)/shard_map/last_b/pallas_call | solution.py:504
  619.9 14.8 %all_to_all.60 = bf16[16,8,768]{2,1,0:T(8,128)(2,1)S(1)} all-to-all(bf16[16,8,768]{2,1,0:T(8,128)(2,1)S(1)} %bitcast.55), channel_id=1, replica_groups=mesh['crops'=2,'tile'=16] {'tile'}, dimensions={0} | all-to-all | bytes 393216 | tf_op jit(solution)/shard_map/all_to_all | solution.py:519
  (127 shorter events, 24.7 us)
Async XLA Ops:
  12.1 1.3 copy-start.20
  13.4 31.0 %all-to-all-start = ((bf16[128,16,512]{2,1,0:T(8,128)(2,1)}), bf16[128,16,512]{2,1,0:T(8,128)(2,1)S(1)}, u32[]{:S(2)}, u32[]{:S(2)}) async-start(bf16[128,16,512]{2,1,0:T(8,128)(2,1)} %copy-done.20), calls=%async_computation | async-start | bytes 4194304 | tf_op jit(solution)/shard_map/all_to_all | solution.py:128
  44.3 4.8 copy-start.2
  44.3 120.4 %all-to-all-start.1 = ((bf16[128,48,512]{2,1,0:T(8,128)(2,1)}), bf16[128,48,512]{2,1,0:T(8,128)(2,1)}, u32[]{:S(2)}, u32[]{:S(2)}) async-start(bf16[128,48,512]{2,1,0:T(8,128)(2,1)} %after.11), calls=%async_computation.1 | async-start | bytes 12582912 | tf_op jit(solution)/shard_map/all_to_all | solution.py:128
  49.2 113.4 %collective-permute-start = (bf16[8,16,16,512]{3,2,1,0:T(8,128)(2,1)S(1)}, bf16[8,16,16,512]{3,2,1,0:T(8,128)(2,1)S(1)}, u32[]{:S(2)}, u32[]{:S(2)}) collective-permute-start(bf16[8,16,16,512]{3,2,1,0:T(8,128)(2,1)S(1)} %bitcast.44), channel_id=1, source_target_pairs={{0,8},{1,9},{2,10},{3,11},{4,12},{5,13},{6,14},{7,15},{8,0},{9,1},... | collective-permute-start | bytes 6291464 | tf_op jit(solution)/shard_map/ppermute | solution.py:140
  162.5 1.4 copy-start.7
  164.7 1.6 copy-start.8
  173.0 72.4 %all-to-all-start.2 = ((bf16[128,32,384]{2,1,0:T(8,128)(2,1)}), bf16[128,32,384]{2,1,0:T(8,128)(2,1)S(1)}, u32[]{:S(2)}, u32[]{:S(2)}) async-start(bf16[128,32,384]{2,1,0:T(8,128)(2,1)} %bitcast.82), calls=%async_computation.2 | async-start | bytes 6291456 | tf_op jit(solution)/shard_map/all_to_all | solution.py:128
  179.1 3.1 copy-start.41
  179.1 3.2 copy-start.24
  182.0 75.1 %collective-permute-start.1 = (bf16[6,16,16,512]{3,2,1,0:T(8,128)(2,1)}, bf16[6,16,16,512]{3,2,1,0:T(8,128)(2,1)}, u32[]{:S(2)}, u32[]{:S(2)}) collective-permute-start(bf16[6,16,16,512]{3,2,1,0:T(8,128)(2,1)} %slice.39), channel_id=1, source_target_pairs={{0,8},{1,9},{2,10},{3,11},{4,12},{5,13},{6,14},{7,15},{8,0},{9,1},... | collective-permute-start | bytes 4718600 | tf_op jit(solution)/shard_map/ppermute | solution.py:140
  245.4 1.7 copy-start
  257.0 6.6 %copy-start.1 = (bf16[128,32,384]{2,1,0:T(8,128)(2,1)S(1)}, bf16[128,32,384]{2,1,0:T(8,128)(2,1)}, u32[]{:S(2)}) copy-start(bf16[128,32,384]{2,1,0:T(8,128)(2,1)} %copy-done) | copy-start | bytes 9437188
  257.0 1.1 copy-start.13
  258.1 37.8 %all-to-all-start.3 = ((bf16[128,32,128]{2,1,0:T(8,128)(2,1)}), bf16[128,32,128]{2,1,0:T(8,128)(2,1)}, u32[]{:S(2)}, u32[]{:S(2)}) async-start(bf16[128,32,128]{2,1,0:T(8,128)(2,1)} %copy-done.13), calls=%async_computation.3 | async-start | bytes 2097152 | tf_op jit(solution)/shard_map/all_to_all | solution.py:128
  263.6 26.4 %collective-permute-start.2 = (bf16[2,16,16,512]{3,2,1,0:T(8,128)(2,1)S(1)}, bf16[2,16,16,512]{3,2,1,0:T(8,128)(2,1)S(1)}, u32[]{:S(2)}, u32[]{:S(2)}) collective-permute-start(bf16[2,16,16,512]{3,2,1,0:T(8,128)(2,1)S(1)} %after.12), channel_id=1, source_target_pairs={{0,8},{1,9},{2,10},{3,11},{4,12},{5,13},{6,14},{7,15},{8,0},{9,1},... | collective-permute-start | bytes 1572872 | tf_op jit(solution)/shard_map/ppermute | solution.py:140
  302.4 42.4 %all-to-all-start.4 = ((bf16[128,32,128]{2,1,0:T(8,128)(2,1)}), bf16[128,32,128]{2,1,0:T(8,128)(2,1)S(1)}, u32[]{:S(2)}, u32[]{:S(2)}) async-start(bf16[128,32,128]{2,1,0:T(8,128)(2,1)} %after.14), calls=%async_computation.4 | async-start | bytes 2097152 | tf_op jit(solution)/shard_map/all_to_all | solution.py:128
  306.1 37.7 %collective-permute-start.3 = (bf16[3,16,16,512]{3,2,1,0:T(8,128)(2,1)}, bf16[3,16,16,512]{3,2,1,0:T(8,128)(2,1)S(1)}, u32[]{:S(2)}, u32[]{:S(2)}) collective-permute-start(bf16[3,16,16,512]{3,2,1,0:T(8,128)(2,1)} %get-tuple-element.32.refs_2_), channel_id=1, source_target_pairs={{0,8},{1,9},{2,10},{3,11},{4,12},{5,13},{6,14},{7,15},{8,0},{9,1},... | collective-permute-start | bytes 2359304 | tf_op jit(solution)/shard_map/ppermute | solution.py:140
  343.8 1.0 copy-start.17
  344.8 1.1 copy-start.18
  345.9 1.3 copy-start.6
  347.2 46.1 %all-to-all-start.5 = ((bf16[128,32,256]{2,1,0:T(8,128)(2,1)}), bf16[128,32,256]{2,1,0:T(8,128)(2,1)S(1)}, u32[]{:S(2)}, u32[]{:S(2)}) async-start(bf16[128,32,256]{2,1,0:T(8,128)(2,1)} %copy-done.6), calls=%async_computation.5 | async-start | bytes 4194304 | tf_op jit(solution)/shard_map/all_to_all | solution.py:128
  350.8 40.5 %collective-permute-start.4 = (bf16[3,16,16,512]{3,2,1,0:T(8,128)(2,1)}, bf16[3,16,16,512]{3,2,1,0:T(8,128)(2,1)S(1)}, u32[]{:S(2)}, u32[]{:S(2)}) collective-permute-start(bf16[3,16,16,512]{3,2,1,0:T(8,128)(2,1)} %copy-done.37), channel_id=1, source_target_pairs={{0,8},{1,9},{2,10},{3,11},{4,12},{5,13},{6,14},{7,15},{8,0},{9,1},... | collective-permute-start | bytes 2359304 | tf_op jit(solution)/shard_map/ppermute | solution.py:140
  360.3 1.0 copy-start.10
  393.3 3.1 copy-start.3
  393.3 2.0 copy-start.11
  395.3 1.1 copy-start.15
  397.4 29.8 %all-to-all-start.6 = ((bf16[128,32,128]{2,1,0:T(8,128)(2,1)}), bf16[128,32,128]{2,1,0:T(8,128)(2,1)S(1)}, u32[]{:S(2)}, u32[]{:S(2)}) async-start(bf16[128,32,128]{2,1,0:T(8,128)(2,1)} %copy-done.12), calls=%async_computation.6 | async-start | bytes 2097152 | tf_op jit(solution)/shard_map/all_to_all | solution.py:128
  401.5 29.8 %collective-permute-start.6 = (bf16[2,16,16,512]{3,2,1,0:T(8,128)(2,1)}, bf16[2,16,16,512]{3,2,1,0:T(8,128)(2,1)}, u32[]{:S(2)}, u32[]{:S(2)}) collective-permute-start(bf16[2,16,16,512]{3,2,1,0:T(8,128)(2,1)} %copy-done.38), channel_id=1, source_target_pairs={{0,8},{1,9},{2,10},{3,11},{4,12},{5,13},{6,14},{7,15},{8,0},{9,1},... | collective-permute-start | bytes 1572872 | tf_op jit(solution)/shard_map/ppermute | solution.py:140
  408.7 18.5 %copy-start.9 = (bf16[8,16,16,512]{3,2,1,0:T(8,128)(2,1)}, bf16[8,16,16,512]{3,2,1,0:T(8,128)(2,1)S(1)}, u32[]{:S(2)}) copy-start(bf16[8,16,16,512]{3,2,1,0:T(8,128)(2,1)S(1)} %get-tuple-element.37.refs_1_.refs_8_) | copy-start | bytes 6291460
  427.2 4.0 copy-start.4
  431.2 1.6 copy-start.16
  431.2 2.1 copy-start.19
  431.2 2.3 copy-start.23
  431.3 1.3 copy-start.5
  442.5 120.4 %all-to-all-start.7 = ((bf16[128,48,512]{2,1,0:T(8,128)(2,1)}), bf16[128,48,512]{2,1,0:T(8,128)(2,1)}, u32[]{:S(2)}, u32[]{:S(2)}) async-start(bf16[128,48,512]{2,1,0:T(8,128)(2,1)} %bitcast.80), calls=%async_computation.7 | async-start | bytes 12582912 | tf_op jit(solution)/shard_map/all_to_all | solution.py:128
  447.3 113.5 %collective-permute-start.5 = (bf16[8,16,16,512]{3,2,1,0:T(8,128)(2,1)}, bf16[8,16,16,512]{3,2,1,0:T(8,128)(2,1)S(1)}, u32[]{:S(2)}, u32[]{:S(2)}) collective-permute-start(bf16[8,16,16,512]{3,2,1,0:T(8,128)(2,1)} %copy-done.5), channel_id=1, source_target_pairs={{0,8},{1,9},{2,10},{3,11},{4,12},{5,13},{6,14},{7,15},{8,0},{9,1},... | collective-permute-start | bytes 6291464 | tf_op jit(solution)/shard_map/ppermute | solution.py:140
  562.9 1.6 copy-start.39
  566.8 4.0 copy-start.40
  566.8 4.1 copy-start.26
  566.8 4.1 copy-start.28
  566.8 4.1 copy-start.30
  566.8 4.1 copy-start.32
  566.9 4.1 copy-start.34
  566.9 4.1 copy-start.36
  566.9 29.6 %all-to-all-start.8 = ((bf16[128,16,512]{2,1,0:T(8,128)(2,1)}), bf16[128,16,512]{2,1,0:T(8,128)(2,1)S(1)}, u32[]{:S(2)}, u32[]{:S(2)}) async-start(bf16[128,16,512]{2,1,0:T(8,128)(2,1)} %bitcast.83), calls=%async_computation.8 | async-start | bytes 4194304 | tf_op jit(solution)/shard_map/all_to_all | solution.py:128
  595.1 1.3 copy-start.21
  604.4 15.4 %all-to-all-start.9 = ((bf16[16,8,768]{2,1,0:T(8,128)(2,1)}), bf16[16,8,768]{2,1,0:T(8,128)(2,1)S(1)}, u32[]{:S(2)}, u32[]{:S(2)}) async-start(bf16[16,8,768]{2,1,0:T(8,128)(2,1)} %pad_maximum_fusion), calls=%async_computation.9 | async-start | bytes 393216 | tf_op jit(solution)/shard_map/all_to_all | solution.py:519
  (11 other events, 8.1 us)

commit v13 on v11

--- a/solution.py
+++ b/solution.py
@@ -9,7 +9,7 @@
 
 HELD = pl.BlockSpec(memory_space=pl.ANY)
 EPS = 1e-05
-CHANS = 4
+CHANS = 8
 F32 = jnp.float32
 BF16 = jnp.bfloat16
 NN = (((1,), (0,)), ((), ()))

time: 618 us -> 615 us (level)
  no operation moved by 1% of the time
where the time goes in v13:
time: 615 us; the launch traced here: 614 us
  waiting for transfers between devices  395 us (64%)
  Pallas kernels  120 us (20%)
  starting transfers between devices  51.6 us (8%)
  local copies, waits for them, and re-layouts  28.3 us (5%)
  blocking collectives  13.4 us (2%)
    ppermute x7, waiting for transfers between devices, exchange(): return lax.ppermute(array, 'tile', self.partner)  265 us
    all_to_all x9, waiting for transfers between devices, swap(): lax.all_to_all(array, 'tile', split_axis=0, concat_axis=0, axis_index_gro...  129 us
    pallas_call x4, Pallas kernels, make_last(): pl.pallas_call(functools.partial(last_kernel, plan.step, mode), grid=(pla...  42.1 us
    all_to_all x9, starting transfers between devices, swap(): lax.all_to_all(array, 'tile', split_axis=0, concat_axis=0, axis_index_gro...  40.2 us
    pallas_call x3, Pallas kernels, make_middle(): pl.pallas_call(functools.partial(middle_kernel, plan.step), grid_spec=plt...  32.2 us
    unnamed x57, local copies, waits for them, and re-layouts  21 us
    pallas_call x2, Pallas kernels, make_factors(): pl.pallas_call(functools.partial(factors_kernel, plan.step, bool(before))...  17 us
    all_to_all x1, blocking collectives, swap_all(): lax.all_to_all(array, 'tile', split_axis=0, concat_axis=0, tiled=True)  13.4 us
  transfers between devices with their start and end apart: 17, of which 13 were waited for; matrix products, arithmetic and copies ran while one was open for 1% of the time, Pallas kernels for 15%

profile of v13, /device:TPU:0, one launch (start us, length us, event | category | flops | bytes accessed | tf_op | source)
XLA Modules:
  0.0 613.5 jit_solution(4959611880635635500)
XLA Ops:
  3.5 8.5 %factors.2 = (bf16[128,48,512]{2,1,0:T(8,128)(2,1)}, bf16[128,16,512]{2,1,0:T(8,128)(2,1)S(1)}) custom-call(bf16[32,16,2,16,128]{4,3,2,1,0:T(8,128)(2,1)} %bitcast.65, f32[32,512]{1,0:T(8,128)S(1)} %broadcast_multiply_fusion.mask_ref.refs_1_, f32[128,4]{1,0:T(8,128)S(1)} %copy.52.norm_ref.refs_5_.refs_4_.refs_3_, bf16[512,128]{1,0:T(8,128)(2,1)S(1)} %bitcast.49), custom_call_target="tpu_custom_call" | custom-call | flops 200000000 | bytes 600000 | tf_op jit(solution)/shard_map/factors/pallas_call | solution.py:201
  13.4 5.3 all-to-all-start
  18.6 8.5 %factors.3.refs_0_ = bf16[128,48,512]{2,1,0:T(8,128)(2,1)} custom-call(bf16[32,16,2,16,128]{4,3,2,1,0:T(8,128)(2,1)} %bitcast.66, f32[32,512]{1,0:T(8,128)S(1)} %broadcast_multiply_fusion.mask_ref.refs_1_, f32[128,4]{1,0:T(8,128)S(1)} %copy.52.norm_ref.refs_5_.refs_4_.refs_3_, bf16[512,128]{1,0:T(8,128)(2,1)S(1)} %bitcast.50, ...), custom_call_target="tpu_custom_call", output_to_operand_aliasing={{}: (4, {})} | custom-call | flops 200000000 | bytes 600000 | tf_op jit(solution)/shard_map/factors/pallas_call | solution.py:201
  27.1 17.2 %all-to-all-done = bf16[128,16,512]{2,1,0:T(8,128)(2,1)S(1)} async-done(((bf16[128,16,512]{2,1,0:T(8,128)(2,1)}), bf16[128,16,512]{2,1,0:T(8,128)(2,1)S(1)}, u32[]{:S(2)}, u32[]{:S(2)}) %all-to-all-start) | async-done | bytes 2097184 | tf_op jit(solution)/shard_map/all_to_all | solution.py:128
  44.3 4.8 all-to-all-start.1
  49.1 2.6 collective-permute-start
  51.8 110.7 %collective-permute-done.refs_2_.refs_3_ = bf16[8,16,16,512]{3,2,1,0:T(8,128)(2,1)S(1)} collective-permute-done((bf16[8,16,16,512]{3,2,1,0:T(8,128)(2,1)S(1)}, bf16[8,16,16,512]{3,2,1,0:T(8,128)(2,1)S(1)}, u32[]{:S(2)}, u32[]{:S(2)}) %collective-permute-start) | collective-permute-done | bytes 2097184 | tf_op jit(solution)/shard_map/ppermute | solution.py:140
  164.7 1.6 copy-done.8
  166.3 5.9 product.2
  172.2 6.0 all-to-all-start.2
  178.2 2.9 slice.39
  181.7 63.0 %all-to-all-done.2.p_ref.refs_1_ = bf16[128,32,384]{2,1,0:T(8,128)(2,1)S(1)} async-done(((bf16[128,32,384]{2,1,0:T(8,128)(2,1)}), bf16[128,32,384]{2,1,0:T(8,128)(2,1)S(1)}, u32[]{:S(2)}, u32[]{:S(2)}) %all-to-all-start.2) | async-done | bytes 3145760 | tf_op jit(solution)/shard_map/all_to_all | solution.py:128
  244.6 1.7 copy-done
  246.3 8.7 %middle.3 = (bf16[128,32,128]{2,1,0:T(8,128)(2,1)S(1)}, bf16[32,128,512]{2,1,0:T(8,128)(2,1)}, f32[128,128]{1,0:T(8,128)S(1)}, f32[128,128]{1,0:T(8,128)S(1)}) custom-call(s32[1,2]{1,0:T(1,128)S(1)} %fusion.7._, bf16[32,16,2,16,128]{4,3,2,1,0:T(8,128)(2,1)} %bitcast.67, bf16[32,16,2,16,128]{4,3,2,1,0:T(8,128)(2,1)} %bitcast.74, ...), custom_call_target="tpu_custom_call" | custom-call | flops 200000000 | bytes 600000 | tf_op jit(solution)/shard_map/middle/pallas_call | solution.py:381
  257.2 4.6 all-to-all-start.3
  261.8 1.9 slice.40.refs_0_
  263.8 14.9 %middle.4 = (bf16[128,32,256]{2,1,0:T(8,128)(2,1)S(1)}, bf16[32,128,512]{2,1,0:T(8,128)(2,1)}, f32[128,128]{1,0:T(8,128)S(1)}, f32[128,128]{1,0:T(8,128)S(1)}) custom-call(s32[2,2]{1,0:T(2,128)S(1)} %pad_add_fusion._, bf16[32,16,2,16,128]{4,3,2,1,0:T(8,128)(2,1)} %bitcast.68, ...), custom_call_target="tpu_custom_call", output_to_operand_aliasing={{1}: (8, {})} | custom-call | flops 200000000 | bytes 600000 | tf_op jit(solution)/shard_map/middle/pallas_call | solution.py:381
  280.0 3.9 all-to-all-done.3
  283.9 3.1 grad_b.3
  287.9 2.2 collective-permute-done.2.refs_3_.refs_7_
  291.0 3.6 all-to-all-start.4
  295.2 4.2 product.3
  299.3 35.8 %collective-permute-done.3.refs_2_.refs_9_ = bf16[3,16,16,512]{3,2,1,0:T(8,128)(2,1)S(1)} collective-permute-done((bf16[3,16,16,512]{3,2,1,0:T(8,128)(2,1)}, bf16[3,16,16,512]{3,2,1,0:T(8,128)(2,1)S(1)}, u32[]{:S(2)}, u32[]{:S(2)}) %collective-permute-start.3) | collective-permute-done | bytes 786464 | tf_op jit(solution)/shard_map/ppermute | solution.py:140
  337.1 1.7 copy-done.12
  338.8 3.7 all-to-all-start.5
  342.5 2.1 collective-permute-start.4
  344.6 4.6 grad_b.4
  349.2 1.4 copy-done.9
  350.6 18.0 %all-to-all-done.5.p_ref = bf16[128,32,128]{2,1,0:T(8,128)(2,1)S(1)} async-done(((bf16[128,32,128]{2,1,0:T(8,128)(2,1)}), bf16[128,32,128]{2,1,0:T(8,128)(2,1)S(1)}, u32[]{:S(2)}, u32[]{:S(2)}) %all-to-all-start.5) | async-done | bytes 1048608 | tf_op jit(solution)/shard_map/all_to_all | solution.py:128
  368.6 8.6 %middle.5 = (bf16[128,32,128]{2,1,0:T(8,128)(2,1)}, bf16[32,128,512]{2,1,0:T(8,128)(2,1)}, f32[128,128]{1,0:T(8,128)S(1)}, f32[128,128]{1,0:T(8,128)S(1)}) custom-call(s32[1,2]{1,0:T(1,128)S(1)} %fusion.5._, bf16[32,16,2,16,128]{4,3,2,1,0:T(8,128)(2,1)} %bitcast.69, bf16[32,16,2,16,128]{4,3,2,1,0:T(8,128)(2,1)} %bitcast.76, ...), custom_call_target="tpu_custom_call", output_to_operand_aliasing={{1}: (8, {})} | custom-call | flops 200000000 | bytes 600000 | tf_op jit(solution)/shard_map/middle/pallas_call | solution.py:381
  377.2 3.2 collective-permute-done.4.refs_1_.refs_10_
  380.4 3.6 all-to-all-start.6
  384.0 2.3 collective-permute-start.6
  386.2 23.4 %all-to-all-done.6 = bf16[128,32,128]{2,1,0:T(8,128)(2,1)S(1)} async-done(((bf16[128,32,128]{2,1,0:T(8,128)(2,1)}), bf16[128,32,128]{2,1,0:T(8,128)(2,1)S(1)}, u32[]{:S(2)}, u32[]{:S(2)}) %all-to-all-start.6) | async-done | bytes 1048608 | tf_op jit(solution)/shard_map/all_to_all | solution.py:128
  409.6 3.1 grad_b.5.refs_1_
  414.4 8.1 %grad_a.1 = bf16[8,16,48,512]{3,2,1,0:T(8,128)(2,1)} custom-call(bf16[8,16,32,128]{3,2,1,0:T(8,128)(2,1)} %bitcast.18.g_ref.refs_1_.refs_0_, bf16[8,16,32,256]{3,2,1,0:T(8,128)(2,1)} %bitcast.46, bf16[8,16,32,128]{3,2,1,0:T(8,128)(2,1)} %bitcast.48, bf16[8,16,16,512]{3,2,1,0:T(8,128)(2,1)} %copy-done.7, bf16[8,16,16,512]{3,2,1,0:T(8,128)(2,1)} %bitcast.43, ...), custom_call_target="tpu_custom_call" | custom-call | flops 200000000 | bytes 600000 | tf_op jit(solution)/shard_map/grad_a/pallas_call | solution.py:323
  422.5 4.8 all-to-all-start.7
  427.3 113.4 %collective-permute-done.5.refs_0_ = bf16[8,16,16,512]{3,2,1,0:T(8,128)(2,1)S(1)} collective-permute-done((bf16[8,16,16,512]{3,2,1,0:T(8,128)(2,1)}, bf16[8,16,16,512]{3,2,1,0:T(8,128)(2,1)S(1)}, u32[]{:S(2)}, u32[]{:S(2)}) %collective-permute-start.5) | collective-permute-done | bytes 2097184 | tf_op jit(solution)/shard_map/ppermute | solution.py:140
  540.7 2.1 all-to-all-done.7.refs_1_.refs_2_.refs_3_
  542.8 1.6 copy-done.24
  544.4 2.3 add_convert_fusion
  546.8 4.0 all-to-all-start.8
  550.9 14.5 %last_both.1 = (bf16[32,16,2,16,128]{4,3,2,1,0:T(8,128)(2,1)}, f32[128,512]{1,0:T(8,128)S(1)}) custom-call(bf16[32,16,2,16,128]{4,3,2,1,0:T(8,128)(2,1)} %bitcast.70, f32[32,512]{1,0:T(8,128)S(1)} %broadcast_multiply_fusion.mask_ref.refs_1_, bf16[128,48,512]{2,1,0:T(8,128)(2,1)} %all-to-all-done.7.refs_1_.refs_2_.refs_3_, ...), custom_call_target="tpu_custom_call" | custom-call | flops 200000000 | bytes 600000 | tf_op jit(solution)/shard_map/last_both/pallas_call | solution.py:504
  565.3 9.6 %last_a.1 = (bf16[16,128,512]{2,1,0:T(8,128)(2,1)S(1)}, f32[128,256]{1,0:T(8,128)S(1)}) custom-call(bf16[32,16,2,16,128]{4,3,2,1,0:T(8,128)(2,1)} %bitcast.71, f32[32,512]{1,0:T(8,128)S(1)} %broadcast_multiply_fusion.mask_ref.refs_1_, bf16[128,48,512]{2,1,0:T(8,128)(2,1)} %all-to-all-done.7.refs_1_.refs_2_.refs_3_, ...), custom_call_target="tpu_custom_call" | custom-call | flops 200000000 | bytes 600000 | tf_op jit(solution)/shard_map/last_a/pallas_call | solution.py:504
  576.3 7.2 %last_b_sum.1 = f32[128,256]{1,0:T(8,128)S(1)} custom-call(bf16[32,16,2,16,128]{4,3,2,1,0:T(8,128)(2,1)} %bitcast.72, f32[32,512]{1,0:T(8,128)S(1)} %broadcast_multiply_fusion.mask_ref.refs_1_, bf16[128,16,512]{2,1,0:T(8,128)(2,1)S(1)} %after.17.refs_2_, f32[128,4]{1,0:T(8,128)S(1)} %copy.52.norm_ref.refs_5_.refs_4_.refs_3_, ...), custom_call_target="tpu_custom_call" | custom-call | flops 200000000 | bytes 600000 | tf_op jit(solution)/shard_map/last_b_sum/pallas_call | solution.py:504
  583.6 13.4 %all_to_all.57 = bf16[16,8,768]{2,1,0:T(8,128)(2,1)S(1)} all-to-all(bf16[16,8,768]{2,1,0:T(8,128)(2,1)S(1)} %pad_maximum_fusion), channel_id=1, replica_groups=mesh['crops'=2,'tile'=16] {'tile'}, dimensions={0} | all-to-all | bytes 393216 | tf_op jit(solution)/shard_map/all_to_all | solution.py:519
  597.8 3.5 all-to-all-start.10
  601.3 10.8 %last_b.1 = bf16[32,16,2,16,128]{4,3,2,1,0:T(8,128)(2,1)} custom-call(bf16[32,16,2,16,128]{4,3,2,1,0:T(8,128)(2,1)} %bitcast.73, f32[32,512]{1,0:T(8,128)S(1)} %broadcast_multiply_fusion.mask_ref.refs_1_, bf16[128,16,512]{2,1,0:T(8,128)(2,1)S(1)} %after.17.refs_2_, bf16[16,128,512]{2,1,0:T(8,128)(2,1)} %copy-done.15, ...), custom_call_target="tpu_custom_call", output_to_operand_aliasing={{}: (7, {})} | custom-call | flops 200000000 | bytes 600000 | tf_op jit(solution)/shard_map/last_b/pallas_call | solution.py:504
  (95 shorter events, 20.2 us)
Async XLA Ops:
  12.1 1.3 copy-start.14
  13.4 31.0 %all-to-all-start = ((bf16[128,16,512]{2,1,0:T(8,128)(2,1)}), bf16[128,16,512]{2,1,0:T(8,128)(2,1)S(1)}, u32[]{:S(2)}, u32[]{:S(2)}) async-start(bf16[128,16,512]{2,1,0:T(8,128)(2,1)} %copy-done.14), calls=%async_computation | async-start | bytes 4194304 | tf_op jit(solution)/shard_map/all_to_all | solution.py:128
  44.3 4.8 copy-start.2
  44.3 120.4 %all-to-all-start.1 = ((bf16[128,48,512]{2,1,0:T(8,128)(2,1)}), bf16[128,48,512]{2,1,0:T(8,128)(2,1)}, u32[]{:S(2)}, u32[]{:S(2)}) async-start(bf16[128,48,512]{2,1,0:T(8,128)(2,1)} %after.9), calls=%async_computation.1 | async-start | bytes 12582912 | tf_op jit(solution)/shard_map/all_to_all | solution.py:128
  49.1 113.4 %collective-permute-start = (bf16[8,16,16,512]{3,2,1,0:T(8,128)(2,1)S(1)}, bf16[8,16,16,512]{3,2,1,0:T(8,128)(2,1)S(1)}, u32[]{:S(2)}, u32[]{:S(2)}) collective-permute-start(bf16[8,16,16,512]{3,2,1,0:T(8,128)(2,1)S(1)} %bitcast.41), channel_id=1, source_target_pairs={{0,8},{1,9},{2,10},{3,11},{4,12},{5,13},{6,14},{7,15},{8,0},{9,1},... | collective-permute-start | bytes 6291464 | tf_op jit(solution)/shard_map/ppermute | solution.py:140
  162.5 1.4 copy-start.7
  164.7 1.6 copy-start.8
  172.2 72.4 %all-to-all-start.2 = ((bf16[128,32,384]{2,1,0:T(8,128)(2,1)}), bf16[128,32,384]{2,1,0:T(8,128)(2,1)S(1)}, u32[]{:S(2)}, u32[]{:S(2)}) async-start(bf16[128,32,384]{2,1,0:T(8,128)(2,1)} %bitcast.78), calls=%async_computation.2 | async-start | bytes 6291456 | tf_op jit(solution)/shard_map/all_to_all | solution.py:128
  178.2 3.1 copy-start.26
  178.2 3.2 copy-start.17
  181.1 75.1 %collective-permute-start.1 = (bf16[6,16,16,512]{3,2,1,0:T(8,128)(2,1)}, bf16[6,16,16,512]{3,2,1,0:T(8,128)(2,1)}, u32[]{:S(2)}, u32[]{:S(2)}) collective-permute-start(bf16[6,16,16,512]{3,2,1,0:T(8,128)(2,1)} %slice.39), channel_id=1, source_target_pairs={{0,8},{1,9},{2,10},{3,11},{4,12},{5,13},{6,14},{7,15},{8,0},{9,1},... | collective-permute-start | bytes 4718600 | tf_op jit(solution)/shard_map/ppermute | solution.py:140
  244.6 1.7 copy-start
  254.9 0.6 copy-start.18
  255.6 0.6 copy-start.20
  256.2 7.5 %copy-start.1 = (bf16[128,32,384]{2,1,0:T(8,128)(2,1)S(1)}, bf16[128,32,384]{2,1,0:T(8,128)(2,1)}, u32[]{:S(2)}) copy-start(bf16[128,32,384]{2,1,0:T(8,128)(2,1)} %copy-done) | copy-start | bytes 9437188
  256.2 1.0 copy-start.10
  257.2 26.8 %all-to-all-start.3 = ((bf16[128,32,128]{2,1,0:T(8,128)(2,1)}), bf16[128,32,128]{2,1,0:T(8,128)(2,1)}, u32[]{:S(2)}, u32[]{:S(2)}) async-start(bf16[128,32,128]{2,1,0:T(8,128)(2,1)} %copy-done.10), calls=%async_computation.3 | async-start | bytes 2097152 | tf_op jit(solution)/shard_map/all_to_all | solution.py:128
  263.7 26.4 %collective-permute-start.2 = (bf16[2,16,16,512]{3,2,1,0:T(8,128)(2,1)}, bf16[2,16,16,512]{3,2,1,0:T(8,128)(2,1)S(1)}, u32[]{:S(2)}, u32[]{:S(2)}) collective-permute-start(bf16[2,16,16,512]{3,2,1,0:T(8,128)(2,1)} %after.11), channel_id=1, source_target_pairs={{0,8},{1,9},{2,10},{3,11},{4,12},{5,13},{6,14},{7,15},{8,0},{9,1},... | collective-permute-start | bytes 1572872 | tf_op jit(solution)/shard_map/ppermute | solution.py:140
  278.7 1.3 copy-start.6
  287.0 0.9 copy-start.22
  287.9 2.2 copy-start.23
  290.1 0.9 copy-start.16
  291.0 46.1 %all-to-all-start.4 = ((bf16[128,32,256]{2,1,0:T(8,128)(2,1)}), bf16[128,32,256]{2,1,0:T(8,128)(2,1)S(1)}, u32[]{:S(2)}, u32[]{:S(2)}) async-start(bf16[128,32,256]{2,1,0:T(8,128)(2,1)} %after.12), calls=%async_computation.4 | async-start | bytes 4194304 | tf_op jit(solution)/shard_map/all_to_all | solution.py:128
  294.6 40.5 %collective-permute-start.3 = (bf16[3,16,16,512]{3,2,1,0:T(8,128)(2,1)}, bf16[3,16,16,512]{3,2,1,0:T(8,128)(2,1)S(1)}, u32[]{:S(2)}, u32[]{:S(2)}) collective-permute-start(bf16[3,16,16,512]{3,2,1,0:T(8,128)(2,1)} %copy-done.16), channel_id=1, source_target_pairs={{0,8},{1,9},{2,10},{3,11},{4,12},{5,13},{6,14},{7,15},{8,0},{9,1},... | collective-permute-start | bytes 2359304 | tf_op jit(solution)/shard_map/ppermute | solution.py:140
  335.1 0.9 copy-start.11
  337.1 1.7 copy-start.3
  337.1 1.7 copy-start.12
  338.8 29.9 %all-to-all-start.5 = ((bf16[128,32,128]{2,1,0:T(8,128)(2,1)}), bf16[128,32,128]{2,1,0:T(8,128)(2,1)S(1)}, u32[]{:S(2)}, u32[]{:S(2)}) async-start(bf16[128,32,128]{2,1,0:T(8,128)(2,1)} %after.13), calls=%async_computation.5 | async-start | bytes 2097152 | tf_op jit(solution)/shard_map/all_to_all | solution.py:128
  342.5 38.0 %collective-permute-start.4 = (bf16[3,16,16,512]{3,2,1,0:T(8,128)(2,1)}, bf16[3,16,16,512]{3,2,1,0:T(8,128)(2,1)S(1)}, u32[]{:S(2)}, u32[]{:S(2)}) collective-permute-start(bf16[3,16,16,512]{3,2,1,0:T(8,128)(2,1)} %copy-done.22), channel_id=1, source_target_pairs={{0,8},{1,9},{2,10},{3,11},{4,12},{5,13},{6,14},{7,15},{8,0},{9,1},... | collective-permute-start | bytes 2359304 | tf_op jit(solution)/shard_map/ppermute | solution.py:140
  349.2 1.4 copy-start.9
  380.4 29.2 %all-to-all-start.6 = ((bf16[128,32,128]{2,1,0:T(8,128)(2,1)}), bf16[128,32,128]{2,1,0:T(8,128)(2,1)S(1)}, u32[]{:S(2)}, u32[]{:S(2)}) async-start(bf16[128,32,128]{2,1,0:T(8,128)(2,1)} %after.14), calls=%async_computation.6 | async-start | bytes 2097152 | tf_op jit(solution)/shard_map/all_to_all | solution.py:128
  384.0 28.8 %collective-permute-start.6 = (bf16[2,16,16,512]{3,2,1,0:T(8,128)(2,1)}, bf16[2,16,16,512]{3,2,1,0:T(8,128)(2,1)S(1)}, u32[]{:S(2)}, u32[]{:S(2)}) collective-permute-start(bf16[2,16,16,512]{3,2,1,0:T(8,128)(2,1)} %copy-done.23), channel_id=1, source_target_pairs={{0,8},{1,9},{2,10},{3,11},{4,12},{5,13},{6,14},{7,15},{8,0},{9,1},... | collective-permute-start | bytes 1572872 | tf_op jit(solution)/shard_map/ppermute | solution.py:140
  409.6 3.1 copy-start.4
  412.7 1.6 copy-start.13
  412.8 1.3 copy-start.5
  422.5 120.4 %all-to-all-start.7 = ((bf16[128,48,512]{2,1,0:T(8,128)(2,1)}), bf16[128,48,512]{2,1,0:T(8,128)(2,1)}, u32[]{:S(2)}, u32[]{:S(2)}) async-start(bf16[128,48,512]{2,1,0:T(8,128)(2,1)} %bitcast.77), calls=%async_computation.7 | async-start | bytes 12582912 | tf_op jit(solution)/shard_map/all_to_all | solution.py:128
  427.3 113.5 %collective-permute-start.5 = (bf16[8,16,16,512]{3,2,1,0:T(8,128)(2,1)}, bf16[8,16,16,512]{3,2,1,0:T(8,128)(2,1)S(1)}, u32[]{:S(2)}, u32[]{:S(2)}) collective-permute-start(bf16[8,16,16,512]{3,2,1,0:T(8,128)(2,1)} %copy-done.5), channel_id=1, source_target_pairs={{0,8},{1,9},{2,10},{3,11},{4,12},{5,13},{6,14},{7,15},{8,0},{9,1},... | collective-permute-start | bytes 6291464 | tf_op jit(solution)/shard_map/ppermute | solution.py:140
  542.8 1.6 copy-start.24
  546.8 4.0 copy-start.25
  546.8 4.1 copy-start.19
  546.8 4.1 copy-start.21
  546.8 29.6 %all-to-all-start.8 = ((bf16[128,16,512]{2,1,0:T(8,128)(2,1)}), bf16[128,16,512]{2,1,0:T(8,128)(2,1)S(1)}, u32[]{:S(2)}, u32[]{:S(2)}) async-start(bf16[128,16,512]{2,1,0:T(8,128)(2,1)} %bitcast.79), calls=%async_computation.8 | async-start | bytes 4194304 | tf_op jit(solution)/shard_map/all_to_all | solution.py:128
  575.0 1.4 copy-start.15
  597.8 14.3 %all-to-all-start.10 = ((bf16[16,8,768]{2,1,0:T(8,128)(2,1)}), bf16[16,8,768]{2,1,0:T(8,128)(2,1)S(1)}, u32[]{:S(2)}, u32[]{:S(2)}) async-start(bf16[16,8,768]{2,1,0:T(8,128)(2,1)} %broadcast_in_dim.2), calls=%async_computation.10 | async-start | bytes 393216 | tf_op jit(solution)/shard_map/all_to_all | solution.py:519

commit v14 on v13

--- a/solution.py
+++ b/solution.py
@@ -550,7 +550,7 @@
 
     plan_cut = plan.cut
     two = plan.subs == 2
-    cut_b, back_a = plan_cut(6, 2), plan_cut(3, 3, 2)
+    cut_b, back_a = plan_cut(6, 2), plan_cut(2, 3, 3)
     small = [norms, w_t, w_cat]
 
     def middle(at, first, before, ready, product):

time: 615 us -> 620 us (level)
    unnamed x57 -> x73, local copies, waits for them, and re-layouts: 21 us -> 23.1 us
  transfers between devices with their start and end apart: 17 -> 17, of which waited for: 13 -> 15; matrix products, arithmetic and copies ran while one was open for 1% -> 1% of each run, Pallas kernels for 15% -> 15%
where the time goes in v14:
time: 620 us; the launch traced here: 619 us
  waiting for transfers between devices  396 us (64%)
  Pallas kernels  121 us (20%)
  starting transfers between devices  51.8 us (8%)
  local copies, waits for them, and re-layouts  30.3 us (5%)
  blocking collectives  14.1 us (2%)
    ppermute x7, waiting for transfers between devices, exchange(): return lax.ppermute(array, 'tile', self.partner)  267 us
    all_to_all x9, waiting for transfers between devices, swap(): lax.all_to_all(array, 'tile', split_axis=0, concat_axis=0, axis_index_gro...  129 us
    pallas_call x4, Pallas kernels, make_last(): pl.pallas_call(functools.partial(last_kernel, plan.step, mode), grid=(pla...  42.1 us
    all_to_all x9, starting transfers between devices, swap(): lax.all_to_all(array, 'tile', split_axis=0, concat_axis=0, axis_index_gro...  40.7 us
    pallas_call x3, Pallas kernels, make_middle(): pl.pallas_call(functools.partial(middle_kernel, plan.step), grid_spec=plt...  32.2 us
    unnamed x73, local copies, waits for them, and re-layouts  23.1 us
    pallas_call x2, Pallas kernels, make_factors(): pl.pallas_call(functools.partial(factors_kernel, plan.step, bool(before))...  17.1 us
    all_to_all x1, blocking collectives, swap_all(): lax.all_to_all(array, 'tile', split_axis=0, concat_axis=0, tiled=True)  14.1 us
  transfers between devices with their start and end apart: 17, of which 15 were waited for; matrix products, arithmetic and copies ran while one was open for 1% of the time, Pallas kernels for 15%

profile of v14, /device:TPU:0, one launch (start us, length us, event | category | flops | bytes accessed | tf_op | source)
XLA Modules:
  0.0 618.9 jit_solution(17037625980538664025)
XLA Ops:
  3.5 8.6 %factors.2 = (bf16[128,48,512]{2,1,0:T(8,128)(2,1)}, bf16[128,16,512]{2,1,0:T(8,128)(2,1)S(1)}) custom-call(bf16[32,16,2,16,128]{4,3,2,1,0:T(8,128)(2,1)} %bitcast.65, f32[32,512]{1,0:T(8,128)S(1)} %broadcast_multiply_fusion.mask_ref.refs_1_, f32[128,4]{1,0:T(8,128)S(1)} %copy.52.norm_ref.refs_5_.refs_4_.refs_3_, bf16[512,128]{1,0:T(8,128)(2,1)S(1)} %bitcast.49), custom_call_target="tpu_custom_call" | custom-call | flops 200000000 | bytes 600000 | tf_op jit(solution)/shard_map/factors/pallas_call | solution.py:201
  13.4 5.3 all-to-all-start
  18.7 8.5 %factors.3.refs_0_ = bf16[128,48,512]{2,1,0:T(8,128)(2,1)} custom-call(bf16[32,16,2,16,128]{4,3,2,1,0:T(8,128)(2,1)} %bitcast.66, f32[32,512]{1,0:T(8,128)S(1)} %broadcast_multiply_fusion.mask_ref.refs_1_, f32[128,4]{1,0:T(8,128)S(1)} %copy.52.norm_ref.refs_5_.refs_4_.refs_3_, bf16[512,128]{1,0:T(8,128)(2,1)S(1)} %bitcast.50, ...), custom_call_target="tpu_custom_call", output_to_operand_aliasing={{}: (4, {})} | custom-call | flops 200000000 | bytes 600000 | tf_op jit(solution)/shard_map/factors/pallas_call | solution.py:201
  27.2 17.2 %all-to-all-done = bf16[128,16,512]{2,1,0:T(8,128)(2,1)S(1)} async-done(((bf16[128,16,512]{2,1,0:T(8,128)(2,1)}), bf16[128,16,512]{2,1,0:T(8,128)(2,1)S(1)}, u32[]{:S(2)}, u32[]{:S(2)}) %all-to-all-start) | async-done | bytes 2097184 | tf_op jit(solution)/shard_map/all_to_all | solution.py:128
  44.4 4.8 all-to-all-start.1
  49.2 2.6 collective-permute-start
  51.8 110.7 %collective-permute-done.refs_2_.refs_3_ = bf16[8,16,16,512]{3,2,1,0:T(8,128)(2,1)S(1)} collective-permute-done((bf16[8,16,16,512]{3,2,1,0:T(8,128)(2,1)S(1)}, bf16[8,16,16,512]{3,2,1,0:T(8,128)(2,1)S(1)}, u32[]{:S(2)}, u32[]{:S(2)}) %collective-permute-start) | collective-permute-done | bytes 2097184 | tf_op jit(solution)/shard_map/ppermute | solution.py:140
  164.7 1.6 copy-done.9
  166.3 5.9 product.2
  172.2 6.0 all-to-all-start.2
  178.3 2.9 slice.39
  181.6 63.0 %all-to-all-done.2.p_ref.refs_1_ = bf16[128,32,384]{2,1,0:T(8,128)(2,1)S(1)} async-done(((bf16[128,32,384]{2,1,0:T(8,128)(2,1)}), bf16[128,32,384]{2,1,0:T(8,128)(2,1)S(1)}, u32[]{:S(2)}, u32[]{:S(2)}) %all-to-all-start.2) | async-done | bytes 3145760 | tf_op jit(solution)/shard_map/all_to_all | solution.py:128
  244.6 1.7 copy-done
  246.3 8.7 %middle.3 = (bf16[128,32,128]{2,1,0:T(8,128)(2,1)S(1)}, bf16[32,128,512]{2,1,0:T(8,128)(2,1)}, f32[128,128]{1,0:T(8,128)S(1)}, f32[128,128]{1,0:T(8,128)S(1)}) custom-call(s32[1,2]{1,0:T(1,128)S(1)} %fusion.7._, bf16[32,16,2,16,128]{4,3,2,1,0:T(8,128)(2,1)} %bitcast.67, bf16[32,16,2,16,128]{4,3,2,1,0:T(8,128)(2,1)} %bitcast.74, ...), custom_call_target="tpu_custom_call" | custom-call | flops 200000000 | bytes 600000 | tf_op jit(solution)/shard_map/middle/pallas_call | solution.py:381
  257.2 4.6 all-to-all-start.3
  261.8 1.9 slice.40.refs_0_
  263.8 14.9 %middle.4 = (bf16[128,32,256]{2,1,0:T(8,128)(2,1)S(1)}, bf16[32,128,512]{2,1,0:T(8,128)(2,1)}, f32[128,128]{1,0:T(8,128)S(1)}, f32[128,128]{1,0:T(8,128)S(1)}) custom-call(s32[2,2]{1,0:T(2,128)S(1)} %pad_add_fusion._, bf16[32,16,2,16,128]{4,3,2,1,0:T(8,128)(2,1)} %bitcast.68, ...), custom_call_target="tpu_custom_call", output_to_operand_aliasing={{1}: (8, {})} | custom-call | flops 200000000 | bytes 600000 | tf_op jit(solution)/shard_map/middle/pallas_call | solution.py:381
  281.3 2.8 all-to-all-done.3
  284.1 3.8 grad_b.3
  290.9 3.6 all-to-all-start.4
  295.1 4.2 product.3
  299.3 30.1 %collective-permute-done.3.refs_2_.refs_9_ = bf16[2,16,16,512]{3,2,1,0:T(8,128)(2,1)S(1)} collective-permute-done((bf16[2,16,16,512]{3,2,1,0:T(8,128)(2,1)}, bf16[2,16,16,512]{3,2,1,0:T(8,128)(2,1)S(1)}, u32[]{:S(2)}, u32[]{:S(2)}) %collective-permute-start.3) | collective-permute-done | bytes 524320 | tf_op jit(solution)/shard_map/ppermute | solution.py:140
  329.4 2.0 all-to-all-done.4
  332.7 3.6 all-to-all-start.5
  336.3 1.5 collective-permute-start.4
  337.9 4.6 grad_b.4
  342.5 1.4 copy-done.10
  343.8 18.0 %all-to-all-done.5.p_ref = bf16[128,32,128]{2,1,0:T(8,128)(2,1)S(1)} async-done(((bf16[128,32,128]{2,1,0:T(8,128)(2,1)}), bf16[128,32,128]{2,1,0:T(8,128)(2,1)S(1)}, u32[]{:S(2)}, u32[]{:S(2)}) %all-to-all-start.5) | async-done | bytes 1048608 | tf_op jit(solution)/shard_map/all_to_all | solution.py:128
  361.9 8.6 %middle.5 = (bf16[128,32,128]{2,1,0:T(8,128)(2,1)}, bf16[32,128,512]{2,1,0:T(8,128)(2,1)}, f32[128,128]{1,0:T(8,128)S(1)}, f32[128,128]{1,0:T(8,128)S(1)}) custom-call(s32[1,2]{1,0:T(1,128)S(1)} %fusion.5._, bf16[32,16,2,16,128]{4,3,2,1,0:T(8,128)(2,1)} %bitcast.69, bf16[32,16,2,16,128]{4,3,2,1,0:T(8,128)(2,1)} %bitcast.76, ...), custom_call_target="tpu_custom_call", output_to_operand_aliasing={{1}: (8, {})} | custom-call | flops 200000000 | bytes 600000 | tf_op jit(solution)/shard_map/middle/pallas_call | solution.py:381
  370.5 3.7 collective-permute-done.4.refs_1_.refs_10_
  375.0 3.6 all-to-all-start.6
  378.6 1.8 collective-permute-start.6
  380.3 24.2 %all-to-all-done.6 = bf16[128,32,128]{2,1,0:T(8,128)(2,1)S(1)} async-done(((bf16[128,32,128]{2,1,0:T(8,128)(2,1)}), bf16[128,32,128]{2,1,0:T(8,128)(2,1)S(1)}, u32[]{:S(2)}, u32[]{:S(2)}) %all-to-all-start.6) | async-done | bytes 1048608 | tf_op jit(solution)/shard_map/all_to_all | solution.py:128
  404.6 3.1 grad_b.5.refs_1_
  407.7 8.8 %collective-permute-done.6.refs_0_ = bf16[3,16,16,512]{3,2,1,0:T(8,128)(2,1)} collective-permute-done((bf16[3,16,16,512]{3,2,1,0:T(8,128)(2,1)}, bf16[3,16,16,512]{3,2,1,0:T(8,128)(2,1)}, u32[]{:S(2)}, u32[]{:S(2)}) %collective-permute-start.6) | collective-permute-done | bytes 786464 | tf_op jit(solution)/shard_map/ppermute | solution.py:140
  416.5 8.3 %grad_a.1 = bf16[8,16,48,512]{3,2,1,0:T(8,128)(2,1)} custom-call(bf16[8,16,32,128]{3,2,1,0:T(8,128)(2,1)} %bitcast.18.g_ref.refs_1_.refs_0_, bf16[8,16,32,256]{3,2,1,0:T(8,128)(2,1)} %bitcast.46, bf16[8,16,32,128]{3,2,1,0:T(8,128)(2,1)} %bitcast.48, bf16[8,16,16,512]{3,2,1,0:T(8,128)(2,1)} %copy-done.8, bf16[8,16,16,512]{3,2,1,0:T(8,128)(2,1)} %bitcast.43, ...), custom_call_target="tpu_custom_call" | custom-call | flops 200000000 | bytes 600000 | tf_op jit(solution)/shard_map/grad_a/pallas_call | solution.py:323
  424.9 4.8 all-to-all-start.7
  430.6 112.5 %collective-permute-done.5.refs_0_ = bf16[8,16,16,512]{3,2,1,0:T(8,128)(2,1)S(1)} collective-permute-done((bf16[8,16,16,512]{3,2,1,0:T(8,128)(2,1)S(1)}, bf16[8,16,16,512]{3,2,1,0:T(8,128)(2,1)S(1)}, u32[]{:S(2)}, u32[]{:S(2)}) %collective-permute-start.5) | collective-permute-done | bytes 2097184 | tf_op jit(solution)/shard_map/ppermute | solution.py:140
  545.2 1.6 copy-done.6
  546.8 1.6 copy-done.31
  548.4 2.4 add_convert_fusion
  550.8 4.6 all-to-all-start.8
  555.6 14.5 %last_both.1 = (bf16[32,16,2,16,128]{4,3,2,1,0:T(8,128)(2,1)}, f32[128,512]{1,0:T(8,128)S(1)}) custom-call(bf16[32,16,2,16,128]{4,3,2,1,0:T(8,128)(2,1)} %bitcast.70, f32[32,512]{1,0:T(8,128)S(1)} %broadcast_multiply_fusion.mask_ref.refs_1_, bf16[128,48,512]{2,1,0:T(8,128)(2,1)} %all-to-all-done.7.refs_1_.refs_2_.refs_3_, ...), custom_call_target="tpu_custom_call" | custom-call | flops 200000000 | bytes 600000 | tf_op jit(solution)/shard_map/last_both/pallas_call | solution.py:504
  570.0 9.6 %last_a.1 = (bf16[16,128,512]{2,1,0:T(8,128)(2,1)S(1)}, f32[128,256]{1,0:T(8,128)S(1)}) custom-call(bf16[32,16,2,16,128]{4,3,2,1,0:T(8,128)(2,1)} %bitcast.71, f32[32,512]{1,0:T(8,128)S(1)} %broadcast_multiply_fusion.mask_ref.refs_1_, bf16[128,48,512]{2,1,0:T(8,128)(2,1)} %all-to-all-done.7.refs_1_.refs_2_.refs_3_, ...), custom_call_target="tpu_custom_call" | custom-call | flops 200000000 | bytes 600000 | tf_op jit(solution)/shard_map/last_a/pallas_call | solution.py:504
  581.1 7.2 %last_b_sum.1 = f32[128,256]{1,0:T(8,128)S(1)} custom-call(bf16[32,16,2,16,128]{4,3,2,1,0:T(8,128)(2,1)} %bitcast.72, f32[32,512]{1,0:T(8,128)S(1)} %broadcast_multiply_fusion.mask_ref.refs_1_, bf16[128,16,512]{2,1,0:T(8,128)(2,1)S(1)} %after.17.refs_2_, f32[128,4]{1,0:T(8,128)S(1)} %copy.52.norm_ref.refs_5_.refs_4_.refs_3_, ...), custom_call_target="tpu_custom_call" | custom-call | flops 200000000 | bytes 600000 | tf_op jit(solution)/shard_map/last_b_sum/pallas_call | solution.py:504
  588.4 14.1 %all_to_all.57 = bf16[16,8,768]{2,1,0:T(8,128)(2,1)S(1)} all-to-all(bf16[16,8,768]{2,1,0:T(8,128)(2,1)S(1)} %pad_maximum_fusion), channel_id=1, replica_groups=mesh['crops'=2,'tile'=16] {'tile'}, dimensions={0} | all-to-all | bytes 393216 | tf_op jit(solution)/shard_map/all_to_all | solution.py:519
  603.2 3.5 all-to-all-start.10
  606.7 10.8 %last_b.1 = bf16[32,16,2,16,128]{4,3,2,1,0:T(8,128)(2,1)} custom-call(bf16[32,16,2,16,128]{4,3,2,1,0:T(8,128)(2,1)} %bitcast.73, f32[32,512]{1,0:T(8,128)S(1)} %broadcast_multiply_fusion.mask_ref.refs_1_, bf16[128,16,512]{2,1,0:T(8,128)(2,1)S(1)} %after.17.refs_2_, bf16[16,128,512]{2,1,0:T(8,128)(2,1)} %copy-done.17, ...), custom_call_target="tpu_custom_call", output_to_operand_aliasing={{}: (7, {})} | custom-call | flops 200000000 | bytes 600000 | tf_op jit(solution)/shard_map/last_b/pallas_call | solution.py:504
  (111 shorter events, 24.6 us)
Async XLA Ops:
  12.1 1.3 copy-start.16
  13.4 31.0 %all-to-all-start = ((bf16[128,16,512]{2,1,0:T(8,128)(2,1)}), bf16[128,16,512]{2,1,0:T(8,128)(2,1)S(1)}, u32[]{:S(2)}, u32[]{:S(2)}) async-start(bf16[128,16,512]{2,1,0:T(8,128)(2,1)} %copy-done.16), calls=%async_computation | async-start | bytes 4194304 | tf_op jit(solution)/shard_map/all_to_all | solution.py:128
  44.4 4.8 copy-start.2
  44.4 120.4 %all-to-all-start.1 = ((bf16[128,48,512]{2,1,0:T(8,128)(2,1)}), bf16[128,48,512]{2,1,0:T(8,128)(2,1)}, u32[]{:S(2)}, u32[]{:S(2)}) async-start(bf16[128,48,512]{2,1,0:T(8,128)(2,1)} %after.9), calls=%async_computation.1 | async-start | bytes 12582912 | tf_op jit(solution)/shard_map/all_to_all | solution.py:128
  49.2 113.4 %collective-permute-start = (bf16[8,16,16,512]{3,2,1,0:T(8,128)(2,1)S(1)}, bf16[8,16,16,512]{3,2,1,0:T(8,128)(2,1)S(1)}, u32[]{:S(2)}, u32[]{:S(2)}) collective-permute-start(bf16[8,16,16,512]{3,2,1,0:T(8,128)(2,1)S(1)} %bitcast.41), channel_id=1, source_target_pairs={{0,8},{1,9},{2,10},{3,11},{4,12},{5,13},{6,14},{7,15},{8,0},{9,1},... | collective-permute-start | bytes 6291464 | tf_op jit(solution)/shard_map/ppermute | solution.py:140
  162.5 1.4 copy-start.8
  164.7 1.6 copy-start.9
  172.2 72.4 %all-to-all-start.2 = ((bf16[128,32,384]{2,1,0:T(8,128)(2,1)}), bf16[128,32,384]{2,1,0:T(8,128)(2,1)S(1)}, u32[]{:S(2)}, u32[]{:S(2)}) async-start(bf16[128,32,384]{2,1,0:T(8,128)(2,1)} %bitcast.78), calls=%async_computation.2 | async-start | bytes 6291456 | tf_op jit(solution)/shard_map/all_to_all | solution.py:128
  178.2 3.1 copy-start.33
  178.3 3.2 copy-start.20
  181.1 75.1 %collective-permute-start.1 = (bf16[6,16,16,512]{3,2,1,0:T(8,128)(2,1)}, bf16[6,16,16,512]{3,2,1,0:T(8,128)(2,1)}, u32[]{:S(2)}, u32[]{:S(2)}) collective-permute-start(bf16[6,16,16,512]{3,2,1,0:T(8,128)(2,1)} %slice.39), channel_id=1, source_target_pairs={{0,8},{1,9},{2,10},{3,11},{4,12},{5,13},{6,14},{7,15},{8,0},{9,1},... | collective-permute-start | bytes 4718600 | tf_op jit(solution)/shard_map/ppermute | solution.py:140
  244.6 1.7 copy-start
  256.2 7.4 %copy-start.1 = (bf16[128,32,384]{2,1,0:T(8,128)(2,1)S(1)}, bf16[128,32,384]{2,1,0:T(8,128)(2,1)}, u32[]{:S(2)}) copy-start(bf16[128,32,384]{2,1,0:T(8,128)(2,1)} %copy-done) | copy-start | bytes 9437188
  256.2 1.0 copy-start.13
  257.2 26.8 %all-to-all-start.3 = ((bf16[128,32,128]{2,1,0:T(8,128)(2,1)}), bf16[128,32,128]{2,1,0:T(8,128)(2,1)}, u32[]{:S(2)}, u32[]{:S(2)}) async-start(bf16[128,32,128]{2,1,0:T(8,128)(2,1)} %copy-done.13), calls=%async_computation.3 | async-start | bytes 2097152 | tf_op jit(solution)/shard_map/all_to_all | solution.py:128
  263.7 26.4 %collective-permute-start.2 = (bf16[2,16,16,512]{3,2,1,0:T(8,128)(2,1)}, bf16[2,16,16,512]{3,2,1,0:T(8,128)(2,1)S(1)}, u32[]{:S(2)}, u32[]{:S(2)}) collective-permute-start(bf16[2,16,16,512]{3,2,1,0:T(8,128)(2,1)} %after.11), channel_id=1, source_target_pairs={{0,8},{1,9},{2,10},{3,11},{4,12},{5,13},{6,14},{7,15},{8,0},{9,1},... | collective-permute-start | bytes 1572872 | tf_op jit(solution)/shard_map/ppermute | solution.py:140
  278.7 1.3 copy-start.7
  287.8 0.9 copy-start.30
  290.1 5.0 copy-start.11
  290.1 0.8 copy-start.21
  290.9 40.5 %all-to-all-start.4 = ((bf16[128,32,256]{2,1,0:T(8,128)(2,1)}), bf16[128,32,256]{2,1,0:T(8,128)(2,1)S(1)}, u32[]{:S(2)}, u32[]{:S(2)}) async-start(bf16[128,32,256]{2,1,0:T(8,128)(2,1)} %after.12), calls=%async_computation.4 | async-start | bytes 4194304 | tf_op jit(solution)/shard_map/all_to_all | solution.py:128
  294.5 34.9 %collective-permute-start.3 = (bf16[2,16,16,512]{3,2,1,0:T(8,128)(2,1)}, bf16[2,16,16,512]{3,2,1,0:T(8,128)(2,1)S(1)}, u32[]{:S(2)}, u32[]{:S(2)}) collective-permute-start(bf16[2,16,16,512]{3,2,1,0:T(8,128)(2,1)} %copy-done.21), channel_id=1, source_target_pairs={{0,8},{1,9},{2,10},{3,11},{4,12},{5,13},{6,14},{7,15},{8,0},{9,1},... | collective-permute-start | bytes 1572872 | tf_op jit(solution)/shard_map/ppermute | solution.py:140
  329.4 2.0 copy-start.18
  331.4 1.3 copy-start.3
  332.7 29.2 %all-to-all-start.5 = ((bf16[128,32,128]{2,1,0:T(8,128)(2,1)}), bf16[128,32,128]{2,1,0:T(8,128)(2,1)S(1)}, u32[]{:S(2)}, u32[]{:S(2)}) async-start(bf16[128,32,128]{2,1,0:T(8,128)(2,1)} %after.13), calls=%async_computation.5 | async-start | bytes 2097152 | tf_op jit(solution)/shard_map/all_to_all | solution.py:128
  336.3 37.9 %collective-permute-start.4 = (bf16[3,16,16,512]{3,2,1,0:T(8,128)(2,1)}, bf16[3,16,16,512]{3,2,1,0:T(8,128)(2,1)S(1)}, u32[]{:S(2)}, u32[]{:S(2)}) collective-permute-start(bf16[3,16,16,512]{3,2,1,0:T(8,128)(2,1)} %copy-done.30), channel_id=1, source_target_pairs={{0,8},{1,9},{2,10},{3,11},{4,12},{5,13},{6,14},{7,15},{8,0},{9,1},... | collective-permute-start | bytes 2359304 | tf_op jit(solution)/shard_map/ppermute | solution.py:140
  342.5 1.4 copy-start.10
  374.1 0.9 copy-start.14
  375.0 29.6 %all-to-all-start.6 = ((bf16[128,32,128]{2,1,0:T(8,128)(2,1)}), bf16[128,32,128]{2,1,0:T(8,128)(2,1)S(1)}, u32[]{:S(2)}, u32[]{:S(2)}) async-start(bf16[128,32,128]{2,1,0:T(8,128)(2,1)} %after.14), calls=%async_computation.6 | async-start | bytes 2097152 | tf_op jit(solution)/shard_map/all_to_all | solution.py:128
  378.6 38.0 %collective-permute-start.6 = (bf16[3,16,16,512]{3,2,1,0:T(8,128)(2,1)}, bf16[3,16,16,512]{3,2,1,0:T(8,128)(2,1)}, u32[]{:S(2)}, u32[]{:S(2)}) collective-permute-start(bf16[3,16,16,512]{3,2,1,0:T(8,128)(2,1)} %get-tuple-element.38), channel_id=1, source_target_pairs={{0,8},{1,9},{2,10},{3,11},{4,12},{5,13},{6,14},{7,15},{8,0},{9,1},... | collective-permute-start | bytes 2359304 | tf_op jit(solution)/shard_map/ppermute | solution.py:140
  404.6 3.1 copy-start.4
  407.7 8.8 %copy-start.12 = (bf16[2,16,16,512]{3,2,1,0:T(8,128)(2,1)S(1)}, bf16[2,16,16,512]{3,2,1,0:T(8,128)(2,1)}, u32[]{:S(2)}) copy-start(bf16[2,16,16,512]{3,2,1,0:T(8,128)(2,1)} %copy-done.11) | copy-start | bytes 1572868
  407.7 8.8 %copy-start.15 = (bf16[3,16,16,512]{3,2,1,0:T(8,128)(2,1)S(1)}, bf16[3,16,16,512]{3,2,1,0:T(8,128)(2,1)}, u32[]{:S(2)}) copy-start(bf16[3,16,16,512]{3,2,1,0:T(8,128)(2,1)} %copy-done.14) | copy-start | bytes 2359300
  407.7 8.8 %copy-start.19 = (bf16[2,16,16,512]{3,2,1,0:T(8,128)(2,1)S(1)}, bf16[2,16,16,512]{3,2,1,0:T(8,128)(2,1)}, u32[]{:S(2)}) copy-start(bf16[2,16,16,512]{3,2,1,0:T(8,128)(2,1)} %copy-done.18) | copy-start | bytes 1572868
  424.9 120.4 %all-to-all-start.7 = ((bf16[128,48,512]{2,1,0:T(8,128)(2,1)}), bf16[128,48,512]{2,1,0:T(8,128)(2,1)}, u32[]{:S(2)}, u32[]{:S(2)}) async-start(bf16[128,48,512]{2,1,0:T(8,128)(2,1)} %bitcast.77), calls=%async_computation.7 | async-start | bytes 12582912 | tf_op jit(solution)/shard_map/all_to_all | solution.py:128
  429.6 113.4 %collective-permute-start.5 = (bf16[8,16,16,512]{3,2,1,0:T(8,128)(2,1)S(1)}, bf16[8,16,16,512]{3,2,1,0:T(8,128)(2,1)S(1)}, u32[]{:S(2)}, u32[]{:S(2)}) collective-permute-start(bf16[8,16,16,512]{3,2,1,0:T(8,128)(2,1)S(1)} %grad_b.5.refs_1_), channel_id=1, source_target_pairs={{0,8},{1,9},{2,10},{3,11},{4,12},{5,13},{6,14},{7,15},{8,0},{9,1},... | collective-permute-start | bytes 6291464 | tf_op jit(solution)/shard_map/ppermute | solution.py:140
  543.0 1.3 copy-start.5
  545.2 1.6 copy-start.6
  546.8 1.6 copy-start.31
  550.8 4.6 copy-start.32
  550.8 4.6 copy-start.34
  550.8 4.7 copy-start.23
  550.8 4.7 copy-start.25
  550.8 4.7 copy-start.27
  550.8 4.7 copy-start.29
  550.8 30.3 %all-to-all-start.8 = ((bf16[128,16,512]{2,1,0:T(8,128)(2,1)}), bf16[128,16,512]{2,1,0:T(8,128)(2,1)S(1)}, u32[]{:S(2)}, u32[]{:S(2)}) async-start(bf16[128,16,512]{2,1,0:T(8,128)(2,1)} %bitcast.79), calls=%async_computation.8 | async-start | bytes 4194304 | tf_op jit(solution)/shard_map/all_to_all | solution.py:128
  579.7 1.3 copy-start.17
  603.2 14.3 %all-to-all-start.10 = ((bf16[16,8,768]{2,1,0:T(8,128)(2,1)}), bf16[16,8,768]{2,1,0:T(8,128)(2,1)S(1)}, u32[]{:S(2)}, u32[]{:S(2)}) async-start(bf16[16,8,768]{2,1,0:T(8,128)(2,1)} %broadcast_in_dim.2), calls=%async_computation.10 | async-start | bytes 393216 | tf_op jit(solution)/shard_map/all_to_all | solution.py:519
  (4 other events, 2.5 us)
